TPU v7x, 768 devices: a whole 4x8x12 slice. The times are simulated.
768 devices in a mesh: grp: 16 (over z_hi, x), tp: 48 (over y, z_lo, core).
Axes of the slice: x: 4, y: 8, z: 12 (z_hi: 4, z_lo: 3; z = z_hi * 3 + z_lo), core: 2. Of those that a mesh axis runs over, the one named last changes fastest.
Arguments:
- tokens: bfloat16 [3072, 4096], P('grp'), may hold values from -6 to 6
- gate_weight: bfloat16 [4096, 18432], P(None, 'tp'), may hold values from -0.09375 to 0.09375
- up_weight: bfloat16 [4096, 18432], P(None, 'tp'), may hold values from -0.09375 to 0.09375
- down_weight: bfloat16 [18432, 4096], P('tp'), may hold values from -0.0625 to 0.0625
- active: int32 [3072, 18432], P('grp', 'tp'), may hold values 0 or 1
- kv_blocks: bfloat16 [256, 96, 2048], P('grp', 'tp'), may hold values from -6 to 6
- lengths: int32 [256], P('grp'), may hold values from 1 to 96
- dest: int32 [16, 16], replicated, may hold values from 0 to 15, each once within a row
Outputs:
- ffn_out: bfloat16 [3072, 4096], P('grp')
- cache: bfloat16 [256, 96, 2048], P('grp', 'tp')
Inputs may be any that keep to these rules, and one draw needn't show every extreme that they name: Each row of dest names every decode group exactly once.
All inputs are finite; a program needn't handle non-finite values. No bound on the sum of `active` on one device may be relied on, other than what follows from the above.
Results may differ from a plain program's by a relative error of at most 0.005.
Values may be sent and summed in bfloat16 or wider, within the bound.
No kernel may reach another device: no remote copies, remote signals or barrier semaphores. Data moves between devices by JAX's collectives and lax.ppermute only.
A program may use at most 64 MiB of HBM per device.

v0:
```python
import jax
import jax.numpy as jnp
from jax import lax
from jax.sharding import PartitionSpec as P


def shards(tokens, gate_weight, up_weight, down_weight, active, kv_blocks, lengths, dest):
    gate = jnp.dot(tokens, gate_weight, preferred_element_type=jnp.float32)
    up = jnp.dot(tokens, up_weight, preferred_element_type=jnp.float32)
    hidden = (jax.nn.silu(gate) * up * active.astype(jnp.float32)).astype(jnp.bfloat16)
    partial_sum = jnp.dot(hidden, down_weight, preferred_element_type=jnp.float32)
    ffn_out = lax.psum(partial_sum, "tp").astype(jnp.bfloat16)
    pos_dev = kv_blocks.shape[1]
    position = lax.axis_index("tp") * pos_dev + lax.iota(jnp.int32, pos_dev)
    keep = position[None, :] < lengths[:, None]
    masked = jnp.where(keep[:, :, None], kv_blocks, jnp.zeros_like(kv_blocks))
    mine = lax.axis_index("grp")
    own_row = lax.dynamic_slice_in_dim(dest, mine, 1, 0)[0]
    order = jnp.argsort(own_row)
    send_buffer = jnp.take(masked, order, axis=0)
    cache = lax.all_to_all(send_buffer, "grp", split_axis=0, concat_axis=0, tiled=True)
    return (ffn_out, cache)


def solution(mesh):
    return jax.shard_map(
        shards,
        mesh=mesh,
        in_specs=(
            P("grp", None),
            P(None, "tp"),
            P(None, "tp"),
            P("tp", None),
            P("grp", "tp"),
            P("grp", "tp", None),
            P("grp"),
            P(),
        ),
        out_specs=(P("grp", None), P("grp", "tp", None)),
        check_vma=False,
    )
```

profile of v0, /device:TPU:192, one launch (start us, length us, event | category | flops | bytes accessed | tf_op | source)
XLA Modules:
  0.0 281.8 jit_solution(2067920726262933389)
XLA Ops:
  0.6 0.0 copy-start
  0.7 0.8 dynamic-slice_bitcast_fusion
  1.5 1.2 sort.17
  2.8 0.7 broadcast_compare_fusion
  3.5 1.1 broadcast_select_fusion.1
  4.6 0.8 gather_fusion
  5.4 0.8 broadcast_select_fusion
  6.3 14.8 %all-to-all-start = ((bf16[16,2,2048]{2,1,0:T(2,128)(2,1)}), bf16[16,2,2048]{2,1,0:T(2,128)(2,1)}, u32[]{:S(2)}, u32[]{:S(2)}) async-start(bf16[16,2,2048]{2,1,0:T(2,128)(2,1)} %broadcast_select_fusion), calls=%async_computation | async-start | bytes 262144 | tf_op jit(solution)/shard_map/all_to_all | solution.py:21
  21.1 3.3 %fusion.11 = f32[192,384]{1,0:T(8,128)S(1)} fusion(bf16[192,4096]{1,0:T(8,128)(2,1)} %param.8, bf16[4096,384]{1,0:T(8,128)(2,1)} %param.9), kind=kOutput, calls=%fused_computation.21 | convolution fusion | flops 603979776 | bytes 5013504 | tf_op jit(solution)/shard_map/dot_general | solution.py:8
  24.4 0.0 copy-done
  24.5 6.0 %fusion.2 = f32[192,4096]{1,0:T(8,128)} fusion(bf16[384,4096]{1,0:T(8,128)(2,1)S(1)} %copy-done, bf16[192,4096]{1,0:T(8,128)(2,1)} %param.8, bf16[4096,384]{1,0:T(8,128)(2,1)} %param.10, s32[192,384]{1,0:T(8,128)} %param.12, f32[192,384]{1,0:T(8,128)S(1)} %fusion.11), kind=kOutput, calls=%fused_computation.4 | convolution fusion | flops 1208549376 | bytes 11599872 | tf_op jit(solution)/shard_map/dot_general | solution.py:11
  30.4 249.7 %all-reduce.1 = bf16[192,4096]{1,0:T(8,128)(2,1)} all-reduce(f32[192,4096]{1,0:T(8,128)} %fusion.2), channel_id=1, replica_groups=mesh['grp'=16,'tp'=48] {'tp'}, use_global_device_ids=true, to_apply=%region_0.1 | all-reduce | flops 786432 | bytes 4718592 | tf_op jit(solution)/shard_map/psum | solution.py:12
  280.2 0.0 all-to-all-done
  280.2 1.7 copy.13
  (5 shorter events, 0.0 us)
Async XLA Ops:
  0.6 23.8 %copy-start = (bf16[384,4096]{1,0:T(8,128)(2,1)S(1)}, bf16[384,4096]{1,0:T(8,128)(2,1)}, u32[]{:S(2)}) copy-start(bf16[384,4096]{1,0:T(8,128)(2,1)} %param.11) | copy-start | bytes 9437188
  6.3 273.9 %all-to-all-start = ((bf16[16,2,2048]{2,1,0:T(2,128)(2,1)}), bf16[16,2,2048]{2,1,0:T(2,128)(2,1)}, u32[]{:S(2)}, u32[]{:S(2)}) async-start(bf16[16,2,2048]{2,1,0:T(2,128)(2,1)} %broadcast_select_fusion), calls=%async_computation | async-start | bytes 262144 | tf_op jit(solution)/shard_map/all_to_all | solution.py:21
where the time goes:
time: 282 us
  blocking collectives  250 us (89%)
  starting transfers between devices  14.8 us (5%)
  matrix products  9.31 us (3%)
  other arithmetic  3.94 us (1%)
  local copies, waits for them, and re-layouts  3.32 us (1%)
    psum x1, blocking collectives, shards(): ffn_out = lax.psum(partial_sum, 'tp').astype(jnp.bfloat16)  250 us
    all_to_all x1, starting transfers between devices, shards(): lax.all_to_all(send_buffer, 'grp', split_axis=0, concat_axis=0, tiled=True)  14.8 us
    dot_general x1, matrix products, shards(): jnp.dot(hidden, down_weight, preferred_element_type=jnp.float32)  5.97 us
  transfers between devices with their start and end apart: 1, of which 0 were waited for; matrix products, arithmetic and copies ran while one was open for 3% of the time, Pallas kernels for 0%

commit v1 on v0

v1 whole, which is shorter than its diff:
```python
import jax
import jax.numpy as jnp
from jax import lax
from jax.sharding import Mesh, PartitionSpec as P

GRP = ("zh", "x")
TP = ("y", "zl", "core")
RING = ("y", "zl")
SWAP = [(0, 1), (1, 0)]


def shards(tokens, gate_weight, up_weight, down_weight, active, kv_blocks, lengths, dest):
    bf16, f32 = jnp.bfloat16, jnp.float32
    core = lax.axis_index("core")

    pos_dev = kv_blocks.shape[1]
    position = lax.axis_index(TP) * pos_dev + lax.iota(jnp.int32, pos_dev)
    keep = position[None, :] < lengths[:, None]
    masked = jnp.where(keep[:, :, None], kv_blocks, jnp.zeros_like(kv_blocks))
    mine = lax.axis_index(GRP)
    own_row = lax.dynamic_slice_in_dim(dest, mine, 1, 0)[0]
    order = jnp.argsort(own_row)
    send_buffer = jnp.take(masked, order, axis=0)
    cache = lax.all_to_all(send_buffer, GRP, split_axis=0, concat_axis=0, tiled=True)

    gate = jnp.dot(tokens, gate_weight, preferred_element_type=f32)
    up = jnp.dot(tokens, up_weight, preferred_element_type=f32)
    hidden = (jax.nn.silu(gate) * up * active.astype(f32)).astype(bf16)

    rows, width = tokens.shape[0], down_weight.shape[1] // 2
    theirs = lax.dynamic_slice_in_dim(down_weight, (1 - core) * width, width, 1)
    ours = lax.dynamic_slice_in_dim(down_weight, core * width, width, 1)
    away = jnp.dot(hidden, theirs, preferred_element_type=f32).astype(bf16)
    arrived = lax.ppermute(away, "core", SWAP)
    total = jnp.dot(hidden, ours, preferred_element_type=f32) + arrived.astype(f32)

    chips = 24
    parts = total.astype(bf16).reshape(chips, rows // chips, width)
    parts = lax.all_to_all(parts, RING, split_axis=0, concat_axis=0, tiled=True)
    summed = jnp.sum(parts.astype(f32), axis=0).astype(bf16)

    spread = jnp.broadcast_to(summed[None], (chips, *summed.shape))
    half = lax.all_to_all(spread, RING, split_axis=0, concat_axis=0, tiled=True)
    half = half.reshape(rows, width)
    other = lax.ppermute(half, "core", SWAP)
    low = jnp.where(core == 0, half, other)
    high = jnp.where(core == 0, other, half)
    return (jnp.concatenate([low, high], axis=1), cache)


def solution(mesh):
    fine = Mesh(mesh.devices.reshape(4, 4, 8, 3, 2), GRP + TP)
    return jax.shard_map(
        shards,
        mesh=fine,
        in_specs=(
            P(GRP, None),
            P(None, TP),
            P(None, TP),
            P(TP, None),
            P(GRP, TP),
            P(GRP, TP, None),
            P(GRP),
            P(),
        ),
        out_specs=(P(GRP, None), P(GRP, TP, None)),
        check_vma=False,
    )
```

time: 282 us -> 113 us (0.40)
  the two profiles are of different devices: /device:TPU:192 before, /device:TPU:1 now
where the time goes in v1:
time: 113 us; the launch traced here: 112 us
  starting transfers between devices  41.1 us (36%)
  waiting for transfers between devices  29.3 us (26%)
  blocking collectives  23.2 us (21%)
  matrix products  7.65 us (7%)
  other arithmetic  6.39 us (6%)
  local copies, waits for them, and re-layouts  3.57 us (3%)
    all_to_all x1, blocking collectives, shards(): parts = lax.all_to_all(parts, RING, split_axis=0, concat_axis=0, tiled=True)  23.2 us
    all_to_all x1, waiting for transfers between devices, shards(): half = lax.all_to_all(spread, RING, split_axis=0, concat_axis=0, tiled=True)  15.5 us
    all_to_all x1, starting transfers between devices, shards(): lax.all_to_all(send_buffer, GRP, split_axis=0, concat_axis=0, tiled=True)  14.3 us
    ppermute x1, starting transfers between devices, shards(): arrived = lax.ppermute(away, 'core', SWAP)  12.4 us
    all_to_all x1, waiting for transfers between devices, shards(): lax.all_to_all(send_buffer, GRP, split_axis=0, concat_axis=0, tiled=True)  11.6 us
    all_to_all x1, starting transfers between devices, shards(): half = lax.all_to_all(spread, RING, split_axis=0, concat_axis=0, tiled=True)  7.51 us
    ppermute x1, starting transfers between devices, shards(): other = lax.ppermute(half, 'core', SWAP)  6.88 us
    dot_general x1, matrix products, shards(): gate = jnp.dot(tokens, gate_weight, preferred_element_type=f32)  3.49 us
  transfers between devices with their start and end apart: 4, of which 3 were waited for; matrix products, arithmetic and copies ran while one was open for 3% of the time, Pallas kernels for 0%

profile of v1, /device:TPU:1, one launch (start us, length us, event | category | flops | bytes accessed | tf_op | source)
XLA Modules:
  0.0 112.1 jit_solution(7318442622397515789)
XLA Ops:
  0.6 0.0 copy-start
  0.7 0.0 copy-start.1
  0.7 0.0 copy-start.4
  0.7 0.0 copy-start.5
  0.7 3.5 %fusion.13 = f32[192,384]{1,0:T(8,128)S(1)} fusion(bf16[192,4096]{1,0:T(8,128)(2,1)} %param.8, bf16[4096,384]{1,0:T(8,128)(2,1)} %param.9), kind=kOutput, calls=%fused_computation.24 | convolution fusion | flops 603979776 | bytes 5013504 | tf_op jit(solution)/shard_map/dot_general | solution.py:26
  4.2 0.0 copy-done.1
  4.2 0.4 copy-done.4
  4.6 0.0 copy-done.5
  4.6 1.0 fusion.9
  5.6 0.0 copy-done
  5.6 1.5 %convolution_convert_fusion = bf16[192,2048]{1,0:T(8,128)(2,1)} fusion(bf16[192,384]{1,0:T(8,128)(2,1)S(1)} %fusion.9, bf16[384,4096]{1,0:T(8,128)(2,1)S(1)} %copy-done, s32[]{:T(128)S(6)} %select_n.36), kind=kOutput, calls=%fused_computation.1 | convolution fusion | flops 302383104 | bytes 2506756 | tf_op jit(solution)/shard_map/dot_general | solution.py:33
  7.1 12.4 %collective-permute-start = (bf16[192,2048]{1,0:T(8,128)(2,1)}, bf16[192,2048]{1,0:T(8,128)(2,1)}, u32[]{:S(2)}, u32[]{:S(2)}) collective-permute-start(bf16[192,2048]{1,0:T(8,128)(2,1)} %convolution_convert_fusion), channel_id=1, source_target_pairs={{0,1},{1,0},{2,3},{3,2},{4,5},{5,4},{6,7},{7,6},{8,9},{9,8},{10,11... | collective-permute-start | bytes 2359304 | tf_op jit(solution)/shard_map/ppermute | solution.py:34
  19.5 2.2 %collective-permute-done = bf16[192,2048]{1,0:T(8,128)(2,1)} collective-permute-done((bf16[192,2048]{1,0:T(8,128)(2,1)}, bf16[192,2048]{1,0:T(8,128)(2,1)}, u32[]{:S(2)}, u32[]{:S(2)}) %collective-permute-start) | collective-permute-done | bytes 786464 | tf_op jit(solution)/shard_map/ppermute | solution.py:34
  21.7 1.7 %fusion.5 = bf16[24,8,2048]{2,1,0:T(8,128)(2,1)S(1)} fusion(bf16[192,2048]{1,0:T(8,128)(2,1)} %collective-permute-done, bf16[192,384]{1,0:T(8,128)(2,1)S(1)} %fusion.9, bf16[384,4096]{1,0:T(8,128)(2,1)S(1)} %copy-done, s32[]{:T(128)S(6)} %select_n.35), kind=kOutput, calls=%fused_computation.7 | convolution fusion | flops 303169536 | bytes 3293188 | tf_op jit(solution)/shard_map/dot_general | solution.py:35
  23.4 23.2 %all_to_all.15 = bf16[24,8,2048]{2,1,0:T(8,128)(2,1)} all-to-all(bf16[24,8,2048]{2,1,0:T(8,128)(2,1)S(1)} %fusion.5), channel_id=1, replica_groups=mesh['zh'=4,'x'=4,'y'=8,'zl'=3,'core'=2] {'y','zl'}, dimensions={0} | all-to-all | bytes 1572864 | tf_op jit(solution)/shard_map/all_to_all | solution.py:39
  46.7 1.3 %reduce_sum.12 = bf16[8,2048]{1,0:T(8,128)(2,1)S(1)} reduce(bf16[24,8,2048]{2,1,0:T(8,128)(2,1)} %all_to_all.15, bf16[]{:T(256)} %constant.13.clone.1), dimensions={0}, to_apply=%region_0.1 | reduce | flops 376832 | bytes 819202 | tf_op jit(solution)/shard_map/reduce_sum | solution.py:40
  48.0 1.0 broadcast_in_dim.32
  48.9 7.5 %all-to-all-start.1 = ((bf16[24,8,2048]{2,1,0:T(8,128)(2,1)}), bf16[24,8,2048]{2,1,0:T(8,128)(2,1)}, u32[]{:S(2)}, u32[]{:S(2)}) async-start(bf16[24,8,2048]{2,1,0:T(8,128)(2,1)} %broadcast_in_dim.32), calls=%async_computation.1 | async-start | bytes 1572864 | tf_op jit(solution)/shard_map/all_to_all | solution.py:43
  56.5 0.7 fusion.12
  57.2 1.2 %sort.17 = (s32[16]{0:T(128)}, s32[16]{0:T(128)S(1)}) sort(s32[16]{0:T(128)S(1)} %fusion.12, s32[16]{0:T(128)S(1)} %iota.9), dimensions={0}, to_apply=%region_1.2 | sort | flops 64 | bytes 256 | tf_op jit(solution)/shard_map/jit(argsort)/sort | solution.py:22
  58.4 0.1 broadcast_compare_fusion
  58.5 0.2 broadcast_select_fusion.3
  58.7 0.8 gather_fusion
  59.5 15.5 %all-to-all-done.1 = bf16[24,8,2048]{2,1,0:T(8,128)(2,1)} async-done(((bf16[24,8,2048]{2,1,0:T(8,128)(2,1)}), bf16[24,8,2048]{2,1,0:T(8,128)(2,1)}, u32[]{:S(2)}, u32[]{:S(2)}) %all-to-all-start.1) | async-done | bytes 786464 | tf_op jit(solution)/shard_map/all_to_all | solution.py:43
  75.0 6.9 %collective-permute-start.1 = (bf16[192,2048]{1,0:T(8,128)(2,1)}, bf16[192,2048]{1,0:T(8,128)(2,1)}, u32[]{:S(2)}, u32[]{:S(2)}) collective-permute-start(bf16[192,2048]{1,0:T(8,128)(2,1)} %bitcast.1), channel_id=1, source_target_pairs={{0,1},{1,0},{2,3},{3,2},{4,5},{5,4},{6,7},{7,6},{8,9},{9,8},{10,11... | collective-permute-start | bytes 2359304 | tf_op jit(solution)/shard_map/ppermute | solution.py:45
  81.9 0.8 broadcast_select_fusion.2
  82.8 14.3 %all-to-all-start.2 = ((bf16[16,2,2048]{2,1,0:T(2,128)(2,1)}), bf16[16,2,2048]{2,1,0:T(2,128)(2,1)S(1)}, u32[]{:S(2)}, u32[]{:S(2)}) async-start(bf16[16,2,2048]{2,1,0:T(2,128)(2,1)} %broadcast_select_fusion.2), calls=%async_computation.2 | async-start | bytes 262144 | tf_op jit(solution)/shard_map/all_to_all | solution.py:24
  97.1 11.6 %all-to-all-done.2 = bf16[16,2,2048]{2,1,0:T(2,128)(2,1)S(1)} async-done(((bf16[16,2,2048]{2,1,0:T(2,128)(2,1)}), bf16[16,2,2048]{2,1,0:T(2,128)(2,1)S(1)}, u32[]{:S(2)}, u32[]{:S(2)}) %all-to-all-start.2) | async-done | bytes 131104 | tf_op jit(solution)/shard_map/all_to_all | solution.py:24
  108.7 0.0 collective-permute-done.1
  108.7 1.5 %broadcast_select_fusion.1 = (bf16[192,2048]{1,0:T(8,128)(2,1)S(1)}, bf16[192,2048]{1,0:T(8,128)(2,1)S(1)}) fusion(bf16[192,2048]{1,0:T(8,128)(2,1)} %collective-permute-done.1, pred[]{:T(512)S(6)} %eq.4, bf16[24,8,2048]{2,1,0:T(8,128)(2,1)} %all-to-all-done.1), kind=kLoop, calls=%fused_computation.12 | loop fusion | flops 786432 | bytes 3145729 | tf_op jit(solution)/shard_map/jit(_where)/select_n | solution.py:46
  110.2 1.3 %pad_maximum_fusion = bf16[192,4096]{1,0:T(8,128)(2,1)} fusion(bf16[192,2048]{1,0:T(8,128)(2,1)S(1)} %get-tuple-element.5, bf16[192,2048]{1,0:T(8,128)(2,1)S(1)} %get-tuple-element.4), kind=kLoop, calls=%fused_computation.2 | loop fusion | flops 3145728 | bytes 3145728 | tf_op jit(solution)/shard_map/concatenate | solution.py:48
  111.4 0.7 copy.11
  (9 shorter events, 0.0 us)
Async XLA Ops:
  0.6 5.0 %copy-start = (bf16[384,4096]{1,0:T(8,128)(2,1)S(1)}, bf16[384,4096]{1,0:T(8,128)(2,1)}, u32[]{:S(2)}) copy-start(bf16[384,4096]{1,0:T(8,128)(2,1)} %param.11) | copy-start | bytes 9437188
  0.7 3.5 %copy-start.1 = (bf16[192,4096]{1,0:T(8,128)(2,1)S(1)}, bf16[192,4096]{1,0:T(8,128)(2,1)}, u32[]{:S(2)}) copy-start(bf16[192,4096]{1,0:T(8,128)(2,1)} %param.8) | copy-start | bytes 4718596
  0.7 3.9 %copy-start.4 = (bf16[4096,384]{1,0:T(8,128)(2,1)S(1)}, bf16[4096,384]{1,0:T(8,128)(2,1)}, u32[]{:S(2)}) copy-start(bf16[4096,384]{1,0:T(8,128)(2,1)} %param.10) | copy-start | bytes 9437188
  0.7 3.9 %copy-start.5 = (s32[192,384]{1,0:T(8,128)S(1)}, s32[192,384]{1,0:T(8,128)}, u32[]{:S(2)}) copy-start(s32[192,384]{1,0:T(8,128)} %param.12) | copy-start | bytes 884740
  7.1 14.7 %collective-permute-start = (bf16[192,2048]{1,0:T(8,128)(2,1)}, bf16[192,2048]{1,0:T(8,128)(2,1)}, u32[]{:S(2)}, u32[]{:S(2)}) collective-permute-start(bf16[192,2048]{1,0:T(8,128)(2,1)} %convolution_convert_fusion), channel_id=1, source_target_pairs={{0,1},{1,0},{2,3},{3,2},{4,5},{5,4},{6,7},{7,6},{8,9},{9,8},{10,11... | collective-permute-start | bytes 2359304 | tf_op jit(solution)/shard_map/ppermute | solution.py:34
  46.7 11.8 %copy-start.3 = (s32[16]{0:T(128)S(1)}, s32[16]{0:T(128)}, u32[]{:S(2)}) copy-start(s32[16]{0:T(128)} %param.14) | copy-start | bytes 196
  46.7 11.8 %copy-start.2 = (bf16[16,2,2048]{2,1,0:T(2,128)(2,1)S(1)}, bf16[16,2,2048]{2,1,0:T(2,128)(2,1)}, u32[]{:S(2)}) copy-start(bf16[16,2,2048]{2,1,0:T(2,128)(2,1)} %param.13) | copy-start | bytes 393220
  48.9 26.1 %all-to-all-start.1 = ((bf16[24,8,2048]{2,1,0:T(8,128)(2,1)}), bf16[24,8,2048]{2,1,0:T(8,128)(2,1)}, u32[]{:S(2)}, u32[]{:S(2)}) async-start(bf16[24,8,2048]{2,1,0:T(8,128)(2,1)} %broadcast_in_dim.32), calls=%async_computation.1 | async-start | bytes 1572864 | tf_op jit(solution)/shard_map/all_to_all | solution.py:43
  75.0 33.7 %collective-permute-start.1 = (bf16[192,2048]{1,0:T(8,128)(2,1)}, bf16[192,2048]{1,0:T(8,128)(2,1)}, u32[]{:S(2)}, u32[]{:S(2)}) collective-permute-start(bf16[192,2048]{1,0:T(8,128)(2,1)} %bitcast.1), channel_id=1, source_target_pairs={{0,1},{1,0},{2,3},{3,2},{4,5},{5,4},{6,7},{7,6},{8,9},{9,8},{10,11... | collective-permute-start | bytes 2359304 | tf_op jit(solution)/shard_map/ppermute | solution.py:45
  82.8 25.9 %all-to-all-start.2 = ((bf16[16,2,2048]{2,1,0:T(2,128)(2,1)}), bf16[16,2,2048]{2,1,0:T(2,128)(2,1)S(1)}, u32[]{:S(2)}, u32[]{:S(2)}) async-start(bf16[16,2,2048]{2,1,0:T(2,128)(2,1)} %broadcast_select_fusion.2), calls=%async_computation.2 | async-start | bytes 262144 | tf_op jit(solution)/shard_map/all_to_all | solution.py:24

commit v2 on v1

v2 whole, which is shorter than its diff:
```python
import jax
import jax.numpy as jnp
from jax import lax
from jax.experimental import pallas as pl
from jax.experimental.pallas import tpu as pltpu
from jax.sharding import Mesh, PartitionSpec as P

GRP = ("zh", "x")
TP = ("y", "zl", "core")
RING = ("y", "zl")
SWAP = [(0, 1), (1, 0)]
SIDE = 4
CHIPS = 24

bf16, f32 = jnp.bfloat16, jnp.float32
MARK = jax.ShapeDtypeStruct((8, 128), f32)
VMEM = pl.BlockSpec(memory_space=pltpu.VMEM)
SMEM = pl.BlockSpec(memory_space=pltpu.SMEM)
LATER = pl.BlockSpec(memory_space=pl.ANY)


def call(body, out_shape, in_specs, out_specs, cost, **more):
    return pl.pallas_call(
        body,
        out_shape=out_shape,
        in_specs=in_specs,
        out_specs=out_specs,
        cost_estimate=pl.CostEstimate(flops=cost, bytes_accessed=cost, transcendentals=0),
        compiler_params=pltpu.CompilerParams(vmem_limit_bytes=16 * 2**20),
        **more,
    )


def sort_body(place_ref, dest_ref, lengths_ref, kv_ref, after_ref, *out_refs):
    x, mine, first = place_ref[0], place_ref[1], place_ref[2]
    row = lax.broadcasted_iota(jnp.int32, kv_ref.shape[1:], 0) + first
    for r in range(kv_ref.shape[0]):
        d = dest_ref[mine, r]
        value = kv_ref[r]
        value = jnp.where(row < lengths_ref[r], value, jnp.zeros_like(value))
        step = lax.rem(lax.rem(d, SIDE) - x + SIDE, SIDE)
        for k in range(SIDE):

            @pl.when(step == k)
            def _():
                out_refs[k][lax.div(d, SIDE)] = value


def turn_body(place_ref, *refs):
    x, zh = place_ref[0], place_ref[3]
    in_refs, out_refs = refs[:SIDE], refs[-SIDE:]
    for k in range(SIDE):
        source = lax.rem(x - k + SIDE, SIDE)
        for j in range(SIDE):
            out_refs[j][source] = in_refs[k][lax.rem(zh + j, SIDE)]


def lay_body(place_ref, *refs):
    zh = place_ref[3]
    in_refs, out_ref, mark_ref = refs[:SIDE], refs[-2], refs[-1]
    mark_ref[...] = jnp.zeros_like(mark_ref)
    for j in range(SIDE):
        source = lax.rem(zh - j + SIDE, SIDE)
        for k in range(SIDE):
            out_ref[source * SIDE + k] = in_refs[j][k]


def add_body(own_ref, arrived_ref, out_ref, mark_ref):
    mark_ref[...] = jnp.zeros_like(mark_ref)
    out_ref[...] = (own_ref[...] + arrived_ref[...].astype(f32)).astype(bf16)


def sum_body(*refs):
    parts_ref, out_ref, mark_ref = refs[0], refs[-2], refs[-1]
    mark_ref[...] = jnp.zeros_like(mark_ref)
    total = parts_ref[0].astype(f32)
    for i in range(1, CHIPS):
        total += parts_ref[i].astype(f32)
    total = total.astype(bf16)
    for i in range(CHIPS):
        out_ref[i] = total


def join_body(core_ref, half_ref, other_ref, out_ref):
    width = half_ref.shape[1]
    for core in range(2):

        @pl.when(core_ref[0] == core)
        def _():
            out_ref[:, core * width : (core + 1) * width] = half_ref[...]
            out_ref[:, (1 - core) * width : (2 - core) * width] = other_ref[...]


def after(value, mark):
    return pl.pallas_call(
        lambda value_ref, mark_ref, out_ref: None,
        out_shape=jax.ShapeDtypeStruct(value.shape, value.dtype),
        in_specs=[LATER] * 2,
        out_specs=LATER,
        input_output_aliases={0: 0},
    )(value, mark)


def shift(value, axis, k):
    if k == 0:
        return value
    return lax.ppermute(value, axis, [(i, (i + k) % SIDE) for i in range(SIDE)])


def shards(tokens, gate_weight, up_weight, down_weight, active, kv_blocks, lengths, dest):
    core = lax.axis_index("core")
    x, zh = lax.axis_index("x"), lax.axis_index("zh")
    place = jnp.stack([x, lax.axis_index(GRP), lax.axis_index(TP) * kv_blocks.shape[1], zh])

    gate = jnp.dot(tokens, gate_weight, preferred_element_type=f32)
    up = jnp.dot(tokens, up_weight, preferred_element_type=f32)
    hidden = (jax.nn.silu(gate) * up * active.astype(f32)).astype(bf16)

    rows, width = tokens.shape[0], down_weight.shape[1] // 2
    theirs = lax.dynamic_slice_in_dim(down_weight, (1 - core) * width, width, 1)
    ours = lax.dynamic_slice_in_dim(down_weight, core * width, width, 1)
    away = jnp.dot(hidden, theirs, preferred_element_type=f32).astype(bf16)
    arrived = lax.ppermute(away, "core", SWAP)
    own = jnp.dot(hidden, ours, preferred_element_type=f32)
    total, mark = call(
        add_body, [jax.ShapeDtypeStruct((rows, width), bf16), MARK], [VMEM] * 2, [VMEM] * 2, 10**6
    )(own, arrived)

    parts = total.reshape(CHIPS, rows // CHIPS, width)
    parts = lax.all_to_all(parts, RING, split_axis=0, concat_axis=0, tiled=True)

    slots = jax.ShapeDtypeStruct((SIDE, *kv_blocks.shape[1:]), bf16)
    bundles = call(sort_body, [slots] * SIDE, [SMEM, SMEM, SMEM, VMEM, LATER], [VMEM] * SIDE, 10**6)(
        place, dest, lengths, kv_blocks, mark
    )
    bundles = [shift(b, "x", k) for k, b in enumerate(bundles)]

    spread, mark = call(
        sum_body, [jax.ShapeDtypeStruct(parts.shape, bf16), MARK], [VMEM] + [LATER] * SIDE, [VMEM] * 2, 10**6
    )(parts, *bundles)

    half = lax.all_to_all(spread, RING, split_axis=0, concat_axis=0, tiled=True).reshape(rows, width)

    bundles = call(turn_body, [slots] * SIDE, [SMEM] + [VMEM] * SIDE + [LATER], [VMEM] * SIDE, 10**6)(
        place, *bundles, mark
    )
    bundles = [shift(b, "zh", k) for k, b in enumerate(bundles)]
    cache, mark = call(
        lay_body,
        [jax.ShapeDtypeStruct(kv_blocks.shape, bf16), MARK],
        [SMEM] + [VMEM] * SIDE,
        [VMEM] * 2,
        10**6,
    )(place, *bundles)

    half = after(half, mark)
    other = lax.ppermute(half, "core", SWAP)
    ffn_out = call(
        join_body, jax.ShapeDtypeStruct((rows, 2 * width), bf16), [SMEM, VMEM, VMEM], VMEM, 10**6
    )(core[None], half, other)
    return (ffn_out, cache)


def solution(mesh):
    fine = Mesh(mesh.devices.reshape(4, 4, 8, 3, 2), GRP + TP)
    return jax.shard_map(
        shards,
        mesh=fine,
        in_specs=(
            P(GRP, None),
            P(None, TP),
            P(None, TP),
            P(TP, None),
            P(GRP, TP),
            P(GRP, TP, None),
            P(GRP),
            P(),
        ),
        out_specs=(P(GRP, None), P(GRP, TP, None)),
        check_vma=False,
    )
```

time: 113 us -> 93.1 us (0.82)
  blocking collectives: 23.2 us -> 0 us
  starting transfers between devices: 41.1 us -> 57 us
  waiting for transfers between devices: 29.3 us -> 16.6 us
  Pallas kernels: 0 us -> 7.87 us
  other arithmetic: 6.39 us -> 0.08 us
  matrix products: 7.65 us -> 6.52 us
    ppermute x0 -> x6, starting transfers between devices: none -> 28.1 us  [shift(): return lax.ppermute(value, axis, [(i, (i + k) % SIDE) for i in range(SIDE)])]
    all_to_all x1 -> x0, blocking collectives: 23.2 us -> none  [shards(): parts = lax.all_to_all(parts, RING, split_axis=0, concat_axis=0, tiled=True)]
    all_to_all x2, waiting for transfers between devices: 27.1 us -> 7.59 us  [the longest x1 7.58 us: shards(): parts = lax.all_to_all(parts, RING, split_axis=0, concat_axis=0, tiled=True)]
    all_to_all x2, starting transfers between devices: 21.8 us -> 12.1 us  [the longest x1 7.51 us: shards(): lax.all_to_all(spread, RING, split_axis=0, concat_axis=0, tiled=True)]
    pallas_call x0 -> x7, Pallas kernels: none -> 7.87 us  [the longest x1 2.38 us: shards(): call(join_body, jax.ShapeDtypeStruct((rows, 2 * width), bf16), [SMEM, VME...]
    ppermute x0 -> x6, waiting for transfers between devices: none -> 5.28 us  [shift(): return lax.ppermute(value, axis, [(i, (i + k) % SIDE) for i in range(SIDE)])]
    ppermute x1, starting transfers between devices: 6.88 us -> 4.35 us  [shards(): other = lax.ppermute(half, 'core', SWAP)]
    select_n x4 -> x0, other arithmetic: 2.51 us -> none  [the longest x1 1.48 us: shards(): low = jnp.where(core == 0, half, other)]
  transfers between devices with their start and end apart: 4 -> 10, of which waited for: 3 -> 7; matrix products, arithmetic and copies ran while one was open for 3% -> 1% of each run, Pallas kernels for 0% -> 3%
where the time goes in v2:
time: 93.1 us; the launch traced here: 91.7 us
  starting transfers between devices  57 us (61%)
  waiting for transfers between devices  16.6 us (18%)
  Pallas kernels  7.87 us (8%)
  matrix products  6.52 us (7%)
  local copies, waits for them, and re-layouts  2.79 us (3%)
    ppermute x6, starting transfers between devices, shift(): return lax.ppermute(value, axis, [(i, (i + k) % SIDE) for i in range(SIDE)])  28.1 us
    ppermute x1, starting transfers between devices, shards(): arrived = lax.ppermute(away, 'core', SWAP)  12.4 us
    all_to_all x1, waiting for transfers between devices, shards(): parts = lax.all_to_all(parts, RING, split_axis=0, concat_axis=0, tiled=True)  7.58 us
    all_to_all x1, starting transfers between devices, shards(): lax.all_to_all(spread, RING, split_axis=0, concat_axis=0, tiled=True)  7.51 us
    ppermute x6, waiting for transfers between devices, shift(): return lax.ppermute(value, axis, [(i, (i + k) % SIDE) for i in range(SIDE)])  5.28 us
    all_to_all x1, starting transfers between devices, shards(): parts = lax.all_to_all(parts, RING, split_axis=0, concat_axis=0, tiled=True)  4.6 us
    ppermute x1, starting transfers between devices, shards(): other = lax.ppermute(half, 'core', SWAP)  4.35 us
    dot_general x1, matrix products, shards(): gate = jnp.dot(tokens, gate_weight, preferred_element_type=f32)  3.49 us
  transfers between devices with their start and end apart: 10, of which 7 were waited for; matrix products, arithmetic and copies ran while one was open for 1% of the time, Pallas kernels for 3%

profile of v2, /device:TPU:1, one launch (start us, length us, event | category | flops | bytes accessed | tf_op | source)
XLA Modules:
  0.0 91.7 jit_solution(979208002649827363)
XLA Ops:
  0.7 3.5 %fusion.7 = f32[192,384]{1,0:T(8,128)S(1)} fusion(bf16[192,4096]{1,0:T(8,128)(2,1)} %param.8, bf16[4096,384]{1,0:T(8,128)(2,1)} %param.9), kind=kOutput, calls=%fused_computation.10 | convolution fusion | flops 603979776 | bytes 5013504 | tf_op jit(solution)/shard_map/dot_general | solution.py:115
  4.2 0.4 copy-done.8
  4.6 1.0 %fusion.4 = bf16[192,384]{1,0:T(8,128)(2,1)S(1)} fusion(bf16[192,4096]{1,0:T(8,128)(2,1)S(1)} %copy-done.7, bf16[4096,384]{1,0:T(8,128)(2,1)S(1)} %copy-done.8, s32[192,384]{1,0:T(8,128)S(1)} %copy-done.9, f32[192,384]{1,0:T(8,128)S(1)} %fusion.7), kind=kOutput, calls=%fused_computation.6 | convolution fusion | flops 604569600 | bytes 5455872 | tf_op jit(solution)/shard_map/dot_general | solution.py:116
  5.6 1.5 %convolution_convert_fusion = bf16[192,2048]{1,0:T(8,128)(2,1)} fusion(bf16[192,384]{1,0:T(8,128)(2,1)S(1)} %fusion.4, bf16[384,4096]{1,0:T(8,128)(2,1)S(1)} %copy-done, s32[]{:T(128)S(6)} %select_n.7), kind=kOutput, calls=%fused_computation | convolution fusion | flops 302383104 | bytes 2506756 | tf_op jit(solution)/shard_map/dot_general | solution.py:122
  7.1 12.4 %collective-permute-start = (bf16[192,2048]{1,0:T(8,128)(2,1)}, bf16[192,2048]{1,0:T(8,128)(2,1)}, u32[]{:S(2)}, u32[]{:S(2)}) collective-permute-start(bf16[192,2048]{1,0:T(8,128)(2,1)} %convolution_convert_fusion), channel_id=1, source_target_pairs={{0,1},{1,0},{2,3},{3,2},{4,5},{5,4},{6,7},{7,6},{8,9},{9,8},{10,11... | collective-permute-start | bytes 2359304 | tf_op jit(solution)/shard_map/ppermute | solution.py:123
  19.5 0.6 fusion.1.own_ref
  20.1 1.6 %collective-permute-done.arrived_ref = bf16[192,2048]{1,0:T(8,128)(2,1)} collective-permute-done((bf16[192,2048]{1,0:T(8,128)(2,1)}, bf16[192,2048]{1,0:T(8,128)(2,1)}, u32[]{:S(2)}, u32[]{:S(2)}) %collective-permute-start) | collective-permute-done | bytes 786464 | tf_op jit(solution)/shard_map/ppermute | solution.py:123
  21.7 1.3 %shard_map.95 = (bf16[192,2048]{1,0:T(8,128)(2,1)S(1)}, f32[8,128]{1,0:T(8,128)S(1)}) custom-call(f32[192,2048]{1,0:T(8,128)S(1)} %fusion.1.own_ref, bf16[192,2048]{1,0:T(8,128)(2,1)} %collective-permute-done.arrived_ref), custom_call_target="tpu_custom_call" | custom-call | flops 1000000 | bytes 1000000 | tf_op jit(solution)/shard_map/pallas_call | solution.py:125
  23.0 0.9 copy-done.1
  23.9 4.6 %all-to-all-start = ((bf16[24,8,2048]{2,1,0:T(8,128)(2,1)}), bf16[24,8,2048]{2,1,0:T(8,128)(2,1)}, u32[]{:S(2)}, u32[]{:S(2)}) async-start(bf16[24,8,2048]{2,1,0:T(8,128)(2,1)} %bitcast.13), calls=%async_computation | async-start | bytes 1572864 | tf_op jit(solution)/shard_map/all_to_all | solution.py:130
  28.5 0.1 pad_add_fusion.place_ref
  28.6 1.2 %shard_map.96 = (bf16[4,2,2048]{2,1,0:T(2,128)(2,1)S(1)}, bf16[4,2,2048]{2,1,0:T(2,128)(2,1)S(1)}, bf16[4,2,2048]{2,1,0:T(2,128)(2,1)S(1)}, bf16[4,2,2048]{2,1,0:T(2,128)(2,1)S(1)}) custom-call(s32[4]{0:T(128)S(1)} %pad_add_fusion.place_ref, s32[16,16]{1,0:T(8,128)S(1)} %copy-done.4, s32[16]{0:T(128)S(1)} %copy-done.6, bf16[16,2,2048]{2,1,0:T(2,128)(2,1)S(1)} %copy-done.3, ...), custom_call_target="tpu_custom_call" | custom-call | flops 1000000 | bytes 1000000 | tf_op jit(solution)/shard_map/pallas_call | solution.py:133
  29.8 1.9 %collective-permute-start.1 = (bf16[4,2,2048]{2,1,0:T(2,128)(2,1)S(1)}, bf16[4,2,2048]{2,1,0:T(2,128)(2,1)S(1)}, u32[]{:S(2)}, u32[]{:S(2)}) collective-permute-start(bf16[4,2,2048]{2,1,0:T(2,128)(2,1)S(1)} %get-tuple-element.19), channel_id=1, source_target_pairs={{0,48},{48,96},{96,144},{144,0},{1,49},{49,97},{97,145},{145,1},{2... | collective-permute-start | bytes 98312 | tf_op jit(solution)/shard_map/ppermute | solution.py:107
  31.7 2.7 %collective-permute-start.2 = (bf16[4,2,2048]{2,1,0:T(2,128)(2,1)S(1)}, bf16[4,2,2048]{2,1,0:T(2,128)(2,1)S(1)}, u32[]{:S(2)}, u32[]{:S(2)}) collective-permute-start(bf16[4,2,2048]{2,1,0:T(2,128)(2,1)S(1)} %get-tuple-element.20), channel_id=1, source_target_pairs={{0,96},{48,144},{96,0},{144,48},{1,97},{49,145},{97,1},{145,49},{2... | collective-permute-start | bytes 98312 | tf_op jit(solution)/shard_map/ppermute | solution.py:107
  34.4 3.8 %collective-permute-start.3 = (bf16[4,2,2048]{2,1,0:T(2,128)(2,1)S(1)}, bf16[4,2,2048]{2,1,0:T(2,128)(2,1)S(1)}, u32[]{:S(2)}, u32[]{:S(2)}) collective-permute-start(bf16[4,2,2048]{2,1,0:T(2,128)(2,1)S(1)} %get-tuple-element.21), channel_id=1, source_target_pairs={{0,144},{48,0},{96,48},{144,96},{1,145},{49,1},{97,49},{145,97},{2... | collective-permute-start | bytes 98312 | tf_op jit(solution)/shard_map/ppermute | solution.py:107
  38.3 2.2 %collective-permute-done.3.refs_4_.refs_3_ = bf16[4,2,2048]{2,1,0:T(2,128)(2,1)S(1)} collective-permute-done((bf16[4,2,2048]{2,1,0:T(2,128)(2,1)S(1)}, bf16[4,2,2048]{2,1,0:T(2,128)(2,1)S(1)}, u32[]{:S(2)}, u32[]{:S(2)}) %collective-permute-start.3) | collective-permute-done | bytes 32800 | tf_op jit(solution)/shard_map/ppermute | solution.py:107
  40.5 7.6 %all-to-all-done.refs_0_ = bf16[24,8,2048]{2,1,0:T(8,128)(2,1)} async-done(((bf16[24,8,2048]{2,1,0:T(8,128)(2,1)}), bf16[24,8,2048]{2,1,0:T(8,128)(2,1)}, u32[]{:S(2)}, u32[]{:S(2)}) %all-to-all-start) | async-done | bytes 786464 | tf_op jit(solution)/shard_map/all_to_all | solution.py:130
  48.1 1.3 %shard_map.97 = (bf16[24,8,2048]{2,1,0:T(8,128)(2,1)S(1)}, f32[8,128]{1,0:T(8,128)S(1)}) custom-call(bf16[24,8,2048]{2,1,0:T(8,128)(2,1)} %all-to-all-done.refs_0_, bf16[4,2,2048]{2,1,0:T(2,128)(2,1)S(1)} %get-tuple-element.18.refs_1_.refs_0_, bf16[4,2,2048]{2,1,0:T(2,128)(2,1)S(1)} %collective-permute-done.1.refs_2_.refs_1_, ...), custom_call_target="tpu_custom_call" | custom-call | flops 1000000 | bytes 1000000 | tf_op jit(solution)/shard_map/pallas_call | solution.py:138
  49.3 0.9 copy-done.2
  50.2 7.5 %all-to-all-start.1 = ((bf16[24,8,2048]{2,1,0:T(8,128)(2,1)}), bf16[24,8,2048]{2,1,0:T(8,128)(2,1)}, u32[]{:S(2)}, u32[]{:S(2)}) async-start(bf16[24,8,2048]{2,1,0:T(8,128)(2,1)} %copy-done.2), calls=%async_computation.1 | async-start | bytes 1572864 | tf_op jit(solution)/shard_map/all_to_all | solution.py:142
  57.7 0.6 shard_map.98
  58.3 7.3 %collective-permute-start.4 = (bf16[4,2,2048]{2,1,0:T(2,128)(2,1)S(1)}, bf16[4,2,2048]{2,1,0:T(2,128)(2,1)S(1)}, u32[]{:S(2)}, u32[]{:S(2)}) collective-permute-start(bf16[4,2,2048]{2,1,0:T(2,128)(2,1)S(1)} %get-tuple-element.25), channel_id=1, source_target_pairs={{0,192},{192,384},{384,576},{576,0},{1,193},{193,385},{385,577},{5... | collective-permute-start | bytes 98312 | tf_op jit(solution)/shard_map/ppermute | solution.py:107
  65.6 8.6 %collective-permute-start.5 = (bf16[4,2,2048]{2,1,0:T(2,128)(2,1)S(1)}, bf16[4,2,2048]{2,1,0:T(2,128)(2,1)S(1)}, u32[]{:S(2)}, u32[]{:S(2)}) collective-permute-start(bf16[4,2,2048]{2,1,0:T(2,128)(2,1)S(1)} %get-tuple-element.26), channel_id=1, source_target_pairs={{0,384},{192,576},{384,0},{576,192},{1,385},{193,577},{385,1},{577... | collective-permute-start | bytes 98312 | tf_op jit(solution)/shard_map/ppermute | solution.py:107
  74.2 3.8 %collective-permute-start.6 = (bf16[4,2,2048]{2,1,0:T(2,128)(2,1)S(1)}, bf16[4,2,2048]{2,1,0:T(2,128)(2,1)S(1)}, u32[]{:S(2)}, u32[]{:S(2)}) collective-permute-start(bf16[4,2,2048]{2,1,0:T(2,128)(2,1)S(1)} %get-tuple-element.27), channel_id=1, source_target_pairs={{0,576},{192,0},{384,192},{576,384},{1,577},{193,1},{385,193},{577... | collective-permute-start | bytes 98312 | tf_op jit(solution)/shard_map/ppermute | solution.py:107
  78.0 0.7 collective-permute-done.4.refs_1_
  78.7 2.2 %collective-permute-done.5.refs_2_ = bf16[4,2,2048]{2,1,0:T(2,128)(2,1)S(1)} collective-permute-done((bf16[4,2,2048]{2,1,0:T(2,128)(2,1)S(1)}, bf16[4,2,2048]{2,1,0:T(2,128)(2,1)S(1)}, u32[]{:S(2)}, u32[]{:S(2)}) %collective-permute-start.5) | collective-permute-done | bytes 32800 | tf_op jit(solution)/shard_map/ppermute | solution.py:107
  80.9 0.1 collective-permute-done.6.refs_3_
  81.1 1.2 %shard_map.99 = (bf16[16,2,2048]{2,1,0:T(2,128)(2,1)}, f32[8,128]{1,0:T(8,128)S(1)}) custom-call(s32[4]{0:T(128)S(1)} %pad_add_fusion.place_ref, bf16[4,2,2048]{2,1,0:T(2,128)(2,1)S(1)} %get-tuple-element.24.refs_0_, bf16[4,2,2048]{2,1,0:T(2,128)(2,1)S(1)} %collective-permute-done.4.refs_1_, bf16[4,2,2048]{2,1,0:T(2,128)(2,1)S(1)} %collective-permute-done.5.refs_2_, ...), custom_call_target="tpu_custom_call" | custom-call | flops 1000000 | bytes 1000000 | tf_op jit(solution)/shard_map/pallas_call | solution.py:148
  82.3 0.6 copy-done.5
  82.9 4.4 %collective-permute-start.7 = (bf16[192,2048]{1,0:T(8,128)(2,1)}, bf16[192,2048]{1,0:T(8,128)(2,1)S(1)}, u32[]{:S(2)}, u32[]{:S(2)}) collective-permute-start(bf16[192,2048]{1,0:T(8,128)(2,1)} %shard_map.100.half_ref), channel_id=1, source_target_pairs={{0,1},{1,0},{2,3},{3,2},{4,5},{5,4},{6,7},{7,6},{8,9},{9,8},{10,11... | collective-permute-start | bytes 2359304 | tf_op jit(solution)/shard_map/ppermute | solution.py:157
  87.2 2.1 %collective-permute-done.7.other_ref = bf16[192,2048]{1,0:T(8,128)(2,1)S(1)} collective-permute-done((bf16[192,2048]{1,0:T(8,128)(2,1)}, bf16[192,2048]{1,0:T(8,128)(2,1)S(1)}, u32[]{:S(2)}, u32[]{:S(2)}) %collective-permute-start.7) | collective-permute-done | bytes 786464 | tf_op jit(solution)/shard_map/ppermute | solution.py:157
  89.3 2.4 %shard_map.101 = bf16[192,4096]{1,0:T(8,128)(2,1)} custom-call(s32[1]{0:T(128)} %bitcast.core_ref, bf16[192,2048]{1,0:T(8,128)(2,1)} %shard_map.100.half_ref, bf16[192,2048]{1,0:T(8,128)(2,1)S(1)} %collective-permute-done.7.other_ref), custom_call_target="tpu_custom_call" | custom-call | flops 1000000 | bytes 1000000 | tf_op jit(solution)/shard_map/pallas_call | solution.py:158
  (20 shorter events, 0.1 us)
Async XLA Ops:
  0.6 5.0 %copy-start = (bf16[384,4096]{1,0:T(8,128)(2,1)S(1)}, bf16[384,4096]{1,0:T(8,128)(2,1)}, u32[]{:S(2)}) copy-start(bf16[384,4096]{1,0:T(8,128)(2,1)} %param.11) | copy-start | bytes 9437188
  0.7 3.5 %copy-start.7 = (bf16[192,4096]{1,0:T(8,128)(2,1)S(1)}, bf16[192,4096]{1,0:T(8,128)(2,1)}, u32[]{:S(2)}) copy-start(bf16[192,4096]{1,0:T(8,128)(2,1)} %param.8) | copy-start | bytes 4718596
  0.7 3.9 %copy-start.8 = (bf16[4096,384]{1,0:T(8,128)(2,1)S(1)}, bf16[4096,384]{1,0:T(8,128)(2,1)}, u32[]{:S(2)}) copy-start(bf16[4096,384]{1,0:T(8,128)(2,1)} %param.10) | copy-start | bytes 9437188
  0.7 3.9 %copy-start.9 = (s32[192,384]{1,0:T(8,128)S(1)}, s32[192,384]{1,0:T(8,128)}, u32[]{:S(2)}) copy-start(s32[192,384]{1,0:T(8,128)} %param.12) | copy-start | bytes 884740
  7.1 14.7 %collective-permute-start = (bf16[192,2048]{1,0:T(8,128)(2,1)}, bf16[192,2048]{1,0:T(8,128)(2,1)}, u32[]{:S(2)}, u32[]{:S(2)}) collective-permute-start(bf16[192,2048]{1,0:T(8,128)(2,1)} %convolution_convert_fusion), channel_id=1, source_target_pairs={{0,1},{1,0},{2,3},{3,2},{4,5},{5,4},{6,7},{7,6},{8,9},{9,8},{10,11... | collective-permute-start | bytes 2359304 | tf_op jit(solution)/shard_map/ppermute | solution.py:123
  20.1 8.5 %copy-start.3 = (bf16[16,2,2048]{2,1,0:T(2,128)(2,1)S(1)}, bf16[16,2,2048]{2,1,0:T(2,128)(2,1)}, u32[]{:S(2)}) copy-start(bf16[16,2,2048]{2,1,0:T(2,128)(2,1)} %kv_ref.1) | copy-start | bytes 393220
  20.1 8.5 %copy-start.4 = (s32[16,16]{1,0:T(8,128)S(1)}, s32[16,16]{1,0:T(8,128)}, u32[]{:S(2)}) copy-start(s32[16,16]{1,0:T(8,128)} %dest_ref.1) | copy-start | bytes 3076
  20.1 8.5 %copy-start.6 = (s32[16]{0:T(128)S(1)}, s32[16]{0:T(128)}, u32[]{:S(2)}) copy-start(s32[16]{0:T(128)} %lengths_ref.1) | copy-start | bytes 196
  23.0 0.9 copy-start.1
  23.9 24.2 %all-to-all-start = ((bf16[24,8,2048]{2,1,0:T(8,128)(2,1)}), bf16[24,8,2048]{2,1,0:T(8,128)(2,1)}, u32[]{:S(2)}, u32[]{:S(2)}) async-start(bf16[24,8,2048]{2,1,0:T(8,128)(2,1)} %bitcast.13), calls=%async_computation | async-start | bytes 1572864 | tf_op jit(solution)/shard_map/all_to_all | solution.py:130
  29.8 8.4 %collective-permute-start.1 = (bf16[4,2,2048]{2,1,0:T(2,128)(2,1)S(1)}, bf16[4,2,2048]{2,1,0:T(2,128)(2,1)S(1)}, u32[]{:S(2)}, u32[]{:S(2)}) collective-permute-start(bf16[4,2,2048]{2,1,0:T(2,128)(2,1)S(1)} %get-tuple-element.19), channel_id=1, source_target_pairs={{0,48},{48,96},{96,144},{144,0},{1,49},{49,97},{97,145},{145,1},{2... | collective-permute-start | bytes 98312 | tf_op jit(solution)/shard_map/ppermute | solution.py:107
  31.7 6.6 %collective-permute-start.2 = (bf16[4,2,2048]{2,1,0:T(2,128)(2,1)S(1)}, bf16[4,2,2048]{2,1,0:T(2,128)(2,1)S(1)}, u32[]{:S(2)}, u32[]{:S(2)}) collective-permute-start(bf16[4,2,2048]{2,1,0:T(2,128)(2,1)S(1)} %get-tuple-element.20), channel_id=1, source_target_pairs={{0,96},{48,144},{96,0},{144,48},{1,97},{49,145},{97,1},{145,49},{2... | collective-permute-start | bytes 98312 | tf_op jit(solution)/shard_map/ppermute | solution.py:107
  34.4 6.0 %collective-permute-start.3 = (bf16[4,2,2048]{2,1,0:T(2,128)(2,1)S(1)}, bf16[4,2,2048]{2,1,0:T(2,128)(2,1)S(1)}, u32[]{:S(2)}, u32[]{:S(2)}) collective-permute-start(bf16[4,2,2048]{2,1,0:T(2,128)(2,1)S(1)} %get-tuple-element.21), channel_id=1, source_target_pairs={{0,144},{48,0},{96,48},{144,96},{1,145},{49,1},{97,49},{145,97},{2... | collective-permute-start | bytes 98312 | tf_op jit(solution)/shard_map/ppermute | solution.py:107
  49.3 0.9 copy-start.2
  50.2 32.6 %all-to-all-start.1 = ((bf16[24,8,2048]{2,1,0:T(8,128)(2,1)}), bf16[24,8,2048]{2,1,0:T(8,128)(2,1)}, u32[]{:S(2)}, u32[]{:S(2)}) async-start(bf16[24,8,2048]{2,1,0:T(8,128)(2,1)} %copy-done.2), calls=%async_computation.1 | async-start | bytes 1572864 | tf_op jit(solution)/shard_map/all_to_all | solution.py:142
  58.3 20.4 %collective-permute-start.4 = (bf16[4,2,2048]{2,1,0:T(2,128)(2,1)S(1)}, bf16[4,2,2048]{2,1,0:T(2,128)(2,1)S(1)}, u32[]{:S(2)}, u32[]{:S(2)}) collective-permute-start(bf16[4,2,2048]{2,1,0:T(2,128)(2,1)S(1)} %get-tuple-element.25), channel_id=1, source_target_pairs={{0,192},{192,384},{384,576},{576,0},{1,193},{193,385},{385,577},{5... | collective-permute-start | bytes 98312 | tf_op jit(solution)/shard_map/ppermute | solution.py:107
  65.6 15.3 %collective-permute-start.5 = (bf16[4,2,2048]{2,1,0:T(2,128)(2,1)S(1)}, bf16[4,2,2048]{2,1,0:T(2,128)(2,1)S(1)}, u32[]{:S(2)}, u32[]{:S(2)}) collective-permute-start(bf16[4,2,2048]{2,1,0:T(2,128)(2,1)S(1)} %get-tuple-element.26), channel_id=1, source_target_pairs={{0,384},{192,576},{384,0},{576,192},{1,385},{193,577},{385,1},{577... | collective-permute-start | bytes 98312 | tf_op jit(solution)/shard_map/ppermute | solution.py:107
  74.2 6.8 %collective-permute-start.6 = (bf16[4,2,2048]{2,1,0:T(2,128)(2,1)S(1)}, bf16[4,2,2048]{2,1,0:T(2,128)(2,1)S(1)}, u32[]{:S(2)}, u32[]{:S(2)}) collective-permute-start(bf16[4,2,2048]{2,1,0:T(2,128)(2,1)S(1)} %get-tuple-element.27), channel_id=1, source_target_pairs={{0,576},{192,0},{384,192},{576,384},{1,577},{193,1},{385,193},{577... | collective-permute-start | bytes 98312 | tf_op jit(solution)/shard_map/ppermute | solution.py:107
  82.3 0.6 copy-start.5
  82.9 6.5 %collective-permute-start.7 = (bf16[192,2048]{1,0:T(8,128)(2,1)}, bf16[192,2048]{1,0:T(8,128)(2,1)S(1)}, u32[]{:S(2)}, u32[]{:S(2)}) collective-permute-start(bf16[192,2048]{1,0:T(8,128)(2,1)} %shard_map.100.half_ref), channel_id=1, source_target_pairs={{0,1},{1,0},{2,3},{3,2},{4,5},{5,4},{6,7},{7,6},{8,9},{9,8},{10,11... | collective-permute-start | bytes 2359304 | tf_op jit(solution)/shard_map/ppermute | solution.py:157

commit v3 on v1

v3 whole, which is shorter than its diff:
```python
import jax
import jax.numpy as jnp
from jax import lax
from jax.experimental import pallas as pl
from jax.experimental.pallas import tpu as pltpu
from jax.sharding import Mesh, PartitionSpec as P

GRP = ("zh", "x")
TP = ("y", "zl", "core")
RING = ("y", "zl")
SWAP = [(0, 1), (1, 0)]
SIDE = 4
CHIPS = 24
STEPS = 4

bf16, f32 = jnp.bfloat16, jnp.float32
MARK = jax.ShapeDtypeStruct((8, 128), f32)
VMEM = pl.BlockSpec(memory_space=pltpu.VMEM)
SMEM = pl.BlockSpec(memory_space=pltpu.SMEM)
ANY = pl.BlockSpec(memory_space=pl.ANY)


def call(body, out_shape, in_specs, out_specs, **more):
    return pl.pallas_call(
        body,
        out_shape=out_shape,
        in_specs=in_specs,
        out_specs=out_specs,
        cost_estimate=pl.CostEstimate(flops=10**6, bytes_accessed=10**6, transcendentals=0),
        compiler_params=pltpu.CompilerParams(vmem_limit_bytes=16 * 2**20),
        **more,
    )


def slots_by_x0(place_ref, dest_ref, lengths_ref, kv_ref, mark_ref, keep_ref, send_ref):
    mine = place_ref[4]
    row = lax.broadcasted_iota(jnp.int32, kv_ref.shape[1:], 0) + place_ref[5]
    for r in range(kv_ref.shape[0]):
        d = dest_ref[mine, r]
        value = kv_ref[r]
        value = jnp.where(row < lengths_ref[r], value, jnp.zeros_like(value))
        spot = ((d >> 1) & 1) * 4 + (d >> 2)

        @pl.when((d & 1) == place_ref[0])
        def _():
            keep_ref[spot] = value

        @pl.when((d & 1) != place_ref[0])
        def _():
            send_ref[spot] = value


def slots_by_x1(place_ref, kept_ref, arrived_ref, keep_ref, send_ref):
    for other, in_ref in enumerate((kept_ref, arrived_ref)):
        source = place_ref[0] ^ other
        for z in range(4):
            keep_ref[source * 4 + z] = in_ref[place_ref[1] * 4 + z]
            send_ref[source * 4 + z] = in_ref[(place_ref[1] ^ 1) * 4 + z]


def slots_by_z1(place_ref, kept_ref, arrived_ref, *refs):
    keep_ref, send_ref = refs[-2:]
    for other, in_ref in enumerate((kept_ref, arrived_ref)):
        source = (place_ref[1] ^ other) * 2
        for s in range(2):
            for z in range(2):
                keep_ref[(source + s) * 2 + z] = in_ref[s * 4 + place_ref[3] * 2 + z]
                send_ref[(source + s) * 2 + z] = in_ref[s * 4 + (place_ref[3] ^ 1) * 2 + z]


def slots_by_z0(place_ref, kept_ref, arrived_ref, *refs):
    keep_ref, send_ref = refs[-2:]
    for other, in_ref in enumerate((kept_ref, arrived_ref)):
        source = (place_ref[3] ^ other) * 4
        for s in range(4):
            keep_ref[source + s] = in_ref[s * 2 + place_ref[2]]
            send_ref[source + s] = in_ref[s * 2 + (place_ref[2] ^ 1)]


def slots_in_place(place_ref, kept_ref, arrived_ref, out_ref, mark_ref):
    mark_ref[...] = jnp.zeros_like(mark_ref)
    for other, in_ref in enumerate((kept_ref, arrived_ref)):
        for z in range(2):
            source = (z * 2 + (place_ref[2] ^ other)) * 4
            for s in range(4):
                out_ref[source + s] = in_ref[z * 4 + s]


def add_body(own_ref, arrived_ref, out_ref, mark_ref):
    mark_ref[...] = jnp.zeros_like(mark_ref)
    rows = out_ref.shape[0]
    block = pl.ds(pl.multiple_of(pl.program_id(0) * rows, rows), rows)
    out_ref[...] = (own_ref[block] + arrived_ref[block].astype(f32)).astype(bf16)


def sum_body(parts_ref, *refs):
    out_ref, mark_ref, total_ref = refs[-3:]

    @pl.when(pl.program_id(0) == 0)
    def _():
        mark_ref[...] = jnp.zeros_like(mark_ref)
        total = parts_ref[0].astype(f32)
        for i in range(1, CHIPS):
            total += parts_ref[i].astype(f32)
        total_ref[...] = total.astype(bf16)

    for i in range(out_ref.shape[0]):
        out_ref[i] = total_ref[...]


def copy_body(where_ref, value_ref, *refs):
    refs[-1][...] = value_ref[...]


def half_of(out_shape, where, value, *into):
    rows, width = value.shape[0] // STEPS, value.shape[1]
    return pl.pallas_call(
        copy_body,
        out_shape=out_shape,
        grid_spec=pltpu.PrefetchScalarGridSpec(
            num_scalar_prefetch=1,
            grid=(STEPS,),
            in_specs=[pl.BlockSpec((rows, width), lambda i, w: (i, 0))] + [ANY] * len(into),
            out_specs=pl.BlockSpec((rows, width), lambda i, w: (i, w[0])),
        ),
        input_output_aliases={2: 0} if into else {},
        cost_estimate=pl.CostEstimate(flops=10**6, bytes_accessed=10**6, transcendentals=0),
        compiler_params=pltpu.CompilerParams(vmem_limit_bytes=16 * 2**20),
    )(where, value, *into)


def after(value, mark):
    return pl.pallas_call(
        lambda value_ref, mark_ref, out_ref: None,
        out_shape=jax.ShapeDtypeStruct(value.shape, value.dtype),
        in_specs=[ANY, VMEM],
        out_specs=ANY,
        input_output_aliases={0: 0},
    )(value, mark)


def flip(value, axis, bit):
    return lax.ppermute(value, axis, [(i, i ^ bit) for i in range(SIDE)])


def shards(tokens, gate_weight, up_weight, down_weight, active, kv_blocks, lengths, dest):
    core = lax.axis_index("core")
    x, zh = lax.axis_index("x"), lax.axis_index("zh")
    place = jnp.stack(
        [x & 1, x >> 1, zh & 1, zh >> 1, lax.axis_index(GRP), lax.axis_index(TP) * kv_blocks.shape[1]]
    )

    gate = jnp.dot(tokens, gate_weight, preferred_element_type=f32)
    up = jnp.dot(tokens, up_weight, preferred_element_type=f32)
    hidden = (jax.nn.silu(gate) * up * active.astype(f32)).astype(bf16)

    rows, width = tokens.shape[0], down_weight.shape[1] // 2
    theirs = lax.dynamic_slice_in_dim(down_weight, (1 - core) * width, width, 1)
    ours = lax.dynamic_slice_in_dim(down_weight, core * width, width, 1)
    away = jnp.dot(hidden, theirs, preferred_element_type=f32).astype(bf16)
    arrived = lax.ppermute(away, "core", SWAP)
    own = jnp.dot(hidden, ours, preferred_element_type=f32)
    total, mark = call(
        add_body,
        [pltpu.HBM((rows, width), bf16), MARK],
        [VMEM] * 2,
        [pl.BlockSpec((rows // STEPS, width), lambda i: (i, 0)), VMEM],
        grid=(STEPS,),
    )(own, arrived)

    parts = total.reshape(CHIPS, rows // CHIPS, width)
    parts = lax.all_to_all(parts, RING, split_axis=0, concat_axis=0, tiled=True)

    pair = [jax.ShapeDtypeStruct((8, *kv_blocks.shape[1:]), bf16)] * 2
    kept, sent = call(slots_by_x0, pair, [SMEM] * 3 + [VMEM] * 2, [VMEM] * 2)(place, dest, lengths, kv_blocks, mark)
    kept, sent = call(slots_by_x1, pair, [SMEM] + [VMEM] * 2, [VMEM] * 2)(place, kept, flip(sent, "x", 1))
    kept, sent = call(slots_by_z1, pair, [SMEM] + [VMEM] * 2, [VMEM] * 2)(place, kept, flip(sent, "x", 2))
    moved = flip(sent, "zh", 2)

    spread, mark = call(
        sum_body,
        [pltpu.HBM(parts.shape, bf16), MARK],
        [VMEM] * 2,
        [pl.BlockSpec((CHIPS // STEPS, *parts.shape[1:]), lambda i: (i, 0, 0)), VMEM],
        grid=(STEPS,),
        scratch_shapes=[pltpu.VMEM(parts.shape[1:], bf16)],
    )(parts, moved)

    half = lax.all_to_all(spread, RING, split_axis=0, concat_axis=0, tiled=True).reshape(rows, width)

    kept, sent = call(slots_by_z0, pair, [SMEM] + [VMEM] * 3, [VMEM] * 2)(place, kept, moved, mark)
    cache, mark = call(
        slots_in_place, [jax.ShapeDtypeStruct(kv_blocks.shape, bf16), MARK], [SMEM] + [VMEM] * 2, [VMEM] * 2
    )(place, kept, flip(sent, "zh", 1))

    half = after(half, mark)
    other = lax.ppermute(half, "core", SWAP)
    ffn_out = jax.ShapeDtypeStruct((rows, 2 * width), bf16)
    ffn_out = half_of(ffn_out, 1 - core[None], other, half_of(ffn_out, core[None], half))
    return (ffn_out, cache)


def solution(mesh):
    fine = Mesh(mesh.devices.reshape(4, 4, 8, 3, 2), GRP + TP)
    return jax.shard_map(
        shards,
        mesh=fine,
        in_specs=(
            P(GRP, None),
            P(None, TP),
            P(None, TP),
            P(TP, None),
            P(GRP, TP),
            P(GRP, TP, None),
            P(GRP),
            P(),
        ),
        out_specs=(P(GRP, None), P(GRP, TP, None)),
        check_vma=False,
    )
```

time: 113 us -> 98.4 us (0.87)
  blocking collectives: 23.2 us -> 0 us
  Pallas kernels: 0 us -> 14.5 us
  starting transfers between devices: 41.1 us -> 54.1 us
  waiting for transfers between devices: 29.3 us -> 20.6 us
  other arithmetic: 6.39 us -> 0 us
  local copies, waits for them, and re-layouts: 3.57 us -> 1.12 us
  matrix products: 7.65 us -> 6.52 us
    all_to_all x1 -> x0, blocking collectives: 23.2 us -> none  [shards(): parts = lax.all_to_all(parts, RING, split_axis=0, concat_axis=0, tiled=True)]
    all_to_all x2, waiting for transfers between devices: 27.1 us -> 5.41 us  [the longest x1 5.41 us: shards(): lax.all_to_all(spread, RING, split_axis=0, concat_axis=0, tiled=True)]
    ppermute x0 -> x4, starting transfers between devices: none -> 19.6 us  [flip(): return lax.ppermute(value, axis, [(i, i ^ bit) for i in range(SIDE)])]
    pallas_call x0 -> x10, Pallas kernels: none -> 14.5 us  [the longest x2 4.71 us: half_of(): pl.pallas_call(copy_body, out_shape=out_shape, grid_spec=pltpu.PrefetchSc...]
    ppermute x0 -> x4, waiting for transfers between devices: none -> 13.6 us  [flip(): return lax.ppermute(value, axis, [(i, i ^ bit) for i in range(SIDE)])]
    all_to_all x2, starting transfers between devices: 21.8 us -> 14.4 us  [the longest x1 9.78 us: shards(): lax.all_to_all(spread, RING, split_axis=0, concat_axis=0, tiled=True)]
    select_n x4 -> x0, other arithmetic: 2.51 us -> none  [the longest x1 1.48 us: shards(): low = jnp.where(core == 0, half, other)]
    reduce_sum x1 -> x0, other arithmetic: 1.29 us -> none  [shards(): summed = jnp.sum(parts.astype(f32), axis=0).astype(bf16)]
  transfers between devices with their start and end apart: 4 -> 8, of which waited for: 3 -> 6; matrix products, arithmetic and copies ran while one was open for 3% -> 1% of each run, Pallas kernels for 0% -> 7%
where the time goes in v3:
time: 98.4 us; the launch traced here: 97.8 us
  starting transfers between devices  54.1 us (55%)
  waiting for transfers between devices  20.6 us (21%)
  Pallas kernels  14.5 us (15%)
  matrix products  6.52 us (7%)
  local copies, waits for them, and re-layouts  1.12 us (1%)
    ppermute x4, starting transfers between devices, flip(): return lax.ppermute(value, axis, [(i, i ^ bit) for i in range(SIDE)])  19.6 us
    ppermute x4, waiting for transfers between devices, flip(): return lax.ppermute(value, axis, [(i, i ^ bit) for i in range(SIDE)])  13.6 us
    ppermute x1, starting transfers between devices, shards(): arrived = lax.ppermute(away, 'core', SWAP)  12.4 us
    all_to_all x1, starting transfers between devices, shards(): lax.all_to_all(spread, RING, split_axis=0, concat_axis=0, tiled=True)  9.78 us
    ppermute x1, starting transfers between devices, shards(): other = lax.ppermute(half, 'core', SWAP)  7.67 us
    all_to_all x1, waiting for transfers between devices, shards(): lax.all_to_all(spread, RING, split_axis=0, concat_axis=0, tiled=True)  5.41 us
    pallas_call x2, Pallas kernels, half_of(): pl.pallas_call(copy_body, out_shape=out_shape, grid_spec=pltpu.PrefetchSc...  4.71 us
    all_to_all x1, starting transfers between devices, shards(): parts = lax.all_to_all(parts, RING, split_axis=0, concat_axis=0, tiled=True)  4.61 us
  transfers between devices with their start and end apart: 8, of which 6 were waited for; matrix products, arithmetic and copies ran while one was open for 1% of the time, Pallas kernels for 7%

profile of v3, /device:TPU:1, one launch (start us, length us, event | category | flops | bytes accessed | tf_op | source)
XLA Modules:
  0.0 97.8 jit_solution(18244604316189286753)
XLA Ops:
  0.7 3.5 %fusion.7 = f32[192,384]{1,0:T(8,128)S(1)} fusion(bf16[192,4096]{1,0:T(8,128)(2,1)} %param.8, bf16[4096,384]{1,0:T(8,128)(2,1)} %param.9), kind=kOutput, calls=%fused_computation.9 | convolution fusion | flops 603979776 | bytes 5013504 | tf_op jit(solution)/shard_map/dot_general | solution.py:153
  4.2 0.4 copy-done.6
  4.6 0.0 copy-done.7
  4.6 1.0 %fusion.4 = bf16[192,384]{1,0:T(8,128)(2,1)S(1)} fusion(bf16[192,4096]{1,0:T(8,128)(2,1)S(1)} %copy-done.5, bf16[4096,384]{1,0:T(8,128)(2,1)S(1)} %copy-done.6, s32[192,384]{1,0:T(8,128)S(1)} %copy-done.7, f32[192,384]{1,0:T(8,128)S(1)} %fusion.7), kind=kOutput, calls=%fused_computation.6 | convolution fusion | flops 604569600 | bytes 5455872 | tf_op jit(solution)/shard_map/dot_general | solution.py:154
  5.6 1.5 %convolution_convert_fusion = bf16[192,2048]{1,0:T(8,128)(2,1)} fusion(bf16[192,384]{1,0:T(8,128)(2,1)S(1)} %fusion.4, bf16[384,4096]{1,0:T(8,128)(2,1)S(1)} %copy-done, s32[]{:T(128)S(6)} %select_n.7), kind=kOutput, calls=%fused_computation | convolution fusion | flops 302383104 | bytes 2506756 | tf_op jit(solution)/shard_map/dot_general | solution.py:160
  7.1 12.4 %collective-permute-start = (bf16[192,2048]{1,0:T(8,128)(2,1)}, bf16[192,2048]{1,0:T(8,128)(2,1)}, u32[]{:S(2)}, u32[]{:S(2)}) collective-permute-start(bf16[192,2048]{1,0:T(8,128)(2,1)} %convolution_convert_fusion), channel_id=1, source_target_pairs={{0,1},{1,0},{2,3},{3,2},{4,5},{5,4},{6,7},{7,6},{8,9},{9,8},{10,11... | collective-permute-start | bytes 2359304 | tf_op jit(solution)/shard_map/ppermute | solution.py:161
  19.5 0.6 fusion.1.own_ref
  20.1 1.6 %collective-permute-done.arrived_ref = bf16[192,2048]{1,0:T(8,128)(2,1)} collective-permute-done((bf16[192,2048]{1,0:T(8,128)(2,1)}, bf16[192,2048]{1,0:T(8,128)(2,1)}, u32[]{:S(2)}, u32[]{:S(2)}) %collective-permute-start) | collective-permute-done | bytes 786464 | tf_op jit(solution)/shard_map/ppermute | solution.py:161
  21.7 2.6 %shard_map.95 = (bf16[192,2048]{1,0:T(8,128)(2,1)}, f32[8,128]{1,0:T(8,128)S(1)}) custom-call(f32[192,2048]{1,0:T(8,128)S(1)} %fusion.1.own_ref, bf16[192,2048]{1,0:T(8,128)(2,1)} %collective-permute-done.arrived_ref), custom_call_target="tpu_custom_call" | custom-call | flops 1000000 | bytes 1000000 | tf_op jit(solution)/shard_map/pallas_call | solution.py:163
  24.3 4.6 %all-to-all-start = ((bf16[24,8,2048]{2,1,0:T(8,128)(2,1)}), bf16[24,8,2048]{2,1,0:T(8,128)(2,1)}, u32[]{:S(2)}, u32[]{:S(2)}) async-start(bf16[24,8,2048]{2,1,0:T(8,128)(2,1)} %bitcast.15), calls=%async_computation | async-start | bytes 1572864 | tf_op jit(solution)/shard_map/all_to_all | solution.py:172
  29.0 0.1 stack.27.place_ref
  29.1 1.0 shard_map.96
  30.1 1.9 %collective-permute-start.1 = (bf16[8,2,2048]{2,1,0:T(2,128)(2,1)S(1)}, bf16[8,2,2048]{2,1,0:T(2,128)(2,1)S(1)}, u32[]{:S(2)}, u32[]{:S(2)}) collective-permute-start(bf16[8,2,2048]{2,1,0:T(2,128)(2,1)S(1)} %get-tuple-element.19), channel_id=1, source_target_pairs={{0,48},{48,0},{96,144},{144,96},{1,49},{49,1},{97,145},{145,97},{2... | collective-permute-start | bytes 196616 | tf_op jit(solution)/shard_map/ppermute | solution.py:143
  32.0 3.5 %collective-permute-done.1.arrived_ref = bf16[8,2,2048]{2,1,0:T(2,128)(2,1)S(1)} collective-permute-done((bf16[8,2,2048]{2,1,0:T(2,128)(2,1)S(1)}, bf16[8,2,2048]{2,1,0:T(2,128)(2,1)S(1)}, u32[]{:S(2)}, u32[]{:S(2)}) %collective-permute-start.1) | collective-permute-done | bytes 65568 | tf_op jit(solution)/shard_map/ppermute | solution.py:143
  35.5 0.6 shard_map.97
  36.0 1.9 %collective-permute-start.2 = (bf16[8,2,2048]{2,1,0:T(2,128)(2,1)S(1)}, bf16[8,2,2048]{2,1,0:T(2,128)(2,1)S(1)}, u32[]{:S(2)}, u32[]{:S(2)}) collective-permute-start(bf16[8,2,2048]{2,1,0:T(2,128)(2,1)S(1)} %get-tuple-element.21), channel_id=1, source_target_pairs={{0,96},{48,144},{96,0},{144,48},{1,97},{49,145},{97,1},{145,49},{2... | collective-permute-start | bytes 196616 | tf_op jit(solution)/shard_map/ppermute | solution.py:143
  38.0 5.0 %collective-permute-done.2.arrived_ref = bf16[8,2,2048]{2,1,0:T(2,128)(2,1)S(1)} collective-permute-done((bf16[8,2,2048]{2,1,0:T(2,128)(2,1)S(1)}, bf16[8,2,2048]{2,1,0:T(2,128)(2,1)S(1)}, u32[]{:S(2)}, u32[]{:S(2)}) %collective-permute-start.2) | collective-permute-done | bytes 65568 | tf_op jit(solution)/shard_map/ppermute | solution.py:143
  42.9 0.6 shard_map.98
  43.5 10.4 %collective-permute-start.3 = (bf16[8,2,2048]{2,1,0:T(2,128)(2,1)S(1)}, bf16[8,2,2048]{2,1,0:T(2,128)(2,1)S(1)}, u32[]{:S(2)}, u32[]{:S(2)}) collective-permute-start(bf16[8,2,2048]{2,1,0:T(2,128)(2,1)S(1)} %get-tuple-element.22), channel_id=1, source_target_pairs={{0,384},{192,576},{384,0},{576,192},{1,385},{193,577},{385,1},{577... | collective-permute-start | bytes 196616 | tf_op jit(solution)/shard_map/ppermute | solution.py:143
  53.9 1.7 %collective-permute-done.3.refs_0_.arrived_ref = bf16[8,2,2048]{2,1,0:T(2,128)(2,1)S(1)} collective-permute-done((bf16[8,2,2048]{2,1,0:T(2,128)(2,1)S(1)}, bf16[8,2,2048]{2,1,0:T(2,128)(2,1)S(1)}, u32[]{:S(2)}, u32[]{:S(2)}) %collective-permute-start.3) | collective-permute-done | bytes 65568 | tf_op jit(solution)/shard_map/ppermute | solution.py:143
  55.6 2.7 %shard_map.99 = (bf16[24,8,2048]{2,1,0:T(8,128)(2,1)}, f32[8,128]{1,0:T(8,128)S(1)}) custom-call(bf16[24,8,2048]{2,1,0:T(8,128)(2,1)} %all-to-all-done.parts_ref, bf16[8,2,2048]{2,1,0:T(2,128)(2,1)S(1)} %collective-permute-done.3.refs_0_.arrived_ref), custom_call_target="tpu_custom_call" | custom-call | flops 1000000 | bytes 1000000 | tf_op jit(solution)/shard_map/pallas_call | solution.py:180
  58.3 9.8 %all-to-all-start.1 = ((bf16[24,8,2048]{2,1,0:T(8,128)(2,1)}), bf16[24,8,2048]{2,1,0:T(8,128)(2,1)}, u32[]{:S(2)}, u32[]{:S(2)}) async-start(bf16[24,8,2048]{2,1,0:T(8,128)(2,1)} %get-tuple-element.23), calls=%async_computation.1 | async-start | bytes 1572864 | tf_op jit(solution)/shard_map/all_to_all | solution.py:189
  68.1 0.6 shard_map.100
  68.7 5.4 %collective-permute-start.4 = (bf16[8,2,2048]{2,1,0:T(2,128)(2,1)S(1)}, bf16[8,2,2048]{2,1,0:T(2,128)(2,1)S(1)}, u32[]{:S(2)}, u32[]{:S(2)}) collective-permute-start(bf16[8,2,2048]{2,1,0:T(2,128)(2,1)S(1)} %get-tuple-element.27), channel_id=1, source_target_pairs={{0,192},{192,0},{384,576},{576,384},{1,193},{193,1},{385,577},{577... | collective-permute-start | bytes 196616 | tf_op jit(solution)/shard_map/ppermute | solution.py:143
  74.1 3.4 %collective-permute-done.4.arrived_ref = bf16[8,2,2048]{2,1,0:T(2,128)(2,1)S(1)} collective-permute-done((bf16[8,2,2048]{2,1,0:T(2,128)(2,1)S(1)}, bf16[8,2,2048]{2,1,0:T(2,128)(2,1)S(1)}, u32[]{:S(2)}, u32[]{:S(2)}) %collective-permute-start.4) | collective-permute-done | bytes 65568 | tf_op jit(solution)/shard_map/ppermute | solution.py:143
  77.5 1.2 %shard_map.101 = (bf16[16,2,2048]{2,1,0:T(2,128)(2,1)}, f32[8,128]{1,0:T(8,128)S(1)}) custom-call(s32[6]{0:T(128)S(1)} %stack.27.place_ref, bf16[8,2,2048]{2,1,0:T(2,128)(2,1)S(1)} %get-tuple-element.26.kept_ref, bf16[8,2,2048]{2,1,0:T(2,128)(2,1)S(1)} %collective-permute-done.4.arrived_ref), custom_call_target="tpu_custom_call" | custom-call | flops 1000000 | bytes 1000000 | tf_op jit(solution)/shard_map/pallas_call | solution.py:192
  78.7 0.6 copy-done.3
  79.3 5.4 %all-to-all-done.1 = bf16[24,8,2048]{2,1,0:T(8,128)(2,1)} async-done(((bf16[24,8,2048]{2,1,0:T(8,128)(2,1)}), bf16[24,8,2048]{2,1,0:T(8,128)(2,1)}, u32[]{:S(2)}, u32[]{:S(2)}) %all-to-all-start.1) | async-done | bytes 786464 | tf_op jit(solution)/shard_map/all_to_all | solution.py:189
  84.7 0.7 shard_map.102.value_ref
  85.4 7.7 %collective-permute-start.5 = (bf16[192,2048]{1,0:T(8,128)(2,1)}, bf16[192,2048]{1,0:T(8,128)(2,1)S(1)}, u32[]{:S(2)}, u32[]{:S(2)}) collective-permute-start(bf16[192,2048]{1,0:T(8,128)(2,1)} %shard_map.102.value_ref), channel_id=1, source_target_pairs={{0,1},{1,0},{2,3},{3,2},{4,5},{5,4},{6,7},{7,6},{8,9},{9,8},{10,11... | collective-permute-start | bytes 2359304 | tf_op jit(solution)/shard_map/ppermute | solution.py:197
  93.0 3.3 %shard_map.103.refs_0_ = bf16[192,4096]{1,0:T(8,128)(2,1)} custom-call(s32[1]{0:T(128)} %bitcast.where_ref, bf16[192,2048]{1,0:T(8,128)(2,1)} %shard_map.102.value_ref), custom_call_target="tpu_custom_call" | custom-call | flops 1000000 | bytes 1000000 | tf_op jit(solution)/shard_map/pallas_call | solution.py:117
  96.3 1.4 %shard_map.104 = bf16[192,4096]{1,0:T(8,128)(2,1)} custom-call(s32[1]{0:T(128)S(6)} %sub.6.where_ref, bf16[192,2048]{1,0:T(8,128)(2,1)S(1)} %collective-permute-done.5.value_ref, bf16[192,4096]{1,0:T(8,128)(2,1)} %shard_map.103.refs_0_), custom_call_target="tpu_custom_call", output_to_operand_aliasing={{}: (2, {})} | custom-call | flops 1000000 | bytes 1000000 | tf_op jit(solution)/shard_map/pallas_call | solution.py:117
  (15 shorter events, 0.0 us)
Async XLA Ops:
  0.6 5.0 %copy-start = (bf16[384,4096]{1,0:T(8,128)(2,1)S(1)}, bf16[384,4096]{1,0:T(8,128)(2,1)}, u32[]{:S(2)}) copy-start(bf16[384,4096]{1,0:T(8,128)(2,1)} %param.11) | copy-start | bytes 9437188
  0.7 3.5 %copy-start.5 = (bf16[192,4096]{1,0:T(8,128)(2,1)S(1)}, bf16[192,4096]{1,0:T(8,128)(2,1)}, u32[]{:S(2)}) copy-start(bf16[192,4096]{1,0:T(8,128)(2,1)} %param.8) | copy-start | bytes 4718596
  0.7 3.9 %copy-start.6 = (bf16[4096,384]{1,0:T(8,128)(2,1)S(1)}, bf16[4096,384]{1,0:T(8,128)(2,1)}, u32[]{:S(2)}) copy-start(bf16[4096,384]{1,0:T(8,128)(2,1)} %param.10) | copy-start | bytes 9437188
  0.7 3.9 %copy-start.7 = (s32[192,384]{1,0:T(8,128)S(1)}, s32[192,384]{1,0:T(8,128)}, u32[]{:S(2)}) copy-start(s32[192,384]{1,0:T(8,128)} %param.12) | copy-start | bytes 884740
  7.1 14.7 %collective-permute-start = (bf16[192,2048]{1,0:T(8,128)(2,1)}, bf16[192,2048]{1,0:T(8,128)(2,1)}, u32[]{:S(2)}, u32[]{:S(2)}) collective-permute-start(bf16[192,2048]{1,0:T(8,128)(2,1)} %convolution_convert_fusion), channel_id=1, source_target_pairs={{0,1},{1,0},{2,3},{3,2},{4,5},{5,4},{6,7},{7,6},{8,9},{9,8},{10,11... | collective-permute-start | bytes 2359304 | tf_op jit(solution)/shard_map/ppermute | solution.py:161
  20.1 9.0 %copy-start.1 = (bf16[16,2,2048]{2,1,0:T(2,128)(2,1)S(1)}, bf16[16,2,2048]{2,1,0:T(2,128)(2,1)}, u32[]{:S(2)}) copy-start(bf16[16,2,2048]{2,1,0:T(2,128)(2,1)} %kv_ref.1) | copy-start | bytes 393220
  20.1 9.0 %copy-start.2 = (s32[16,16]{1,0:T(8,128)S(1)}, s32[16,16]{1,0:T(8,128)}, u32[]{:S(2)}) copy-start(s32[16,16]{1,0:T(8,128)} %dest_ref.1) | copy-start | bytes 3076
  20.1 9.0 %copy-start.4 = (s32[16]{0:T(128)S(1)}, s32[16]{0:T(128)}, u32[]{:S(2)}) copy-start(s32[16]{0:T(128)} %lengths_ref.1) | copy-start | bytes 196
  24.3 31.3 %all-to-all-start = ((bf16[24,8,2048]{2,1,0:T(8,128)(2,1)}), bf16[24,8,2048]{2,1,0:T(8,128)(2,1)}, u32[]{:S(2)}, u32[]{:S(2)}) async-start(bf16[24,8,2048]{2,1,0:T(8,128)(2,1)} %bitcast.15), calls=%async_computation | async-start | bytes 1572864 | tf_op jit(solution)/shard_map/all_to_all | solution.py:172
  30.1 5.4 %collective-permute-start.1 = (bf16[8,2,2048]{2,1,0:T(2,128)(2,1)S(1)}, bf16[8,2,2048]{2,1,0:T(2,128)(2,1)S(1)}, u32[]{:S(2)}, u32[]{:S(2)}) collective-permute-start(bf16[8,2,2048]{2,1,0:T(2,128)(2,1)S(1)} %get-tuple-element.19), channel_id=1, source_target_pairs={{0,48},{48,0},{96,144},{144,96},{1,49},{49,1},{97,145},{145,97},{2... | collective-permute-start | bytes 196616 | tf_op jit(solution)/shard_map/ppermute | solution.py:143
  36.0 6.9 %collective-permute-start.2 = (bf16[8,2,2048]{2,1,0:T(2,128)(2,1)S(1)}, bf16[8,2,2048]{2,1,0:T(2,128)(2,1)S(1)}, u32[]{:S(2)}, u32[]{:S(2)}) collective-permute-start(bf16[8,2,2048]{2,1,0:T(2,128)(2,1)S(1)} %get-tuple-element.21), channel_id=1, source_target_pairs={{0,96},{48,144},{96,0},{144,48},{1,97},{49,145},{97,1},{145,49},{2... | collective-permute-start | bytes 196616 | tf_op jit(solution)/shard_map/ppermute | solution.py:143
  43.5 12.1 %collective-permute-start.3 = (bf16[8,2,2048]{2,1,0:T(2,128)(2,1)S(1)}, bf16[8,2,2048]{2,1,0:T(2,128)(2,1)S(1)}, u32[]{:S(2)}, u32[]{:S(2)}) collective-permute-start(bf16[8,2,2048]{2,1,0:T(2,128)(2,1)S(1)} %get-tuple-element.22), channel_id=1, source_target_pairs={{0,384},{192,576},{384,0},{576,192},{1,385},{193,577},{385,1},{577... | collective-permute-start | bytes 196616 | tf_op jit(solution)/shard_map/ppermute | solution.py:143
  58.3 26.4 %all-to-all-start.1 = ((bf16[24,8,2048]{2,1,0:T(8,128)(2,1)}), bf16[24,8,2048]{2,1,0:T(8,128)(2,1)}, u32[]{:S(2)}, u32[]{:S(2)}) async-start(bf16[24,8,2048]{2,1,0:T(8,128)(2,1)} %get-tuple-element.23), calls=%async_computation.1 | async-start | bytes 1572864 | tf_op jit(solution)/shard_map/all_to_all | solution.py:189
  68.7 8.8 %collective-permute-start.4 = (bf16[8,2,2048]{2,1,0:T(2,128)(2,1)S(1)}, bf16[8,2,2048]{2,1,0:T(2,128)(2,1)S(1)}, u32[]{:S(2)}, u32[]{:S(2)}) collective-permute-start(bf16[8,2,2048]{2,1,0:T(2,128)(2,1)S(1)} %get-tuple-element.27), channel_id=1, source_target_pairs={{0,192},{192,0},{384,576},{576,384},{1,193},{193,1},{385,577},{577... | collective-permute-start | bytes 196616 | tf_op jit(solution)/shard_map/ppermute | solution.py:143
  78.7 0.6 copy-start.3
  85.4 11.0 %collective-permute-start.5 = (bf16[192,2048]{1,0:T(8,128)(2,1)}, bf16[192,2048]{1,0:T(8,128)(2,1)S(1)}, u32[]{:S(2)}, u32[]{:S(2)}) collective-permute-start(bf16[192,2048]{1,0:T(8,128)(2,1)} %shard_map.102.value_ref), channel_id=1, source_target_pairs={{0,1},{1,0},{2,3},{3,2},{4,5},{5,4},{6,7},{7,6},{8,9},{9,8},{10,11... | collective-permute-start | bytes 2359304 | tf_op jit(solution)/shard_map/ppermute | solution.py:197

commit v4 on v2

v4 whole, which is shorter than its diff:
```python
import jax
import jax.numpy as jnp
from jax import lax
from jax.experimental import pallas as pl
from jax.experimental.pallas import tpu as pltpu
from jax.sharding import Mesh, PartitionSpec as P

GRP = ("zh", "x")
TP = ("y", "zl", "core")
RING = ("y", "zl")
SWAP = [(0, 1), (1, 0)]
SIDE = 4
CHIPS = 24
STEPS = 4

bf16, f32 = jnp.bfloat16, jnp.float32
MARK = jax.ShapeDtypeStruct((8, 128), f32)
VMEM = pl.BlockSpec(memory_space=pltpu.VMEM)
SMEM = pl.BlockSpec(memory_space=pltpu.SMEM)
ANY = pl.BlockSpec(memory_space=pl.ANY)


def call(body, out_shape, in_specs, out_specs, **more):
    return pl.pallas_call(
        body,
        out_shape=out_shape,
        in_specs=in_specs,
        out_specs=out_specs,
        cost_estimate=pl.CostEstimate(flops=10**6, bytes_accessed=10**6, transcendentals=0),
        compiler_params=pltpu.CompilerParams(vmem_limit_bytes=16 * 2**20),
        **more,
    )


def sort_body(place_ref, dest_ref, lengths_ref, kv_ref, mark_ref, *out_refs):
    x, mine, first = place_ref[0], place_ref[1], place_ref[2]
    row = lax.broadcasted_iota(jnp.int32, kv_ref.shape[1:], 0) + first
    for r in range(kv_ref.shape[0]):
        d = dest_ref[mine, r]
        value = kv_ref[r]
        value = jnp.where(row < lengths_ref[r], value, jnp.zeros_like(value))
        step = lax.rem(lax.rem(d, SIDE) - x + SIDE, SIDE)
        for k in range(SIDE):

            @pl.when(step == k)
            def _():
                out_refs[k][lax.div(d, SIDE)] = value


def turn_body(shifts, place_ref, *refs):
    x, zh = place_ref[0], place_ref[3]
    in_refs, out_refs = refs[:SIDE], refs[-len(shifts) :]
    for k in range(SIDE):
        source = lax.rem(x - k + SIDE, SIDE)
        for out_ref, j in zip(out_refs, shifts):
            out_ref[source] = in_refs[k][lax.rem(zh + j, SIDE)]


def lay_body(place_ref, *refs):
    zh = place_ref[3]
    in_refs, out_ref, mark_ref = refs[:SIDE], refs[-2], refs[-1]
    mark_ref[...] = jnp.zeros_like(mark_ref)
    for j in range(SIDE):
        source = lax.rem(zh - j + SIDE, SIDE)
        for k in range(SIDE):
            out_ref[source * SIDE + k] = in_refs[j][k]


def add_body(own_ref, arrived_ref, out_ref, mark_ref, total_ref, sems):
    mark_ref[...] = jnp.zeros_like(mark_ref)
    rows = out_ref.shape[0] // STEPS
    copies = []
    for i in range(STEPS):
        block = pl.ds(i * rows, rows)
        total_ref[block] = (own_ref[block] + arrived_ref[block].astype(f32)).astype(bf16)
        copies.append(pltpu.make_async_copy(total_ref.at[block], out_ref.at[block], sems.at[i]))
        copies[-1].start()
    for copy in copies:
        copy.wait()


def sum_body(parts_ref, after_ref, out_ref, mark_ref, total_ref, sems):
    mark_ref[...] = jnp.zeros_like(mark_ref)
    total = parts_ref[0].astype(f32)
    for i in range(1, CHIPS):
        total += parts_ref[i].astype(f32)
    total_ref[...] = total.astype(bf16)
    copies = [pltpu.make_async_copy(total_ref, out_ref.at[i], sems.at[i]) for i in range(CHIPS)]
    for copy in copies:
        copy.start()
    for copy in copies:
        copy.wait()


def half_body(which, core_ref, value_ref, *refs):
    out_ref, sem = refs[-2:]
    width = value_ref.shape[1]
    first = pl.multiple_of((core_ref[0] ^ which) * width, width)
    copy = pltpu.make_async_copy(value_ref, out_ref.at[:, pl.ds(first, width)], sem)
    copy.start()
    copy.wait()


def half_of(out_shape, which, core, value, *into):
    return call(
        lambda *refs: half_body(which, *refs),
        out_shape,
        [SMEM] + [ANY] * (1 + len(into)),
        ANY,
        scratch_shapes=[pltpu.SemaphoreType.DMA(())],
        input_output_aliases={2: 0} if into else {},
    )(core, value, *into)


def after(value, mark):
    return pl.pallas_call(
        lambda value_ref, mark_ref, out_ref: None,
        out_shape=jax.ShapeDtypeStruct(value.shape, value.dtype),
        in_specs=[ANY] * 2,
        out_specs=ANY,
        input_output_aliases={0: 0},
    )(value, mark)


def shift(value, axis, k):
    return lax.ppermute(value, axis, [(i, (i + k) % SIDE) for i in range(SIDE)])


def shards(tokens, gate_weight, up_weight, down_weight, active, kv_blocks, lengths, dest):
    core = lax.axis_index("core")
    x, zh = lax.axis_index("x"), lax.axis_index("zh")
    place = jnp.stack([x, lax.axis_index(GRP), lax.axis_index(TP) * kv_blocks.shape[1], zh])

    gate = jnp.dot(tokens, gate_weight, preferred_element_type=f32)
    up = jnp.dot(tokens, up_weight, preferred_element_type=f32)
    hidden = (jax.nn.silu(gate) * up * active.astype(f32)).astype(bf16)

    rows, width = tokens.shape[0], down_weight.shape[1] // 2
    theirs = lax.dynamic_slice_in_dim(down_weight, (1 - core) * width, width, 1)
    ours = lax.dynamic_slice_in_dim(down_weight, core * width, width, 1)
    away = jnp.dot(hidden, theirs, preferred_element_type=f32).astype(bf16)
    arrived = lax.ppermute(away, "core", SWAP)
    own = jnp.dot(hidden, ours, preferred_element_type=f32)
    total, mark = call(
        add_body,
        [pltpu.HBM((rows, width), bf16), MARK],
        [VMEM] * 2,
        [ANY, VMEM],
        scratch_shapes=[pltpu.VMEM((rows, width), bf16), pltpu.SemaphoreType.DMA((STEPS,))],
    )(own, arrived)

    parts = total.reshape(CHIPS, rows // CHIPS, width)
    parts = lax.all_to_all(parts, RING, split_axis=0, concat_axis=0, tiled=True)

    slots = jax.ShapeDtypeStruct((SIDE, *kv_blocks.shape[1:]), bf16)
    bundles = call(sort_body, [slots] * SIDE, [SMEM] * 3 + [VMEM] * 2, [VMEM] * SIDE)(
        place, dest, lengths, kv_blocks, mark
    )
    bundles = [bundles[0]] + [shift(bundles[k], "x", k) for k in range(1, SIDE)]
    first = call(lambda *refs: turn_body((0, 1), *refs), [slots] * 2, [SMEM] + [VMEM] * SIDE, [VMEM] * 2)(
        place, *bundles
    )
    moved = shift(first[1], "zh", 1)

    spread, mark = call(
        sum_body,
        [pltpu.HBM(parts.shape, bf16), MARK],
        [VMEM, ANY],
        [ANY, VMEM],
        scratch_shapes=[pltpu.VMEM(parts.shape[1:], bf16), pltpu.SemaphoreType.DMA((CHIPS,))],
    )(parts, moved)

    half = lax.all_to_all(spread, RING, split_axis=0, concat_axis=0, tiled=True).reshape(rows, width)

    others = call(lambda *refs: turn_body((2, 3), *refs), [slots] * 2, [SMEM] + [VMEM] * (SIDE + 1), [VMEM] * 2)(
        place, *bundles, mark
    )
    cache, mark = call(
        lay_body, [jax.ShapeDtypeStruct(kv_blocks.shape, bf16), MARK], [SMEM] + [VMEM] * SIDE, [VMEM] * 2
    )(place, first[0], moved, shift(others[0], "zh", 2), shift(others[1], "zh", 3))

    half = after(half, mark)
    other = lax.ppermute(half, "core", SWAP)
    ffn_out = jax.ShapeDtypeStruct((rows, 2 * width), bf16)
    ffn_out = half_of(ffn_out, 1, core[None], other, half_of(ffn_out, 0, core[None], half))
    return (ffn_out, cache)


def solution(mesh):
    fine = Mesh(mesh.devices.reshape(4, 4, 8, 3, 2), GRP + TP)
    return jax.shard_map(
        shards,
        mesh=fine,
        in_specs=(
            P(GRP, None),
            P(None, TP),
            P(None, TP),
            P(TP, None),
            P(GRP, TP),
            P(GRP, TP, None),
            P(GRP),
            P(),
        ),
        out_specs=(P(GRP, None), P(GRP, TP, None)),
        check_vma=False,
    )
```

time: 93.1 us -> 116 us (1.25); the launches traced: 91.7 us -> 116 us
  Pallas kernels: 7.87 us -> 33.7 us
  waiting for transfers between devices: 16.6 us -> 13.8 us
  starting transfers between devices: 57 us -> 59.7 us
  local copies, waits for them, and re-layouts: 2.79 us -> 1.04 us
    pallas_call x5 -> x7, Pallas kernels: 6.66 us -> 32.5 us  [the longest x2 25.8 us: half_of(): call(lambda *refs: half_body(which, *refs), out_shape, [SMEM] + [ANY] * (...]
    all_to_all x1, waiting for transfers between devices: 7.58 us -> 0.01 us  [shards(): parts = lax.all_to_all(parts, RING, split_axis=0, concat_axis=0, tiled=True)]
    ppermute x6, waiting for transfers between devices: 5.28 us -> 12.2 us  [shift(): return lax.ppermute(value, axis, [(i, (i + k) % SIDE) for i in range(SIDE)])]
    ppermute x1, starting transfers between devices: 4.35 us -> 7.21 us  [shards(): other = lax.ppermute(half, 'core', SWAP)]
    ppermute x1, waiting for transfers between devices: 2.1 us -> 0.01 us  [shards(): other = lax.ppermute(half, 'core', SWAP)]
    ppermute x6, starting transfers between devices: 28.1 us -> 26.2 us  [shift(): return lax.ppermute(value, axis, [(i, (i + k) % SIDE) for i in range(SIDE)])]
    all_to_all x1, starting transfers between devices: 7.51 us -> 9.29 us  [shards(): lax.all_to_all(spread, RING, split_axis=0, concat_axis=0, tiled=True)]
    unnamed x20 -> x16, local copies, waits for them, and re-layouts: 2.79 us -> 1.04 us
  transfers between devices with their start and end apart: 10 -> 10, of which waited for: 7 -> 5; matrix products, arithmetic and copies ran while one was open for 1% -> 1% of each run, Pallas kernels for 3% -> 25%
where the time goes in v4:
time: 116 us
  starting transfers between devices  59.7 us (51%)
  Pallas kernels  33.7 us (29%)
  waiting for transfers between devices  13.8 us (12%)
  matrix products  6.52 us (6%)
    ppermute x6, starting transfers between devices, shift(): return lax.ppermute(value, axis, [(i, (i + k) % SIDE) for i in range(SIDE)])  26.2 us
    pallas_call x2, Pallas kernels, half_of(): call(lambda *refs: half_body(which, *refs), out_shape, [SMEM] + [ANY] * (...  25.8 us
    ppermute x1, starting transfers between devices, shards(): arrived = lax.ppermute(away, 'core', SWAP)  12.4 us
    ppermute x6, waiting for transfers between devices, shift(): return lax.ppermute(value, axis, [(i, (i + k) % SIDE) for i in range(SIDE)])  12.2 us
    all_to_all x1, starting transfers between devices, shards(): lax.all_to_all(spread, RING, split_axis=0, concat_axis=0, tiled=True)  9.29 us
    ppermute x1, starting transfers between devices, shards(): other = lax.ppermute(half, 'core', SWAP)  7.21 us
    all_to_all x1, starting transfers between devices, shards(): parts = lax.all_to_all(parts, RING, split_axis=0, concat_axis=0, tiled=True)  4.61 us
    dot_general x1, matrix products, shards(): gate = jnp.dot(tokens, gate_weight, preferred_element_type=f32)  3.49 us
  transfers between devices with their start and end apart: 10, of which 5 were waited for; matrix products, arithmetic and copies ran while one was open for 1% of the time, Pallas kernels for 25%

profile of v4, /device:TPU:1, one launch (start us, length us, event | category | flops | bytes accessed | tf_op | source)
XLA Modules:
  0.0 115.8 jit_solution(1101526372180163213)
XLA Ops:
  0.7 3.5 %fusion.7 = f32[192,384]{1,0:T(8,128)S(1)} fusion(bf16[192,4096]{1,0:T(8,128)(2,1)} %param.8, bf16[4096,384]{1,0:T(8,128)(2,1)} %param.9), kind=kOutput, calls=%fused_computation.10 | convolution fusion | flops 603979776 | bytes 5013504 | tf_op jit(solution)/shard_map/dot_general | solution.py:134
  4.2 0.4 copy-done.6
  4.6 0.0 copy-done.7
  4.6 1.0 fusion.4
  5.6 1.5 %convolution_convert_fusion = bf16[192,2048]{1,0:T(8,128)(2,1)} fusion(bf16[192,384]{1,0:T(8,128)(2,1)S(1)} %fusion.4, bf16[384,4096]{1,0:T(8,128)(2,1)S(1)} %copy-done, s32[]{:T(128)S(6)} %select_n.7), kind=kOutput, calls=%fused_computation | convolution fusion | flops 302383104 | bytes 2506756 | tf_op jit(solution)/shard_map/dot_general | solution.py:141
  7.1 12.4 %collective-permute-start = (bf16[192,2048]{1,0:T(8,128)(2,1)}, bf16[192,2048]{1,0:T(8,128)(2,1)}, u32[]{:S(2)}, u32[]{:S(2)}) collective-permute-start(bf16[192,2048]{1,0:T(8,128)(2,1)} %convolution_convert_fusion), channel_id=1, source_target_pairs={{0,1},{1,0},{2,3},{3,2},{4,5},{5,4},{6,7},{7,6},{8,9},{9,8},{10,11... | collective-permute-start | bytes 2359304 | tf_op jit(solution)/shard_map/ppermute | solution.py:142
  19.5 0.6 fusion.1.own_ref
  20.1 1.6 %collective-permute-done.arrived_ref = bf16[192,2048]{1,0:T(8,128)(2,1)} collective-permute-done((bf16[192,2048]{1,0:T(8,128)(2,1)}, bf16[192,2048]{1,0:T(8,128)(2,1)}, u32[]{:S(2)}, u32[]{:S(2)}) %collective-permute-start) | collective-permute-done | bytes 786464 | tf_op jit(solution)/shard_map/ppermute | solution.py:142
  21.7 2.1 %shard_map.95 = (bf16[192,2048]{1,0:T(8,128)(2,1)}, f32[8,128]{1,0:T(8,128)S(1)}) custom-call(f32[192,2048]{1,0:T(8,128)S(1)} %fusion.1.own_ref, bf16[192,2048]{1,0:T(8,128)(2,1)} %collective-permute-done.arrived_ref), custom_call_target="tpu_custom_call" | custom-call | flops 1000000 | bytes 1000000 | tf_op jit(solution)/shard_map/pallas_call | solution.py:144
  23.8 4.6 %all-to-all-start = ((bf16[24,8,2048]{2,1,0:T(8,128)(2,1)}), bf16[24,8,2048]{2,1,0:T(8,128)(2,1)}, u32[]{:S(2)}, u32[]{:S(2)}) async-start(bf16[24,8,2048]{2,1,0:T(8,128)(2,1)} %bitcast.13), calls=%async_computation | async-start | bytes 1572864 | tf_op jit(solution)/shard_map/all_to_all | solution.py:153
  28.4 0.1 pad_add_fusion.place_ref.refs_0_
  28.5 1.2 %shard_map.96 = (bf16[4,2,2048]{2,1,0:T(2,128)(2,1)S(1)}, bf16[4,2,2048]{2,1,0:T(2,128)(2,1)S(1)}, bf16[4,2,2048]{2,1,0:T(2,128)(2,1)S(1)}, bf16[4,2,2048]{2,1,0:T(2,128)(2,1)S(1)}) custom-call(s32[4]{0:T(128)S(1)} %pad_add_fusion.place_ref.refs_0_, s32[16,16]{1,0:T(8,128)S(1)} %copy-done.2, s32[16]{0:T(128)S(1)} %copy-done.4, ...), custom_call_target="tpu_custom_call" | custom-call | flops 1000000 | bytes 1000000 | tf_op jit(solution)/shard_map/pallas_call | solution.py:156
  29.7 1.9 %collective-permute-start.1 = (bf16[4,2,2048]{2,1,0:T(2,128)(2,1)S(1)}, bf16[4,2,2048]{2,1,0:T(2,128)(2,1)S(1)}, u32[]{:S(2)}, u32[]{:S(2)}) collective-permute-start(bf16[4,2,2048]{2,1,0:T(2,128)(2,1)S(1)} %get-tuple-element.19), channel_id=1, source_target_pairs={{0,48},{48,96},{96,144},{144,0},{1,49},{49,97},{97,145},{145,1},{2... | collective-permute-start | bytes 98312 | tf_op jit(solution)/shard_map/ppermute | solution.py:126
  31.6 2.7 %collective-permute-start.2 = (bf16[4,2,2048]{2,1,0:T(2,128)(2,1)S(1)}, bf16[4,2,2048]{2,1,0:T(2,128)(2,1)S(1)}, u32[]{:S(2)}, u32[]{:S(2)}) collective-permute-start(bf16[4,2,2048]{2,1,0:T(2,128)(2,1)S(1)} %get-tuple-element.20), channel_id=1, source_target_pairs={{0,96},{48,144},{96,0},{144,48},{1,97},{49,145},{97,1},{145,49},{2... | collective-permute-start | bytes 98312 | tf_op jit(solution)/shard_map/ppermute | solution.py:126
  34.4 3.8 %collective-permute-start.3 = (bf16[4,2,2048]{2,1,0:T(2,128)(2,1)S(1)}, bf16[4,2,2048]{2,1,0:T(2,128)(2,1)S(1)}, u32[]{:S(2)}, u32[]{:S(2)}) collective-permute-start(bf16[4,2,2048]{2,1,0:T(2,128)(2,1)S(1)} %get-tuple-element.21), channel_id=1, source_target_pairs={{0,144},{48,0},{96,48},{144,96},{1,145},{49,1},{97,49},{145,97},{2... | collective-permute-start | bytes 98312 | tf_op jit(solution)/shard_map/ppermute | solution.py:126
  38.2 0.0 collective-permute-done.2.refs_3_
  38.2 2.2 %collective-permute-done.3.refs_4_ = bf16[4,2,2048]{2,1,0:T(2,128)(2,1)S(1)} collective-permute-done((bf16[4,2,2048]{2,1,0:T(2,128)(2,1)S(1)}, bf16[4,2,2048]{2,1,0:T(2,128)(2,1)S(1)}, u32[]{:S(2)}, u32[]{:S(2)}) %collective-permute-start.3) | collective-permute-done | bytes 32800 | tf_op jit(solution)/shard_map/ppermute | solution.py:126
  40.4 0.6 shard_map.97
  41.0 7.9 %collective-permute-start.4 = (bf16[4,2,2048]{2,1,0:T(2,128)(2,1)S(1)}, bf16[4,2,2048]{2,1,0:T(2,128)(2,1)S(1)}, u32[]{:S(2)}, u32[]{:S(2)}) collective-permute-start(bf16[4,2,2048]{2,1,0:T(2,128)(2,1)S(1)} %get-tuple-element.22), channel_id=1, source_target_pairs={{0,192},{192,384},{384,576},{576,0},{1,193},{193,385},{385,577},{5... | collective-permute-start | bytes 98312 | tf_op jit(solution)/shard_map/ppermute | solution.py:126
  48.9 5.0 %collective-permute-done.4.after_ref.refs_1_ = bf16[4,2,2048]{2,1,0:T(2,128)(2,1)S(1)} collective-permute-done((bf16[4,2,2048]{2,1,0:T(2,128)(2,1)S(1)}, bf16[4,2,2048]{2,1,0:T(2,128)(2,1)S(1)}, u32[]{:S(2)}, u32[]{:S(2)}) %collective-permute-start.4) | collective-permute-done | bytes 32800 | tf_op jit(solution)/shard_map/ppermute | solution.py:126
  53.9 2.3 %shard_map.98 = (bf16[24,8,2048]{2,1,0:T(8,128)(2,1)}, f32[8,128]{1,0:T(8,128)S(1)}) custom-call(bf16[24,8,2048]{2,1,0:T(8,128)(2,1)} %all-to-all-done.parts_ref, bf16[4,2,2048]{2,1,0:T(2,128)(2,1)S(1)} %collective-permute-done.4.after_ref.refs_1_), custom_call_target="tpu_custom_call" | custom-call | flops 1000000 | bytes 1000000 | tf_op jit(solution)/shard_map/pallas_call | solution.py:165
  56.2 9.3 %all-to-all-start.1 = ((bf16[24,8,2048]{2,1,0:T(8,128)(2,1)}), bf16[24,8,2048]{2,1,0:T(8,128)(2,1)}, u32[]{:S(2)}, u32[]{:S(2)}) async-start(bf16[24,8,2048]{2,1,0:T(8,128)(2,1)} %get-tuple-element.23), calls=%async_computation.1 | async-start | bytes 1572864 | tf_op jit(solution)/shard_map/all_to_all | solution.py:173
  65.5 0.6 shard_map.99
  66.1 8.0 %collective-permute-start.5 = (bf16[4,2,2048]{2,1,0:T(2,128)(2,1)S(1)}, bf16[4,2,2048]{2,1,0:T(2,128)(2,1)S(1)}, u32[]{:S(2)}, u32[]{:S(2)}) collective-permute-start(bf16[4,2,2048]{2,1,0:T(2,128)(2,1)S(1)} %get-tuple-element.26), channel_id=1, source_target_pairs={{0,384},{192,576},{384,0},{576,192},{1,385},{193,577},{385,1},{577... | collective-permute-start | bytes 98312 | tf_op jit(solution)/shard_map/ppermute | solution.py:126
  74.1 1.9 %collective-permute-start.6 = (bf16[4,2,2048]{2,1,0:T(2,128)(2,1)S(1)}, bf16[4,2,2048]{2,1,0:T(2,128)(2,1)S(1)}, u32[]{:S(2)}, u32[]{:S(2)}) collective-permute-start(bf16[4,2,2048]{2,1,0:T(2,128)(2,1)S(1)} %get-tuple-element.27), channel_id=1, source_target_pairs={{0,576},{192,0},{384,192},{576,384},{1,577},{193,1},{385,193},{577... | collective-permute-start | bytes 98312 | tf_op jit(solution)/shard_map/ppermute | solution.py:126
  76.0 4.7 %collective-permute-done.5.refs_2_ = bf16[4,2,2048]{2,1,0:T(2,128)(2,1)S(1)} collective-permute-done((bf16[4,2,2048]{2,1,0:T(2,128)(2,1)S(1)}, bf16[4,2,2048]{2,1,0:T(2,128)(2,1)S(1)}, u32[]{:S(2)}, u32[]{:S(2)}) %collective-permute-start.5) | collective-permute-done | bytes 32800 | tf_op jit(solution)/shard_map/ppermute | solution.py:126
  80.7 0.2 collective-permute-done.6.refs_3_
  80.9 1.2 %shard_map.100 = (bf16[16,2,2048]{2,1,0:T(2,128)(2,1)}, f32[8,128]{1,0:T(8,128)S(1)}) custom-call(s32[4]{0:T(128)S(1)} %pad_add_fusion.place_ref.refs_0_, bf16[4,2,2048]{2,1,0:T(2,128)(2,1)S(1)} %get-tuple-element.24.refs_0_, bf16[4,2,2048]{2,1,0:T(2,128)(2,1)S(1)} %collective-permute-done.4.after_ref.refs_1_, ...), custom_call_target="tpu_custom_call" | custom-call | flops 1000000 | bytes 1000000 | tf_op jit(solution)/shard_map/pallas_call | solution.py:178
  82.1 0.6 copy-done.3
  82.7 7.2 %collective-permute-start.7 = (bf16[192,2048]{1,0:T(8,128)(2,1)}, bf16[192,2048]{1,0:T(8,128)(2,1)S(1)}, u32[]{:S(2)}, u32[]{:S(2)}) collective-permute-start(bf16[192,2048]{1,0:T(8,128)(2,1)} %shard_map.101.refs_1_), channel_id=1, source_target_pairs={{0,1},{1,0},{2,3},{3,2},{4,5},{5,4},{6,7},{7,6},{8,9},{9,8},{10,11... | collective-permute-start | bytes 2359304 | tf_op jit(solution)/shard_map/ppermute | solution.py:183
  89.9 24.9 %shard_map.102.refs_2_ = bf16[192,4096]{1,0:T(8,128)(2,1)} custom-call(s32[1]{0:T(128)} %bitcast.refs_0_, bf16[192,2048]{1,0:T(8,128)(2,1)} %shard_map.101.refs_1_), custom_call_target="tpu_custom_call" | custom-call | flops 1000000 | bytes 1000000 | tf_op jit(solution)/shard_map/pallas_call | solution.py:105
  114.9 0.9 shard_map.103
  (18 shorter events, 0.0 us)
Async XLA Ops:
  0.6 5.0 %copy-start = (bf16[384,4096]{1,0:T(8,128)(2,1)S(1)}, bf16[384,4096]{1,0:T(8,128)(2,1)}, u32[]{:S(2)}) copy-start(bf16[384,4096]{1,0:T(8,128)(2,1)} %param.11) | copy-start | bytes 9437188
  0.7 3.5 %copy-start.5 = (bf16[192,4096]{1,0:T(8,128)(2,1)S(1)}, bf16[192,4096]{1,0:T(8,128)(2,1)}, u32[]{:S(2)}) copy-start(bf16[192,4096]{1,0:T(8,128)(2,1)} %param.8) | copy-start | bytes 4718596
  0.7 3.9 %copy-start.6 = (bf16[4096,384]{1,0:T(8,128)(2,1)S(1)}, bf16[4096,384]{1,0:T(8,128)(2,1)}, u32[]{:S(2)}) copy-start(bf16[4096,384]{1,0:T(8,128)(2,1)} %param.10) | copy-start | bytes 9437188
  0.7 3.9 %copy-start.7 = (s32[192,384]{1,0:T(8,128)S(1)}, s32[192,384]{1,0:T(8,128)}, u32[]{:S(2)}) copy-start(s32[192,384]{1,0:T(8,128)} %param.12) | copy-start | bytes 884740
  7.1 14.7 %collective-permute-start = (bf16[192,2048]{1,0:T(8,128)(2,1)}, bf16[192,2048]{1,0:T(8,128)(2,1)}, u32[]{:S(2)}, u32[]{:S(2)}) collective-permute-start(bf16[192,2048]{1,0:T(8,128)(2,1)} %convolution_convert_fusion), channel_id=1, source_target_pairs={{0,1},{1,0},{2,3},{3,2},{4,5},{5,4},{6,7},{7,6},{8,9},{9,8},{10,11... | collective-permute-start | bytes 2359304 | tf_op jit(solution)/shard_map/ppermute | solution.py:142
  20.1 8.4 %copy-start.1 = (bf16[16,2,2048]{2,1,0:T(2,128)(2,1)S(1)}, bf16[16,2,2048]{2,1,0:T(2,128)(2,1)}, u32[]{:S(2)}) copy-start(bf16[16,2,2048]{2,1,0:T(2,128)(2,1)} %kv_ref.1) | copy-start | bytes 393220
  20.1 8.4 %copy-start.2 = (s32[16,16]{1,0:T(8,128)S(1)}, s32[16,16]{1,0:T(8,128)}, u32[]{:S(2)}) copy-start(s32[16,16]{1,0:T(8,128)} %dest_ref.1) | copy-start | bytes 3076
  20.1 8.4 %copy-start.4 = (s32[16]{0:T(128)S(1)}, s32[16]{0:T(128)}, u32[]{:S(2)}) copy-start(s32[16]{0:T(128)} %lengths_ref.1) | copy-start | bytes 196
  23.8 30.1 %all-to-all-start = ((bf16[24,8,2048]{2,1,0:T(8,128)(2,1)}), bf16[24,8,2048]{2,1,0:T(8,128)(2,1)}, u32[]{:S(2)}, u32[]{:S(2)}) async-start(bf16[24,8,2048]{2,1,0:T(8,128)(2,1)} %bitcast.13), calls=%async_computation | async-start | bytes 1572864 | tf_op jit(solution)/shard_map/all_to_all | solution.py:153
  29.7 8.4 %collective-permute-start.1 = (bf16[4,2,2048]{2,1,0:T(2,128)(2,1)S(1)}, bf16[4,2,2048]{2,1,0:T(2,128)(2,1)S(1)}, u32[]{:S(2)}, u32[]{:S(2)}) collective-permute-start(bf16[4,2,2048]{2,1,0:T(2,128)(2,1)S(1)} %get-tuple-element.19), channel_id=1, source_target_pairs={{0,48},{48,96},{96,144},{144,0},{1,49},{49,97},{97,145},{145,1},{2... | collective-permute-start | bytes 98312 | tf_op jit(solution)/shard_map/ppermute | solution.py:126
  31.6 6.6 %collective-permute-start.2 = (bf16[4,2,2048]{2,1,0:T(2,128)(2,1)S(1)}, bf16[4,2,2048]{2,1,0:T(2,128)(2,1)S(1)}, u32[]{:S(2)}, u32[]{:S(2)}) collective-permute-start(bf16[4,2,2048]{2,1,0:T(2,128)(2,1)S(1)} %get-tuple-element.20), channel_id=1, source_target_pairs={{0,96},{48,144},{96,0},{144,48},{1,97},{49,145},{97,1},{145,49},{2... | collective-permute-start | bytes 98312 | tf_op jit(solution)/shard_map/ppermute | solution.py:126
  34.4 6.0 %collective-permute-start.3 = (bf16[4,2,2048]{2,1,0:T(2,128)(2,1)S(1)}, bf16[4,2,2048]{2,1,0:T(2,128)(2,1)S(1)}, u32[]{:S(2)}, u32[]{:S(2)}) collective-permute-start(bf16[4,2,2048]{2,1,0:T(2,128)(2,1)S(1)} %get-tuple-element.21), channel_id=1, source_target_pairs={{0,144},{48,0},{96,48},{144,96},{1,145},{49,1},{97,49},{145,97},{2... | collective-permute-start | bytes 98312 | tf_op jit(solution)/shard_map/ppermute | solution.py:126
  41.0 12.9 %collective-permute-start.4 = (bf16[4,2,2048]{2,1,0:T(2,128)(2,1)S(1)}, bf16[4,2,2048]{2,1,0:T(2,128)(2,1)S(1)}, u32[]{:S(2)}, u32[]{:S(2)}) collective-permute-start(bf16[4,2,2048]{2,1,0:T(2,128)(2,1)S(1)} %get-tuple-element.22), channel_id=1, source_target_pairs={{0,192},{192,384},{384,576},{576,0},{1,193},{193,385},{385,577},{5... | collective-permute-start | bytes 98312 | tf_op jit(solution)/shard_map/ppermute | solution.py:126
  56.2 26.5 %all-to-all-start.1 = ((bf16[24,8,2048]{2,1,0:T(8,128)(2,1)}), bf16[24,8,2048]{2,1,0:T(8,128)(2,1)}, u32[]{:S(2)}, u32[]{:S(2)}) async-start(bf16[24,8,2048]{2,1,0:T(8,128)(2,1)} %get-tuple-element.23), calls=%async_computation.1 | async-start | bytes 1572864 | tf_op jit(solution)/shard_map/all_to_all | solution.py:173
  66.1 14.7 %collective-permute-start.5 = (bf16[4,2,2048]{2,1,0:T(2,128)(2,1)S(1)}, bf16[4,2,2048]{2,1,0:T(2,128)(2,1)S(1)}, u32[]{:S(2)}, u32[]{:S(2)}) collective-permute-start(bf16[4,2,2048]{2,1,0:T(2,128)(2,1)S(1)} %get-tuple-element.26), channel_id=1, source_target_pairs={{0,384},{192,576},{384,0},{576,192},{1,385},{193,577},{385,1},{577... | collective-permute-start | bytes 98312 | tf_op jit(solution)/shard_map/ppermute | solution.py:126
  74.1 6.9 %collective-permute-start.6 = (bf16[4,2,2048]{2,1,0:T(2,128)(2,1)S(1)}, bf16[4,2,2048]{2,1,0:T(2,128)(2,1)S(1)}, u32[]{:S(2)}, u32[]{:S(2)}) collective-permute-start(bf16[4,2,2048]{2,1,0:T(2,128)(2,1)S(1)} %get-tuple-element.27), channel_id=1, source_target_pairs={{0,576},{192,0},{384,192},{576,384},{1,577},{193,1},{385,193},{577... | collective-permute-start | bytes 98312 | tf_op jit(solution)/shard_map/ppermute | solution.py:126
  82.1 0.6 copy-start.3
  82.7 32.2 %collective-permute-start.7 = (bf16[192,2048]{1,0:T(8,128)(2,1)}, bf16[192,2048]{1,0:T(8,128)(2,1)S(1)}, u32[]{:S(2)}, u32[]{:S(2)}) collective-permute-start(bf16[192,2048]{1,0:T(8,128)(2,1)} %shard_map.101.refs_1_), channel_id=1, source_target_pairs={{0,1},{1,0},{2,3},{3,2},{4,5},{5,4},{6,7},{7,6},{8,9},{9,8},{10,11... | collective-permute-start | bytes 2359304 | tf_op jit(solution)/shard_map/ppermute | solution.py:183

commit v5 on v4

--- a/solution.py
+++ b/solution.py
@@ -7,11 +7,10 @@
 
 GRP = ("zh", "x")
 TP = ("y", "zl", "core")
-RING = ("y", "zl")
 SWAP = [(0, 1), (1, 0)]
 SIDE = 4
-CHIPS = 24
-STEPS = 4
+RING = 8
+RUN = 3
 
 bf16, f32 = jnp.bfloat16, jnp.float32
 MARK = jax.ShapeDtypeStruct((8, 128), f32)
@@ -66,26 +65,32 @@
             out_ref[source * SIDE + k] = in_refs[j][k]
 
 
-def add_body(own_ref, arrived_ref, out_ref, mark_ref, total_ref, sems):
+def add_body(zl_ref, own_ref, arrived_ref, keep_ref, *refs):
+    rows = keep_ref.shape[0]
+    refs[-1][...] = jnp.zeros_like(refs[-1])
+    for k in range(RUN):
+        block = pl.ds(pl.multiple_of(lax.rem(zl_ref[0] + k, RUN) * rows, rows), rows)
+        total = own_ref[block] + arrived_ref[block].astype(f32)
+        if k == 0:
+            keep_ref[...] = total
+        else:
+            refs[k - 1][...] = total.astype(bf16)
+
+
+def run_body(keep_ref, first_ref, second_ref, *refs):
+    out_ref, mark_ref = refs[-2:]
     mark_ref[...] = jnp.zeros_like(mark_ref)
-    rows = out_ref.shape[0] // STEPS
-    copies = []
-    for i in range(STEPS):
-        block = pl.ds(i * rows, rows)
-        total_ref[block] = (own_ref[block] + arrived_ref[block].astype(f32)).astype(bf16)
-        copies.append(pltpu.make_async_copy(total_ref.at[block], out_ref.at[block], sems.at[i]))
-        copies[-1].start()
-    for copy in copies:
-        copy.wait()
-
-
-def sum_body(parts_ref, after_ref, out_ref, mark_ref, total_ref, sems):
+    total = keep_ref[...] + first_ref[...].astype(f32) + second_ref[...].astype(f32)
+    out_ref[...] = total.astype(bf16)
+
+
+def ring_body(parts_ref, after_ref, out_ref, mark_ref, total_ref, sems):
     mark_ref[...] = jnp.zeros_like(mark_ref)
     total = parts_ref[0].astype(f32)
-    for i in range(1, CHIPS):
+    for i in range(1, RING):
         total += parts_ref[i].astype(f32)
     total_ref[...] = total.astype(bf16)
-    copies = [pltpu.make_async_copy(total_ref, out_ref.at[i], sems.at[i]) for i in range(CHIPS)]
+    copies = [pltpu.make_async_copy(total_ref, out_ref.at[i], sems.at[i]) for i in range(RING)]
     for copy in copies:
         copy.start()
     for copy in copies:
@@ -105,7 +110,7 @@
     return call(
         lambda *refs: half_body(which, *refs),
         out_shape,
-        [SMEM] + [ANY] * (1 + len(into)),
+        [SMEM, VMEM] + [ANY] * len(into),
         ANY,
         scratch_shapes=[pltpu.SemaphoreType.DMA(())],
         input_output_aliases={2: 0} if into else {},
@@ -122,8 +127,8 @@
     )(value, mark)
 
 
-def shift(value, axis, k):
-    return lax.ppermute(value, axis, [(i, (i + k) % SIDE) for i in range(SIDE)])
+def shift(value, axis, k, size=SIDE):
+    return lax.ppermute(value, axis, [(i, (i + k) % size) for i in range(size)])
 
 
 def shards(tokens, gate_weight, up_weight, down_weight, active, kv_blocks, lengths, dest):
@@ -141,36 +146,42 @@
     away = jnp.dot(hidden, theirs, preferred_element_type=f32).astype(bf16)
     arrived = lax.ppermute(away, "core", SWAP)
     own = jnp.dot(hidden, ours, preferred_element_type=f32)
-    total, mark = call(
+    piece = rows // RUN
+    keep, *sends, mark = call(
         add_body,
-        [pltpu.HBM((rows, width), bf16), MARK],
-        [VMEM] * 2,
-        [ANY, VMEM],
-        scratch_shapes=[pltpu.VMEM((rows, width), bf16), pltpu.SemaphoreType.DMA((STEPS,))],
-    )(own, arrived)
-
-    parts = total.reshape(CHIPS, rows // CHIPS, width)
-    parts = lax.all_to_all(parts, RING, split_axis=0, concat_axis=0, tiled=True)
+        [pltpu.HBM((piece, width), f32)] + [jax.ShapeDtypeStruct((piece, width), bf16)] * 2 + [MARK],
+        [SMEM] + [VMEM] * 2,
+        [VMEM] * 4,
+    )(lax.axis_index("zl")[None], own, arrived)
+
+    sends = [shift(sends[k - 1], "zl", k, RUN) for k in range(1, RUN)]
 
     slots = jax.ShapeDtypeStruct((SIDE, *kv_blocks.shape[1:]), bf16)
     bundles = call(sort_body, [slots] * SIDE, [SMEM] * 3 + [VMEM] * 2, [VMEM] * SIDE)(
         place, dest, lengths, kv_blocks, mark
     )
     bundles = [bundles[0]] + [shift(bundles[k], "x", k) for k in range(1, SIDE)]
-    first = call(lambda *refs: turn_body((0, 1), *refs), [slots] * 2, [SMEM] + [VMEM] * SIDE, [VMEM] * 2)(
-        place, *bundles
+
+    total, mark = call(
+        run_body, [pltpu.HBM((piece, width), bf16), MARK], [VMEM] * 3 + [ANY] * 3, [VMEM] * 2
+    )(keep, *sends, *bundles[1:])
+    parts = total.reshape(RING, piece // RING, width)
+    parts = lax.all_to_all(parts, "y", split_axis=0, concat_axis=0, tiled=True)
+
+    first = call(lambda *refs: turn_body((0, 1), *refs), [slots] * 2, [SMEM] + [VMEM] * (SIDE + 1), [VMEM] * 2)(
+        place, *bundles, mark
     )
     moved = shift(first[1], "zh", 1)
 
     spread, mark = call(
-        sum_body,
+        ring_body,
         [pltpu.HBM(parts.shape, bf16), MARK],
         [VMEM, ANY],
         [ANY, VMEM],
-        scratch_shapes=[pltpu.VMEM(parts.shape[1:], bf16), pltpu.SemaphoreType.DMA((CHIPS,))],
+        scratch_shapes=[pltpu.VMEM(parts.shape[1:], bf16), pltpu.SemaphoreType.DMA((RING,))],
     )(parts, moved)
 
-    half = lax.all_to_all(spread, RING, split_axis=0, concat_axis=0, tiled=True).reshape(rows, width)
+    third = lax.all_to_all(spread, "y", split_axis=0, concat_axis=0, tiled=True).reshape(piece, width)
 
     others = call(lambda *refs: turn_body((2, 3), *refs), [slots] * 2, [SMEM] + [VMEM] * (SIDE + 1), [VMEM] * 2)(
         place, *bundles, mark
@@ -179,7 +190,7 @@
         lay_body, [jax.ShapeDtypeStruct(kv_blocks.shape, bf16), MARK], [SMEM] + [VMEM] * SIDE, [VMEM] * 2
     )(place, first[0], moved, shift(others[0], "zh", 2), shift(others[1], "zh", 3))
 
-    half = after(half, mark)
+    half = lax.all_gather(after(third, mark), "zl", axis=0, tiled=True)
     other = lax.ppermute(half, "core", SWAP)
     ffn_out = jax.ShapeDtypeStruct((rows, 2 * width), bf16)
     ffn_out = half_of(ffn_out, 1, core[None], other, half_of(ffn_out, 0, core[None], half))

time: 116 us -> 112 us (0.966)
  Pallas kernels: 33.7 us -> 10 us
  blocking collectives: 0 us -> 11.7 us
  local copies, waits for them, and re-layouts: 1.04 us -> 5.45 us
  starting transfers between devices: 59.7 us -> 62 us
    pallas_call x4 -> x5, Pallas kernels: 30.2 us -> 6.53 us  [the longest x1 2.22 us: shards(): call(add_body, [pltpu.HBM((piece, width), f32)] + [jax.ShapeDtypeStruct((...]
    all_gather x0 -> x1, blocking collectives: none -> 11.7 us  [shards(): half = lax.all_gather(after(third, mark), 'zl', axis=0, tiled=True)]
    ppermute x6 -> x8, starting transfers between devices: 26.2 us -> 31.2 us  [shift(): return lax.ppermute(value, axis, [(i, (i + k) % size) for i in range(size)])]
    unnamed x16 -> x28, local copies, waits for them, and re-layouts: 1.04 us -> 5.45 us
    all_to_all x2, starting transfers between devices: 13.9 us -> 10.1 us  [the longest x1 6.65 us: shards(): lax.all_to_all(spread, 'y', split_axis=0, concat_axis=0, tiled=True)]
    ppermute x1, starting transfers between devices: 7.21 us -> 8.39 us  [shards(): other = lax.ppermute(half, 'core', SWAP)]
    ppermute x6 -> x8, waiting for transfers between devices: 12.2 us -> 12 us  [shift(): return lax.ppermute(value, axis, [(i, (i + k) % size) for i in range(size)])]
  transfers between devices with their start and end apart: 10 -> 12, of which waited for: 5 -> 6; matrix products, arithmetic and copies ran while one was open for 1% -> 1% of each run, Pallas kernels for 25% -> 4%
where the time goes in v5:
time: 112 us; the launch traced here: 111 us
  starting transfers between devices  62 us (55%)
  waiting for transfers between devices  14.6 us (13%)
  blocking collectives  11.7 us (10%)
  Pallas kernels  10 us (9%)
  matrix products  6.52 us (6%)
  local copies, waits for them, and re-layouts  5.45 us (5%)
    ppermute x8, starting transfers between devices, shift(): return lax.ppermute(value, axis, [(i, (i + k) % size) for i in range(size)])  31.2 us
    ppermute x1, starting transfers between devices, shards(): arrived = lax.ppermute(away, 'core', SWAP)  12.4 us
    ppermute x8, waiting for transfers between devices, shift(): return lax.ppermute(value, axis, [(i, (i + k) % size) for i in range(size)])  12 us
    all_gather x1, blocking collectives, shards(): half = lax.all_gather(after(third, mark), 'zl', axis=0, tiled=True)  11.7 us
    ppermute x1, starting transfers between devices, shards(): other = lax.ppermute(half, 'core', SWAP)  8.39 us
    all_to_all x1, starting transfers between devices, shards(): lax.all_to_all(spread, 'y', split_axis=0, concat_axis=0, tiled=True)  6.65 us
    unnamed x28, local copies, waits for them, and re-layouts  5.45 us
    dot_general x1, matrix products, shards(): gate = jnp.dot(tokens, gate_weight, preferred_element_type=f32)  3.49 us
  transfers between devices with their start and end apart: 12, of which 6 were waited for; matrix products, arithmetic and copies ran while one was open for 1% of the time, Pallas kernels for 4%

profile of v5, /device:TPU:1, one launch (start us, length us, event | category | flops | bytes accessed | tf_op | source)
XLA Modules:
  0.0 111.3 jit_solution(12120818866688174970)
XLA Ops:
  0.7 3.5 %fusion.7 = f32[192,384]{1,0:T(8,128)S(1)} fusion(bf16[192,4096]{1,0:T(8,128)(2,1)} %param.8, bf16[4096,384]{1,0:T(8,128)(2,1)} %param.9), kind=kOutput, calls=%fused_computation.10 | convolution fusion | flops 603979776 | bytes 5013504 | tf_op jit(solution)/shard_map/dot_general | solution.py:139
  4.6 1.0 fusion.4
  5.6 1.5 %convolution_convert_fusion = bf16[192,2048]{1,0:T(8,128)(2,1)} fusion(bf16[192,384]{1,0:T(8,128)(2,1)S(1)} %fusion.4, bf16[384,4096]{1,0:T(8,128)(2,1)S(1)} %copy-done, s32[]{:T(128)S(6)} %select_n.7), kind=kOutput, calls=%fused_computation | convolution fusion | flops 302383104 | bytes 2506756 | tf_op jit(solution)/shard_map/dot_general | solution.py:146
  7.1 12.4 %collective-permute-start = (bf16[192,2048]{1,0:T(8,128)(2,1)}, bf16[192,2048]{1,0:T(8,128)(2,1)}, u32[]{:S(2)}, u32[]{:S(2)}) collective-permute-start(bf16[192,2048]{1,0:T(8,128)(2,1)} %convolution_convert_fusion), channel_id=1, source_target_pairs={{0,1},{1,0},{2,3},{3,2},{4,5},{5,4},{6,7},{7,6},{8,9},{9,8},{10,11... | collective-permute-start | bytes 2359304 | tf_op jit(solution)/shard_map/ppermute | solution.py:147
  20.1 1.6 %collective-permute-done.arrived_ref = bf16[192,2048]{1,0:T(8,128)(2,1)} collective-permute-done((bf16[192,2048]{1,0:T(8,128)(2,1)}, bf16[192,2048]{1,0:T(8,128)(2,1)}, u32[]{:S(2)}, u32[]{:S(2)}) %collective-permute-start) | collective-permute-done | bytes 786464 | tf_op jit(solution)/shard_map/ppermute | solution.py:147
  21.7 2.2 %shard_map.95 = (f32[64,2048]{1,0:T(8,128)}, bf16[64,2048]{1,0:T(8,128)(2,1)}, bf16[64,2048]{1,0:T(8,128)(2,1)}, f32[8,128]{1,0:T(8,128)S(1)}) custom-call(s32[1]{0:T(128)} %bitcast.1.zl_ref, f32[192,2048]{1,0:T(8,128)S(1)} %fusion.1.own_ref, bf16[192,2048]{1,0:T(8,128)(2,1)} %collective-permute-done.arrived_ref), custom_call_target="tpu_custom_call" | custom-call | flops 1000000 | bytes 1000000 | tf_op jit(solution)/shard_map/pallas_call | solution.py:150
  23.9 1.9 %collective-permute-start.1 = (bf16[64,2048]{1,0:T(8,128)(2,1)}, bf16[64,2048]{1,0:T(8,128)(2,1)S(1)}, u32[]{:S(2)}, u32[]{:S(2)}) collective-permute-start(bf16[64,2048]{1,0:T(8,128)(2,1)} %get-tuple-element.21), channel_id=1, source_target_pairs={{0,2},{2,4},{4,0},{1,3},{3,5},{5,1},{6,8},{8,10},{10,6},{7,9},{9,1... | collective-permute-start | bytes 786440 | tf_op jit(solution)/shard_map/ppermute | solution.py:131
  25.9 4.3 %collective-permute-start.2 = (bf16[64,2048]{1,0:T(8,128)(2,1)}, bf16[64,2048]{1,0:T(8,128)(2,1)}, u32[]{:S(2)}, u32[]{:S(2)}) collective-permute-start(bf16[64,2048]{1,0:T(8,128)(2,1)} %get-tuple-element.22), channel_id=1, source_target_pairs={{0,4},{2,0},{4,2},{1,5},{3,1},{5,3},{6,10},{8,6},{10,8},{7,11},{9,... | collective-permute-start | bytes 786440 | tf_op jit(solution)/shard_map/ppermute | solution.py:131
  30.9 1.2 %shard_map.96 = (bf16[4,2,2048]{2,1,0:T(2,128)(2,1)S(1)}, bf16[4,2,2048]{2,1,0:T(2,128)(2,1)S(1)}, bf16[4,2,2048]{2,1,0:T(2,128)(2,1)S(1)}, bf16[4,2,2048]{2,1,0:T(2,128)(2,1)S(1)}) custom-call(s32[4]{0:T(128)S(1)} %pad_add_fusion.place_ref.refs_0_, s32[16,16]{1,0:T(8,128)S(1)} %copy-done.8, s32[16]{0:T(128)S(1)} %copy-done.10, ...), custom_call_target="tpu_custom_call" | custom-call | flops 1000000 | bytes 1000000 | tf_op jit(solution)/shard_map/pallas_call | solution.py:160
  32.7 1.9 %collective-permute-start.3 = (bf16[4,2,2048]{2,1,0:T(2,128)(2,1)S(1)}, bf16[4,2,2048]{2,1,0:T(2,128)(2,1)S(1)}, u32[]{:S(2)}, u32[]{:S(2)}) collective-permute-start(bf16[4,2,2048]{2,1,0:T(2,128)(2,1)S(1)} %get-tuple-element.24), channel_id=1, source_target_pairs={{0,48},{48,96},{96,144},{144,0},{1,49},{49,97},{97,145},{145,1},{2... | collective-permute-start | bytes 98312 | tf_op jit(solution)/shard_map/ppermute | solution.py:131
  34.6 1.9 %collective-permute-start.4 = (bf16[4,2,2048]{2,1,0:T(2,128)(2,1)S(1)}, bf16[4,2,2048]{2,1,0:T(2,128)(2,1)S(1)}, u32[]{:S(2)}, u32[]{:S(2)}) collective-permute-start(bf16[4,2,2048]{2,1,0:T(2,128)(2,1)S(1)} %get-tuple-element.25), channel_id=1, source_target_pairs={{0,96},{48,144},{96,0},{144,48},{1,97},{49,145},{97,1},{145,49},{2... | collective-permute-start | bytes 98312 | tf_op jit(solution)/shard_map/ppermute | solution.py:131
  36.5 4.6 %collective-permute-start.5 = (bf16[4,2,2048]{2,1,0:T(2,128)(2,1)S(1)}, bf16[4,2,2048]{2,1,0:T(2,128)(2,1)S(1)}, u32[]{:S(2)}, u32[]{:S(2)}) collective-permute-start(bf16[4,2,2048]{2,1,0:T(2,128)(2,1)S(1)} %get-tuple-element.26), channel_id=1, source_target_pairs={{0,144},{48,0},{96,48},{144,96},{1,145},{49,1},{97,49},{145,97},{2... | collective-permute-start | bytes 98312 | tf_op jit(solution)/shard_map/ppermute | solution.py:131
  41.1 1.9 %collective-permute-done.5.refs_2_.refs_4_ = bf16[4,2,2048]{2,1,0:T(2,128)(2,1)S(1)} collective-permute-done((bf16[4,2,2048]{2,1,0:T(2,128)(2,1)S(1)}, bf16[4,2,2048]{2,1,0:T(2,128)(2,1)S(1)}, u32[]{:S(2)}, u32[]{:S(2)}) %collective-permute-start.5) | collective-permute-done | bytes 32800 | tf_op jit(solution)/shard_map/ppermute | solution.py:131
  43.1 1.0 copy-done.1
  44.1 1.7 %shard_map.97 = (bf16[64,2048]{1,0:T(8,128)(2,1)}, f32[8,128]{1,0:T(8,128)S(1)}) custom-call(f32[64,2048]{1,0:T(8,128)S(1)} %copy-done.1, bf16[64,2048]{1,0:T(8,128)(2,1)S(1)} %collective-permute-done.1.first_ref, bf16[64,2048]{1,0:T(8,128)(2,1)} %collective-permute-done.2.second_ref, bf16[4,2,2048]{2,1,0:T(2,128)(2,1)S(1)} %collective-permute-done.3.refs_0_.refs_2_, ...), custom_call_target="tpu_custom_call" | custom-call | flops 1000000 | bytes 1000000 | tf_op jit(solution)/shard_map/pallas_call | solution.py:165
  45.9 3.4 %all-to-all-start = ((bf16[8,8,2048]{2,1,0:T(8,128)(2,1)}), bf16[8,8,2048]{2,1,0:T(8,128)(2,1)S(1)}, u32[]{:S(2)}, u32[]{:S(2)}) async-start(bf16[8,8,2048]{2,1,0:T(8,128)(2,1)} %bitcast.14), calls=%async_computation | async-start | bytes 524288 | tf_op jit(solution)/shard_map/all_to_all | solution.py:169
  50.5 6.5 %collective-permute-start.6 = (bf16[4,2,2048]{2,1,0:T(2,128)(2,1)S(1)}, bf16[4,2,2048]{2,1,0:T(2,128)(2,1)S(1)}, u32[]{:S(2)}, u32[]{:S(2)}) collective-permute-start(bf16[4,2,2048]{2,1,0:T(2,128)(2,1)S(1)} %get-tuple-element.30), channel_id=1, source_target_pairs={{0,192},{192,384},{384,576},{576,0},{1,193},{193,385},{385,577},{5... | collective-permute-start | bytes 98312 | tf_op jit(solution)/shard_map/ppermute | solution.py:131
  57.0 5.2 %collective-permute-done.6.after_ref.refs_1_ = bf16[4,2,2048]{2,1,0:T(2,128)(2,1)S(1)} collective-permute-done((bf16[4,2,2048]{2,1,0:T(2,128)(2,1)S(1)}, bf16[4,2,2048]{2,1,0:T(2,128)(2,1)S(1)}, u32[]{:S(2)}, u32[]{:S(2)}) %collective-permute-start.6) | collective-permute-done | bytes 32800 | tf_op jit(solution)/shard_map/ppermute | solution.py:131
  62.2 0.8 shard_map.99
  63.0 6.7 %all-to-all-start.1 = ((bf16[8,8,2048]{2,1,0:T(8,128)(2,1)}), bf16[8,8,2048]{2,1,0:T(8,128)(2,1)}, u32[]{:S(2)}, u32[]{:S(2)}) async-start(bf16[8,8,2048]{2,1,0:T(8,128)(2,1)} %get-tuple-element.31), calls=%async_computation.1 | async-start | bytes 524288 | tf_op jit(solution)/shard_map/all_to_all | solution.py:184
  69.7 0.8 copy-done.5
  71.0 8.2 %collective-permute-start.7 = (bf16[4,2,2048]{2,1,0:T(2,128)(2,1)S(1)}, bf16[4,2,2048]{2,1,0:T(2,128)(2,1)S(1)}, u32[]{:S(2)}, u32[]{:S(2)}) collective-permute-start(bf16[4,2,2048]{2,1,0:T(2,128)(2,1)S(1)} %get-tuple-element.34), channel_id=1, source_target_pairs={{0,384},{192,576},{384,0},{576,192},{1,385},{193,577},{385,1},{577... | collective-permute-start | bytes 98312 | tf_op jit(solution)/shard_map/ppermute | solution.py:131
  79.1 1.9 %collective-permute-start.8 = (bf16[4,2,2048]{2,1,0:T(2,128)(2,1)S(1)}, bf16[4,2,2048]{2,1,0:T(2,128)(2,1)S(1)}, u32[]{:S(2)}, u32[]{:S(2)}) collective-permute-start(bf16[4,2,2048]{2,1,0:T(2,128)(2,1)S(1)} %get-tuple-element.35), channel_id=1, source_target_pairs={{0,576},{192,0},{384,192},{576,384},{1,577},{193,1},{385,193},{577... | collective-permute-start | bytes 98312 | tf_op jit(solution)/shard_map/ppermute | solution.py:131
  81.1 0.9 collective-permute-done.7.refs_2_
  82.0 3.9 %collective-permute-done.8.refs_3_ = bf16[4,2,2048]{2,1,0:T(2,128)(2,1)S(1)} collective-permute-done((bf16[4,2,2048]{2,1,0:T(2,128)(2,1)S(1)}, bf16[4,2,2048]{2,1,0:T(2,128)(2,1)S(1)}, u32[]{:S(2)}, u32[]{:S(2)}) %collective-permute-start.8) | collective-permute-done | bytes 32800 | tf_op jit(solution)/shard_map/ppermute | solution.py:131
  85.9 0.8 copy-done.7
  86.7 1.2 %shard_map.101 = (bf16[16,2,2048]{2,1,0:T(2,128)(2,1)}, f32[8,128]{1,0:T(8,128)S(1)}) custom-call(s32[4]{0:T(128)S(1)} %pad_add_fusion.place_ref.refs_0_, bf16[4,2,2048]{2,1,0:T(2,128)(2,1)S(1)} %copy-done.7, bf16[4,2,2048]{2,1,0:T(2,128)(2,1)S(1)} %collective-permute-done.6.after_ref.refs_1_, bf16[4,2,2048]{2,1,0:T(2,128)(2,1)S(1)} %collective-permute-done.7.refs_2_, ...), custom_call_target="tpu_custom_call" | custom-call | flops 1000000 | bytes 1000000 | tf_op jit(solution)/shard_map/pallas_call | solution.py:189
  88.5 11.7 %all_gather.3.refs_1_ = bf16[192,2048]{1,0:T(8,128)(2,1)S(1)} all-gather(bf16[64,2048]{1,0:T(8,128)(2,1)} %shard_map.102), channel_id=1, replica_groups=mesh['zh'=4,'x'=4,'y'=8,'zl'=3,'core'=2] {'zl'}, dimensions={0}, use_global_device_ids=true | all-gather | bytes 1048576 | tf_op jit(solution)/shard_map/all_gather | solution.py:193
  100.1 8.4 %collective-permute-start.9 = (bf16[192,2048]{1,0:T(8,128)(2,1)S(1)}, bf16[192,2048]{1,0:T(8,128)(2,1)S(1)}, u32[]{:S(2)}, u32[]{:S(2)}) collective-permute-start(bf16[192,2048]{1,0:T(8,128)(2,1)S(1)} %all_gather.3.refs_1_), channel_id=1, source_target_pairs={{0,1},{1,0},{2,3},{3,2},{4,5},{5,4},{6,7},{7,6},{8,9},{9,8},{10,11... | collective-permute-start | bytes 2359304 | tf_op jit(solution)/shard_map/ppermute | solution.py:194
  108.5 0.9 shard_map.103.refs_2_
  109.4 1.0 collective-permute-done.9.refs_1_
  110.4 0.9 shard_map.104
  (36 shorter events, 4.7 us)
Async XLA Ops:
  0.6 5.0 %copy-start = (bf16[384,4096]{1,0:T(8,128)(2,1)S(1)}, bf16[384,4096]{1,0:T(8,128)(2,1)}, u32[]{:S(2)}) copy-start(bf16[384,4096]{1,0:T(8,128)(2,1)} %param.11) | copy-start | bytes 9437188
  0.7 3.5 %copy-start.11 = (bf16[192,4096]{1,0:T(8,128)(2,1)S(1)}, bf16[192,4096]{1,0:T(8,128)(2,1)}, u32[]{:S(2)}) copy-start(bf16[192,4096]{1,0:T(8,128)(2,1)} %param.8) | copy-start | bytes 4718596
  0.7 3.9 %copy-start.12 = (bf16[4096,384]{1,0:T(8,128)(2,1)S(1)}, bf16[4096,384]{1,0:T(8,128)(2,1)}, u32[]{:S(2)}) copy-start(bf16[4096,384]{1,0:T(8,128)(2,1)} %param.10) | copy-start | bytes 9437188
  0.7 3.9 %copy-start.13 = (s32[192,384]{1,0:T(8,128)S(1)}, s32[192,384]{1,0:T(8,128)}, u32[]{:S(2)}) copy-start(s32[192,384]{1,0:T(8,128)} %param.12) | copy-start | bytes 884740
  7.1 14.7 %collective-permute-start = (bf16[192,2048]{1,0:T(8,128)(2,1)}, bf16[192,2048]{1,0:T(8,128)(2,1)}, u32[]{:S(2)}, u32[]{:S(2)}) collective-permute-start(bf16[192,2048]{1,0:T(8,128)(2,1)} %convolution_convert_fusion), channel_id=1, source_target_pairs={{0,1},{1,0},{2,3},{3,2},{4,5},{5,4},{6,7},{7,6},{8,9},{9,8},{10,11... | collective-permute-start | bytes 2359304 | tf_op jit(solution)/shard_map/ppermute | solution.py:147
  20.1 10.1 %copy-start.2 = (bf16[16,2,2048]{2,1,0:T(2,128)(2,1)S(1)}, bf16[16,2,2048]{2,1,0:T(2,128)(2,1)}, u32[]{:S(2)}) copy-start(bf16[16,2,2048]{2,1,0:T(2,128)(2,1)} %kv_ref.1) | copy-start | bytes 393220
  20.1 10.1 %copy-start.8 = (s32[16,16]{1,0:T(8,128)S(1)}, s32[16,16]{1,0:T(8,128)}, u32[]{:S(2)}) copy-start(s32[16,16]{1,0:T(8,128)} %dest_ref.1) | copy-start | bytes 3076
  23.9 19.1 %collective-permute-start.1 = (bf16[64,2048]{1,0:T(8,128)(2,1)}, bf16[64,2048]{1,0:T(8,128)(2,1)S(1)}, u32[]{:S(2)}, u32[]{:S(2)}) collective-permute-start(bf16[64,2048]{1,0:T(8,128)(2,1)} %get-tuple-element.21), channel_id=1, source_target_pairs={{0,2},{2,4},{4,0},{1,3},{3,5},{5,1},{6,8},{8,10},{10,6},{7,9},{9,1... | collective-permute-start | bytes 786440 | tf_op jit(solution)/shard_map/ppermute | solution.py:131
  25.9 17.2 %collective-permute-start.2 = (bf16[64,2048]{1,0:T(8,128)(2,1)}, bf16[64,2048]{1,0:T(8,128)(2,1)}, u32[]{:S(2)}, u32[]{:S(2)}) collective-permute-start(bf16[64,2048]{1,0:T(8,128)(2,1)} %get-tuple-element.22), channel_id=1, source_target_pairs={{0,4},{2,0},{4,2},{1,5},{3,1},{5,3},{6,10},{8,6},{10,8},{7,11},{9,... | collective-permute-start | bytes 786440 | tf_op jit(solution)/shard_map/ppermute | solution.py:131
  30.2 0.7 copy-start.10
  32.1 0.6 copy-start.3
  32.7 8.4 %collective-permute-start.3 = (bf16[4,2,2048]{2,1,0:T(2,128)(2,1)S(1)}, bf16[4,2,2048]{2,1,0:T(2,128)(2,1)S(1)}, u32[]{:S(2)}, u32[]{:S(2)}) collective-permute-start(bf16[4,2,2048]{2,1,0:T(2,128)(2,1)S(1)} %get-tuple-element.24), channel_id=1, source_target_pairs={{0,48},{48,96},{96,144},{144,0},{1,49},{49,97},{97,145},{145,1},{2... | collective-permute-start | bytes 98312 | tf_op jit(solution)/shard_map/ppermute | solution.py:131
  34.6 6.5 %collective-permute-start.4 = (bf16[4,2,2048]{2,1,0:T(2,128)(2,1)S(1)}, bf16[4,2,2048]{2,1,0:T(2,128)(2,1)S(1)}, u32[]{:S(2)}, u32[]{:S(2)}) collective-permute-start(bf16[4,2,2048]{2,1,0:T(2,128)(2,1)S(1)} %get-tuple-element.25), channel_id=1, source_target_pairs={{0,96},{48,144},{96,0},{144,48},{1,97},{49,145},{97,1},{145,49},{2... | collective-permute-start | bytes 98312 | tf_op jit(solution)/shard_map/ppermute | solution.py:131
  36.5 6.5 %collective-permute-start.5 = (bf16[4,2,2048]{2,1,0:T(2,128)(2,1)S(1)}, bf16[4,2,2048]{2,1,0:T(2,128)(2,1)S(1)}, u32[]{:S(2)}, u32[]{:S(2)}) collective-permute-start(bf16[4,2,2048]{2,1,0:T(2,128)(2,1)S(1)} %get-tuple-element.26), channel_id=1, source_target_pairs={{0,144},{48,0},{96,48},{144,96},{1,145},{49,1},{97,49},{145,97},{2... | collective-permute-start | bytes 98312 | tf_op jit(solution)/shard_map/ppermute | solution.py:131
  43.1 1.0 copy-start.1
  44.1 5.2 %copy-start.4 = (bf16[4,2,2048]{2,1,0:T(2,128)(2,1)S(1)}, bf16[4,2,2048]{2,1,0:T(2,128)(2,1)}, u32[]{:S(2)}) copy-start(bf16[4,2,2048]{2,1,0:T(2,128)(2,1)} %copy-done.3) | copy-start | bytes 98308
  45.9 16.3 %all-to-all-start = ((bf16[8,8,2048]{2,1,0:T(8,128)(2,1)}), bf16[8,8,2048]{2,1,0:T(8,128)(2,1)S(1)}, u32[]{:S(2)}, u32[]{:S(2)}) async-start(bf16[8,8,2048]{2,1,0:T(8,128)(2,1)} %bitcast.14), calls=%async_computation | async-start | bytes 524288 | tf_op jit(solution)/shard_map/all_to_all | solution.py:169
  49.9 0.6 copy-start.6
  50.5 11.7 %collective-permute-start.6 = (bf16[4,2,2048]{2,1,0:T(2,128)(2,1)S(1)}, bf16[4,2,2048]{2,1,0:T(2,128)(2,1)S(1)}, u32[]{:S(2)}, u32[]{:S(2)}) collective-permute-start(bf16[4,2,2048]{2,1,0:T(2,128)(2,1)S(1)} %get-tuple-element.30), channel_id=1, source_target_pairs={{0,192},{192,384},{384,576},{576,0},{1,193},{193,385},{385,577},{5... | collective-permute-start | bytes 98312 | tf_op jit(solution)/shard_map/ppermute | solution.py:131
  63.0 25.5 %all-to-all-start.1 = ((bf16[8,8,2048]{2,1,0:T(8,128)(2,1)}), bf16[8,8,2048]{2,1,0:T(8,128)(2,1)}, u32[]{:S(2)}, u32[]{:S(2)}) async-start(bf16[8,8,2048]{2,1,0:T(8,128)(2,1)} %get-tuple-element.31), calls=%async_computation.1 | async-start | bytes 524288 | tf_op jit(solution)/shard_map/all_to_all | solution.py:184
  69.7 0.8 copy-start.5
  71.0 11.0 %collective-permute-start.7 = (bf16[4,2,2048]{2,1,0:T(2,128)(2,1)S(1)}, bf16[4,2,2048]{2,1,0:T(2,128)(2,1)S(1)}, u32[]{:S(2)}, u32[]{:S(2)}) collective-permute-start(bf16[4,2,2048]{2,1,0:T(2,128)(2,1)S(1)} %get-tuple-element.34), channel_id=1, source_target_pairs={{0,384},{192,576},{384,0},{576,192},{1,385},{193,577},{385,1},{577... | collective-permute-start | bytes 98312 | tf_op jit(solution)/shard_map/ppermute | solution.py:131
  79.1 6.8 %collective-permute-start.8 = (bf16[4,2,2048]{2,1,0:T(2,128)(2,1)S(1)}, bf16[4,2,2048]{2,1,0:T(2,128)(2,1)S(1)}, u32[]{:S(2)}, u32[]{:S(2)}) collective-permute-start(bf16[4,2,2048]{2,1,0:T(2,128)(2,1)S(1)} %get-tuple-element.35), channel_id=1, source_target_pairs={{0,576},{192,0},{384,192},{576,384},{1,577},{193,1},{385,193},{577... | collective-permute-start | bytes 98312 | tf_op jit(solution)/shard_map/ppermute | solution.py:131
  85.9 0.8 copy-start.7
  87.9 0.6 copy-start.9
  100.1 10.3 %collective-permute-start.9 = (bf16[192,2048]{1,0:T(8,128)(2,1)S(1)}, bf16[192,2048]{1,0:T(8,128)(2,1)S(1)}, u32[]{:S(2)}, u32[]{:S(2)}) collective-permute-start(bf16[192,2048]{1,0:T(8,128)(2,1)S(1)} %all_gather.3.refs_1_), channel_id=1, source_target_pairs={{0,1},{1,0},{2,3},{3,2},{4,5},{5,4},{6,7},{7,6},{8,9},{9,8},{10,11... | collective-permute-start | bytes 2359304 | tf_op jit(solution)/shard_map/ppermute | solution.py:194

commit v6 on v3

v6 whole, which is shorter than its diff:
```python
import jax
import jax.numpy as jnp
from jax import lax
from jax.experimental import pallas as pl
from jax.experimental.pallas import tpu as pltpu
from jax.sharding import Mesh, PartitionSpec as P

GRP = ("zh", "x")
TP = ("y", "zl", "core")
RING = ("y", "zl")
SWAP = [(0, 1), (1, 0)]
SIDE = 4
CHIPS = 24
STEPS = 4

bf16, f32 = jnp.bfloat16, jnp.float32
MARK = jax.ShapeDtypeStruct((8, 128), f32)
VMEM = pl.BlockSpec(memory_space=pltpu.VMEM)
SMEM = pl.BlockSpec(memory_space=pltpu.SMEM)
ANY = pl.BlockSpec(memory_space=pl.ANY)


def call(body, out_shape, in_specs, out_specs, **more):
    return pl.pallas_call(
        body,
        out_shape=out_shape,
        in_specs=in_specs,
        out_specs=out_specs,
        cost_estimate=pl.CostEstimate(flops=10**6, bytes_accessed=10**6, transcendentals=0),
        compiler_params=pltpu.CompilerParams(vmem_limit_bytes=16 * 2**20),
        **more,
    )


def slots_by_z1(place_ref, dest_ref, lengths_ref, kv_ref, keep_ref, send_ref):
    mine = place_ref[4]
    row = lax.broadcasted_iota(jnp.int32, kv_ref.shape[1:], 0) + place_ref[5]
    for r in range(kv_ref.shape[0]):
        d = dest_ref[mine, r]
        value = kv_ref[r]
        value = jnp.where(row < lengths_ref[r], value, jnp.zeros_like(value))
        spot = (d & 1) * 4 + ((d >> 1) & 1) * 2 + ((d >> 2) & 1)

        @pl.when(((d >> 3) & 1) == place_ref[3])
        def _():
            keep_ref[spot] = value

        @pl.when(((d >> 3) & 1) != place_ref[3])
        def _():
            send_ref[spot] = value


def slots_by_x0(place_ref, kept_ref, arrived_ref, keep_ref, send_ref):
    for other, in_ref in enumerate((kept_ref, arrived_ref)):
        source = (place_ref[3] ^ other) * 4
        for r in range(4):
            keep_ref[source + r] = in_ref[place_ref[0] * 4 + r]
            send_ref[source + r] = in_ref[(place_ref[0] ^ 1) * 4 + r]


def slots_by_x1(place_ref, kept_ref, arrived_ref, after_ref, keep_ref, send_ref):
    for other, in_ref in enumerate((kept_ref, arrived_ref)):
        source = (place_ref[0] ^ other) * 4
        for s in range(2):
            for z in range(2):
                keep_ref[source + s * 2 + z] = in_ref[s * 4 + place_ref[1] * 2 + z]
                send_ref[source + s * 2 + z] = in_ref[s * 4 + (place_ref[1] ^ 1) * 2 + z]


def slots_by_z0(place_ref, kept_ref, arrived_ref, keep_ref, send_ref):
    for other, in_ref in enumerate((kept_ref, arrived_ref)):
        source = (place_ref[1] ^ other) * 4
        for s in range(4):
            keep_ref[source + s] = in_ref[s * 2 + place_ref[2]]
            send_ref[source + s] = in_ref[s * 2 + (place_ref[2] ^ 1)]


def slots_in_place(place_ref, kept_ref, arrived_ref, out_ref, mark_ref):
    mark_ref[...] = jnp.zeros_like(mark_ref)
    for other, in_ref in enumerate((kept_ref, arrived_ref)):
        for z in range(2):
            source = (z * 2 + (place_ref[2] ^ other)) * 4
            for s in range(4):
                out_ref[source + s] = in_ref[s * 2 + z]


def sum_body(parts_ref, after_ref, out_ref, mark_ref, held_ref, total_ref, in_sems, out_sems):
    mark_ref[...] = jnp.zeros_like(mark_ref)
    count = CHIPS // STEPS
    blocks = [pl.ds(i * count, count) for i in range(STEPS)]
    loads = [pltpu.make_async_copy(parts_ref.at[b], held_ref.at[b], in_sems.at[i]) for i, b in enumerate(blocks)]
    for load in loads:
        load.start()
    total = jnp.zeros(total_ref.shape, f32)
    for i, load in enumerate(loads):
        load.wait()
        for k in range(i * count, (i + 1) * count):
            total += held_ref[k].astype(f32)
    total_ref[...] = total.astype(bf16)
    copies = [pltpu.make_async_copy(total_ref, out_ref.at[i], out_sems.at[i]) for i in range(CHIPS)]
    for copy in copies:
        copy.start()
    for copy in copies:
        copy.wait()


def half_body(which, core_ref, value_ref, *refs):
    out_ref, sem = refs[-2:]
    width = value_ref.shape[1]
    first = pl.multiple_of((core_ref[0] ^ which) * width, width)
    copy = pltpu.make_async_copy(value_ref, out_ref.at[:, pl.ds(first, width)], sem)
    copy.start()
    copy.wait()


def half_of(out_shape, which, core, value, *into):
    return call(
        lambda *refs: half_body(which, *refs),
        out_shape,
        [SMEM, VMEM] + [ANY] * len(into),
        ANY,
        scratch_shapes=[pltpu.SemaphoreType.DMA(())],
        input_output_aliases={2: 0} if into else {},
    )(core, value, *into)


def after(value, mark):
    return pl.pallas_call(
        lambda value_ref, mark_ref, out_ref: None,
        out_shape=jax.ShapeDtypeStruct(value.shape, value.dtype),
        in_specs=[ANY] * 2,
        out_specs=ANY,
        input_output_aliases={0: 0},
    )(value, mark)


def flip(value, axis, bit):
    return lax.ppermute(value, axis, [(i, i ^ bit) for i in range(SIDE)])


def shards(tokens, gate_weight, up_weight, down_weight, active, kv_blocks, lengths, dest):
    core = lax.axis_index("core")
    x, zh = lax.axis_index("x"), lax.axis_index("zh")
    place = jnp.stack(
        [x & 1, x >> 1, zh & 1, zh >> 1, lax.axis_index(GRP), lax.axis_index(TP) * kv_blocks.shape[1]]
    )

    gate = jnp.dot(tokens, gate_weight, preferred_element_type=f32)
    up = jnp.dot(tokens, up_weight, preferred_element_type=f32)
    hidden = (jax.nn.silu(gate) * up * active.astype(f32)).astype(bf16)

    rows, width = tokens.shape[0], down_weight.shape[1] // 2
    theirs = lax.dynamic_slice_in_dim(down_weight, (1 - core) * width, width, 1)
    ours = lax.dynamic_slice_in_dim(down_weight, core * width, width, 1)
    away = jnp.dot(hidden, theirs, preferred_element_type=f32).astype(bf16)
    arrived = lax.ppermute(away, "core", SWAP)
    total = jnp.dot(hidden, ours, preferred_element_type=f32) + arrived.astype(f32)

    total = total.astype(bf16).reshape(CHIPS, rows // CHIPS, width)
    parts = lax.all_to_all(total, RING, split_axis=0, concat_axis=0, tiled=True)

    pair = [jax.ShapeDtypeStruct((8, *kv_blocks.shape[1:]), bf16)] * 2
    kept, sent = call(slots_by_z1, pair, [SMEM] * 3 + [VMEM], [VMEM] * 2)(place, dest, lengths, kv_blocks)
    kept, sent = call(slots_by_x0, pair, [SMEM] + [VMEM] * 2, [VMEM] * 2)(place, kept, flip(sent, "zh", 2))
    moved = flip(sent, "x", 1)

    spread, mark = call(
        sum_body,
        [pltpu.HBM(parts.shape, bf16), MARK],
        [ANY] * 2,
        [ANY, VMEM],
        scratch_shapes=[
            pltpu.VMEM(parts.shape, bf16),
            pltpu.VMEM(parts.shape[1:], bf16),
            pltpu.SemaphoreType.DMA((STEPS,)),
            pltpu.SemaphoreType.DMA((CHIPS,)),
        ],
    )(parts, moved)

    half = lax.all_to_all(spread, RING, split_axis=0, concat_axis=0, tiled=True).reshape(rows, width)

    kept, sent = call(slots_by_x1, pair, [SMEM] + [VMEM] * 3, [VMEM] * 2)(place, kept, moved, mark)
    kept, sent = call(slots_by_z0, pair, [SMEM] + [VMEM] * 2, [VMEM] * 2)(place, kept, flip(sent, "x", 2))
    cache, mark = call(
        slots_in_place, [jax.ShapeDtypeStruct(kv_blocks.shape, bf16), MARK], [SMEM] + [VMEM] * 2, [VMEM] * 2
    )(place, kept, flip(sent, "zh", 1))

    half = after(half, mark)
    other = lax.ppermute(half, "core", SWAP)
    ffn_out = jax.ShapeDtypeStruct((rows, 2 * width), bf16)
    ffn_out = half_of(ffn_out, 1, core[None], other, half_of(ffn_out, 0, core[None], half))
    return (ffn_out, cache)


def solution(mesh):
    fine = Mesh(mesh.devices.reshape(4, 4, 8, 3, 2), GRP + TP)
    return jax.shard_map(
        shards,
        mesh=fine,
        in_specs=(
            P(GRP, None),
            P(None, TP),
            P(None, TP),
            P(TP, None),
            P(GRP, TP),
            P(GRP, TP, None),
            P(GRP),
            P(),
        ),
        out_specs=(P(GRP, None), P(GRP, TP, None)),
        check_vma=False,
    )
```

time: 98.4 us -> 97.2 us (0.988)
  Pallas kernels: 14.5 us -> 9.11 us
  starting transfers between devices: 54.1 us -> 58.1 us
  matrix products: 6.52 us -> 8.53 us
  waiting for transfers between devices: 20.6 us -> 18.9 us
    ppermute x4, starting transfers between devices: 19.6 us -> 27.9 us  [flip(): return lax.ppermute(value, axis, [(i, i ^ bit) for i in range(SIDE)])]
    all_to_all x1, waiting for transfers between devices: 5.41 us -> 0.01 us  [shards(): lax.all_to_all(spread, RING, split_axis=0, concat_axis=0, tiled=True)]
    pallas_call x8 -> x7, Pallas kernels: 12.6 us -> 7.91 us  [the longest x2 2.91 us: half_of(): call(lambda *refs: half_body(which, *refs), out_shape, [SMEM, VMEM] + [AN...]
    all_to_all x1, starting transfers between devices: 9.78 us -> 6.63 us  [shards(): lax.all_to_all(spread, RING, split_axis=0, concat_axis=0, tiled=True)]
    ppermute x4, waiting for transfers between devices: 13.6 us -> 16.6 us  [flip(): return lax.ppermute(value, axis, [(i, i ^ bit) for i in range(SIDE)])]
    dot_general x1, matrix products: 0.58 us -> 2.59 us  [shards(): jnp.dot(hidden, ours, preferred_element_type=f32) + arrived.astype(f32)]
    ppermute x1, starting transfers between devices: 7.67 us -> 6.5 us  [shards(): other = lax.ppermute(half, 'core', SWAP)]
  transfers between devices with their start and end apart: 8 -> 8, of which waited for: 6 -> 6; matrix products, arithmetic and copies ran while one was open for 1% -> 0% of each run, Pallas kernels for 7% -> 6%
where the time goes in v6:
time: 97.2 us; the launch traced here: 96.6 us
  starting transfers between devices  58.1 us (60%)
  waiting for transfers between devices  18.9 us (19%)
  Pallas kernels  9.11 us (9%)
  matrix products  8.53 us (9%)
  local copies, waits for them, and re-layouts  1.12 us (1%)
    ppermute x4, starting transfers between devices, flip(): return lax.ppermute(value, axis, [(i, i ^ bit) for i in range(SIDE)])  27.9 us
    ppermute x4, waiting for transfers between devices, flip(): return lax.ppermute(value, axis, [(i, i ^ bit) for i in range(SIDE)])  16.6 us
    ppermute x1, starting transfers between devices, shards(): arrived = lax.ppermute(away, 'core', SWAP)  12.4 us
    all_to_all x1, starting transfers between devices, shards(): lax.all_to_all(spread, RING, split_axis=0, concat_axis=0, tiled=True)  6.63 us
    ppermute x1, starting transfers between devices, shards(): other = lax.ppermute(half, 'core', SWAP)  6.5 us
    all_to_all x1, starting transfers between devices, shards(): parts = lax.all_to_all(total, RING, split_axis=0, concat_axis=0, tiled=True)  4.72 us
    dot_general x1, matrix products, shards(): gate = jnp.dot(tokens, gate_weight, preferred_element_type=f32)  3.49 us
    pallas_call x2, Pallas kernels, half_of(): call(lambda *refs: half_body(which, *refs), out_shape, [SMEM, VMEM] + [AN...  2.91 us
  transfers between devices with their start and end apart: 8, of which 6 were waited for; matrix products, arithmetic and copies ran while one was open for 0% of the time, Pallas kernels for 6%

profile of v6, /device:TPU:1, one launch (start us, length us, event | category | flops | bytes accessed | tf_op | source)
XLA Modules:
  0.0 96.6 jit_solution(2931067407500727672)
XLA Ops:
  0.6 0.0 copy-start
  0.7 3.5 %fusion.12 = f32[192,384]{1,0:T(8,128)S(1)} fusion(bf16[192,4096]{1,0:T(8,128)(2,1)} %param.8, bf16[4096,384]{1,0:T(8,128)(2,1)} %param.9), kind=kOutput, calls=%fused_computation.11 | convolution fusion | flops 603979776 | bytes 5013504 | tf_op jit(solution)/shard_map/dot_general | solution.py:148
  4.2 0.4 copy-done.6
  4.6 0.0 copy-done.7
  4.6 1.0 %fusion.9 = bf16[192,384]{1,0:T(8,128)(2,1)S(1)} fusion(bf16[192,4096]{1,0:T(8,128)(2,1)S(1)} %copy-done.5, bf16[4096,384]{1,0:T(8,128)(2,1)S(1)} %copy-done.6, s32[192,384]{1,0:T(8,128)S(1)} %copy-done.7, f32[192,384]{1,0:T(8,128)S(1)} %fusion.12), kind=kOutput, calls=%fused_computation.8 | convolution fusion | flops 604569600 | bytes 5455872 | tf_op jit(solution)/shard_map/dot_general | solution.py:149
  5.6 1.5 %convolution_convert_fusion = bf16[192,2048]{1,0:T(8,128)(2,1)} fusion(bf16[192,384]{1,0:T(8,128)(2,1)S(1)} %fusion.9, bf16[384,4096]{1,0:T(8,128)(2,1)S(1)} %copy-done, s32[]{:T(128)S(6)} %select_n.7), kind=kOutput, calls=%fused_computation | convolution fusion | flops 302383104 | bytes 2506756 | tf_op jit(solution)/shard_map/dot_general | solution.py:155
  7.1 12.4 %collective-permute-start = (bf16[192,2048]{1,0:T(8,128)(2,1)}, bf16[192,2048]{1,0:T(8,128)(2,1)}, u32[]{:S(2)}, u32[]{:S(2)}) collective-permute-start(bf16[192,2048]{1,0:T(8,128)(2,1)} %convolution_convert_fusion), channel_id=1, source_target_pairs={{0,1},{1,0},{2,3},{3,2},{4,5},{5,4},{6,7},{7,6},{8,9},{9,8},{10,11... | collective-permute-start | bytes 2359304 | tf_op jit(solution)/shard_map/ppermute | solution.py:156
  19.5 2.2 %collective-permute-done = bf16[192,2048]{1,0:T(8,128)(2,1)} collective-permute-done((bf16[192,2048]{1,0:T(8,128)(2,1)}, bf16[192,2048]{1,0:T(8,128)(2,1)}, u32[]{:S(2)}, u32[]{:S(2)}) %collective-permute-start) | collective-permute-done | bytes 786464 | tf_op jit(solution)/shard_map/ppermute | solution.py:156
  21.7 2.6 %fusion.5 = bf16[24,8,2048]{2,1,0:T(8,128)(2,1)} fusion(bf16[192,2048]{1,0:T(8,128)(2,1)} %collective-permute-done, bf16[192,384]{1,0:T(8,128)(2,1)S(1)} %fusion.9, bf16[384,4096]{1,0:T(8,128)(2,1)S(1)} %copy-done, s32[]{:T(128)S(6)} %select_n.6), kind=kOutput, calls=%fused_computation.5 | convolution fusion | flops 303169536 | bytes 3293188 | tf_op jit(solution)/shard_map/dot_general | solution.py:157
  24.3 4.7 %all-to-all-start = ((bf16[24,8,2048]{2,1,0:T(8,128)(2,1)}), bf16[24,8,2048]{2,1,0:T(8,128)(2,1)}, u32[]{:S(2)}, u32[]{:S(2)}) async-start(bf16[24,8,2048]{2,1,0:T(8,128)(2,1)} %fusion.5), calls=%async_computation | async-start | bytes 1572864 | tf_op jit(solution)/shard_map/all_to_all | solution.py:160
  29.1 0.1 stack.27.place_ref
  29.2 1.0 %shard_map.95 = (bf16[8,2,2048]{2,1,0:T(2,128)(2,1)S(1)}, bf16[8,2,2048]{2,1,0:T(2,128)(2,1)S(1)}) custom-call(s32[6]{0:T(128)S(1)} %stack.27.place_ref, s32[16,16]{1,0:T(8,128)S(1)} %copy-done.2, s32[16]{0:T(128)S(1)} %copy-done.4, bf16[16,2,2048]{2,1,0:T(2,128)(2,1)S(1)} %copy-done.1), custom_call_target="tpu_custom_call" | custom-call | flops 1000000 | bytes 1000000 | tf_op jit(solution)/shard_map/pallas_call | solution.py:163
  30.2 10.8 %collective-permute-start.1 = (bf16[8,2,2048]{2,1,0:T(2,128)(2,1)S(1)}, bf16[8,2,2048]{2,1,0:T(2,128)(2,1)S(1)}, u32[]{:S(2)}, u32[]{:S(2)}) collective-permute-start(bf16[8,2,2048]{2,1,0:T(2,128)(2,1)S(1)} %get-tuple-element.15), channel_id=1, source_target_pairs={{0,384},{192,576},{384,0},{576,192},{1,385},{193,577},{385,1},{577... | collective-permute-start | bytes 196616 | tf_op jit(solution)/shard_map/ppermute | solution.py:138
  41.0 10.7 %collective-permute-done.1.arrived_ref = bf16[8,2,2048]{2,1,0:T(2,128)(2,1)S(1)} collective-permute-done((bf16[8,2,2048]{2,1,0:T(2,128)(2,1)S(1)}, bf16[8,2,2048]{2,1,0:T(2,128)(2,1)S(1)}, u32[]{:S(2)}, u32[]{:S(2)}) %collective-permute-start.1) | collective-permute-done | bytes 65568 | tf_op jit(solution)/shard_map/ppermute | solution.py:138
  51.7 0.6 shard_map.96
  52.3 3.1 %collective-permute-start.2 = (bf16[8,2,2048]{2,1,0:T(2,128)(2,1)S(1)}, bf16[8,2,2048]{2,1,0:T(2,128)(2,1)S(1)}, u32[]{:S(2)}, u32[]{:S(2)}) collective-permute-start(bf16[8,2,2048]{2,1,0:T(2,128)(2,1)S(1)} %get-tuple-element.16), channel_id=1, source_target_pairs={{0,48},{48,0},{96,144},{144,96},{1,49},{49,1},{97,145},{145,97},{2... | collective-permute-start | bytes 196616 | tf_op jit(solution)/shard_map/ppermute | solution.py:138
  55.4 1.9 %collective-permute-done.2.after_ref.arrived_ref = bf16[8,2,2048]{2,1,0:T(2,128)(2,1)S(1)} collective-permute-done((bf16[8,2,2048]{2,1,0:T(2,128)(2,1)S(1)}, bf16[8,2,2048]{2,1,0:T(2,128)(2,1)S(1)}, u32[]{:S(2)}, u32[]{:S(2)}) %collective-permute-start.2) | collective-permute-done | bytes 65568 | tf_op jit(solution)/shard_map/ppermute | solution.py:138
  57.3 0.0 all-to-all-done.parts_ref
  57.3 2.4 %shard_map.97 = (bf16[24,8,2048]{2,1,0:T(8,128)(2,1)}, f32[8,128]{1,0:T(8,128)S(1)}) custom-call(bf16[24,8,2048]{2,1,0:T(8,128)(2,1)} %all-to-all-done.parts_ref, bf16[8,2,2048]{2,1,0:T(2,128)(2,1)S(1)} %collective-permute-done.2.after_ref.arrived_ref), custom_call_target="tpu_custom_call" | custom-call | flops 1000000 | bytes 1000000 | tf_op jit(solution)/shard_map/pallas_call | solution.py:167
  59.7 6.6 %all-to-all-start.1 = ((bf16[24,8,2048]{2,1,0:T(8,128)(2,1)}), bf16[24,8,2048]{2,1,0:T(8,128)(2,1)}, u32[]{:S(2)}, u32[]{:S(2)}) async-start(bf16[24,8,2048]{2,1,0:T(8,128)(2,1)} %get-tuple-element.17), calls=%async_computation.1 | async-start | bytes 1572864 | tf_op jit(solution)/shard_map/all_to_all | solution.py:180
  66.3 0.6 shard_map.98
  66.9 4.6 %collective-permute-start.3 = (bf16[8,2,2048]{2,1,0:T(2,128)(2,1)S(1)}, bf16[8,2,2048]{2,1,0:T(2,128)(2,1)S(1)}, u32[]{:S(2)}, u32[]{:S(2)}) collective-permute-start(bf16[8,2,2048]{2,1,0:T(2,128)(2,1)S(1)} %get-tuple-element.21), channel_id=1, source_target_pairs={{0,96},{48,144},{96,0},{144,48},{1,97},{49,145},{97,1},{145,49},{2... | collective-permute-start | bytes 196616 | tf_op jit(solution)/shard_map/ppermute | solution.py:138
  71.5 1.9 %collective-permute-done.3.arrived_ref = bf16[8,2,2048]{2,1,0:T(2,128)(2,1)S(1)} collective-permute-done((bf16[8,2,2048]{2,1,0:T(2,128)(2,1)S(1)}, bf16[8,2,2048]{2,1,0:T(2,128)(2,1)S(1)}, u32[]{:S(2)}, u32[]{:S(2)}) %collective-permute-start.3) | collective-permute-done | bytes 65568 | tf_op jit(solution)/shard_map/ppermute | solution.py:138
  73.4 0.6 shard_map.99
  73.9 9.3 %collective-permute-start.4 = (bf16[8,2,2048]{2,1,0:T(2,128)(2,1)S(1)}, bf16[8,2,2048]{2,1,0:T(2,128)(2,1)S(1)}, u32[]{:S(2)}, u32[]{:S(2)}) collective-permute-start(bf16[8,2,2048]{2,1,0:T(2,128)(2,1)S(1)} %get-tuple-element.23), channel_id=1, source_target_pairs={{0,192},{192,0},{384,576},{576,384},{1,193},{193,1},{385,577},{577... | collective-permute-start | bytes 196616 | tf_op jit(solution)/shard_map/ppermute | solution.py:138
  83.3 2.0 %collective-permute-done.4.arrived_ref = bf16[8,2,2048]{2,1,0:T(2,128)(2,1)S(1)} collective-permute-done((bf16[8,2,2048]{2,1,0:T(2,128)(2,1)S(1)}, bf16[8,2,2048]{2,1,0:T(2,128)(2,1)S(1)}, u32[]{:S(2)}, u32[]{:S(2)}) %collective-permute-start.4) | collective-permute-done | bytes 65568 | tf_op jit(solution)/shard_map/ppermute | solution.py:138
  85.3 1.2 %shard_map.100 = (bf16[16,2,2048]{2,1,0:T(2,128)(2,1)}, f32[8,128]{1,0:T(8,128)S(1)}) custom-call(s32[6]{0:T(128)S(1)} %stack.27.place_ref, bf16[8,2,2048]{2,1,0:T(2,128)(2,1)S(1)} %get-tuple-element.22.kept_ref, bf16[8,2,2048]{2,1,0:T(2,128)(2,1)S(1)} %collective-permute-done.4.arrived_ref), custom_call_target="tpu_custom_call" | custom-call | flops 1000000 | bytes 1000000 | tf_op jit(solution)/shard_map/pallas_call | solution.py:184
  86.5 0.6 copy-done.3
  87.1 6.5 %collective-permute-start.5 = (bf16[192,2048]{1,0:T(8,128)(2,1)}, bf16[192,2048]{1,0:T(8,128)(2,1)S(1)}, u32[]{:S(2)}, u32[]{:S(2)}) collective-permute-start(bf16[192,2048]{1,0:T(8,128)(2,1)} %shard_map.101.refs_1_), channel_id=1, source_target_pairs={{0,1},{1,0},{2,3},{3,2},{4,5},{5,4},{6,7},{7,6},{8,9},{9,8},{10,11... | collective-permute-start | bytes 2359304 | tf_op jit(solution)/shard_map/ppermute | solution.py:189
  93.6 2.0 %shard_map.102.refs_2_ = bf16[192,4096]{1,0:T(8,128)(2,1)} custom-call(s32[1]{0:T(128)} %bitcast.refs_0_, bf16[192,2048]{1,0:T(8,128)(2,1)} %shard_map.101.refs_1_), custom_call_target="tpu_custom_call" | custom-call | flops 1000000 | bytes 1000000 | tf_op jit(solution)/shard_map/pallas_call | solution.py:117
  95.7 0.1 collective-permute-done.5.refs_1_
  95.7 0.9 shard_map.103
  (14 shorter events, 0.0 us)
Async XLA Ops:
  0.6 5.0 %copy-start = (bf16[384,4096]{1,0:T(8,128)(2,1)S(1)}, bf16[384,4096]{1,0:T(8,128)(2,1)}, u32[]{:S(2)}) copy-start(bf16[384,4096]{1,0:T(8,128)(2,1)} %param.11) | copy-start | bytes 9437188
  0.7 3.5 %copy-start.5 = (bf16[192,4096]{1,0:T(8,128)(2,1)S(1)}, bf16[192,4096]{1,0:T(8,128)(2,1)}, u32[]{:S(2)}) copy-start(bf16[192,4096]{1,0:T(8,128)(2,1)} %param.8) | copy-start | bytes 4718596
  0.7 3.9 %copy-start.6 = (bf16[4096,384]{1,0:T(8,128)(2,1)S(1)}, bf16[4096,384]{1,0:T(8,128)(2,1)}, u32[]{:S(2)}) copy-start(bf16[4096,384]{1,0:T(8,128)(2,1)} %param.10) | copy-start | bytes 9437188
  0.7 3.9 %copy-start.7 = (s32[192,384]{1,0:T(8,128)S(1)}, s32[192,384]{1,0:T(8,128)}, u32[]{:S(2)}) copy-start(s32[192,384]{1,0:T(8,128)} %param.12) | copy-start | bytes 884740
  7.1 14.7 %collective-permute-start = (bf16[192,2048]{1,0:T(8,128)(2,1)}, bf16[192,2048]{1,0:T(8,128)(2,1)}, u32[]{:S(2)}, u32[]{:S(2)}) collective-permute-start(bf16[192,2048]{1,0:T(8,128)(2,1)} %convolution_convert_fusion), channel_id=1, source_target_pairs={{0,1},{1,0},{2,3},{3,2},{4,5},{5,4},{6,7},{7,6},{8,9},{9,8},{10,11... | collective-permute-start | bytes 2359304 | tf_op jit(solution)/shard_map/ppermute | solution.py:156
  24.3 4.8 %copy-start.1 = (bf16[16,2,2048]{2,1,0:T(2,128)(2,1)S(1)}, bf16[16,2,2048]{2,1,0:T(2,128)(2,1)}, u32[]{:S(2)}) copy-start(bf16[16,2,2048]{2,1,0:T(2,128)(2,1)} %kv_ref.1) | copy-start | bytes 393220
  24.3 4.9 %copy-start.2 = (s32[16,16]{1,0:T(8,128)S(1)}, s32[16,16]{1,0:T(8,128)}, u32[]{:S(2)}) copy-start(s32[16,16]{1,0:T(8,128)} %dest_ref.1) | copy-start | bytes 3076
  24.3 4.9 %copy-start.4 = (s32[16]{0:T(128)S(1)}, s32[16]{0:T(128)}, u32[]{:S(2)}) copy-start(s32[16]{0:T(128)} %lengths_ref.1) | copy-start | bytes 196
  24.3 33.0 %all-to-all-start = ((bf16[24,8,2048]{2,1,0:T(8,128)(2,1)}), bf16[24,8,2048]{2,1,0:T(8,128)(2,1)}, u32[]{:S(2)}, u32[]{:S(2)}) async-start(bf16[24,8,2048]{2,1,0:T(8,128)(2,1)} %fusion.5), calls=%async_computation | async-start | bytes 1572864 | tf_op jit(solution)/shard_map/all_to_all | solution.py:160
  30.2 21.6 %collective-permute-start.1 = (bf16[8,2,2048]{2,1,0:T(2,128)(2,1)S(1)}, bf16[8,2,2048]{2,1,0:T(2,128)(2,1)S(1)}, u32[]{:S(2)}, u32[]{:S(2)}) collective-permute-start(bf16[8,2,2048]{2,1,0:T(2,128)(2,1)S(1)} %get-tuple-element.15), channel_id=1, source_target_pairs={{0,384},{192,576},{384,0},{576,192},{1,385},{193,577},{385,1},{577... | collective-permute-start | bytes 196616 | tf_op jit(solution)/shard_map/ppermute | solution.py:138
  52.3 5.0 %collective-permute-start.2 = (bf16[8,2,2048]{2,1,0:T(2,128)(2,1)S(1)}, bf16[8,2,2048]{2,1,0:T(2,128)(2,1)S(1)}, u32[]{:S(2)}, u32[]{:S(2)}) collective-permute-start(bf16[8,2,2048]{2,1,0:T(2,128)(2,1)S(1)} %get-tuple-element.16), channel_id=1, source_target_pairs={{0,48},{48,0},{96,144},{144,96},{1,49},{49,1},{97,145},{145,97},{2... | collective-permute-start | bytes 196616 | tf_op jit(solution)/shard_map/ppermute | solution.py:138
  59.7 27.5 %all-to-all-start.1 = ((bf16[24,8,2048]{2,1,0:T(8,128)(2,1)}), bf16[24,8,2048]{2,1,0:T(8,128)(2,1)}, u32[]{:S(2)}, u32[]{:S(2)}) async-start(bf16[24,8,2048]{2,1,0:T(8,128)(2,1)} %get-tuple-element.17), calls=%async_computation.1 | async-start | bytes 1572864 | tf_op jit(solution)/shard_map/all_to_all | solution.py:180
  66.9 6.5 %collective-permute-start.3 = (bf16[8,2,2048]{2,1,0:T(2,128)(2,1)S(1)}, bf16[8,2,2048]{2,1,0:T(2,128)(2,1)S(1)}, u32[]{:S(2)}, u32[]{:S(2)}) collective-permute-start(bf16[8,2,2048]{2,1,0:T(2,128)(2,1)S(1)} %get-tuple-element.21), channel_id=1, source_target_pairs={{0,96},{48,144},{96,0},{144,48},{1,97},{49,145},{97,1},{145,49},{2... | collective-permute-start | bytes 196616 | tf_op jit(solution)/shard_map/ppermute | solution.py:138
  73.9 11.4 %collective-permute-start.4 = (bf16[8,2,2048]{2,1,0:T(2,128)(2,1)S(1)}, bf16[8,2,2048]{2,1,0:T(2,128)(2,1)S(1)}, u32[]{:S(2)}, u32[]{:S(2)}) collective-permute-start(bf16[8,2,2048]{2,1,0:T(2,128)(2,1)S(1)} %get-tuple-element.23), channel_id=1, source_target_pairs={{0,192},{192,0},{384,576},{576,384},{1,193},{193,1},{385,577},{577... | collective-permute-start | bytes 196616 | tf_op jit(solution)/shard_map/ppermute | solution.py:138
  86.5 0.6 copy-start.3
  87.1 8.6 %collective-permute-start.5 = (bf16[192,2048]{1,0:T(8,128)(2,1)}, bf16[192,2048]{1,0:T(8,128)(2,1)S(1)}, u32[]{:S(2)}, u32[]{:S(2)}) collective-permute-start(bf16[192,2048]{1,0:T(8,128)(2,1)} %shard_map.101.refs_1_), channel_id=1, source_target_pairs={{0,1},{1,0},{2,3},{3,2},{4,5},{5,4},{6,7},{7,6},{8,9},{9,8},{10,11... | collective-permute-start | bytes 2359304 | tf_op jit(solution)/shard_map/ppermute | solution.py:189

commit v7 on v4

--- a/solution.py
+++ b/solution.py
@@ -32,7 +32,9 @@
     )
 
 
-def sort_body(place_ref, dest_ref, lengths_ref, kv_ref, mark_ref, *out_refs):
+def sort_body(place_ref, dest_ref, lengths_ref, kv_ref, *refs):
+    out_refs, mark_ref = refs[:SIDE], refs[SIDE]
+    mark_ref[...] = jnp.zeros_like(mark_ref)
     x, mine, first = place_ref[0], place_ref[1], place_ref[2]
     row = lax.broadcasted_iota(jnp.int32, kv_ref.shape[1:], 0) + first
     for r in range(kv_ref.shape[0]):
@@ -47,27 +49,25 @@
                 out_refs[k][lax.div(d, SIDE)] = value
 
 
-def turn_body(shifts, place_ref, *refs):
+def turn_body(place_ref, *refs):
     x, zh = place_ref[0], place_ref[3]
-    in_refs, out_refs = refs[:SIDE], refs[-len(shifts) :]
+    in_refs, out_refs = refs[:SIDE], refs[SIDE:]
     for k in range(SIDE):
         source = lax.rem(x - k + SIDE, SIDE)
-        for out_ref, j in zip(out_refs, shifts):
+        for j, out_ref in enumerate(out_refs):
             out_ref[source] = in_refs[k][lax.rem(zh + j, SIDE)]
 
 
 def lay_body(place_ref, *refs):
     zh = place_ref[3]
-    in_refs, out_ref, mark_ref = refs[:SIDE], refs[-2], refs[-1]
-    mark_ref[...] = jnp.zeros_like(mark_ref)
+    in_refs, out_ref = refs[:SIDE], refs[-1]
     for j in range(SIDE):
         source = lax.rem(zh - j + SIDE, SIDE)
         for k in range(SIDE):
             out_ref[source * SIDE + k] = in_refs[j][k]
 
 
-def add_body(own_ref, arrived_ref, out_ref, mark_ref, total_ref, sems):
-    mark_ref[...] = jnp.zeros_like(mark_ref)
+def add_body(own_ref, arrived_ref, after_ref, out_ref, total_ref, sems):
     rows = out_ref.shape[0] // STEPS
     copies = []
     for i in range(STEPS):
@@ -79,8 +79,8 @@
         copy.wait()
 
 
-def sum_body(parts_ref, after_ref, out_ref, mark_ref, total_ref, sems):
-    mark_ref[...] = jnp.zeros_like(mark_ref)
+def sum_body(parts_ref, *refs):
+    out_ref, total_ref, sems = refs[-3:]
     total = parts_ref[0].astype(f32)
     for i in range(1, CHIPS):
         total += parts_ref[i].astype(f32)
@@ -105,21 +105,21 @@
     return call(
         lambda *refs: half_body(which, *refs),
         out_shape,
-        [SMEM] + [ANY] * (1 + len(into)),
+        [SMEM, VMEM] + [ANY] * len(into),
         ANY,
         scratch_shapes=[pltpu.SemaphoreType.DMA(())],
         input_output_aliases={2: 0} if into else {},
     )(core, value, *into)
 
 
-def after(value, mark):
-    return pl.pallas_call(
-        lambda value_ref, mark_ref, out_ref: None,
-        out_shape=jax.ShapeDtypeStruct(value.shape, value.dtype),
-        in_specs=[ANY] * 2,
-        out_specs=ANY,
+def after(value, *others):
+    return call(
+        lambda *refs: None,
+        jax.ShapeDtypeStruct(value.shape, value.dtype),
+        [ANY] * (1 + len(others)),
+        ANY,
         input_output_aliases={0: 0},
-    )(value, mark)
+    )(value, *others)
 
 
 def shift(value, axis, k):
@@ -130,6 +130,11 @@
     core = lax.axis_index("core")
     x, zh = lax.axis_index("x"), lax.axis_index("zh")
     place = jnp.stack([x, lax.axis_index(GRP), lax.axis_index(TP) * kv_blocks.shape[1], zh])
+
+    slots = jax.ShapeDtypeStruct((SIDE, *kv_blocks.shape[1:]), bf16)
+    *bundles, mark = call(sort_body, [slots] * SIDE + [MARK], [SMEM] * 3 + [VMEM], [VMEM] * (SIDE + 1))(
+        place, dest, lengths, kv_blocks
+    )
 
     gate = jnp.dot(tokens, gate_weight, preferred_element_type=f32)
     up = jnp.dot(tokens, up_weight, preferred_element_type=f32)
@@ -141,45 +146,34 @@
     away = jnp.dot(hidden, theirs, preferred_element_type=f32).astype(bf16)
     arrived = lax.ppermute(away, "core", SWAP)
     own = jnp.dot(hidden, ours, preferred_element_type=f32)
-    total, mark = call(
+    total = call(
         add_body,
-        [pltpu.HBM((rows, width), bf16), MARK],
-        [VMEM] * 2,
-        [ANY, VMEM],
+        pltpu.HBM((rows, width), bf16),
+        [VMEM] * 3,
+        ANY,
         scratch_shapes=[pltpu.VMEM((rows, width), bf16), pltpu.SemaphoreType.DMA((STEPS,))],
-    )(own, arrived)
+    )(own, arrived, mark)
 
     parts = total.reshape(CHIPS, rows // CHIPS, width)
     parts = lax.all_to_all(parts, RING, split_axis=0, concat_axis=0, tiled=True)
 
-    slots = jax.ShapeDtypeStruct((SIDE, *kv_blocks.shape[1:]), bf16)
-    bundles = call(sort_body, [slots] * SIDE, [SMEM] * 3 + [VMEM] * 2, [VMEM] * SIDE)(
-        place, dest, lengths, kv_blocks, mark
-    )
     bundles = [bundles[0]] + [shift(bundles[k], "x", k) for k in range(1, SIDE)]
-    first = call(lambda *refs: turn_body((0, 1), *refs), [slots] * 2, [SMEM] + [VMEM] * SIDE, [VMEM] * 2)(
-        place, *bundles
-    )
-    moved = shift(first[1], "zh", 1)
-
-    spread, mark = call(
+    bundles = call(turn_body, [slots] * SIDE, [SMEM] + [VMEM] * SIDE, [VMEM] * SIDE)(place, *bundles)
+
+    spread = call(
         sum_body,
-        [pltpu.HBM(parts.shape, bf16), MARK],
-        [VMEM, ANY],
-        [ANY, VMEM],
+        pltpu.HBM(parts.shape, bf16),
+        [VMEM] + [ANY] * SIDE,
+        ANY,
         scratch_shapes=[pltpu.VMEM(parts.shape[1:], bf16), pltpu.SemaphoreType.DMA((CHIPS,))],
-    )(parts, moved)
+    )(parts, *bundles)
 
     half = lax.all_to_all(spread, RING, split_axis=0, concat_axis=0, tiled=True).reshape(rows, width)
 
-    others = call(lambda *refs: turn_body((2, 3), *refs), [slots] * 2, [SMEM] + [VMEM] * (SIDE + 1), [VMEM] * 2)(
-        place, *bundles, mark
-    )
-    cache, mark = call(
-        lay_body, [jax.ShapeDtypeStruct(kv_blocks.shape, bf16), MARK], [SMEM] + [VMEM] * SIDE, [VMEM] * 2
-    )(place, first[0], moved, shift(others[0], "zh", 2), shift(others[1], "zh", 3))
-
-    half = after(half, mark)
+    bundles = [bundles[0]] + [shift(bundles[k], "zh", k) for k in range(1, SIDE)]
+    cache = call(lay_body, jax.ShapeDtypeStruct(kv_blocks.shape, bf16), [SMEM] + [VMEM] * SIDE, VMEM)(place, *bundles)
+
+    half = after(half, *bundles[1:])
     other = lax.ppermute(half, "core", SWAP)
     ffn_out = jax.ShapeDtypeStruct((rows, 2 * width), bf16)
     ffn_out = half_of(ffn_out, 1, core[None], other, half_of(ffn_out, 0, core[None], half))

time: 116 us -> 92 us (0.79)
  Pallas kernels: 33.7 us -> 10.3 us
  starting transfers between devices: 59.7 us -> 55.3 us
  waiting for transfers between devices: 13.8 us -> 15.7 us
    pallas_call x9 -> x8, Pallas kernels: 33.7 us -> 10.3 us  [the longest x2 2.91 us: half_of(): call(lambda *refs: half_body(which, *refs), out_shape, [SMEM, VMEM] + [AN...]
    all_to_all x1, waiting for transfers between devices: 0.01 us -> 9.38 us  [shards(): parts = lax.all_to_all(parts, RING, split_axis=0, concat_axis=0, tiled=True)]
    ppermute x6, waiting for transfers between devices: 12.2 us -> 6.31 us  [shift(): return lax.ppermute(value, axis, [(i, (i + k) % SIDE) for i in range(SIDE)])]
    ppermute x1, starting transfers between devices: 7.21 us -> 3.65 us  [shards(): other = lax.ppermute(half, 'core', SWAP)]
    all_to_all x1, starting transfers between devices: 9.29 us -> 6.48 us  [shards(): lax.all_to_all(spread, RING, split_axis=0, concat_axis=0, tiled=True)]
    ppermute x6, starting transfers between devices: 26.2 us -> 28.1 us  [shift(): return lax.ppermute(value, axis, [(i, (i + k) % SIDE) for i in range(SIDE)])]
    ppermute x1, waiting for transfers between devices: 1.61 us -> 0.01 us  [shards(): arrived = lax.ppermute(away, 'core', SWAP)]
  transfers between devices with their start and end apart: 10 -> 10, of which waited for: 5 -> 4; matrix products, arithmetic and copies ran while one was open for 1% -> 2% of each run, Pallas kernels for 25% -> 5%
where the time goes in v7:
time: 92 us; the launch traced here: 90.8 us
  starting transfers between devices  55.3 us (60%)
  waiting for transfers between devices  15.7 us (17%)
  Pallas kernels  10.3 us (11%)
  matrix products  7.44 us (8%)
  local copies, waits for them, and re-layouts  1.09 us (1%)
    ppermute x6, starting transfers between devices, shift(): return lax.ppermute(value, axis, [(i, (i + k) % SIDE) for i in range(SIDE)])  28.1 us
    ppermute x1, starting transfers between devices, shards(): arrived = lax.ppermute(away, 'core', SWAP)  12.4 us
    all_to_all x1, waiting for transfers between devices, shards(): parts = lax.all_to_all(parts, RING, split_axis=0, concat_axis=0, tiled=True)  9.38 us
    all_to_all x1, starting transfers between devices, shards(): lax.all_to_all(spread, RING, split_axis=0, concat_axis=0, tiled=True)  6.48 us
    ppermute x6, waiting for transfers between devices, shift(): return lax.ppermute(value, axis, [(i, (i + k) % SIDE) for i in range(SIDE)])  6.31 us
    all_to_all x1, starting transfers between devices, shards(): parts = lax.all_to_all(parts, RING, split_axis=0, concat_axis=0, tiled=True)  4.61 us
    ppermute x1, starting transfers between devices, shards(): other = lax.ppermute(half, 'core', SWAP)  3.65 us
    dot_general x1, matrix products, shards(): gate = jnp.dot(tokens, gate_weight, preferred_element_type=f32)  3.49 us
  transfers between devices with their start and end apart: 10, of which 4 were waited for; matrix products, arithmetic and copies ran while one was open for 2% of the time, Pallas kernels for 5%

profile of v7, /device:TPU:1, one launch (start us, length us, event | category | flops | bytes accessed | tf_op | source)
XLA Modules:
  0.0 90.8 jit_solution(3976552888848892198)
XLA Ops:
  0.6 0.0 copy-start
  0.7 3.5 %fusion.7 = f32[192,384]{1,0:T(8,128)S(1)} fusion(bf16[192,4096]{1,0:T(8,128)(2,1)} %param.8, bf16[4096,384]{1,0:T(8,128)(2,1)} %param.9), kind=kOutput, calls=%fused_computation.10 | convolution fusion | flops 603979776 | bytes 5013504 | tf_op jit(solution)/shard_map/dot_general | solution.py:139
  4.2 0.4 copy-done.6
  4.6 0.0 copy-done.7
  4.6 1.0 %fusion.4 = bf16[192,384]{1,0:T(8,128)(2,1)S(1)} fusion(bf16[192,4096]{1,0:T(8,128)(2,1)S(1)} %copy-done.4, bf16[4096,384]{1,0:T(8,128)(2,1)S(1)} %copy-done.6, s32[192,384]{1,0:T(8,128)S(1)} %copy-done.7, f32[192,384]{1,0:T(8,128)S(1)} %fusion.7), kind=kOutput, calls=%fused_computation.6 | convolution fusion | flops 604569600 | bytes 5455872 | tf_op jit(solution)/shard_map/dot_general | solution.py:140
  5.6 0.6 copy-done.5
  6.3 1.5 %convolution_convert_fusion = bf16[192,2048]{1,0:T(8,128)(2,1)} fusion(bf16[192,384]{1,0:T(8,128)(2,1)S(1)} %fusion.4, bf16[384,4096]{1,0:T(8,128)(2,1)S(1)} %copy-done, s32[]{:T(128)S(6)} %select_n.7), kind=kOutput, calls=%fused_computation | convolution fusion | flops 302383104 | bytes 2506756 | tf_op jit(solution)/shard_map/dot_general | solution.py:146
  7.7 12.4 %collective-permute-start = (bf16[192,2048]{1,0:T(8,128)(2,1)}, bf16[192,2048]{1,0:T(8,128)(2,1)}, u32[]{:S(2)}, u32[]{:S(2)}) collective-permute-start(bf16[192,2048]{1,0:T(8,128)(2,1)} %convolution_convert_fusion), channel_id=1, source_target_pairs={{0,1},{1,0},{2,3},{3,2},{4,5},{5,4},{6,7},{7,6},{8,9},{9,8},{10,11... | collective-permute-start | bytes 2359304 | tf_op jit(solution)/shard_map/ppermute | solution.py:147
  20.2 0.1 pad_add_fusion.place_ref
  20.3 1.2 %shard_map.95 = (bf16[4,2,2048]{2,1,0:T(2,128)(2,1)S(1)}, bf16[4,2,2048]{2,1,0:T(2,128)(2,1)S(1)}, bf16[4,2,2048]{2,1,0:T(2,128)(2,1)S(1)}, bf16[4,2,2048]{2,1,0:T(2,128)(2,1)S(1)}, f32[8,128]{1,0:T(8,128)S(1)}) custom-call(s32[4]{0:T(128)S(1)} %pad_add_fusion.place_ref, s32[16,16]{1,0:T(8,128)S(1)} %copy-done.2, s32[16]{0:T(128)S(1)} %copy-done.3, ...), custom_call_target="tpu_custom_call" | custom-call | flops 1000000 | bytes 1000000 | tf_op jit(solution)/shard_map/pallas_call | solution.py:135
  21.5 1.5 %fusion.1.own_ref = f32[192,2048]{1,0:T(8,128)S(1)} fusion(bf16[192,384]{1,0:T(8,128)(2,1)} %copy-done.5, bf16[384,4096]{1,0:T(8,128)(2,1)S(1)} %copy-done, s32[]{:T(128)S(6)} %select_n.6), kind=kOutput, calls=%fused_computation.2 | convolution fusion | flops 301989888 | bytes 3293188 | tf_op jit(solution)/shard_map/dot_general | solution.py:148
  23.0 2.1 %shard_map.96 = bf16[192,2048]{1,0:T(8,128)(2,1)} custom-call(f32[192,2048]{1,0:T(8,128)S(1)} %fusion.1.own_ref, bf16[192,2048]{1,0:T(8,128)(2,1)} %collective-permute-done.arrived_ref, f32[8,128]{1,0:T(8,128)S(1)} %get-tuple-element.11.after_ref), custom_call_target="tpu_custom_call" | custom-call | flops 1000000 | bytes 1000000 | tf_op jit(solution)/shard_map/pallas_call | solution.py:149
  25.1 4.6 %all-to-all-start = ((bf16[24,8,2048]{2,1,0:T(8,128)(2,1)}), bf16[24,8,2048]{2,1,0:T(8,128)(2,1)}, u32[]{:S(2)}, u32[]{:S(2)}) async-start(bf16[24,8,2048]{2,1,0:T(8,128)(2,1)} %bitcast.13), calls=%async_computation | async-start | bytes 1572864 | tf_op jit(solution)/shard_map/all_to_all | solution.py:158
  29.7 1.9 %collective-permute-start.1 = (bf16[4,2,2048]{2,1,0:T(2,128)(2,1)S(1)}, bf16[4,2,2048]{2,1,0:T(2,128)(2,1)S(1)}, u32[]{:S(2)}, u32[]{:S(2)}) collective-permute-start(bf16[4,2,2048]{2,1,0:T(2,128)(2,1)S(1)} %get-tuple-element.13), channel_id=1, source_target_pairs={{0,48},{48,96},{96,144},{144,0},{1,49},{49,97},{97,145},{145,1},{2... | collective-permute-start | bytes 98312 | tf_op jit(solution)/shard_map/ppermute | solution.py:126
  31.6 2.7 %collective-permute-start.2 = (bf16[4,2,2048]{2,1,0:T(2,128)(2,1)S(1)}, bf16[4,2,2048]{2,1,0:T(2,128)(2,1)S(1)}, u32[]{:S(2)}, u32[]{:S(2)}) collective-permute-start(bf16[4,2,2048]{2,1,0:T(2,128)(2,1)S(1)} %get-tuple-element.14), channel_id=1, source_target_pairs={{0,96},{48,144},{96,0},{144,48},{1,97},{49,145},{97,1},{145,49},{2... | collective-permute-start | bytes 98312 | tf_op jit(solution)/shard_map/ppermute | solution.py:126
  34.3 3.8 %collective-permute-start.3 = (bf16[4,2,2048]{2,1,0:T(2,128)(2,1)S(1)}, bf16[4,2,2048]{2,1,0:T(2,128)(2,1)S(1)}, u32[]{:S(2)}, u32[]{:S(2)}) collective-permute-start(bf16[4,2,2048]{2,1,0:T(2,128)(2,1)S(1)} %get-tuple-element.15), channel_id=1, source_target_pairs={{0,144},{48,0},{96,48},{144,96},{1,145},{49,1},{97,49},{145,97},{2... | collective-permute-start | bytes 98312 | tf_op jit(solution)/shard_map/ppermute | solution.py:126
  38.1 0.0 collective-permute-done.1.refs_1_
  38.1 0.0 collective-permute-done.2.refs_2_
  38.2 2.2 %collective-permute-done.3.refs_3_ = bf16[4,2,2048]{2,1,0:T(2,128)(2,1)S(1)} collective-permute-done((bf16[4,2,2048]{2,1,0:T(2,128)(2,1)S(1)}, bf16[4,2,2048]{2,1,0:T(2,128)(2,1)S(1)}, u32[]{:S(2)}, u32[]{:S(2)}) %collective-permute-start.3) | collective-permute-done | bytes 32800 | tf_op jit(solution)/shard_map/ppermute | solution.py:126
  40.4 0.6 shard_map.97
  40.9 9.4 %all-to-all-done.parts_ref = bf16[24,8,2048]{2,1,0:T(8,128)(2,1)} async-done(((bf16[24,8,2048]{2,1,0:T(8,128)(2,1)}), bf16[24,8,2048]{2,1,0:T(8,128)(2,1)}, u32[]{:S(2)}, u32[]{:S(2)}) %all-to-all-start) | async-done | bytes 786464 | tf_op jit(solution)/shard_map/all_to_all | solution.py:158
  50.3 2.3 %shard_map.98 = bf16[24,8,2048]{2,1,0:T(8,128)(2,1)} custom-call(bf16[24,8,2048]{2,1,0:T(8,128)(2,1)} %all-to-all-done.parts_ref, bf16[4,2,2048]{2,1,0:T(2,128)(2,1)S(1)} %get-tuple-element.16.refs_0_, bf16[4,2,2048]{2,1,0:T(2,128)(2,1)S(1)} %get-tuple-element.17.refs_1_, bf16[4,2,2048]{2,1,0:T(2,128)(2,1)S(1)} %get-tuple-element.18.refs_2_, ...), custom_call_target="tpu_custom_call" | custom-call | flops 1000000 | bytes 1000000 | tf_op jit(solution)/shard_map/pallas_call | solution.py:163
  52.6 6.5 %all-to-all-start.1 = ((bf16[24,8,2048]{2,1,0:T(8,128)(2,1)}), bf16[24,8,2048]{2,1,0:T(8,128)(2,1)}, u32[]{:S(2)}, u32[]{:S(2)}) async-start(bf16[24,8,2048]{2,1,0:T(8,128)(2,1)} %shard_map.98), calls=%async_computation.1 | async-start | bytes 1572864 | tf_op jit(solution)/shard_map/all_to_all | solution.py:171
  59.1 7.4 %collective-permute-start.4 = (bf16[4,2,2048]{2,1,0:T(2,128)(2,1)S(1)}, bf16[4,2,2048]{2,1,0:T(2,128)(2,1)S(1)}, u32[]{:S(2)}, u32[]{:S(2)}) collective-permute-start(bf16[4,2,2048]{2,1,0:T(2,128)(2,1)S(1)} %get-tuple-element.17.refs_1_), channel_id=1, source_target_pairs={{0,192},{192,384},{384,576},{576,0},{1,193},{193,385},{385,577},{5... | collective-permute-start | bytes 98312 | tf_op jit(solution)/shard_map/ppermute | solution.py:126
  66.5 8.4 %collective-permute-start.5 = (bf16[4,2,2048]{2,1,0:T(2,128)(2,1)S(1)}, bf16[4,2,2048]{2,1,0:T(2,128)(2,1)S(1)}, u32[]{:S(2)}, u32[]{:S(2)}) collective-permute-start(bf16[4,2,2048]{2,1,0:T(2,128)(2,1)S(1)} %get-tuple-element.18.refs_2_), channel_id=1, source_target_pairs={{0,384},{192,576},{384,0},{576,192},{1,385},{193,577},{385,1},{577... | collective-permute-start | bytes 98312 | tf_op jit(solution)/shard_map/ppermute | solution.py:126
  74.9 4.0 %collective-permute-start.6 = (bf16[4,2,2048]{2,1,0:T(2,128)(2,1)S(1)}, bf16[4,2,2048]{2,1,0:T(2,128)(2,1)S(1)}, u32[]{:S(2)}, u32[]{:S(2)}) collective-permute-start(bf16[4,2,2048]{2,1,0:T(2,128)(2,1)S(1)} %get-tuple-element.19.refs_3_), channel_id=1, source_target_pairs={{0,576},{192,0},{384,192},{576,384},{1,577},{193,1},{385,193},{577... | collective-permute-start | bytes 98312 | tf_op jit(solution)/shard_map/ppermute | solution.py:126
  78.9 1.4 %collective-permute-done.4.refs_1_ = bf16[4,2,2048]{2,1,0:T(2,128)(2,1)S(1)} collective-permute-done((bf16[4,2,2048]{2,1,0:T(2,128)(2,1)S(1)}, bf16[4,2,2048]{2,1,0:T(2,128)(2,1)S(1)}, u32[]{:S(2)}, u32[]{:S(2)}) %collective-permute-start.4) | collective-permute-done | bytes 32800 | tf_op jit(solution)/shard_map/ppermute | solution.py:126
  80.2 2.7 %collective-permute-done.5.refs_2_ = bf16[4,2,2048]{2,1,0:T(2,128)(2,1)S(1)} collective-permute-done((bf16[4,2,2048]{2,1,0:T(2,128)(2,1)S(1)}, bf16[4,2,2048]{2,1,0:T(2,128)(2,1)S(1)}, u32[]{:S(2)}, u32[]{:S(2)}) %collective-permute-start.5) | collective-permute-done | bytes 32800 | tf_op jit(solution)/shard_map/ppermute | solution.py:126
  82.9 3.7 %collective-permute-start.7 = (bf16[192,2048]{1,0:T(8,128)(2,1)}, bf16[192,2048]{1,0:T(8,128)(2,1)S(1)}, u32[]{:S(2)}, u32[]{:S(2)}) collective-permute-start(bf16[192,2048]{1,0:T(8,128)(2,1)} %shard_map.99.refs_1_), channel_id=1, source_target_pairs={{0,1},{1,0},{2,3},{3,2},{4,5},{5,4},{6,7},{7,6},{8,9},{9,8},{10,11... | collective-permute-start | bytes 2359304 | tf_op jit(solution)/shard_map/ppermute | solution.py:177
  86.6 1.2 %shard_map.102 = bf16[16,2,2048]{2,1,0:T(2,128)(2,1)} custom-call(s32[4]{0:T(128)S(1)} %pad_add_fusion.place_ref, bf16[4,2,2048]{2,1,0:T(2,128)(2,1)S(1)} %get-tuple-element.16.refs_0_, bf16[4,2,2048]{2,1,0:T(2,128)(2,1)S(1)} %collective-permute-done.4.refs_1_, bf16[4,2,2048]{2,1,0:T(2,128)(2,1)S(1)} %collective-permute-done.5.refs_2_, ...), custom_call_target="tpu_custom_call" | custom-call | flops 1000000 | bytes 1000000 | tf_op jit(solution)/shard_map/pallas_call | solution.py:174
  87.8 2.0 %shard_map.100.refs_2_ = bf16[192,4096]{1,0:T(8,128)(2,1)} custom-call(s32[1]{0:T(128)} %bitcast.refs_0_, bf16[192,2048]{1,0:T(8,128)(2,1)} %shard_map.99.refs_1_), custom_call_target="tpu_custom_call" | custom-call | flops 1000000 | bytes 1000000 | tf_op jit(solution)/shard_map/pallas_call | solution.py:105
  89.9 0.9 shard_map.101
  (17 shorter events, 0.0 us)
Async XLA Ops:
  0.6 5.6 %copy-start = (bf16[384,4096]{1,0:T(8,128)(2,1)S(1)}, bf16[384,4096]{1,0:T(8,128)(2,1)}, u32[]{:S(2)}) copy-start(bf16[384,4096]{1,0:T(8,128)(2,1)} %param.11) | copy-start | bytes 9437188
  0.7 3.5 %copy-start.4 = (bf16[192,4096]{1,0:T(8,128)(2,1)S(1)}, bf16[192,4096]{1,0:T(8,128)(2,1)}, u32[]{:S(2)}) copy-start(bf16[192,4096]{1,0:T(8,128)(2,1)} %param.8) | copy-start | bytes 4718596
  0.7 3.9 %copy-start.6 = (bf16[4096,384]{1,0:T(8,128)(2,1)S(1)}, bf16[4096,384]{1,0:T(8,128)(2,1)}, u32[]{:S(2)}) copy-start(bf16[4096,384]{1,0:T(8,128)(2,1)} %param.10) | copy-start | bytes 9437188
  0.7 3.9 %copy-start.7 = (s32[192,384]{1,0:T(8,128)S(1)}, s32[192,384]{1,0:T(8,128)}, u32[]{:S(2)}) copy-start(s32[192,384]{1,0:T(8,128)} %param.12) | copy-start | bytes 884740
  5.6 0.7 copy-start.5
  6.3 14.0 %copy-start.1 = (bf16[16,2,2048]{2,1,0:T(2,128)(2,1)S(1)}, bf16[16,2,2048]{2,1,0:T(2,128)(2,1)}, u32[]{:S(2)}) copy-start(bf16[16,2,2048]{2,1,0:T(2,128)(2,1)} %kv_ref.1) | copy-start | bytes 393220
  6.3 14.0 %copy-start.2 = (s32[16,16]{1,0:T(8,128)S(1)}, s32[16,16]{1,0:T(8,128)}, u32[]{:S(2)}) copy-start(s32[16,16]{1,0:T(8,128)} %dest_ref.1) | copy-start | bytes 3076
  6.3 14.0 %copy-start.3 = (s32[16]{0:T(128)S(1)}, s32[16]{0:T(128)}, u32[]{:S(2)}) copy-start(s32[16]{0:T(128)} %lengths_ref.1) | copy-start | bytes 196
  7.7 15.2 %collective-permute-start = (bf16[192,2048]{1,0:T(8,128)(2,1)}, bf16[192,2048]{1,0:T(8,128)(2,1)}, u32[]{:S(2)}, u32[]{:S(2)}) collective-permute-start(bf16[192,2048]{1,0:T(8,128)(2,1)} %convolution_convert_fusion), channel_id=1, source_target_pairs={{0,1},{1,0},{2,3},{3,2},{4,5},{5,4},{6,7},{7,6},{8,9},{9,8},{10,11... | collective-permute-start | bytes 2359304 | tf_op jit(solution)/shard_map/ppermute | solution.py:147
  25.1 25.3 %all-to-all-start = ((bf16[24,8,2048]{2,1,0:T(8,128)(2,1)}), bf16[24,8,2048]{2,1,0:T(8,128)(2,1)}, u32[]{:S(2)}, u32[]{:S(2)}) async-start(bf16[24,8,2048]{2,1,0:T(8,128)(2,1)} %bitcast.13), calls=%async_computation | async-start | bytes 1572864 | tf_op jit(solution)/shard_map/all_to_all | solution.py:158
  29.7 8.4 %collective-permute-start.1 = (bf16[4,2,2048]{2,1,0:T(2,128)(2,1)S(1)}, bf16[4,2,2048]{2,1,0:T(2,128)(2,1)S(1)}, u32[]{:S(2)}, u32[]{:S(2)}) collective-permute-start(bf16[4,2,2048]{2,1,0:T(2,128)(2,1)S(1)} %get-tuple-element.13), channel_id=1, source_target_pairs={{0,48},{48,96},{96,144},{144,0},{1,49},{49,97},{97,145},{145,1},{2... | collective-permute-start | bytes 98312 | tf_op jit(solution)/shard_map/ppermute | solution.py:126
  31.6 6.6 %collective-permute-start.2 = (bf16[4,2,2048]{2,1,0:T(2,128)(2,1)S(1)}, bf16[4,2,2048]{2,1,0:T(2,128)(2,1)S(1)}, u32[]{:S(2)}, u32[]{:S(2)}) collective-permute-start(bf16[4,2,2048]{2,1,0:T(2,128)(2,1)S(1)} %get-tuple-element.14), channel_id=1, source_target_pairs={{0,96},{48,144},{96,0},{144,48},{1,97},{49,145},{97,1},{145,49},{2... | collective-permute-start | bytes 98312 | tf_op jit(solution)/shard_map/ppermute | solution.py:126
  34.3 6.0 %collective-permute-start.3 = (bf16[4,2,2048]{2,1,0:T(2,128)(2,1)S(1)}, bf16[4,2,2048]{2,1,0:T(2,128)(2,1)S(1)}, u32[]{:S(2)}, u32[]{:S(2)}) collective-permute-start(bf16[4,2,2048]{2,1,0:T(2,128)(2,1)S(1)} %get-tuple-element.15), channel_id=1, source_target_pairs={{0,144},{48,0},{96,48},{144,96},{1,145},{49,1},{97,49},{145,97},{2... | collective-permute-start | bytes 98312 | tf_op jit(solution)/shard_map/ppermute | solution.py:126
  52.6 30.3 %all-to-all-start.1 = ((bf16[24,8,2048]{2,1,0:T(8,128)(2,1)}), bf16[24,8,2048]{2,1,0:T(8,128)(2,1)}, u32[]{:S(2)}, u32[]{:S(2)}) async-start(bf16[24,8,2048]{2,1,0:T(8,128)(2,1)} %shard_map.98), calls=%async_computation.1 | async-start | bytes 1572864 | tf_op jit(solution)/shard_map/all_to_all | solution.py:171
  59.1 21.1 %collective-permute-start.4 = (bf16[4,2,2048]{2,1,0:T(2,128)(2,1)S(1)}, bf16[4,2,2048]{2,1,0:T(2,128)(2,1)S(1)}, u32[]{:S(2)}, u32[]{:S(2)}) collective-permute-start(bf16[4,2,2048]{2,1,0:T(2,128)(2,1)S(1)} %get-tuple-element.17.refs_1_), channel_id=1, source_target_pairs={{0,192},{192,384},{384,576},{576,0},{1,193},{193,385},{385,577},{5... | collective-permute-start | bytes 98312 | tf_op jit(solution)/shard_map/ppermute | solution.py:126
  66.5 16.4 %collective-permute-start.5 = (bf16[4,2,2048]{2,1,0:T(2,128)(2,1)S(1)}, bf16[4,2,2048]{2,1,0:T(2,128)(2,1)S(1)}, u32[]{:S(2)}, u32[]{:S(2)}) collective-permute-start(bf16[4,2,2048]{2,1,0:T(2,128)(2,1)S(1)} %get-tuple-element.18.refs_2_), channel_id=1, source_target_pairs={{0,384},{192,576},{384,0},{576,192},{1,385},{193,577},{385,1},{577... | collective-permute-start | bytes 98312 | tf_op jit(solution)/shard_map/ppermute | solution.py:126
  74.9 8.1 %collective-permute-start.6 = (bf16[4,2,2048]{2,1,0:T(2,128)(2,1)S(1)}, bf16[4,2,2048]{2,1,0:T(2,128)(2,1)S(1)}, u32[]{:S(2)}, u32[]{:S(2)}) collective-permute-start(bf16[4,2,2048]{2,1,0:T(2,128)(2,1)S(1)} %get-tuple-element.19.refs_3_), channel_id=1, source_target_pairs={{0,576},{192,0},{384,192},{576,384},{1,577},{193,1},{385,193},{577... | collective-permute-start | bytes 98312 | tf_op jit(solution)/shard_map/ppermute | solution.py:126
  82.9 6.9 %collective-permute-start.7 = (bf16[192,2048]{1,0:T(8,128)(2,1)}, bf16[192,2048]{1,0:T(8,128)(2,1)S(1)}, u32[]{:S(2)}, u32[]{:S(2)}) collective-permute-start(bf16[192,2048]{1,0:T(8,128)(2,1)} %shard_map.99.refs_1_), channel_id=1, source_target_pairs={{0,1},{1,0},{2,3},{3,2},{4,5},{5,4},{6,7},{7,6},{8,9},{9,8},{10,11... | collective-permute-start | bytes 2359304 | tf_op jit(solution)/shard_map/ppermute | solution.py:177

commit v8 on v7

--- a/solution.py
+++ b/solution.py
@@ -11,6 +11,7 @@
 SWAP = [(0, 1), (1, 0)]
 SIDE = 4
 CHIPS = 24
+ORDER = (0, 2, 1, 3)
 STEPS = 4
 
 bf16, f32 = jnp.bfloat16, jnp.float32
@@ -32,9 +33,7 @@
     )
 
 
-def sort_body(place_ref, dest_ref, lengths_ref, kv_ref, *refs):
-    out_refs, mark_ref = refs[:SIDE], refs[SIDE]
-    mark_ref[...] = jnp.zeros_like(mark_ref)
+def sort_body(place_ref, dest_ref, lengths_ref, kv_ref, mark_ref, *out_refs):
     x, mine, first = place_ref[0], place_ref[1], place_ref[2]
     row = lax.broadcasted_iota(jnp.int32, kv_ref.shape[1:], 0) + first
     for r in range(kv_ref.shape[0]):
@@ -54,20 +53,21 @@
     in_refs, out_refs = refs[:SIDE], refs[SIDE:]
     for k in range(SIDE):
         source = lax.rem(x - k + SIDE, SIDE)
-        for j, out_ref in enumerate(out_refs):
+        for out_ref, j in zip(out_refs, ORDER):
             out_ref[source] = in_refs[k][lax.rem(zh + j, SIDE)]
 
 
 def lay_body(place_ref, *refs):
     zh = place_ref[3]
     in_refs, out_ref = refs[:SIDE], refs[-1]
-    for j in range(SIDE):
+    for in_ref, j in zip(in_refs, ORDER):
         source = lax.rem(zh - j + SIDE, SIDE)
         for k in range(SIDE):
-            out_ref[source * SIDE + k] = in_refs[j][k]
-
-
-def add_body(own_ref, arrived_ref, after_ref, out_ref, total_ref, sems):
+            out_ref[source * SIDE + k] = in_ref[k]
+
+
+def add_body(own_ref, arrived_ref, out_ref, mark_ref, total_ref, sems):
+    mark_ref[...] = jnp.zeros_like(mark_ref)
     rows = out_ref.shape[0] // STEPS
     copies = []
     for i in range(STEPS):
@@ -93,21 +93,40 @@
 
 
 def half_body(which, core_ref, value_ref, *refs):
-    out_ref, sem = refs[-2:]
-    width = value_ref.shape[1]
+    if which == 0:
+        out_ref, held_ref, in_sems, out_sems = refs
+    else:
+        out_ref, out_sems = refs[-2:]
+        held_ref = value_ref
+    rows, width = value_ref.shape[0] // STEPS, value_ref.shape[1]
     first = pl.multiple_of((core_ref[0] ^ which) * width, width)
-    copy = pltpu.make_async_copy(value_ref, out_ref.at[:, pl.ds(first, width)], sem)
-    copy.start()
-    copy.wait()
-
-
-def half_of(out_shape, which, core, value, *into):
+    blocks = [pl.ds(i * rows, rows) for i in range(STEPS)]
+    stores = [
+        pltpu.make_async_copy(held_ref.at[b], out_ref.at[b, pl.ds(first, width)], out_sems.at[i])
+        for i, b in enumerate(blocks)
+    ]
+    if which == 0:
+        loads = [pltpu.make_async_copy(value_ref.at[b], held_ref.at[b], in_sems.at[i]) for i, b in enumerate(blocks)]
+        for load in loads:
+            load.start()
+        for load, store in zip(loads, stores):
+            load.wait()
+            store.start()
+    else:
+        for store in stores:
+            store.start()
+    for store in stores:
+        store.wait()
+
+
+def half_of(out_shape, core, value, *into):
+    sems = pltpu.SemaphoreType.DMA((STEPS,))
     return call(
-        lambda *refs: half_body(which, *refs),
+        lambda *refs: half_body(len(into), *refs),
         out_shape,
-        [SMEM, VMEM] + [ANY] * len(into),
+        [SMEM, VMEM if into else ANY] + [ANY] * len(into),
         ANY,
-        scratch_shapes=[pltpu.SemaphoreType.DMA(())],
+        scratch_shapes=[sems] if into else [pltpu.VMEM(value.shape, bf16), sems, sems],
         input_output_aliases={2: 0} if into else {},
     )(core, value, *into)
 
@@ -131,11 +150,6 @@
     x, zh = lax.axis_index("x"), lax.axis_index("zh")
     place = jnp.stack([x, lax.axis_index(GRP), lax.axis_index(TP) * kv_blocks.shape[1], zh])
 
-    slots = jax.ShapeDtypeStruct((SIDE, *kv_blocks.shape[1:]), bf16)
-    *bundles, mark = call(sort_body, [slots] * SIDE + [MARK], [SMEM] * 3 + [VMEM], [VMEM] * (SIDE + 1))(
-        place, dest, lengths, kv_blocks
-    )
-
     gate = jnp.dot(tokens, gate_weight, preferred_element_type=f32)
     up = jnp.dot(tokens, up_weight, preferred_element_type=f32)
     hidden = (jax.nn.silu(gate) * up * active.astype(f32)).astype(bf16)
@@ -146,17 +160,21 @@
     away = jnp.dot(hidden, theirs, preferred_element_type=f32).astype(bf16)
     arrived = lax.ppermute(away, "core", SWAP)
     own = jnp.dot(hidden, ours, preferred_element_type=f32)
-    total = call(
+    total, mark = call(
         add_body,
-        pltpu.HBM((rows, width), bf16),
-        [VMEM] * 3,
-        ANY,
+        [pltpu.HBM((rows, width), bf16), MARK],
+        [VMEM] * 2,
+        [ANY, VMEM],
         scratch_shapes=[pltpu.VMEM((rows, width), bf16), pltpu.SemaphoreType.DMA((STEPS,))],
-    )(own, arrived, mark)
+    )(own, arrived)
 
     parts = total.reshape(CHIPS, rows // CHIPS, width)
     parts = lax.all_to_all(parts, RING, split_axis=0, concat_axis=0, tiled=True)
 
+    slots = jax.ShapeDtypeStruct((SIDE, *kv_blocks.shape[1:]), bf16)
+    bundles = call(sort_body, [slots] * SIDE, [SMEM] * 3 + [VMEM] * 2, [VMEM] * SIDE)(
+        place, dest, lengths, kv_blocks, mark
+    )
     bundles = [bundles[0]] + [shift(bundles[k], "x", k) for k in range(1, SIDE)]
     bundles = call(turn_body, [slots] * SIDE, [SMEM] + [VMEM] * SIDE, [VMEM] * SIDE)(place, *bundles)
 
@@ -170,13 +188,13 @@
 
     half = lax.all_to_all(spread, RING, split_axis=0, concat_axis=0, tiled=True).reshape(rows, width)
 
-    bundles = [bundles[0]] + [shift(bundles[k], "zh", k) for k in range(1, SIDE)]
+    bundles = [bundles[0]] + [shift(b, "zh", j) for b, j in zip(bundles[1:], ORDER[1:])]
     cache = call(lay_body, jax.ShapeDtypeStruct(kv_blocks.shape, bf16), [SMEM] + [VMEM] * SIDE, VMEM)(place, *bundles)
 
     half = after(half, *bundles[1:])
     other = lax.ppermute(half, "core", SWAP)
     ffn_out = jax.ShapeDtypeStruct((rows, 2 * width), bf16)
-    ffn_out = half_of(ffn_out, 1, core[None], other, half_of(ffn_out, 0, core[None], half))
+    ffn_out = half_of(ffn_out, core[None], other, half_of(ffn_out, core[None], half))
     return (ffn_out, cache)
 
 

time: 92 us -> 89.9 us (0.977)
  starting transfers between devices: 55.3 us -> 57.3 us
  waiting for transfers between devices: 15.7 us -> 13.8 us
  matrix products: 7.44 us -> 6.52 us
    all_to_all x1, waiting for transfers between devices: 9.38 us -> 7.01 us  [shards(): parts = lax.all_to_all(parts, RING, split_axis=0, concat_axis=0, tiled=True)]
    ppermute x1, waiting for transfers between devices: 0.01 us -> 1.61 us  [shards(): arrived = lax.ppermute(away, 'core', SWAP)]
    ppermute x6, waiting for transfers between devices: 6.31 us -> 5.15 us  [shift(): return lax.ppermute(value, axis, [(i, (i + k) % SIDE) for i in range(SIDE)])]
    all_to_all x1, starting transfers between devices: 6.48 us -> 7.52 us  [shards(): lax.all_to_all(spread, RING, split_axis=0, concat_axis=0, tiled=True)]
  transfers between devices with their start and end apart: 10 -> 10, of which waited for: 4 -> 4; matrix products, arithmetic and copies ran while one was open for 2% -> 1% of each run, Pallas kernels for 5% -> 6%
where the time goes in v8:
time: 89.9 us; the launch traced here: 89.3 us
  starting transfers between devices  57.3 us (64%)
  waiting for transfers between devices  13.8 us (15%)
  Pallas kernels  10.2 us (11%)
  matrix products  6.52 us (7%)
  between operations  0.91 us (1%)
    ppermute x6, starting transfers between devices, shift(): return lax.ppermute(value, axis, [(i, (i + k) % SIDE) for i in range(SIDE)])  28.7 us
    ppermute x1, starting transfers between devices, shards(): arrived = lax.ppermute(away, 'core', SWAP)  12.4 us
    all_to_all x1, starting transfers between devices, shards(): lax.all_to_all(spread, RING, split_axis=0, concat_axis=0, tiled=True)  7.52 us
    all_to_all x1, waiting for transfers between devices, shards(): parts = lax.all_to_all(parts, RING, split_axis=0, concat_axis=0, tiled=True)  7.01 us
    ppermute x6, waiting for transfers between devices, shift(): return lax.ppermute(value, axis, [(i, (i + k) % SIDE) for i in range(SIDE)])  5.15 us
    all_to_all x1, starting transfers between devices, shards(): parts = lax.all_to_all(parts, RING, split_axis=0, concat_axis=0, tiled=True)  4.61 us
    ppermute x1, starting transfers between devices, shards(): other = lax.ppermute(half, 'core', SWAP)  4.06 us
    dot_general x1, matrix products, shards(): gate = jnp.dot(tokens, gate_weight, preferred_element_type=f32)  3.49 us
  transfers between devices with their start and end apart: 10, of which 4 were waited for; matrix products, arithmetic and copies ran while one was open for 1% of the time, Pallas kernels for 6%

profile of v8, /device:TPU:1, one launch (start us, length us, event | category | flops | bytes accessed | tf_op | source)
XLA Modules:
  0.0 89.3 jit_solution(7401007112406775648)
XLA Ops:
  0.6 0.0 copy-start
  0.7 3.5 %fusion.7 = f32[192,384]{1,0:T(8,128)S(1)} fusion(bf16[192,4096]{1,0:T(8,128)(2,1)} %param.8, bf16[4096,384]{1,0:T(8,128)(2,1)} %param.9), kind=kOutput, calls=%fused_computation.10 | convolution fusion | flops 603979776 | bytes 5013504 | tf_op jit(solution)/shard_map/dot_general | solution.py:153
  4.2 0.4 copy-done.5
  4.6 0.0 copy-done.6
  4.6 1.0 %fusion.4 = bf16[192,384]{1,0:T(8,128)(2,1)S(1)} fusion(bf16[192,4096]{1,0:T(8,128)(2,1)S(1)} %copy-done.4, bf16[4096,384]{1,0:T(8,128)(2,1)S(1)} %copy-done.5, s32[192,384]{1,0:T(8,128)S(1)} %copy-done.6, f32[192,384]{1,0:T(8,128)S(1)} %fusion.7), kind=kOutput, calls=%fused_computation.6 | convolution fusion | flops 604569600 | bytes 5455872 | tf_op jit(solution)/shard_map/dot_general | solution.py:154
  5.6 1.5 %convolution_convert_fusion = bf16[192,2048]{1,0:T(8,128)(2,1)} fusion(bf16[192,384]{1,0:T(8,128)(2,1)S(1)} %fusion.4, bf16[384,4096]{1,0:T(8,128)(2,1)S(1)} %copy-done, s32[]{:T(128)S(6)} %select_n.7), kind=kOutput, calls=%fused_computation | convolution fusion | flops 302383104 | bytes 2506756 | tf_op jit(solution)/shard_map/dot_general | solution.py:160
  7.1 12.4 %collective-permute-start = (bf16[192,2048]{1,0:T(8,128)(2,1)}, bf16[192,2048]{1,0:T(8,128)(2,1)}, u32[]{:S(2)}, u32[]{:S(2)}) collective-permute-start(bf16[192,2048]{1,0:T(8,128)(2,1)} %convolution_convert_fusion), channel_id=1, source_target_pairs={{0,1},{1,0},{2,3},{3,2},{4,5},{5,4},{6,7},{7,6},{8,9},{9,8},{10,11... | collective-permute-start | bytes 2359304 | tf_op jit(solution)/shard_map/ppermute | solution.py:161
  19.5 0.6 fusion.1.own_ref
  20.1 0.0 copy-start.1
  20.1 0.0 copy-start.2
  20.1 1.6 %collective-permute-done.arrived_ref = bf16[192,2048]{1,0:T(8,128)(2,1)} collective-permute-done((bf16[192,2048]{1,0:T(8,128)(2,1)}, bf16[192,2048]{1,0:T(8,128)(2,1)}, u32[]{:S(2)}, u32[]{:S(2)}) %collective-permute-start) | collective-permute-done | bytes 786464 | tf_op jit(solution)/shard_map/ppermute | solution.py:161
  21.7 2.1 %shard_map.95 = (bf16[192,2048]{1,0:T(8,128)(2,1)}, f32[8,128]{1,0:T(8,128)S(1)}) custom-call(f32[192,2048]{1,0:T(8,128)S(1)} %fusion.1.own_ref, bf16[192,2048]{1,0:T(8,128)(2,1)} %collective-permute-done.arrived_ref), custom_call_target="tpu_custom_call" | custom-call | flops 1000000 | bytes 1000000 | tf_op jit(solution)/shard_map/pallas_call | solution.py:163
  23.8 4.6 %all-to-all-start = ((bf16[24,8,2048]{2,1,0:T(8,128)(2,1)}), bf16[24,8,2048]{2,1,0:T(8,128)(2,1)}, u32[]{:S(2)}, u32[]{:S(2)}) async-start(bf16[24,8,2048]{2,1,0:T(8,128)(2,1)} %bitcast.13), calls=%async_computation | async-start | bytes 1572864 | tf_op jit(solution)/shard_map/all_to_all | solution.py:172
  28.4 0.1 pad_add_fusion.place_ref
  28.5 1.2 %shard_map.96 = (bf16[4,2,2048]{2,1,0:T(2,128)(2,1)S(1)}, bf16[4,2,2048]{2,1,0:T(2,128)(2,1)S(1)}, bf16[4,2,2048]{2,1,0:T(2,128)(2,1)S(1)}, bf16[4,2,2048]{2,1,0:T(2,128)(2,1)S(1)}) custom-call(s32[4]{0:T(128)S(1)} %pad_add_fusion.place_ref, s32[16,16]{1,0:T(8,128)S(1)} %copy-done.2, s32[16]{0:T(128)S(1)} %copy-done.3, bf16[16,2,2048]{2,1,0:T(2,128)(2,1)S(1)} %copy-done.1, ...), custom_call_target="tpu_custom_call" | custom-call | flops 1000000 | bytes 1000000 | tf_op jit(solution)/shard_map/pallas_call | solution.py:175
  29.7 1.9 %collective-permute-start.1 = (bf16[4,2,2048]{2,1,0:T(2,128)(2,1)S(1)}, bf16[4,2,2048]{2,1,0:T(2,128)(2,1)S(1)}, u32[]{:S(2)}, u32[]{:S(2)}) collective-permute-start(bf16[4,2,2048]{2,1,0:T(2,128)(2,1)S(1)} %get-tuple-element.15), channel_id=1, source_target_pairs={{0,48},{48,96},{96,144},{144,0},{1,49},{49,97},{97,145},{145,1},{2... | collective-permute-start | bytes 98312 | tf_op jit(solution)/shard_map/ppermute | solution.py:145
  31.6 2.7 %collective-permute-start.2 = (bf16[4,2,2048]{2,1,0:T(2,128)(2,1)S(1)}, bf16[4,2,2048]{2,1,0:T(2,128)(2,1)S(1)}, u32[]{:S(2)}, u32[]{:S(2)}) collective-permute-start(bf16[4,2,2048]{2,1,0:T(2,128)(2,1)S(1)} %get-tuple-element.16), channel_id=1, source_target_pairs={{0,96},{48,144},{96,0},{144,48},{1,97},{49,145},{97,1},{145,49},{2... | collective-permute-start | bytes 98312 | tf_op jit(solution)/shard_map/ppermute | solution.py:145
  34.4 3.8 %collective-permute-start.3 = (bf16[4,2,2048]{2,1,0:T(2,128)(2,1)S(1)}, bf16[4,2,2048]{2,1,0:T(2,128)(2,1)S(1)}, u32[]{:S(2)}, u32[]{:S(2)}) collective-permute-start(bf16[4,2,2048]{2,1,0:T(2,128)(2,1)S(1)} %get-tuple-element.17), channel_id=1, source_target_pairs={{0,144},{48,0},{96,48},{144,96},{1,145},{49,1},{97,49},{145,97},{2... | collective-permute-start | bytes 98312 | tf_op jit(solution)/shard_map/ppermute | solution.py:145
  38.2 0.0 collective-permute-done.2.refs_2_
  38.2 2.2 %collective-permute-done.3.refs_3_ = bf16[4,2,2048]{2,1,0:T(2,128)(2,1)S(1)} collective-permute-done((bf16[4,2,2048]{2,1,0:T(2,128)(2,1)S(1)}, bf16[4,2,2048]{2,1,0:T(2,128)(2,1)S(1)}, u32[]{:S(2)}, u32[]{:S(2)}) %collective-permute-start.3) | collective-permute-done | bytes 32800 | tf_op jit(solution)/shard_map/ppermute | solution.py:145
  40.4 0.6 shard_map.97
  41.0 7.0 %all-to-all-done.parts_ref = bf16[24,8,2048]{2,1,0:T(8,128)(2,1)} async-done(((bf16[24,8,2048]{2,1,0:T(8,128)(2,1)}), bf16[24,8,2048]{2,1,0:T(8,128)(2,1)}, u32[]{:S(2)}, u32[]{:S(2)}) %all-to-all-start) | async-done | bytes 786464 | tf_op jit(solution)/shard_map/all_to_all | solution.py:172
  48.0 2.3 %shard_map.98 = bf16[24,8,2048]{2,1,0:T(8,128)(2,1)} custom-call(bf16[24,8,2048]{2,1,0:T(8,128)(2,1)} %all-to-all-done.parts_ref, bf16[4,2,2048]{2,1,0:T(2,128)(2,1)S(1)} %get-tuple-element.18.refs_0_, bf16[4,2,2048]{2,1,0:T(2,128)(2,1)S(1)} %get-tuple-element.19.refs_1_, bf16[4,2,2048]{2,1,0:T(2,128)(2,1)S(1)} %get-tuple-element.20.refs_2_, ...), custom_call_target="tpu_custom_call" | custom-call | flops 1000000 | bytes 1000000 | tf_op jit(solution)/shard_map/pallas_call | solution.py:181
  50.3 7.5 %all-to-all-start.1 = ((bf16[24,8,2048]{2,1,0:T(8,128)(2,1)}), bf16[24,8,2048]{2,1,0:T(8,128)(2,1)}, u32[]{:S(2)}, u32[]{:S(2)}) async-start(bf16[24,8,2048]{2,1,0:T(8,128)(2,1)} %shard_map.98), calls=%async_computation.1 | async-start | bytes 1572864 | tf_op jit(solution)/shard_map/all_to_all | solution.py:189
  57.8 12.0 %collective-permute-start.4 = (bf16[4,2,2048]{2,1,0:T(2,128)(2,1)S(1)}, bf16[4,2,2048]{2,1,0:T(2,128)(2,1)S(1)}, u32[]{:S(2)}, u32[]{:S(2)}) collective-permute-start(bf16[4,2,2048]{2,1,0:T(2,128)(2,1)S(1)} %get-tuple-element.19.refs_1_), channel_id=1, source_target_pairs={{0,384},{192,576},{384,0},{576,192},{1,385},{193,577},{385,1},{577... | collective-permute-start | bytes 98312 | tf_op jit(solution)/shard_map/ppermute | solution.py:145
  69.9 3.3 %collective-permute-start.5 = (bf16[4,2,2048]{2,1,0:T(2,128)(2,1)S(1)}, bf16[4,2,2048]{2,1,0:T(2,128)(2,1)S(1)}, u32[]{:S(2)}, u32[]{:S(2)}) collective-permute-start(bf16[4,2,2048]{2,1,0:T(2,128)(2,1)S(1)} %get-tuple-element.20.refs_2_), channel_id=1, source_target_pairs={{0,192},{192,384},{384,576},{576,0},{1,193},{193,385},{385,577},{5... | collective-permute-start | bytes 98312 | tf_op jit(solution)/shard_map/ppermute | solution.py:145
  73.2 5.0 %collective-permute-start.6 = (bf16[4,2,2048]{2,1,0:T(2,128)(2,1)S(1)}, bf16[4,2,2048]{2,1,0:T(2,128)(2,1)S(1)}, u32[]{:S(2)}, u32[]{:S(2)}) collective-permute-start(bf16[4,2,2048]{2,1,0:T(2,128)(2,1)S(1)} %get-tuple-element.21.refs_3_), channel_id=1, source_target_pairs={{0,576},{192,0},{384,192},{576,384},{1,577},{193,1},{385,193},{577... | collective-permute-start | bytes 98312 | tf_op jit(solution)/shard_map/ppermute | solution.py:145
  78.2 2.9 %collective-permute-done.4.refs_1_ = bf16[4,2,2048]{2,1,0:T(2,128)(2,1)S(1)} collective-permute-done((bf16[4,2,2048]{2,1,0:T(2,128)(2,1)S(1)}, bf16[4,2,2048]{2,1,0:T(2,128)(2,1)S(1)}, u32[]{:S(2)}, u32[]{:S(2)}) %collective-permute-start.4) | collective-permute-done | bytes 32800 | tf_op jit(solution)/shard_map/ppermute | solution.py:145
  81.1 4.1 %collective-permute-start.7 = (bf16[192,2048]{1,0:T(8,128)(2,1)}, bf16[192,2048]{1,0:T(8,128)(2,1)S(1)}, u32[]{:S(2)}, u32[]{:S(2)}) collective-permute-start(bf16[192,2048]{1,0:T(8,128)(2,1)} %shard_map.99.refs_1_), channel_id=1, source_target_pairs={{0,1},{1,0},{2,3},{3,2},{4,5},{5,4},{6,7},{7,6},{8,9},{9,8},{10,11... | collective-permute-start | bytes 2359304 | tf_op jit(solution)/shard_map/ppermute | solution.py:195
  85.2 1.2 %shard_map.102 = bf16[16,2,2048]{2,1,0:T(2,128)(2,1)} custom-call(s32[4]{0:T(128)S(1)} %pad_add_fusion.place_ref, bf16[4,2,2048]{2,1,0:T(2,128)(2,1)S(1)} %get-tuple-element.18.refs_0_, bf16[4,2,2048]{2,1,0:T(2,128)(2,1)S(1)} %collective-permute-done.4.refs_1_, bf16[4,2,2048]{2,1,0:T(2,128)(2,1)S(1)} %collective-permute-done.5.refs_2_, ...), custom_call_target="tpu_custom_call" | custom-call | flops 1000000 | bytes 1000000 | tf_op jit(solution)/shard_map/pallas_call | solution.py:192
  86.4 2.0 %shard_map.100.refs_2_ = bf16[192,4096]{1,0:T(8,128)(2,1)} custom-call(s32[1]{0:T(128)} %bitcast.refs_0_, bf16[192,2048]{1,0:T(8,128)(2,1)} %shard_map.99.refs_1_), custom_call_target="tpu_custom_call" | custom-call | flops 1000000 | bytes 1000000 | tf_op jit(solution)/shard_map/pallas_call | solution.py:124
  88.3 0.9 %shard_map.101 = bf16[192,4096]{1,0:T(8,128)(2,1)} custom-call(s32[1]{0:T(128)} %bitcast.refs_0_, bf16[192,2048]{1,0:T(8,128)(2,1)S(1)} %collective-permute-done.7.refs_1_, bf16[192,4096]{1,0:T(8,128)(2,1)} %shard_map.100.refs_2_), custom_call_target="tpu_custom_call", output_to_operand_aliasing={{}: (2, {})} | custom-call | flops 1000000 | bytes 1000000 | tf_op jit(solution)/shard_map/pallas_call | solution.py:124
  (15 shorter events, 0.0 us)
Async XLA Ops:
  0.6 5.0 %copy-start = (bf16[384,4096]{1,0:T(8,128)(2,1)S(1)}, bf16[384,4096]{1,0:T(8,128)(2,1)}, u32[]{:S(2)}) copy-start(bf16[384,4096]{1,0:T(8,128)(2,1)} %param.11) | copy-start | bytes 9437188
  0.7 3.5 %copy-start.4 = (bf16[192,4096]{1,0:T(8,128)(2,1)S(1)}, bf16[192,4096]{1,0:T(8,128)(2,1)}, u32[]{:S(2)}) copy-start(bf16[192,4096]{1,0:T(8,128)(2,1)} %param.8) | copy-start | bytes 4718596
  0.7 3.9 %copy-start.5 = (bf16[4096,384]{1,0:T(8,128)(2,1)S(1)}, bf16[4096,384]{1,0:T(8,128)(2,1)}, u32[]{:S(2)}) copy-start(bf16[4096,384]{1,0:T(8,128)(2,1)} %param.10) | copy-start | bytes 9437188
  0.7 3.9 %copy-start.6 = (s32[192,384]{1,0:T(8,128)S(1)}, s32[192,384]{1,0:T(8,128)}, u32[]{:S(2)}) copy-start(s32[192,384]{1,0:T(8,128)} %param.12) | copy-start | bytes 884740
  7.1 14.7 %collective-permute-start = (bf16[192,2048]{1,0:T(8,128)(2,1)}, bf16[192,2048]{1,0:T(8,128)(2,1)}, u32[]{:S(2)}, u32[]{:S(2)}) collective-permute-start(bf16[192,2048]{1,0:T(8,128)(2,1)} %convolution_convert_fusion), channel_id=1, source_target_pairs={{0,1},{1,0},{2,3},{3,2},{4,5},{5,4},{6,7},{7,6},{8,9},{9,8},{10,11... | collective-permute-start | bytes 2359304 | tf_op jit(solution)/shard_map/ppermute | solution.py:161
  20.1 8.4 %copy-start.1 = (bf16[16,2,2048]{2,1,0:T(2,128)(2,1)S(1)}, bf16[16,2,2048]{2,1,0:T(2,128)(2,1)}, u32[]{:S(2)}) copy-start(bf16[16,2,2048]{2,1,0:T(2,128)(2,1)} %kv_ref.1) | copy-start | bytes 393220
  20.1 8.4 %copy-start.2 = (s32[16,16]{1,0:T(8,128)S(1)}, s32[16,16]{1,0:T(8,128)}, u32[]{:S(2)}) copy-start(s32[16,16]{1,0:T(8,128)} %dest_ref.1) | copy-start | bytes 3076
  20.1 8.4 %copy-start.3 = (s32[16]{0:T(128)S(1)}, s32[16]{0:T(128)}, u32[]{:S(2)}) copy-start(s32[16]{0:T(128)} %lengths_ref.1) | copy-start | bytes 196
  23.8 24.2 %all-to-all-start = ((bf16[24,8,2048]{2,1,0:T(8,128)(2,1)}), bf16[24,8,2048]{2,1,0:T(8,128)(2,1)}, u32[]{:S(2)}, u32[]{:S(2)}) async-start(bf16[24,8,2048]{2,1,0:T(8,128)(2,1)} %bitcast.13), calls=%async_computation | async-start | bytes 1572864 | tf_op jit(solution)/shard_map/all_to_all | solution.py:172
  29.7 8.4 %collective-permute-start.1 = (bf16[4,2,2048]{2,1,0:T(2,128)(2,1)S(1)}, bf16[4,2,2048]{2,1,0:T(2,128)(2,1)S(1)}, u32[]{:S(2)}, u32[]{:S(2)}) collective-permute-start(bf16[4,2,2048]{2,1,0:T(2,128)(2,1)S(1)} %get-tuple-element.15), channel_id=1, source_target_pairs={{0,48},{48,96},{96,144},{144,0},{1,49},{49,97},{97,145},{145,1},{2... | collective-permute-start | bytes 98312 | tf_op jit(solution)/shard_map/ppermute | solution.py:145
  31.6 6.6 %collective-permute-start.2 = (bf16[4,2,2048]{2,1,0:T(2,128)(2,1)S(1)}, bf16[4,2,2048]{2,1,0:T(2,128)(2,1)S(1)}, u32[]{:S(2)}, u32[]{:S(2)}) collective-permute-start(bf16[4,2,2048]{2,1,0:T(2,128)(2,1)S(1)} %get-tuple-element.16), channel_id=1, source_target_pairs={{0,96},{48,144},{96,0},{144,48},{1,97},{49,145},{97,1},{145,49},{2... | collective-permute-start | bytes 98312 | tf_op jit(solution)/shard_map/ppermute | solution.py:145
  34.4 6.0 %collective-permute-start.3 = (bf16[4,2,2048]{2,1,0:T(2,128)(2,1)S(1)}, bf16[4,2,2048]{2,1,0:T(2,128)(2,1)S(1)}, u32[]{:S(2)}, u32[]{:S(2)}) collective-permute-start(bf16[4,2,2048]{2,1,0:T(2,128)(2,1)S(1)} %get-tuple-element.17), channel_id=1, source_target_pairs={{0,144},{48,0},{96,48},{144,96},{1,145},{49,1},{97,49},{145,97},{2... | collective-permute-start | bytes 98312 | tf_op jit(solution)/shard_map/ppermute | solution.py:145
  50.3 30.8 %all-to-all-start.1 = ((bf16[24,8,2048]{2,1,0:T(8,128)(2,1)}), bf16[24,8,2048]{2,1,0:T(8,128)(2,1)}, u32[]{:S(2)}, u32[]{:S(2)}) async-start(bf16[24,8,2048]{2,1,0:T(8,128)(2,1)} %shard_map.98), calls=%async_computation.1 | async-start | bytes 1572864 | tf_op jit(solution)/shard_map/all_to_all | solution.py:189
  57.8 23.2 %collective-permute-start.4 = (bf16[4,2,2048]{2,1,0:T(2,128)(2,1)S(1)}, bf16[4,2,2048]{2,1,0:T(2,128)(2,1)S(1)}, u32[]{:S(2)}, u32[]{:S(2)}) collective-permute-start(bf16[4,2,2048]{2,1,0:T(2,128)(2,1)S(1)} %get-tuple-element.19.refs_1_), channel_id=1, source_target_pairs={{0,384},{192,576},{384,0},{576,192},{1,385},{193,577},{385,1},{577... | collective-permute-start | bytes 98312 | tf_op jit(solution)/shard_map/ppermute | solution.py:145
  69.9 11.2 %collective-permute-start.5 = (bf16[4,2,2048]{2,1,0:T(2,128)(2,1)S(1)}, bf16[4,2,2048]{2,1,0:T(2,128)(2,1)S(1)}, u32[]{:S(2)}, u32[]{:S(2)}) collective-permute-start(bf16[4,2,2048]{2,1,0:T(2,128)(2,1)S(1)} %get-tuple-element.20.refs_2_), channel_id=1, source_target_pairs={{0,192},{192,384},{384,576},{576,0},{1,193},{193,385},{385,577},{5... | collective-permute-start | bytes 98312 | tf_op jit(solution)/shard_map/ppermute | solution.py:145
  73.2 7.9 %collective-permute-start.6 = (bf16[4,2,2048]{2,1,0:T(2,128)(2,1)S(1)}, bf16[4,2,2048]{2,1,0:T(2,128)(2,1)S(1)}, u32[]{:S(2)}, u32[]{:S(2)}) collective-permute-start(bf16[4,2,2048]{2,1,0:T(2,128)(2,1)S(1)} %get-tuple-element.21.refs_3_), channel_id=1, source_target_pairs={{0,576},{192,0},{384,192},{576,384},{1,577},{193,1},{385,193},{577... | collective-permute-start | bytes 98312 | tf_op jit(solution)/shard_map/ppermute | solution.py:145
  81.1 7.3 %collective-permute-start.7 = (bf16[192,2048]{1,0:T(8,128)(2,1)}, bf16[192,2048]{1,0:T(8,128)(2,1)S(1)}, u32[]{:S(2)}, u32[]{:S(2)}) collective-permute-start(bf16[192,2048]{1,0:T(8,128)(2,1)} %shard_map.99.refs_1_), channel_id=1, source_target_pairs={{0,1},{1,0},{2,3},{3,2},{4,5},{5,4},{6,7},{7,6},{8,9},{9,8},{10,11... | collective-permute-start | bytes 2359304 | tf_op jit(solution)/shard_map/ppermute | solution.py:195

commit v9 on v8

--- a/solution.py
+++ b/solution.py
@@ -12,6 +12,7 @@
 SIDE = 4
 CHIPS = 24
 ORDER = (0, 2, 1, 3)
+CHUNKS = 8
 STEPS = 4
 
 bf16, f32 = jnp.bfloat16, jnp.float32
@@ -21,16 +22,62 @@
 ANY = pl.BlockSpec(memory_space=pl.ANY)
 
 
-def call(body, out_shape, in_specs, out_specs, **more):
+def call(body, out_shape, in_specs, out_specs, vmem=16, **more):
     return pl.pallas_call(
         body,
         out_shape=out_shape,
         in_specs=in_specs,
         out_specs=out_specs,
         cost_estimate=pl.CostEstimate(flops=10**6, bytes_accessed=10**6, transcendentals=0),
-        compiler_params=pltpu.CompilerParams(vmem_limit_bytes=16 * 2**20),
+        compiler_params=pltpu.CompilerParams(vmem_limit_bytes=vmem * 2**20),
         **more,
     )
+
+
+def hidden_body(core_ref, tokens_ref, gate_ref, up_ref, down_ref, active_ref, hidden_ref, away_ref, *scratch):
+    *held, theirs_ref, mask_ref, sent_ref, sems, last_sems, out_sems = scratch
+    depth = tokens_ref.shape[1] // CHUNKS
+    copies = []
+    for i in range(CHUNKS):
+        block = pl.ds(i * depth, depth)
+        pieces = zip((tokens_ref, gate_ref, up_ref), held, ((slice(None), block), (block,), (block,)))
+        copies.append(
+            [
+                pltpu.make_async_copy(ref.at[place], to.at[place], sems.at[n, i])
+                for n, (ref, to, place) in enumerate(pieces)
+            ]
+        )
+    width = away_ref.shape[1]
+    first = pl.multiple_of((1 - core_ref[0]) * width, width)
+    last = [
+        pltpu.make_async_copy(active_ref, mask_ref, last_sems.at[0]),
+        pltpu.make_async_copy(down_ref.at[:, pl.ds(first, width)], theirs_ref, last_sems.at[1]),
+    ]
+    for chunk in copies + [last]:
+        for copy in chunk:
+            copy.start()
+    gate = jnp.zeros(hidden_ref.shape, f32)
+    up = jnp.zeros(hidden_ref.shape, f32)
+    for i, chunk in enumerate(copies):
+        for copy in chunk:
+            copy.wait()
+        block = slice(i * depth, (i + 1) * depth)
+        part = held[0][:, block]
+        gate += jnp.dot(part, held[1][block], preferred_element_type=f32)
+        up += jnp.dot(part, held[2][block], preferred_element_type=f32)
+    for copy in last:
+        copy.wait()
+    hidden = (gate / (1 + jnp.exp(-gate)) * up * mask_ref[...].astype(f32)).astype(bf16)
+    hidden_ref[...] = hidden
+    columns = width // STEPS
+    stores = []
+    for i in range(STEPS):
+        block = pl.ds(i * columns, columns)
+        sent_ref[:, block] = jnp.dot(hidden, theirs_ref[:, block], preferred_element_type=f32).astype(bf16)
+        stores.append(pltpu.make_async_copy(sent_ref.at[:, block], away_ref.at[:, block], out_sems.at[i]))
+        stores[-1].start()
+    for store in stores:
+        store.wait()
 
 
 def sort_body(place_ref, dest_ref, lengths_ref, kv_ref, mark_ref, *out_refs):
@@ -93,40 +140,25 @@
 
 
 def half_body(which, core_ref, value_ref, *refs):
-    if which == 0:
-        out_ref, held_ref, in_sems, out_sems = refs
-    else:
-        out_ref, out_sems = refs[-2:]
-        held_ref = value_ref
+    out_ref, sems = refs[-2:]
     rows, width = value_ref.shape[0] // STEPS, value_ref.shape[1]
     first = pl.multiple_of((core_ref[0] ^ which) * width, width)
-    blocks = [pl.ds(i * rows, rows) for i in range(STEPS)]
-    stores = [
-        pltpu.make_async_copy(held_ref.at[b], out_ref.at[b, pl.ds(first, width)], out_sems.at[i])
-        for i, b in enumerate(blocks)
-    ]
-    if which == 0:
-        loads = [pltpu.make_async_copy(value_ref.at[b], held_ref.at[b], in_sems.at[i]) for i, b in enumerate(blocks)]
-        for load in loads:
-            load.start()
-        for load, store in zip(loads, stores):
-            load.wait()
-            store.start()
-    else:
-        for store in stores:
-            store.start()
-    for store in stores:
-        store.wait()
+    copies = []
+    for i in range(STEPS):
+        block = pl.ds(i * rows, rows)
+        copies.append(pltpu.make_async_copy(value_ref.at[block], out_ref.at[block, pl.ds(first, width)], sems.at[i]))
+        copies[-1].start()
+    for copy in copies:
+        copy.wait()
 
 
 def half_of(out_shape, core, value, *into):
-    sems = pltpu.SemaphoreType.DMA((STEPS,))
     return call(
         lambda *refs: half_body(len(into), *refs),
         out_shape,
-        [SMEM, VMEM if into else ANY] + [ANY] * len(into),
+        [SMEM, VMEM] + [ANY] * len(into),
         ANY,
-        scratch_shapes=[sems] if into else [pltpu.VMEM(value.shape, bf16), sems, sems],
+        scratch_shapes=[pltpu.SemaphoreType.DMA((STEPS,))],
         input_output_aliases={2: 0} if into else {},
     )(core, value, *into)
 
@@ -150,14 +182,27 @@
     x, zh = lax.axis_index("x"), lax.axis_index("zh")
     place = jnp.stack([x, lax.axis_index(GRP), lax.axis_index(TP) * kv_blocks.shape[1], zh])
 
-    gate = jnp.dot(tokens, gate_weight, preferred_element_type=f32)
-    up = jnp.dot(tokens, up_weight, preferred_element_type=f32)
-    hidden = (jax.nn.silu(gate) * up * active.astype(f32)).astype(bf16)
-
     rows, width = tokens.shape[0], down_weight.shape[1] // 2
-    theirs = lax.dynamic_slice_in_dim(down_weight, (1 - core) * width, width, 1)
+    hidden, away = call(
+        hidden_body,
+        [jax.ShapeDtypeStruct(active.shape, bf16), pltpu.HBM((rows, width), bf16)],
+        [SMEM] + [ANY] * 5,
+        [VMEM, ANY],
+        vmem=56,
+        scratch_shapes=[
+            pltpu.VMEM(tokens.shape, bf16),
+            pltpu.VMEM(gate_weight.shape, bf16),
+            pltpu.VMEM(up_weight.shape, bf16),
+            pltpu.VMEM((active.shape[1], width), bf16),
+            pltpu.VMEM(active.shape, jnp.int32),
+            pltpu.VMEM((rows, width), bf16),
+            pltpu.SemaphoreType.DMA((3, CHUNKS)),
+            pltpu.SemaphoreType.DMA((2,)),
+            pltpu.SemaphoreType.DMA((STEPS,)),
+        ],
+    )(core[None], tokens, gate_weight, up_weight, down_weight, active)
+
     ours = lax.dynamic_slice_in_dim(down_weight, core * width, width, 1)
-    away = jnp.dot(hidden, theirs, preferred_element_type=f32).astype(bf16)
     arrived = lax.ppermute(away, "core", SWAP)
     own = jnp.dot(hidden, ours, preferred_element_type=f32)
     total, mark = call(

time: 89.9 us -> 86.5 us (0.962)
  matrix products: 6.52 us -> 2.07 us
  Pallas kernels: 10.2 us -> 13.5 us
  waiting for transfers between devices: 13.8 us -> 12.2 us
    dot_general x3 -> x0, matrix products: 5.95 us -> none  [the longest x1 3.49 us: shards(): gate = jnp.dot(tokens, gate_weight, preferred_element_type=f32)]
    pallas_call x2 -> x3, Pallas kernels: 2.87 us -> 8.38 us  [the longest x1 6.56 us: shards(): call(hidden_body, [jax.ShapeDtypeStruct(active.shape, bf16), pltpu.HBM((r...]
    ppermute x1, waiting for transfers between devices: 1.61 us -> 0.01 us  [shards(): arrived = lax.ppermute(away, 'core', SWAP)]
    dot_general x1, matrix products: 0.58 us -> 2.07 us  [shards(): own = jnp.dot(hidden, ours, preferred_element_type=f32)]
    pallas_call x1, Pallas kernels: 2.31 us -> 1.18 us  [shards(): call(sum_body, pltpu.HBM(parts.shape, bf16), [VMEM] + [ANY] * SIDE, ANY,...]
    pallas_call x1, Pallas kernels: 2.07 us -> 0.94 us  [shards(): call(add_body, [pltpu.HBM((rows, width), bf16), MARK], [VMEM] * 2, [ANY,...]
  transfers between devices with their start and end apart: 10 -> 10, of which waited for: 4 -> 3; matrix products, arithmetic and copies ran while one was open for 1% -> 3% of each run, Pallas kernels for 6% -> 4%
where the time goes in v9:
time: 86.5 us; the launch traced here: 85.9 us
  starting transfers between devices  57.2 us (66%)
  Pallas kernels  13.5 us (16%)
  waiting for transfers between devices  12.2 us (14%)
  matrix products  2.07 us (2%)
  between operations  0.87 us (1%)
    ppermute x6, starting transfers between devices, shift(): return lax.ppermute(value, axis, [(i, (i + k) % SIDE) for i in range(SIDE)])  29.3 us
    ppermute x1, starting transfers between devices, shards(): arrived = lax.ppermute(away, 'core', SWAP)  12.4 us
    all_to_all x1, starting transfers between devices, shards(): lax.all_to_all(spread, RING, split_axis=0, concat_axis=0, tiled=True)  7.5 us
    all_to_all x1, waiting for transfers between devices, shards(): parts = lax.all_to_all(parts, RING, split_axis=0, concat_axis=0, tiled=True)  7.03 us
    pallas_call x1, Pallas kernels, shards(): call(hidden_body, [jax.ShapeDtypeStruct(active.shape, bf16), pltpu.HBM((r...  6.56 us
    ppermute x6, waiting for transfers between devices, shift(): return lax.ppermute(value, axis, [(i, (i + k) % SIDE) for i in range(SIDE)])  5.18 us
    ppermute x1, starting transfers between devices, shards(): other = lax.ppermute(half, 'core', SWAP)  4.01 us
    all_to_all x1, starting transfers between devices, shards(): parts = lax.all_to_all(parts, RING, split_axis=0, concat_axis=0, tiled=True)  3.91 us
  transfers between devices with their start and end apart: 10, of which 3 were waited for; matrix products, arithmetic and copies ran while one was open for 3% of the time, Pallas kernels for 4%

profile of v9, /device:TPU:1, one launch (start us, length us, event | category | flops | bytes accessed | tf_op | source)
XLA Modules:
  0.0 85.9 jit_solution(8211374721659285931)
XLA Ops:
  0.6 6.6 %shard_map.95 = (bf16[192,384]{1,0:T(8,128)(2,1)}, bf16[192,2048]{1,0:T(8,128)(2,1)}) custom-call(s32[1]{0:T(128)} %bitcast.core_ref.refs_0_, bf16[192,4096]{1,0:T(8,128)(2,1)} %tokens_ref.1, bf16[4096,384]{1,0:T(8,128)(2,1)} %gate_ref.1, bf16[4096,384]{1,0:T(8,128)(2,1)} %up_ref.1, bf16[384,4096]{1,0:T(8,128)(2,1)} %down_ref.1, s32[192,384]{1,0:T(8,128)} %active_ref.1), custom_call_target="tpu_custom_call" | custom-call | flops 1000000 | bytes 1000000 | tf_op jit(solution)/shard_map/pallas_call | solution.py:186
  7.2 12.4 %collective-permute-start = (bf16[192,2048]{1,0:T(8,128)(2,1)}, bf16[192,2048]{1,0:T(8,128)(2,1)S(1)}, u32[]{:S(2)}, u32[]{:S(2)}) collective-permute-start(bf16[192,2048]{1,0:T(8,128)(2,1)} %get-tuple-element.15), channel_id=1, source_target_pairs={{0,1},{1,0},{2,3},{3,2},{4,5},{5,4},{6,7},{7,6},{8,9},{9,8},{10,11... | collective-permute-start | bytes 2359304 | tf_op jit(solution)/shard_map/ppermute | solution.py:206
  19.6 2.1 %fusion.own_ref = f32[192,2048]{1,0:T(8,128)S(1)} fusion(bf16[192,384]{1,0:T(8,128)(2,1)} %get-tuple-element.14, bf16[384,4096]{1,0:T(8,128)(2,1)} %down_ref.1, s32[]{:T(128)S(6)} %select_n.3), kind=kOutput, calls=%fused_computation | convolution fusion | flops 301989888 | bytes 3293188 | tf_op jit(solution)/shard_map/dot_general | solution.py:207
  21.7 0.0 copy-start
  21.7 0.0 copy-start.1
  21.7 0.0 copy-start.2
  21.8 0.0 collective-permute-done.arrived_ref
  21.8 0.9 %shard_map.96 = (bf16[192,2048]{1,0:T(8,128)(2,1)}, f32[8,128]{1,0:T(8,128)S(1)}) custom-call(f32[192,2048]{1,0:T(8,128)S(1)} %fusion.own_ref, bf16[192,2048]{1,0:T(8,128)(2,1)S(1)} %collective-permute-done.arrived_ref), custom_call_target="tpu_custom_call" | custom-call | flops 1000000 | bytes 1000000 | tf_op jit(solution)/shard_map/pallas_call | solution.py:208
  22.7 3.9 %all-to-all-start = ((bf16[24,8,2048]{2,1,0:T(8,128)(2,1)}), bf16[24,8,2048]{2,1,0:T(8,128)(2,1)S(1)}, u32[]{:S(2)}, u32[]{:S(2)}) async-start(bf16[24,8,2048]{2,1,0:T(8,128)(2,1)} %bitcast.9), calls=%async_computation | async-start | bytes 1572864 | tf_op jit(solution)/shard_map/all_to_all | solution.py:217
  26.7 0.1 pad_add_fusion.place_ref
  26.7 1.2 %shard_map.97 = (bf16[4,2,2048]{2,1,0:T(2,128)(2,1)S(1)}, bf16[4,2,2048]{2,1,0:T(2,128)(2,1)S(1)}, bf16[4,2,2048]{2,1,0:T(2,128)(2,1)S(1)}, bf16[4,2,2048]{2,1,0:T(2,128)(2,1)S(1)}) custom-call(s32[4]{0:T(128)S(1)} %pad_add_fusion.place_ref, s32[16,16]{1,0:T(8,128)S(1)} %copy-done.1, s32[16]{0:T(128)S(1)} %copy-done.2, bf16[16,2,2048]{2,1,0:T(2,128)(2,1)S(1)} %copy-done, ...), custom_call_target="tpu_custom_call" | custom-call | flops 1000000 | bytes 1000000 | tf_op jit(solution)/shard_map/pallas_call | solution.py:220
  27.9 1.9 %collective-permute-start.1 = (bf16[4,2,2048]{2,1,0:T(2,128)(2,1)S(1)}, bf16[4,2,2048]{2,1,0:T(2,128)(2,1)S(1)}, u32[]{:S(2)}, u32[]{:S(2)}) collective-permute-start(bf16[4,2,2048]{2,1,0:T(2,128)(2,1)S(1)} %get-tuple-element.19), channel_id=1, source_target_pairs={{0,48},{48,96},{96,144},{144,0},{1,49},{49,97},{97,145},{145,1},{2... | collective-permute-start | bytes 98312 | tf_op jit(solution)/shard_map/ppermute | solution.py:177
  29.9 3.3 %collective-permute-start.2 = (bf16[4,2,2048]{2,1,0:T(2,128)(2,1)S(1)}, bf16[4,2,2048]{2,1,0:T(2,128)(2,1)S(1)}, u32[]{:S(2)}, u32[]{:S(2)}) collective-permute-start(bf16[4,2,2048]{2,1,0:T(2,128)(2,1)S(1)} %get-tuple-element.20), channel_id=1, source_target_pairs={{0,96},{48,144},{96,0},{144,48},{1,97},{49,145},{97,1},{145,49},{2... | collective-permute-start | bytes 98312 | tf_op jit(solution)/shard_map/ppermute | solution.py:177
  33.2 3.2 %collective-permute-start.3 = (bf16[4,2,2048]{2,1,0:T(2,128)(2,1)S(1)}, bf16[4,2,2048]{2,1,0:T(2,128)(2,1)S(1)}, u32[]{:S(2)}, u32[]{:S(2)}) collective-permute-start(bf16[4,2,2048]{2,1,0:T(2,128)(2,1)S(1)} %get-tuple-element.21), channel_id=1, source_target_pairs={{0,144},{48,0},{96,48},{144,96},{1,145},{49,1},{97,49},{145,97},{2... | collective-permute-start | bytes 98312 | tf_op jit(solution)/shard_map/ppermute | solution.py:177
  36.4 0.0 collective-permute-done.1.refs_1_
  36.4 0.0 collective-permute-done.2.refs_2_
  36.4 2.1 %collective-permute-done.3.refs_3_ = bf16[4,2,2048]{2,1,0:T(2,128)(2,1)S(1)} collective-permute-done((bf16[4,2,2048]{2,1,0:T(2,128)(2,1)S(1)}, bf16[4,2,2048]{2,1,0:T(2,128)(2,1)S(1)}, u32[]{:S(2)}, u32[]{:S(2)}) %collective-permute-start.3) | collective-permute-done | bytes 32800 | tf_op jit(solution)/shard_map/ppermute | solution.py:177
  38.5 0.6 shard_map.98
  39.1 7.0 %all-to-all-done.parts_ref = bf16[24,8,2048]{2,1,0:T(8,128)(2,1)S(1)} async-done(((bf16[24,8,2048]{2,1,0:T(8,128)(2,1)}), bf16[24,8,2048]{2,1,0:T(8,128)(2,1)S(1)}, u32[]{:S(2)}, u32[]{:S(2)}) %all-to-all-start) | async-done | bytes 786464 | tf_op jit(solution)/shard_map/all_to_all | solution.py:217
  46.1 1.2 %shard_map.99 = bf16[24,8,2048]{2,1,0:T(8,128)(2,1)} custom-call(bf16[24,8,2048]{2,1,0:T(8,128)(2,1)S(1)} %all-to-all-done.parts_ref, bf16[4,2,2048]{2,1,0:T(2,128)(2,1)S(1)} %get-tuple-element.22.refs_0_, bf16[4,2,2048]{2,1,0:T(2,128)(2,1)S(1)} %get-tuple-element.23.refs_1_, bf16[4,2,2048]{2,1,0:T(2,128)(2,1)S(1)} %get-tuple-element.24.refs_2_, ...), custom_call_target="tpu_custom_call" | custom-call | flops 1000000 | bytes 1000000 | tf_op jit(solution)/shard_map/pallas_call | solution.py:226
  47.3 7.5 %all-to-all-start.1 = ((bf16[24,8,2048]{2,1,0:T(8,128)(2,1)}), bf16[24,8,2048]{2,1,0:T(8,128)(2,1)S(1)}, u32[]{:S(2)}, u32[]{:S(2)}) async-start(bf16[24,8,2048]{2,1,0:T(8,128)(2,1)} %shard_map.99), calls=%async_computation.1 | async-start | bytes 1572864 | tf_op jit(solution)/shard_map/all_to_all | solution.py:234
  54.8 12.6 %collective-permute-start.4 = (bf16[4,2,2048]{2,1,0:T(2,128)(2,1)S(1)}, bf16[4,2,2048]{2,1,0:T(2,128)(2,1)S(1)}, u32[]{:S(2)}, u32[]{:S(2)}) collective-permute-start(bf16[4,2,2048]{2,1,0:T(2,128)(2,1)S(1)} %get-tuple-element.23.refs_1_), channel_id=1, source_target_pairs={{0,384},{192,576},{384,0},{576,192},{1,385},{193,577},{385,1},{577... | collective-permute-start | bytes 98312 | tf_op jit(solution)/shard_map/ppermute | solution.py:177
  67.5 3.2 %collective-permute-start.5 = (bf16[4,2,2048]{2,1,0:T(2,128)(2,1)S(1)}, bf16[4,2,2048]{2,1,0:T(2,128)(2,1)S(1)}, u32[]{:S(2)}, u32[]{:S(2)}) collective-permute-start(bf16[4,2,2048]{2,1,0:T(2,128)(2,1)S(1)} %get-tuple-element.24.refs_2_), channel_id=1, source_target_pairs={{0,192},{192,384},{384,576},{576,0},{1,193},{193,385},{385,577},{5... | collective-permute-start | bytes 98312 | tf_op jit(solution)/shard_map/ppermute | solution.py:177
  70.7 5.1 %collective-permute-start.6 = (bf16[4,2,2048]{2,1,0:T(2,128)(2,1)S(1)}, bf16[4,2,2048]{2,1,0:T(2,128)(2,1)S(1)}, u32[]{:S(2)}, u32[]{:S(2)}) collective-permute-start(bf16[4,2,2048]{2,1,0:T(2,128)(2,1)S(1)} %get-tuple-element.25.refs_3_), channel_id=1, source_target_pairs={{0,576},{192,0},{384,192},{576,384},{1,577},{193,1},{385,193},{577... | collective-permute-start | bytes 98312 | tf_op jit(solution)/shard_map/ppermute | solution.py:177
  75.8 3.0 %collective-permute-done.4.refs_1_ = bf16[4,2,2048]{2,1,0:T(2,128)(2,1)S(1)} collective-permute-done((bf16[4,2,2048]{2,1,0:T(2,128)(2,1)S(1)}, bf16[4,2,2048]{2,1,0:T(2,128)(2,1)S(1)}, u32[]{:S(2)}, u32[]{:S(2)}) %collective-permute-start.4) | collective-permute-done | bytes 32800 | tf_op jit(solution)/shard_map/ppermute | solution.py:177
  78.8 0.0 collective-permute-done.5.refs_2_
  78.8 0.0 all-to-all-done.1
  78.8 4.0 %collective-permute-start.7 = (bf16[192,2048]{1,0:T(8,128)(2,1)S(1)}, bf16[192,2048]{1,0:T(8,128)(2,1)S(1)}, u32[]{:S(2)}, u32[]{:S(2)}) collective-permute-start(bf16[192,2048]{1,0:T(8,128)(2,1)S(1)} %shard_map.100.refs_1_), channel_id=1, source_target_pairs={{0,1},{1,0},{2,3},{3,2},{4,5},{5,4},{6,7},{7,6},{8,9},{9,8},{10,11... | collective-permute-start | bytes 2359304 | tf_op jit(solution)/shard_map/ppermute | solution.py:240
  82.8 1.2 %shard_map.103 = bf16[16,2,2048]{2,1,0:T(2,128)(2,1)} custom-call(s32[4]{0:T(128)S(1)} %pad_add_fusion.place_ref, bf16[4,2,2048]{2,1,0:T(2,128)(2,1)S(1)} %get-tuple-element.22.refs_0_, bf16[4,2,2048]{2,1,0:T(2,128)(2,1)S(1)} %collective-permute-done.4.refs_1_, bf16[4,2,2048]{2,1,0:T(2,128)(2,1)S(1)} %collective-permute-done.5.refs_2_, ...), custom_call_target="tpu_custom_call" | custom-call | flops 1000000 | bytes 1000000 | tf_op jit(solution)/shard_map/pallas_call | solution.py:237
  84.1 0.9 %shard_map.101.refs_2_ = bf16[192,4096]{1,0:T(8,128)(2,1)} custom-call(s32[1]{0:T(128)} %bitcast.core_ref.refs_0_, bf16[192,2048]{1,0:T(8,128)(2,1)S(1)} %shard_map.100.refs_1_), custom_call_target="tpu_custom_call" | custom-call | flops 1000000 | bytes 1000000 | tf_op jit(solution)/shard_map/pallas_call | solution.py:156
  85.0 0.0 collective-permute-done.7.refs_1_
  85.0 0.9 %shard_map.102 = bf16[192,4096]{1,0:T(8,128)(2,1)} custom-call(s32[1]{0:T(128)} %bitcast.core_ref.refs_0_, bf16[192,2048]{1,0:T(8,128)(2,1)S(1)} %collective-permute-done.7.refs_1_, bf16[192,4096]{1,0:T(8,128)(2,1)} %shard_map.101.refs_2_), custom_call_target="tpu_custom_call", output_to_operand_aliasing={{}: (2, {})} | custom-call | flops 1000000 | bytes 1000000 | tf_op jit(solution)/shard_map/pallas_call | solution.py:156
  (5 shorter events, 0.0 us)
Async XLA Ops:
  7.2 14.6 %collective-permute-start = (bf16[192,2048]{1,0:T(8,128)(2,1)}, bf16[192,2048]{1,0:T(8,128)(2,1)S(1)}, u32[]{:S(2)}, u32[]{:S(2)}) collective-permute-start(bf16[192,2048]{1,0:T(8,128)(2,1)} %get-tuple-element.15), channel_id=1, source_target_pairs={{0,1},{1,0},{2,3},{3,2},{4,5},{5,4},{6,7},{7,6},{8,9},{9,8},{10,11... | collective-permute-start | bytes 2359304 | tf_op jit(solution)/shard_map/ppermute | solution.py:206
  21.7 5.0 %copy-start = (bf16[16,2,2048]{2,1,0:T(2,128)(2,1)S(1)}, bf16[16,2,2048]{2,1,0:T(2,128)(2,1)}, u32[]{:S(2)}) copy-start(bf16[16,2,2048]{2,1,0:T(2,128)(2,1)} %kv_ref.1) | copy-start | bytes 393220
  21.7 5.0 %copy-start.1 = (s32[16,16]{1,0:T(8,128)S(1)}, s32[16,16]{1,0:T(8,128)}, u32[]{:S(2)}) copy-start(s32[16,16]{1,0:T(8,128)} %dest_ref.1) | copy-start | bytes 3076
  21.7 5.0 %copy-start.2 = (s32[16]{0:T(128)S(1)}, s32[16]{0:T(128)}, u32[]{:S(2)}) copy-start(s32[16]{0:T(128)} %lengths_ref.1) | copy-start | bytes 196
  22.7 23.4 %all-to-all-start = ((bf16[24,8,2048]{2,1,0:T(8,128)(2,1)}), bf16[24,8,2048]{2,1,0:T(8,128)(2,1)S(1)}, u32[]{:S(2)}, u32[]{:S(2)}) async-start(bf16[24,8,2048]{2,1,0:T(8,128)(2,1)} %bitcast.9), calls=%async_computation | async-start | bytes 1572864 | tf_op jit(solution)/shard_map/all_to_all | solution.py:217
  27.9 8.4 %collective-permute-start.1 = (bf16[4,2,2048]{2,1,0:T(2,128)(2,1)S(1)}, bf16[4,2,2048]{2,1,0:T(2,128)(2,1)S(1)}, u32[]{:S(2)}, u32[]{:S(2)}) collective-permute-start(bf16[4,2,2048]{2,1,0:T(2,128)(2,1)S(1)} %get-tuple-element.19), channel_id=1, source_target_pairs={{0,48},{48,96},{96,144},{144,0},{1,49},{49,97},{97,145},{145,1},{2... | collective-permute-start | bytes 98312 | tf_op jit(solution)/shard_map/ppermute | solution.py:177
  29.9 6.5 %collective-permute-start.2 = (bf16[4,2,2048]{2,1,0:T(2,128)(2,1)S(1)}, bf16[4,2,2048]{2,1,0:T(2,128)(2,1)S(1)}, u32[]{:S(2)}, u32[]{:S(2)}) collective-permute-start(bf16[4,2,2048]{2,1,0:T(2,128)(2,1)S(1)} %get-tuple-element.20), channel_id=1, source_target_pairs={{0,96},{48,144},{96,0},{144,48},{1,97},{49,145},{97,1},{145,49},{2... | collective-permute-start | bytes 98312 | tf_op jit(solution)/shard_map/ppermute | solution.py:177
  33.2 5.3 %collective-permute-start.3 = (bf16[4,2,2048]{2,1,0:T(2,128)(2,1)S(1)}, bf16[4,2,2048]{2,1,0:T(2,128)(2,1)S(1)}, u32[]{:S(2)}, u32[]{:S(2)}) collective-permute-start(bf16[4,2,2048]{2,1,0:T(2,128)(2,1)S(1)} %get-tuple-element.21), channel_id=1, source_target_pairs={{0,144},{48,0},{96,48},{144,96},{1,145},{49,1},{97,49},{145,97},{2... | collective-permute-start | bytes 98312 | tf_op jit(solution)/shard_map/ppermute | solution.py:177
  47.3 31.5 %all-to-all-start.1 = ((bf16[24,8,2048]{2,1,0:T(8,128)(2,1)}), bf16[24,8,2048]{2,1,0:T(8,128)(2,1)S(1)}, u32[]{:S(2)}, u32[]{:S(2)}) async-start(bf16[24,8,2048]{2,1,0:T(8,128)(2,1)} %shard_map.99), calls=%async_computation.1 | async-start | bytes 1572864 | tf_op jit(solution)/shard_map/all_to_all | solution.py:234
  54.8 24.0 %collective-permute-start.4 = (bf16[4,2,2048]{2,1,0:T(2,128)(2,1)S(1)}, bf16[4,2,2048]{2,1,0:T(2,128)(2,1)S(1)}, u32[]{:S(2)}, u32[]{:S(2)}) collective-permute-start(bf16[4,2,2048]{2,1,0:T(2,128)(2,1)S(1)} %get-tuple-element.23.refs_1_), channel_id=1, source_target_pairs={{0,384},{192,576},{384,0},{576,192},{1,385},{193,577},{385,1},{577... | collective-permute-start | bytes 98312 | tf_op jit(solution)/shard_map/ppermute | solution.py:177
  67.5 11.3 %collective-permute-start.5 = (bf16[4,2,2048]{2,1,0:T(2,128)(2,1)S(1)}, bf16[4,2,2048]{2,1,0:T(2,128)(2,1)S(1)}, u32[]{:S(2)}, u32[]{:S(2)}) collective-permute-start(bf16[4,2,2048]{2,1,0:T(2,128)(2,1)S(1)} %get-tuple-element.24.refs_2_), channel_id=1, source_target_pairs={{0,192},{192,384},{384,576},{576,0},{1,193},{193,385},{385,577},{5... | collective-permute-start | bytes 98312 | tf_op jit(solution)/shard_map/ppermute | solution.py:177
  70.7 8.1 %collective-permute-start.6 = (bf16[4,2,2048]{2,1,0:T(2,128)(2,1)S(1)}, bf16[4,2,2048]{2,1,0:T(2,128)(2,1)S(1)}, u32[]{:S(2)}, u32[]{:S(2)}) collective-permute-start(bf16[4,2,2048]{2,1,0:T(2,128)(2,1)S(1)} %get-tuple-element.25.refs_3_), channel_id=1, source_target_pairs={{0,576},{192,0},{384,192},{576,384},{1,577},{193,1},{385,193},{577... | collective-permute-start | bytes 98312 | tf_op jit(solution)/shard_map/ppermute | solution.py:177
  78.8 6.1 %collective-permute-start.7 = (bf16[192,2048]{1,0:T(8,128)(2,1)S(1)}, bf16[192,2048]{1,0:T(8,128)(2,1)S(1)}, u32[]{:S(2)}, u32[]{:S(2)}) collective-permute-start(bf16[192,2048]{1,0:T(8,128)(2,1)S(1)} %shard_map.100.refs_1_), channel_id=1, source_target_pairs={{0,1},{1,0},{2,3},{3,2},{4,5},{5,4},{6,7},{7,6},{8,9},{9,8},{10,11... | collective-permute-start | bytes 2359304 | tf_op jit(solution)/shard_map/ppermute | solution.py:240

commit v10 on v9

--- a/solution.py
+++ b/solution.py
@@ -7,12 +7,12 @@
 
 GRP = ("zh", "x")
 TP = ("y", "zl", "core")
-RING = ("y", "zl")
+RING = ("zl", "y")
 SWAP = [(0, 1), (1, 0)]
 SIDE = 4
 CHIPS = 24
 ORDER = (0, 2, 1, 3)
-CHUNKS = 8
+CHUNKS = 4
 STEPS = 4
 
 bf16, f32 = jnp.bfloat16, jnp.float32
@@ -35,16 +35,16 @@
 
 
 def hidden_body(core_ref, tokens_ref, gate_ref, up_ref, down_ref, active_ref, hidden_ref, away_ref, *scratch):
-    *held, theirs_ref, mask_ref, sent_ref, sems, last_sems, out_sems = scratch
-    depth = tokens_ref.shape[1] // CHUNKS
+    tokens, weights, theirs_ref, mask_ref, sent_ref, sems, last_sems, out_sems = scratch
+    depth, units = tokens_ref.shape[1] // CHUNKS, hidden_ref.shape[1]
     copies = []
     for i in range(CHUNKS):
         block = pl.ds(i * depth, depth)
-        pieces = zip((tokens_ref, gate_ref, up_ref), held, ((slice(None), block), (block,), (block,)))
         copies.append(
             [
-                pltpu.make_async_copy(ref.at[place], to.at[place], sems.at[n, i])
-                for n, (ref, to, place) in enumerate(pieces)
+                pltpu.make_async_copy(tokens_ref.at[:, block], tokens.at[:, block], sems.at[0, i]),
+                pltpu.make_async_copy(gate_ref.at[block], weights.at[block, pl.ds(0, units)], sems.at[1, i]),
+                pltpu.make_async_copy(up_ref.at[block], weights.at[block, pl.ds(units, units)], sems.at[2, i]),
             ]
         )
     width = away_ref.shape[1]
@@ -56,17 +56,15 @@
     for chunk in copies + [last]:
         for copy in chunk:
             copy.start()
-    gate = jnp.zeros(hidden_ref.shape, f32)
-    up = jnp.zeros(hidden_ref.shape, f32)
+    both = jnp.zeros((hidden_ref.shape[0], 2 * units), f32)
     for i, chunk in enumerate(copies):
         for copy in chunk:
             copy.wait()
         block = slice(i * depth, (i + 1) * depth)
-        part = held[0][:, block]
-        gate += jnp.dot(part, held[1][block], preferred_element_type=f32)
-        up += jnp.dot(part, held[2][block], preferred_element_type=f32)
+        both += jnp.dot(tokens[:, block], weights[block], preferred_element_type=f32)
     for copy in last:
         copy.wait()
+    gate, up = both[:, :units], both[:, units:]
     hidden = (gate / (1 + jnp.exp(-gate)) * up * mask_ref[...].astype(f32)).astype(bf16)
     hidden_ref[...] = hidden
     columns = width // STEPS
@@ -191,8 +189,7 @@
         vmem=56,
         scratch_shapes=[
             pltpu.VMEM(tokens.shape, bf16),
-            pltpu.VMEM(gate_weight.shape, bf16),
-            pltpu.VMEM(up_weight.shape, bf16),
+            pltpu.VMEM((gate_weight.shape[0], 2 * gate_weight.shape[1]), bf16),
             pltpu.VMEM((active.shape[1], width), bf16),
             pltpu.VMEM(active.shape, jnp.int32),
             pltpu.VMEM((rows, width), bf16),

time: 86.5 us -> 87.1 us (level)
  starting transfers between devices: 57.2 us -> 60.5 us
  waiting for transfers between devices: 12.2 us -> 9.66 us
    all_to_all x1, starting transfers between devices: 7.5 us -> 9.86 us  [shards(): lax.all_to_all(spread, RING, split_axis=0, concat_axis=0, tiled=True)]
    ppermute x1, starting transfers between devices: 4.01 us -> 5.68 us  [shards(): other = lax.ppermute(half, 'core', SWAP)]
    all_to_all x1, waiting for transfers between devices: 7.03 us -> 5.42 us  [shards(): parts = lax.all_to_all(parts, RING, split_axis=0, concat_axis=0, tiled=True)]
    ppermute x6, waiting for transfers between devices: 5.18 us -> 4.23 us  [shift(): return lax.ppermute(value, axis, [(i, (i + k) % SIDE) for i in range(SIDE)])]
  transfers between devices with their start and end apart: 10 -> 10, of which waited for: 3 -> 4; matrix products, arithmetic and copies ran while one was open for 3% -> 2% of each run, Pallas kernels for 4% -> 4%
where the time goes in v10:
time: 87.1 us; the launch traced here: 86.5 us
  starting transfers between devices  60.5 us (69%)
  Pallas kernels  13.3 us (15%)
  waiting for transfers between devices  9.66 us (11%)
  matrix products  2.07 us (2%)
    ppermute x6, starting transfers between devices, shift(): return lax.ppermute(value, axis, [(i, (i + k) % SIDE) for i in range(SIDE)])  28.6 us
    ppermute x1, starting transfers between devices, shards(): arrived = lax.ppermute(away, 'core', SWAP)  12.4 us
    all_to_all x1, starting transfers between devices, shards(): lax.all_to_all(spread, RING, split_axis=0, concat_axis=0, tiled=True)  9.86 us
    pallas_call x1, Pallas kernels, shards(): call(hidden_body, [jax.ShapeDtypeStruct(active.shape, bf16), pltpu.HBM((r...  6.44 us
    ppermute x1, starting transfers between devices, shards(): other = lax.ppermute(half, 'core', SWAP)  5.68 us
    all_to_all x1, waiting for transfers between devices, shards(): parts = lax.all_to_all(parts, RING, split_axis=0, concat_axis=0, tiled=True)  5.42 us
    ppermute x6, waiting for transfers between devices, shift(): return lax.ppermute(value, axis, [(i, (i + k) % SIDE) for i in range(SIDE)])  4.23 us
    all_to_all x1, starting transfers between devices, shards(): parts = lax.all_to_all(parts, RING, split_axis=0, concat_axis=0, tiled=True)  3.91 us
  transfers between devices with their start and end apart: 10, of which 4 were waited for; matrix products, arithmetic and copies ran while one was open for 2% of the time, Pallas kernels for 4%

profile of v10, /device:TPU:1, one launch (start us, length us, event | category | flops | bytes accessed | tf_op | source)
XLA Modules:
  0.0 86.5 jit_solution(8070205460555388650)
XLA Ops:
  0.6 6.4 %shard_map.95 = (bf16[192,384]{1,0:T(8,128)(2,1)}, bf16[192,2048]{1,0:T(8,128)(2,1)}) custom-call(s32[1]{0:T(128)} %bitcast.core_ref.refs_0_, bf16[192,4096]{1,0:T(8,128)(2,1)} %tokens_ref.1, bf16[4096,384]{1,0:T(8,128)(2,1)} %gate_ref.1, bf16[4096,384]{1,0:T(8,128)(2,1)} %up_ref.1, bf16[384,4096]{1,0:T(8,128)(2,1)} %down_ref.1, s32[192,384]{1,0:T(8,128)} %active_ref.1), custom_call_target="tpu_custom_call" | custom-call | flops 1000000 | bytes 1000000 | tf_op jit(solution)/shard_map/pallas_call | solution.py:184
  7.1 12.4 %collective-permute-start = (bf16[192,2048]{1,0:T(8,128)(2,1)}, bf16[192,2048]{1,0:T(8,128)(2,1)S(1)}, u32[]{:S(2)}, u32[]{:S(2)}) collective-permute-start(bf16[192,2048]{1,0:T(8,128)(2,1)} %get-tuple-element.15), channel_id=1, source_target_pairs={{0,1},{1,0},{2,3},{3,2},{4,5},{5,4},{6,7},{7,6},{8,9},{9,8},{10,11... | collective-permute-start | bytes 2359304 | tf_op jit(solution)/shard_map/ppermute | solution.py:203
  19.5 2.1 %fusion.own_ref = f32[192,2048]{1,0:T(8,128)S(1)} fusion(bf16[192,384]{1,0:T(8,128)(2,1)} %get-tuple-element.14, bf16[384,4096]{1,0:T(8,128)(2,1)} %down_ref.1, s32[]{:T(128)S(6)} %select_n.3), kind=kOutput, calls=%fused_computation | convolution fusion | flops 301989888 | bytes 3293188 | tf_op jit(solution)/shard_map/dot_general | solution.py:204
  21.6 0.0 copy-start
  21.6 0.0 copy-start.1
  21.6 0.0 copy-start.2
  21.6 0.0 collective-permute-done.arrived_ref
  21.6 0.9 %shard_map.96 = (bf16[192,2048]{1,0:T(8,128)(2,1)}, f32[8,128]{1,0:T(8,128)S(1)}) custom-call(f32[192,2048]{1,0:T(8,128)S(1)} %fusion.own_ref, bf16[192,2048]{1,0:T(8,128)(2,1)S(1)} %collective-permute-done.arrived_ref), custom_call_target="tpu_custom_call" | custom-call | flops 1000000 | bytes 1000000 | tf_op jit(solution)/shard_map/pallas_call | solution.py:205
  22.6 3.9 %all-to-all-start = ((bf16[24,8,2048]{2,1,0:T(8,128)(2,1)}), bf16[24,8,2048]{2,1,0:T(8,128)(2,1)S(1)}, u32[]{:S(2)}, u32[]{:S(2)}) async-start(bf16[24,8,2048]{2,1,0:T(8,128)(2,1)} %bitcast.9), calls=%async_computation | async-start | bytes 1572864 | tf_op jit(solution)/shard_map/all_to_all | solution.py:214
  26.5 0.1 pad_add_fusion.place_ref
  26.6 1.2 %shard_map.97 = (bf16[4,2,2048]{2,1,0:T(2,128)(2,1)S(1)}, bf16[4,2,2048]{2,1,0:T(2,128)(2,1)S(1)}, bf16[4,2,2048]{2,1,0:T(2,128)(2,1)S(1)}, bf16[4,2,2048]{2,1,0:T(2,128)(2,1)S(1)}) custom-call(s32[4]{0:T(128)S(1)} %pad_add_fusion.place_ref, s32[16,16]{1,0:T(8,128)S(1)} %copy-done.1, s32[16]{0:T(128)S(1)} %copy-done.2, bf16[16,2,2048]{2,1,0:T(2,128)(2,1)S(1)} %copy-done, ...), custom_call_target="tpu_custom_call" | custom-call | flops 1000000 | bytes 1000000 | tf_op jit(solution)/shard_map/pallas_call | solution.py:217
  27.8 1.9 %collective-permute-start.1 = (bf16[4,2,2048]{2,1,0:T(2,128)(2,1)S(1)}, bf16[4,2,2048]{2,1,0:T(2,128)(2,1)S(1)}, u32[]{:S(2)}, u32[]{:S(2)}) collective-permute-start(bf16[4,2,2048]{2,1,0:T(2,128)(2,1)S(1)} %get-tuple-element.19), channel_id=1, source_target_pairs={{0,48},{48,96},{96,144},{144,0},{1,49},{49,97},{97,145},{145,1},{2... | collective-permute-start | bytes 98312 | tf_op jit(solution)/shard_map/ppermute | solution.py:175
  29.7 3.3 %collective-permute-start.2 = (bf16[4,2,2048]{2,1,0:T(2,128)(2,1)S(1)}, bf16[4,2,2048]{2,1,0:T(2,128)(2,1)S(1)}, u32[]{:S(2)}, u32[]{:S(2)}) collective-permute-start(bf16[4,2,2048]{2,1,0:T(2,128)(2,1)S(1)} %get-tuple-element.20), channel_id=1, source_target_pairs={{0,96},{48,144},{96,0},{144,48},{1,97},{49,145},{97,1},{145,49},{2... | collective-permute-start | bytes 98312 | tf_op jit(solution)/shard_map/ppermute | solution.py:175
  33.1 3.2 %collective-permute-start.3 = (bf16[4,2,2048]{2,1,0:T(2,128)(2,1)S(1)}, bf16[4,2,2048]{2,1,0:T(2,128)(2,1)S(1)}, u32[]{:S(2)}, u32[]{:S(2)}) collective-permute-start(bf16[4,2,2048]{2,1,0:T(2,128)(2,1)S(1)} %get-tuple-element.21), channel_id=1, source_target_pairs={{0,144},{48,0},{96,48},{144,96},{1,145},{49,1},{97,49},{145,97},{2... | collective-permute-start | bytes 98312 | tf_op jit(solution)/shard_map/ppermute | solution.py:175
  36.2 0.0 collective-permute-done.1.refs_1_
  36.3 0.0 collective-permute-done.2.refs_2_
  36.3 2.1 %collective-permute-done.3.refs_3_ = bf16[4,2,2048]{2,1,0:T(2,128)(2,1)S(1)} collective-permute-done((bf16[4,2,2048]{2,1,0:T(2,128)(2,1)S(1)}, bf16[4,2,2048]{2,1,0:T(2,128)(2,1)S(1)}, u32[]{:S(2)}, u32[]{:S(2)}) %collective-permute-start.3) | collective-permute-done | bytes 32800 | tf_op jit(solution)/shard_map/ppermute | solution.py:175
  38.4 0.6 shard_map.98
  39.0 5.4 %all-to-all-done.parts_ref = bf16[24,8,2048]{2,1,0:T(8,128)(2,1)S(1)} async-done(((bf16[24,8,2048]{2,1,0:T(8,128)(2,1)}), bf16[24,8,2048]{2,1,0:T(8,128)(2,1)S(1)}, u32[]{:S(2)}, u32[]{:S(2)}) %all-to-all-start) | async-done | bytes 786464 | tf_op jit(solution)/shard_map/all_to_all | solution.py:214
  44.4 1.2 %shard_map.99 = bf16[24,8,2048]{2,1,0:T(8,128)(2,1)} custom-call(bf16[24,8,2048]{2,1,0:T(8,128)(2,1)S(1)} %all-to-all-done.parts_ref, bf16[4,2,2048]{2,1,0:T(2,128)(2,1)S(1)} %get-tuple-element.22.refs_0_, bf16[4,2,2048]{2,1,0:T(2,128)(2,1)S(1)} %get-tuple-element.23.refs_1_, bf16[4,2,2048]{2,1,0:T(2,128)(2,1)S(1)} %get-tuple-element.24.refs_2_, ...), custom_call_target="tpu_custom_call" | custom-call | flops 1000000 | bytes 1000000 | tf_op jit(solution)/shard_map/pallas_call | solution.py:223
  45.6 9.9 %all-to-all-start.1 = ((bf16[24,8,2048]{2,1,0:T(8,128)(2,1)}), bf16[24,8,2048]{2,1,0:T(8,128)(2,1)S(1)}, u32[]{:S(2)}, u32[]{:S(2)}) async-start(bf16[24,8,2048]{2,1,0:T(8,128)(2,1)} %shard_map.99), calls=%async_computation.1 | async-start | bytes 1572864 | tf_op jit(solution)/shard_map/all_to_all | solution.py:231
  55.4 11.9 %collective-permute-start.4 = (bf16[4,2,2048]{2,1,0:T(2,128)(2,1)S(1)}, bf16[4,2,2048]{2,1,0:T(2,128)(2,1)S(1)}, u32[]{:S(2)}, u32[]{:S(2)}) collective-permute-start(bf16[4,2,2048]{2,1,0:T(2,128)(2,1)S(1)} %get-tuple-element.23.refs_1_), channel_id=1, source_target_pairs={{0,384},{192,576},{384,0},{576,192},{1,385},{193,577},{385,1},{577... | collective-permute-start | bytes 98312 | tf_op jit(solution)/shard_map/ppermute | solution.py:175
  67.4 3.4 %collective-permute-start.5 = (bf16[4,2,2048]{2,1,0:T(2,128)(2,1)S(1)}, bf16[4,2,2048]{2,1,0:T(2,128)(2,1)S(1)}, u32[]{:S(2)}, u32[]{:S(2)}) collective-permute-start(bf16[4,2,2048]{2,1,0:T(2,128)(2,1)S(1)} %get-tuple-element.24.refs_2_), channel_id=1, source_target_pairs={{0,192},{192,384},{384,576},{576,0},{1,193},{193,385},{385,577},{5... | collective-permute-start | bytes 98312 | tf_op jit(solution)/shard_map/ppermute | solution.py:175
  70.8 4.8 %collective-permute-start.6 = (bf16[4,2,2048]{2,1,0:T(2,128)(2,1)S(1)}, bf16[4,2,2048]{2,1,0:T(2,128)(2,1)S(1)}, u32[]{:S(2)}, u32[]{:S(2)}) collective-permute-start(bf16[4,2,2048]{2,1,0:T(2,128)(2,1)S(1)} %get-tuple-element.25.refs_3_), channel_id=1, source_target_pairs={{0,576},{192,0},{384,192},{576,384},{1,577},{193,1},{385,193},{577... | collective-permute-start | bytes 98312 | tf_op jit(solution)/shard_map/ppermute | solution.py:175
  75.7 1.9 %collective-permute-done.4.refs_1_ = bf16[4,2,2048]{2,1,0:T(2,128)(2,1)S(1)} collective-permute-done((bf16[4,2,2048]{2,1,0:T(2,128)(2,1)S(1)}, bf16[4,2,2048]{2,1,0:T(2,128)(2,1)S(1)}, u32[]{:S(2)}, u32[]{:S(2)}) %collective-permute-start.4) | collective-permute-done | bytes 32800 | tf_op jit(solution)/shard_map/ppermute | solution.py:175
  77.6 0.0 collective-permute-done.5.refs_2_
  77.6 0.2 collective-permute-done.6.refs_3_
  77.8 5.7 %collective-permute-start.7 = (bf16[192,2048]{1,0:T(8,128)(2,1)S(1)}, bf16[192,2048]{1,0:T(8,128)(2,1)S(1)}, u32[]{:S(2)}, u32[]{:S(2)}) collective-permute-start(bf16[192,2048]{1,0:T(8,128)(2,1)S(1)} %shard_map.100.refs_1_), channel_id=1, source_target_pairs={{0,1},{1,0},{2,3},{3,2},{4,5},{5,4},{6,7},{7,6},{8,9},{9,8},{10,11... | collective-permute-start | bytes 2359304 | tf_op jit(solution)/shard_map/ppermute | solution.py:237
  83.4 1.2 %shard_map.103 = bf16[16,2,2048]{2,1,0:T(2,128)(2,1)} custom-call(s32[4]{0:T(128)S(1)} %pad_add_fusion.place_ref, bf16[4,2,2048]{2,1,0:T(2,128)(2,1)S(1)} %get-tuple-element.22.refs_0_, bf16[4,2,2048]{2,1,0:T(2,128)(2,1)S(1)} %collective-permute-done.4.refs_1_, bf16[4,2,2048]{2,1,0:T(2,128)(2,1)S(1)} %collective-permute-done.5.refs_2_, ...), custom_call_target="tpu_custom_call" | custom-call | flops 1000000 | bytes 1000000 | tf_op jit(solution)/shard_map/pallas_call | solution.py:234
  84.7 0.9 %shard_map.101.refs_2_ = bf16[192,4096]{1,0:T(8,128)(2,1)} custom-call(s32[1]{0:T(128)} %bitcast.core_ref.refs_0_, bf16[192,2048]{1,0:T(8,128)(2,1)S(1)} %shard_map.100.refs_1_), custom_call_target="tpu_custom_call" | custom-call | flops 1000000 | bytes 1000000 | tf_op jit(solution)/shard_map/pallas_call | solution.py:154
  85.6 0.0 collective-permute-done.7.refs_1_
  85.6 0.9 %shard_map.102 = bf16[192,4096]{1,0:T(8,128)(2,1)} custom-call(s32[1]{0:T(128)} %bitcast.core_ref.refs_0_, bf16[192,2048]{1,0:T(8,128)(2,1)S(1)} %collective-permute-done.7.refs_1_, bf16[192,4096]{1,0:T(8,128)(2,1)} %shard_map.101.refs_2_), custom_call_target="tpu_custom_call", output_to_operand_aliasing={{}: (2, {})} | custom-call | flops 1000000 | bytes 1000000 | tf_op jit(solution)/shard_map/pallas_call | solution.py:154
  (5 shorter events, 0.0 us)
Async XLA Ops:
  7.1 14.6 %collective-permute-start = (bf16[192,2048]{1,0:T(8,128)(2,1)}, bf16[192,2048]{1,0:T(8,128)(2,1)S(1)}, u32[]{:S(2)}, u32[]{:S(2)}) collective-permute-start(bf16[192,2048]{1,0:T(8,128)(2,1)} %get-tuple-element.15), channel_id=1, source_target_pairs={{0,1},{1,0},{2,3},{3,2},{4,5},{5,4},{6,7},{7,6},{8,9},{9,8},{10,11... | collective-permute-start | bytes 2359304 | tf_op jit(solution)/shard_map/ppermute | solution.py:203
  21.6 5.0 %copy-start = (bf16[16,2,2048]{2,1,0:T(2,128)(2,1)S(1)}, bf16[16,2,2048]{2,1,0:T(2,128)(2,1)}, u32[]{:S(2)}) copy-start(bf16[16,2,2048]{2,1,0:T(2,128)(2,1)} %kv_ref.1) | copy-start | bytes 393220
  21.6 5.0 %copy-start.1 = (s32[16,16]{1,0:T(8,128)S(1)}, s32[16,16]{1,0:T(8,128)}, u32[]{:S(2)}) copy-start(s32[16,16]{1,0:T(8,128)} %dest_ref.1) | copy-start | bytes 3076
  21.6 5.0 %copy-start.2 = (s32[16]{0:T(128)S(1)}, s32[16]{0:T(128)}, u32[]{:S(2)}) copy-start(s32[16]{0:T(128)} %lengths_ref.1) | copy-start | bytes 196
  22.6 21.8 %all-to-all-start = ((bf16[24,8,2048]{2,1,0:T(8,128)(2,1)}), bf16[24,8,2048]{2,1,0:T(8,128)(2,1)S(1)}, u32[]{:S(2)}, u32[]{:S(2)}) async-start(bf16[24,8,2048]{2,1,0:T(8,128)(2,1)} %bitcast.9), calls=%async_computation | async-start | bytes 1572864 | tf_op jit(solution)/shard_map/all_to_all | solution.py:214
  27.8 8.4 %collective-permute-start.1 = (bf16[4,2,2048]{2,1,0:T(2,128)(2,1)S(1)}, bf16[4,2,2048]{2,1,0:T(2,128)(2,1)S(1)}, u32[]{:S(2)}, u32[]{:S(2)}) collective-permute-start(bf16[4,2,2048]{2,1,0:T(2,128)(2,1)S(1)} %get-tuple-element.19), channel_id=1, source_target_pairs={{0,48},{48,96},{96,144},{144,0},{1,49},{49,97},{97,145},{145,1},{2... | collective-permute-start | bytes 98312 | tf_op jit(solution)/shard_map/ppermute | solution.py:175
  29.7 6.5 %collective-permute-start.2 = (bf16[4,2,2048]{2,1,0:T(2,128)(2,1)S(1)}, bf16[4,2,2048]{2,1,0:T(2,128)(2,1)S(1)}, u32[]{:S(2)}, u32[]{:S(2)}) collective-permute-start(bf16[4,2,2048]{2,1,0:T(2,128)(2,1)S(1)} %get-tuple-element.20), channel_id=1, source_target_pairs={{0,96},{48,144},{96,0},{144,48},{1,97},{49,145},{97,1},{145,49},{2... | collective-permute-start | bytes 98312 | tf_op jit(solution)/shard_map/ppermute | solution.py:175
  33.1 5.3 %collective-permute-start.3 = (bf16[4,2,2048]{2,1,0:T(2,128)(2,1)S(1)}, bf16[4,2,2048]{2,1,0:T(2,128)(2,1)S(1)}, u32[]{:S(2)}, u32[]{:S(2)}) collective-permute-start(bf16[4,2,2048]{2,1,0:T(2,128)(2,1)S(1)} %get-tuple-element.21), channel_id=1, source_target_pairs={{0,144},{48,0},{96,48},{144,96},{1,145},{49,1},{97,49},{145,97},{2... | collective-permute-start | bytes 98312 | tf_op jit(solution)/shard_map/ppermute | solution.py:175
  45.6 32.2 %all-to-all-start.1 = ((bf16[24,8,2048]{2,1,0:T(8,128)(2,1)}), bf16[24,8,2048]{2,1,0:T(8,128)(2,1)S(1)}, u32[]{:S(2)}, u32[]{:S(2)}) async-start(bf16[24,8,2048]{2,1,0:T(8,128)(2,1)} %shard_map.99), calls=%async_computation.1 | async-start | bytes 1572864 | tf_op jit(solution)/shard_map/all_to_all | solution.py:231
  55.4 22.1 %collective-permute-start.4 = (bf16[4,2,2048]{2,1,0:T(2,128)(2,1)S(1)}, bf16[4,2,2048]{2,1,0:T(2,128)(2,1)S(1)}, u32[]{:S(2)}, u32[]{:S(2)}) collective-permute-start(bf16[4,2,2048]{2,1,0:T(2,128)(2,1)S(1)} %get-tuple-element.23.refs_1_), channel_id=1, source_target_pairs={{0,384},{192,576},{384,0},{576,192},{1,385},{193,577},{385,1},{577... | collective-permute-start | bytes 98312 | tf_op jit(solution)/shard_map/ppermute | solution.py:175
  67.4 10.2 %collective-permute-start.5 = (bf16[4,2,2048]{2,1,0:T(2,128)(2,1)S(1)}, bf16[4,2,2048]{2,1,0:T(2,128)(2,1)S(1)}, u32[]{:S(2)}, u32[]{:S(2)}) collective-permute-start(bf16[4,2,2048]{2,1,0:T(2,128)(2,1)S(1)} %get-tuple-element.24.refs_2_), channel_id=1, source_target_pairs={{0,192},{192,384},{384,576},{576,0},{1,193},{193,385},{385,577},{5... | collective-permute-start | bytes 98312 | tf_op jit(solution)/shard_map/ppermute | solution.py:175
  70.8 6.9 %collective-permute-start.6 = (bf16[4,2,2048]{2,1,0:T(2,128)(2,1)S(1)}, bf16[4,2,2048]{2,1,0:T(2,128)(2,1)S(1)}, u32[]{:S(2)}, u32[]{:S(2)}) collective-permute-start(bf16[4,2,2048]{2,1,0:T(2,128)(2,1)S(1)} %get-tuple-element.25.refs_3_), channel_id=1, source_target_pairs={{0,576},{192,0},{384,192},{576,384},{1,577},{193,1},{385,193},{577... | collective-permute-start | bytes 98312 | tf_op jit(solution)/shard_map/ppermute | solution.py:175
  77.8 7.8 %collective-permute-start.7 = (bf16[192,2048]{1,0:T(8,128)(2,1)S(1)}, bf16[192,2048]{1,0:T(8,128)(2,1)S(1)}, u32[]{:S(2)}, u32[]{:S(2)}) collective-permute-start(bf16[192,2048]{1,0:T(8,128)(2,1)S(1)} %shard_map.100.refs_1_), channel_id=1, source_target_pairs={{0,1},{1,0},{2,3},{3,2},{4,5},{5,4},{6,7},{7,6},{8,9},{9,8},{10,11... | collective-permute-start | bytes 2359304 | tf_op jit(solution)/shard_map/ppermute | solution.py:237

commit v11 on v10

--- a/solution.py
+++ b/solution.py
@@ -7,7 +7,7 @@
 
 GRP = ("zh", "x")
 TP = ("y", "zl", "core")
-RING = ("zl", "y")
+RING = ("y", "zl")
 SWAP = [(0, 1), (1, 0)]
 SIDE = 4
 CHIPS = 24
@@ -35,7 +35,7 @@
 
 
 def hidden_body(core_ref, tokens_ref, gate_ref, up_ref, down_ref, active_ref, hidden_ref, away_ref, *scratch):
-    tokens, weights, theirs_ref, mask_ref, sent_ref, sems, last_sems, out_sems = scratch
+    tokens, weights, theirs_ref, mask_ref, sems, last_sems = scratch
     depth, units = tokens_ref.shape[1] // CHUNKS, hidden_ref.shape[1]
     copies = []
     for i in range(CHUNKS):
@@ -67,15 +67,7 @@
     gate, up = both[:, :units], both[:, units:]
     hidden = (gate / (1 + jnp.exp(-gate)) * up * mask_ref[...].astype(f32)).astype(bf16)
     hidden_ref[...] = hidden
-    columns = width // STEPS
-    stores = []
-    for i in range(STEPS):
-        block = pl.ds(i * columns, columns)
-        sent_ref[:, block] = jnp.dot(hidden, theirs_ref[:, block], preferred_element_type=f32).astype(bf16)
-        stores.append(pltpu.make_async_copy(sent_ref.at[:, block], away_ref.at[:, block], out_sems.at[i]))
-        stores[-1].start()
-    for store in stores:
-        store.wait()
+    away_ref[...] = jnp.dot(hidden, theirs_ref[...], preferred_element_type=f32).astype(bf16)
 
 
 def sort_body(place_ref, dest_ref, lengths_ref, kv_ref, mark_ref, *out_refs):
@@ -183,19 +175,17 @@
     rows, width = tokens.shape[0], down_weight.shape[1] // 2
     hidden, away = call(
         hidden_body,
-        [jax.ShapeDtypeStruct(active.shape, bf16), pltpu.HBM((rows, width), bf16)],
+        [pltpu.VMEM(active.shape, bf16), pltpu.VMEM((rows, width), bf16)],
         [SMEM] + [ANY] * 5,
-        [VMEM, ANY],
+        [VMEM, VMEM],
         vmem=56,
         scratch_shapes=[
             pltpu.VMEM(tokens.shape, bf16),
             pltpu.VMEM((gate_weight.shape[0], 2 * gate_weight.shape[1]), bf16),
             pltpu.VMEM((active.shape[1], width), bf16),
             pltpu.VMEM(active.shape, jnp.int32),
-            pltpu.VMEM((rows, width), bf16),
             pltpu.SemaphoreType.DMA((3, CHUNKS)),
             pltpu.SemaphoreType.DMA((2,)),
-            pltpu.SemaphoreType.DMA((STEPS,)),
         ],
     )(core[None], tokens, gate_weight, up_weight, down_weight, active)
 

time: 87.1 us -> 86 us (0.987)
  starting transfers between devices: 60.5 us -> 57.2 us
  waiting for transfers between devices: 9.66 us -> 12.7 us
  Pallas kernels: 13.3 us -> 12 us
    all_to_all x1, starting transfers between devices: 9.86 us -> 7.14 us  [shards(): lax.all_to_all(spread, RING, split_axis=0, concat_axis=0, tiled=True)]
    all_to_all x1, waiting for transfers between devices: 5.42 us -> 7.43 us  [shards(): parts = lax.all_to_all(parts, RING, split_axis=0, concat_axis=0, tiled=True)]
    ppermute x1, starting transfers between devices: 5.68 us -> 3.91 us  [shards(): other = lax.ppermute(half, 'core', SWAP)]
    pallas_call x1, Pallas kernels: 6.44 us -> 5.07 us  [shards(): call(hidden_body, [pltpu.VMEM(active.shape, bf16), pltpu.VMEM((rows, widt...]
    ppermute x6, starting transfers between devices: 28.6 us -> 29.8 us  [shift(): return lax.ppermute(value, axis, [(i, (i + k) % SIDE) for i in range(SIDE)])]
    ppermute x6, waiting for transfers between devices: 4.23 us -> 5.29 us  [shift(): return lax.ppermute(value, axis, [(i, (i + k) % SIDE) for i in range(SIDE)])]
  transfers between devices with their start and end apart: 10 -> 10, of which waited for: 4 -> 3; matrix products, arithmetic and copies ran while one was open for 2% -> 2% of each run, Pallas kernels for 4% -> 5%
where the time goes in v11:
time: 86 us; the launch traced here: 84.8 us
  starting transfers between devices  57.2 us (67%)
  waiting for transfers between devices  12.7 us (15%)
  Pallas kernels  12 us (14%)
  matrix products  1.99 us (2%)
  between operations  0.87 us (1%)
    ppermute x6, starting transfers between devices, shift(): return lax.ppermute(value, axis, [(i, (i + k) % SIDE) for i in range(SIDE)])  29.8 us
    ppermute x1, starting transfers between devices, shards(): arrived = lax.ppermute(away, 'core', SWAP)  12.4 us
    all_to_all x1, waiting for transfers between devices, shards(): parts = lax.all_to_all(parts, RING, split_axis=0, concat_axis=0, tiled=True)  7.43 us
    all_to_all x1, starting transfers between devices, shards(): lax.all_to_all(spread, RING, split_axis=0, concat_axis=0, tiled=True)  7.14 us
    ppermute x6, waiting for transfers between devices, shift(): return lax.ppermute(value, axis, [(i, (i + k) % SIDE) for i in range(SIDE)])  5.29 us
    pallas_call x1, Pallas kernels, shards(): call(hidden_body, [pltpu.VMEM(active.shape, bf16), pltpu.VMEM((rows, widt...  5.07 us
    all_to_all x1, starting transfers between devices, shards(): parts = lax.all_to_all(parts, RING, split_axis=0, concat_axis=0, tiled=True)  3.91 us
    ppermute x1, starting transfers between devices, shards(): other = lax.ppermute(half, 'core', SWAP)  3.91 us
  transfers between devices with their start and end apart: 10, of which 3 were waited for; matrix products, arithmetic and copies ran while one was open for 2% of the time, Pallas kernels for 5%

profile of v11, /device:TPU:1, one launch (start us, length us, event | category | flops | bytes accessed | tf_op | source)
XLA Modules:
  0.0 84.8 jit_solution(13737430964831283885)
XLA Ops:
  0.6 5.1 %shard_map.95 = (bf16[192,384]{1,0:T(8,128)(2,1)S(1)}, bf16[192,2048]{1,0:T(8,128)(2,1)S(1)}) custom-call(s32[1]{0:T(128)} %bitcast.core_ref.refs_0_, bf16[192,4096]{1,0:T(8,128)(2,1)} %tokens_ref.1, bf16[4096,384]{1,0:T(8,128)(2,1)} %gate_ref.1, bf16[4096,384]{1,0:T(8,128)(2,1)} %up_ref.1, bf16[384,4096]{1,0:T(8,128)(2,1)} %down_ref.1, s32[192,384]{1,0:T(8,128)} %active_ref.1), custom_call_target="tpu_custom_call" | custom-call | flops 1000000 | bytes 1000000 | tf_op jit(solution)/shard_map/pallas_call | solution.py:176
  5.7 12.4 %collective-permute-start = (bf16[192,2048]{1,0:T(8,128)(2,1)S(1)}, bf16[192,2048]{1,0:T(8,128)(2,1)S(1)}, u32[]{:S(2)}, u32[]{:S(2)}) collective-permute-start(bf16[192,2048]{1,0:T(8,128)(2,1)S(1)} %get-tuple-element.15), channel_id=1, source_target_pairs={{0,1},{1,0},{2,3},{3,2},{4,5},{5,4},{6,7},{7,6},{8,9},{9,8},{10,11... | collective-permute-start | bytes 2359304 | tf_op jit(solution)/shard_map/ppermute | solution.py:193
  18.1 2.0 %fusion.own_ref = f32[192,2048]{1,0:T(8,128)S(1)} fusion(bf16[192,384]{1,0:T(8,128)(2,1)S(1)} %get-tuple-element.14, bf16[384,4096]{1,0:T(8,128)(2,1)} %down_ref.1, s32[]{:T(128)S(6)} %select_n.3), kind=kOutput, calls=%fused_computation | convolution fusion | flops 301989888 | bytes 3293188 | tf_op jit(solution)/shard_map/dot_general | solution.py:194
  20.1 0.0 copy-start
  20.1 0.0 copy-start.1
  20.2 0.0 copy-start.2
  20.2 0.0 collective-permute-done.arrived_ref
  20.2 1.0 %shard_map.96 = (bf16[192,2048]{1,0:T(8,128)(2,1)}, f32[8,128]{1,0:T(8,128)S(1)}) custom-call(f32[192,2048]{1,0:T(8,128)S(1)} %fusion.own_ref, bf16[192,2048]{1,0:T(8,128)(2,1)S(1)} %collective-permute-done.arrived_ref), custom_call_target="tpu_custom_call" | custom-call | flops 1000000 | bytes 1000000 | tf_op jit(solution)/shard_map/pallas_call | solution.py:195
  21.1 3.9 %all-to-all-start = ((bf16[24,8,2048]{2,1,0:T(8,128)(2,1)}), bf16[24,8,2048]{2,1,0:T(8,128)(2,1)S(1)}, u32[]{:S(2)}, u32[]{:S(2)}) async-start(bf16[24,8,2048]{2,1,0:T(8,128)(2,1)} %bitcast.9), calls=%async_computation | async-start | bytes 1572864 | tf_op jit(solution)/shard_map/all_to_all | solution.py:204
  25.1 0.1 pad_add_fusion.place_ref
  25.2 1.2 %shard_map.97 = (bf16[4,2,2048]{2,1,0:T(2,128)(2,1)S(1)}, bf16[4,2,2048]{2,1,0:T(2,128)(2,1)S(1)}, bf16[4,2,2048]{2,1,0:T(2,128)(2,1)S(1)}, bf16[4,2,2048]{2,1,0:T(2,128)(2,1)S(1)}) custom-call(s32[4]{0:T(128)S(1)} %pad_add_fusion.place_ref, s32[16,16]{1,0:T(8,128)S(1)} %copy-done.1, s32[16]{0:T(128)S(1)} %copy-done.2, bf16[16,2,2048]{2,1,0:T(2,128)(2,1)S(1)} %copy-done, ...), custom_call_target="tpu_custom_call" | custom-call | flops 1000000 | bytes 1000000 | tf_op jit(solution)/shard_map/pallas_call | solution.py:207
  26.4 1.9 %collective-permute-start.1 = (bf16[4,2,2048]{2,1,0:T(2,128)(2,1)S(1)}, bf16[4,2,2048]{2,1,0:T(2,128)(2,1)S(1)}, u32[]{:S(2)}, u32[]{:S(2)}) collective-permute-start(bf16[4,2,2048]{2,1,0:T(2,128)(2,1)S(1)} %get-tuple-element.19), channel_id=1, source_target_pairs={{0,48},{48,96},{96,144},{144,0},{1,49},{49,97},{97,145},{145,1},{2... | collective-permute-start | bytes 98312 | tf_op jit(solution)/shard_map/ppermute | solution.py:167
  28.3 3.3 %collective-permute-start.2 = (bf16[4,2,2048]{2,1,0:T(2,128)(2,1)S(1)}, bf16[4,2,2048]{2,1,0:T(2,128)(2,1)S(1)}, u32[]{:S(2)}, u32[]{:S(2)}) collective-permute-start(bf16[4,2,2048]{2,1,0:T(2,128)(2,1)S(1)} %get-tuple-element.20), channel_id=1, source_target_pairs={{0,96},{48,144},{96,0},{144,48},{1,97},{49,145},{97,1},{145,49},{2... | collective-permute-start | bytes 98312 | tf_op jit(solution)/shard_map/ppermute | solution.py:167
  31.6 3.2 %collective-permute-start.3 = (bf16[4,2,2048]{2,1,0:T(2,128)(2,1)S(1)}, bf16[4,2,2048]{2,1,0:T(2,128)(2,1)S(1)}, u32[]{:S(2)}, u32[]{:S(2)}) collective-permute-start(bf16[4,2,2048]{2,1,0:T(2,128)(2,1)S(1)} %get-tuple-element.21), channel_id=1, source_target_pairs={{0,144},{48,0},{96,48},{144,96},{1,145},{49,1},{97,49},{145,97},{2... | collective-permute-start | bytes 98312 | tf_op jit(solution)/shard_map/ppermute | solution.py:167
  34.8 0.0 collective-permute-done.1.refs_1_
  34.8 0.0 collective-permute-done.2.refs_2_
  34.8 2.1 %collective-permute-done.3.refs_3_ = bf16[4,2,2048]{2,1,0:T(2,128)(2,1)S(1)} collective-permute-done((bf16[4,2,2048]{2,1,0:T(2,128)(2,1)S(1)}, bf16[4,2,2048]{2,1,0:T(2,128)(2,1)S(1)}, u32[]{:S(2)}, u32[]{:S(2)}) %collective-permute-start.3) | collective-permute-done | bytes 32800 | tf_op jit(solution)/shard_map/ppermute | solution.py:167
  36.9 0.6 shard_map.98
  37.5 7.4 %all-to-all-done.parts_ref = bf16[24,8,2048]{2,1,0:T(8,128)(2,1)S(1)} async-done(((bf16[24,8,2048]{2,1,0:T(8,128)(2,1)}), bf16[24,8,2048]{2,1,0:T(8,128)(2,1)S(1)}, u32[]{:S(2)}, u32[]{:S(2)}) %all-to-all-start) | async-done | bytes 786464 | tf_op jit(solution)/shard_map/all_to_all | solution.py:204
  44.9 1.2 %shard_map.99 = bf16[24,8,2048]{2,1,0:T(8,128)(2,1)} custom-call(bf16[24,8,2048]{2,1,0:T(8,128)(2,1)S(1)} %all-to-all-done.parts_ref, bf16[4,2,2048]{2,1,0:T(2,128)(2,1)S(1)} %get-tuple-element.22.refs_0_, bf16[4,2,2048]{2,1,0:T(2,128)(2,1)S(1)} %get-tuple-element.23.refs_1_, bf16[4,2,2048]{2,1,0:T(2,128)(2,1)S(1)} %get-tuple-element.24.refs_2_, ...), custom_call_target="tpu_custom_call" | custom-call | flops 1000000 | bytes 1000000 | tf_op jit(solution)/shard_map/pallas_call | solution.py:213
  46.1 7.1 %all-to-all-start.1 = ((bf16[24,8,2048]{2,1,0:T(8,128)(2,1)}), bf16[24,8,2048]{2,1,0:T(8,128)(2,1)S(1)}, u32[]{:S(2)}, u32[]{:S(2)}) async-start(bf16[24,8,2048]{2,1,0:T(8,128)(2,1)} %shard_map.99), calls=%async_computation.1 | async-start | bytes 1572864 | tf_op jit(solution)/shard_map/all_to_all | solution.py:221
  53.3 13.1 %collective-permute-start.4 = (bf16[4,2,2048]{2,1,0:T(2,128)(2,1)S(1)}, bf16[4,2,2048]{2,1,0:T(2,128)(2,1)S(1)}, u32[]{:S(2)}, u32[]{:S(2)}) collective-permute-start(bf16[4,2,2048]{2,1,0:T(2,128)(2,1)S(1)} %get-tuple-element.23.refs_1_), channel_id=1, source_target_pairs={{0,384},{192,576},{384,0},{576,192},{1,385},{193,577},{385,1},{577... | collective-permute-start | bytes 98312 | tf_op jit(solution)/shard_map/ppermute | solution.py:167
  66.4 2.7 %collective-permute-start.5 = (bf16[4,2,2048]{2,1,0:T(2,128)(2,1)S(1)}, bf16[4,2,2048]{2,1,0:T(2,128)(2,1)S(1)}, u32[]{:S(2)}, u32[]{:S(2)}) collective-permute-start(bf16[4,2,2048]{2,1,0:T(2,128)(2,1)S(1)} %get-tuple-element.24.refs_2_), channel_id=1, source_target_pairs={{0,192},{192,384},{384,576},{576,0},{1,193},{193,385},{385,577},{5... | collective-permute-start | bytes 98312 | tf_op jit(solution)/shard_map/ppermute | solution.py:167
  69.1 5.6 %collective-permute-start.6 = (bf16[4,2,2048]{2,1,0:T(2,128)(2,1)S(1)}, bf16[4,2,2048]{2,1,0:T(2,128)(2,1)S(1)}, u32[]{:S(2)}, u32[]{:S(2)}) collective-permute-start(bf16[4,2,2048]{2,1,0:T(2,128)(2,1)S(1)} %get-tuple-element.25.refs_3_), channel_id=1, source_target_pairs={{0,576},{192,0},{384,192},{576,384},{1,577},{193,1},{385,193},{577... | collective-permute-start | bytes 98312 | tf_op jit(solution)/shard_map/ppermute | solution.py:167
  74.7 3.1 %collective-permute-done.4.refs_1_ = bf16[4,2,2048]{2,1,0:T(2,128)(2,1)S(1)} collective-permute-done((bf16[4,2,2048]{2,1,0:T(2,128)(2,1)S(1)}, bf16[4,2,2048]{2,1,0:T(2,128)(2,1)S(1)}, u32[]{:S(2)}, u32[]{:S(2)}) %collective-permute-start.4) | collective-permute-done | bytes 32800 | tf_op jit(solution)/shard_map/ppermute | solution.py:167
  77.9 0.0 collective-permute-done.6.refs_3_
  77.9 0.0 all-to-all-done.1
  77.9 3.9 %collective-permute-start.7 = (bf16[192,2048]{1,0:T(8,128)(2,1)S(1)}, bf16[192,2048]{1,0:T(8,128)(2,1)S(1)}, u32[]{:S(2)}, u32[]{:S(2)}) collective-permute-start(bf16[192,2048]{1,0:T(8,128)(2,1)S(1)} %shard_map.100.refs_1_), channel_id=1, source_target_pairs={{0,1},{1,0},{2,3},{3,2},{4,5},{5,4},{6,7},{7,6},{8,9},{9,8},{10,11... | collective-permute-start | bytes 2359304 | tf_op jit(solution)/shard_map/ppermute | solution.py:227
  81.8 1.2 %shard_map.103 = bf16[16,2,2048]{2,1,0:T(2,128)(2,1)} custom-call(s32[4]{0:T(128)S(1)} %pad_add_fusion.place_ref, bf16[4,2,2048]{2,1,0:T(2,128)(2,1)S(1)} %get-tuple-element.22.refs_0_, bf16[4,2,2048]{2,1,0:T(2,128)(2,1)S(1)} %collective-permute-done.4.refs_1_, bf16[4,2,2048]{2,1,0:T(2,128)(2,1)S(1)} %collective-permute-done.5.refs_2_, ...), custom_call_target="tpu_custom_call" | custom-call | flops 1000000 | bytes 1000000 | tf_op jit(solution)/shard_map/pallas_call | solution.py:224
  83.0 0.9 %shard_map.101.refs_2_ = bf16[192,4096]{1,0:T(8,128)(2,1)} custom-call(s32[1]{0:T(128)} %bitcast.core_ref.refs_0_, bf16[192,2048]{1,0:T(8,128)(2,1)S(1)} %shard_map.100.refs_1_), custom_call_target="tpu_custom_call" | custom-call | flops 1000000 | bytes 1000000 | tf_op jit(solution)/shard_map/pallas_call | solution.py:146
  83.9 0.0 collective-permute-done.7.refs_1_
  83.9 0.9 %shard_map.102 = bf16[192,4096]{1,0:T(8,128)(2,1)} custom-call(s32[1]{0:T(128)} %bitcast.core_ref.refs_0_, bf16[192,2048]{1,0:T(8,128)(2,1)S(1)} %collective-permute-done.7.refs_1_, bf16[192,4096]{1,0:T(8,128)(2,1)} %shard_map.101.refs_2_), custom_call_target="tpu_custom_call", output_to_operand_aliasing={{}: (2, {})} | custom-call | flops 1000000 | bytes 1000000 | tf_op jit(solution)/shard_map/pallas_call | solution.py:146
  (5 shorter events, 0.0 us)
Async XLA Ops:
  5.7 14.5 %collective-permute-start = (bf16[192,2048]{1,0:T(8,128)(2,1)S(1)}, bf16[192,2048]{1,0:T(8,128)(2,1)S(1)}, u32[]{:S(2)}, u32[]{:S(2)}) collective-permute-start(bf16[192,2048]{1,0:T(8,128)(2,1)S(1)} %get-tuple-element.15), channel_id=1, source_target_pairs={{0,1},{1,0},{2,3},{3,2},{4,5},{5,4},{6,7},{7,6},{8,9},{9,8},{10,11... | collective-permute-start | bytes 2359304 | tf_op jit(solution)/shard_map/ppermute | solution.py:193
  20.1 5.0 %copy-start = (bf16[16,2,2048]{2,1,0:T(2,128)(2,1)S(1)}, bf16[16,2,2048]{2,1,0:T(2,128)(2,1)}, u32[]{:S(2)}) copy-start(bf16[16,2,2048]{2,1,0:T(2,128)(2,1)} %kv_ref.1) | copy-start | bytes 393220
  20.1 5.0 %copy-start.1 = (s32[16,16]{1,0:T(8,128)S(1)}, s32[16,16]{1,0:T(8,128)}, u32[]{:S(2)}) copy-start(s32[16,16]{1,0:T(8,128)} %dest_ref.1) | copy-start | bytes 3076
  20.2 5.0 %copy-start.2 = (s32[16]{0:T(128)S(1)}, s32[16]{0:T(128)}, u32[]{:S(2)}) copy-start(s32[16]{0:T(128)} %lengths_ref.1) | copy-start | bytes 196
  21.1 23.8 %all-to-all-start = ((bf16[24,8,2048]{2,1,0:T(8,128)(2,1)}), bf16[24,8,2048]{2,1,0:T(8,128)(2,1)S(1)}, u32[]{:S(2)}, u32[]{:S(2)}) async-start(bf16[24,8,2048]{2,1,0:T(8,128)(2,1)} %bitcast.9), calls=%async_computation | async-start | bytes 1572864 | tf_op jit(solution)/shard_map/all_to_all | solution.py:204
  26.4 8.4 %collective-permute-start.1 = (bf16[4,2,2048]{2,1,0:T(2,128)(2,1)S(1)}, bf16[4,2,2048]{2,1,0:T(2,128)(2,1)S(1)}, u32[]{:S(2)}, u32[]{:S(2)}) collective-permute-start(bf16[4,2,2048]{2,1,0:T(2,128)(2,1)S(1)} %get-tuple-element.19), channel_id=1, source_target_pairs={{0,48},{48,96},{96,144},{144,0},{1,49},{49,97},{97,145},{145,1},{2... | collective-permute-start | bytes 98312 | tf_op jit(solution)/shard_map/ppermute | solution.py:167
  28.3 6.5 %collective-permute-start.2 = (bf16[4,2,2048]{2,1,0:T(2,128)(2,1)S(1)}, bf16[4,2,2048]{2,1,0:T(2,128)(2,1)S(1)}, u32[]{:S(2)}, u32[]{:S(2)}) collective-permute-start(bf16[4,2,2048]{2,1,0:T(2,128)(2,1)S(1)} %get-tuple-element.20), channel_id=1, source_target_pairs={{0,96},{48,144},{96,0},{144,48},{1,97},{49,145},{97,1},{145,49},{2... | collective-permute-start | bytes 98312 | tf_op jit(solution)/shard_map/ppermute | solution.py:167
  31.6 5.3 %collective-permute-start.3 = (bf16[4,2,2048]{2,1,0:T(2,128)(2,1)S(1)}, bf16[4,2,2048]{2,1,0:T(2,128)(2,1)S(1)}, u32[]{:S(2)}, u32[]{:S(2)}) collective-permute-start(bf16[4,2,2048]{2,1,0:T(2,128)(2,1)S(1)} %get-tuple-element.21), channel_id=1, source_target_pairs={{0,144},{48,0},{96,48},{144,96},{1,145},{49,1},{97,49},{145,97},{2... | collective-permute-start | bytes 98312 | tf_op jit(solution)/shard_map/ppermute | solution.py:167
  46.1 31.7 %all-to-all-start.1 = ((bf16[24,8,2048]{2,1,0:T(8,128)(2,1)}), bf16[24,8,2048]{2,1,0:T(8,128)(2,1)S(1)}, u32[]{:S(2)}, u32[]{:S(2)}) async-start(bf16[24,8,2048]{2,1,0:T(8,128)(2,1)} %shard_map.99), calls=%async_computation.1 | async-start | bytes 1572864 | tf_op jit(solution)/shard_map/all_to_all | solution.py:221
  53.3 24.6 %collective-permute-start.4 = (bf16[4,2,2048]{2,1,0:T(2,128)(2,1)S(1)}, bf16[4,2,2048]{2,1,0:T(2,128)(2,1)S(1)}, u32[]{:S(2)}, u32[]{:S(2)}) collective-permute-start(bf16[4,2,2048]{2,1,0:T(2,128)(2,1)S(1)} %get-tuple-element.23.refs_1_), channel_id=1, source_target_pairs={{0,384},{192,576},{384,0},{576,192},{1,385},{193,577},{385,1},{577... | collective-permute-start | bytes 98312 | tf_op jit(solution)/shard_map/ppermute | solution.py:167
  66.4 11.5 %collective-permute-start.5 = (bf16[4,2,2048]{2,1,0:T(2,128)(2,1)S(1)}, bf16[4,2,2048]{2,1,0:T(2,128)(2,1)S(1)}, u32[]{:S(2)}, u32[]{:S(2)}) collective-permute-start(bf16[4,2,2048]{2,1,0:T(2,128)(2,1)S(1)} %get-tuple-element.24.refs_2_), channel_id=1, source_target_pairs={{0,192},{192,384},{384,576},{576,0},{1,193},{193,385},{385,577},{5... | collective-permute-start | bytes 98312 | tf_op jit(solution)/shard_map/ppermute | solution.py:167
  69.1 8.8 %collective-permute-start.6 = (bf16[4,2,2048]{2,1,0:T(2,128)(2,1)S(1)}, bf16[4,2,2048]{2,1,0:T(2,128)(2,1)S(1)}, u32[]{:S(2)}, u32[]{:S(2)}) collective-permute-start(bf16[4,2,2048]{2,1,0:T(2,128)(2,1)S(1)} %get-tuple-element.25.refs_3_), channel_id=1, source_target_pairs={{0,576},{192,0},{384,192},{576,384},{1,577},{193,1},{385,193},{577... | collective-permute-start | bytes 98312 | tf_op jit(solution)/shard_map/ppermute | solution.py:167
  77.9 6.0 %collective-permute-start.7 = (bf16[192,2048]{1,0:T(8,128)(2,1)S(1)}, bf16[192,2048]{1,0:T(8,128)(2,1)S(1)}, u32[]{:S(2)}, u32[]{:S(2)}) collective-permute-start(bf16[192,2048]{1,0:T(8,128)(2,1)S(1)} %shard_map.100.refs_1_), channel_id=1, source_target_pairs={{0,1},{1,0},{2,3},{3,2},{4,5},{5,4},{6,7},{7,6},{8,9},{9,8},{10,11... | collective-permute-start | bytes 2359304 | tf_op jit(solution)/shard_map/ppermute | solution.py:227

commit v12 on v11

--- a/solution.py
+++ b/solution.py
@@ -71,36 +71,36 @@
 
 
 def sort_body(place_ref, dest_ref, lengths_ref, kv_ref, mark_ref, *out_refs):
-    x, mine, first = place_ref[0], place_ref[1], place_ref[2]
+    mine, first, zh = place_ref[1], place_ref[2], place_ref[3]
     row = lax.broadcasted_iota(jnp.int32, kv_ref.shape[1:], 0) + first
     for r in range(kv_ref.shape[0]):
         d = dest_ref[mine, r]
         value = kv_ref[r]
         value = jnp.where(row < lengths_ref[r], value, jnp.zeros_like(value))
-        step = lax.rem(lax.rem(d, SIDE) - x + SIDE, SIDE)
-        for k in range(SIDE):
-
-            @pl.when(step == k)
+        step = lax.rem(lax.div(d, SIDE) - zh + SIDE, SIDE)
+        for out_ref, j in zip(out_refs, ORDER):
+
+            @pl.when(step == j)
             def _():
-                out_refs[k][lax.div(d, SIDE)] = value
+                out_ref[lax.rem(d, SIDE)] = value
 
 
 def turn_body(place_ref, *refs):
     x, zh = place_ref[0], place_ref[3]
     in_refs, out_refs = refs[:SIDE], refs[SIDE:]
-    for k in range(SIDE):
-        source = lax.rem(x - k + SIDE, SIDE)
-        for out_ref, j in zip(out_refs, ORDER):
-            out_ref[source] = in_refs[k][lax.rem(zh + j, SIDE)]
-
-
-def lay_body(place_ref, *refs):
-    zh = place_ref[3]
-    in_refs, out_ref = refs[:SIDE], refs[-1]
     for in_ref, j in zip(in_refs, ORDER):
         source = lax.rem(zh - j + SIDE, SIDE)
-        for k in range(SIDE):
-            out_ref[source * SIDE + k] = in_ref[k]
+        for k, out_ref in enumerate(out_refs):
+            out_ref[source] = in_ref[lax.rem(x + k, SIDE)]
+
+
+def lay_body(place_ref, *refs):
+    x = place_ref[0]
+    in_refs, out_ref = refs[:SIDE], refs[-1]
+    for k, in_ref in enumerate(in_refs):
+        column = lax.rem(x - k + SIDE, SIDE)
+        for source in range(SIDE):
+            out_ref[source * SIDE + column] = in_ref[source]
 
 
 def add_body(own_ref, arrived_ref, out_ref, mark_ref, total_ref, sems):
@@ -207,7 +207,7 @@
     bundles = call(sort_body, [slots] * SIDE, [SMEM] * 3 + [VMEM] * 2, [VMEM] * SIDE)(
         place, dest, lengths, kv_blocks, mark
     )
-    bundles = [bundles[0]] + [shift(bundles[k], "x", k) for k in range(1, SIDE)]
+    bundles = [bundles[0]] + [shift(b, "zh", j) for b, j in zip(bundles[1:], ORDER[1:])]
     bundles = call(turn_body, [slots] * SIDE, [SMEM] + [VMEM] * SIDE, [VMEM] * SIDE)(place, *bundles)
 
     spread = call(
@@ -220,7 +220,7 @@
 
     half = lax.all_to_all(spread, RING, split_axis=0, concat_axis=0, tiled=True).reshape(rows, width)
 
-    bundles = [bundles[0]] + [shift(b, "zh", j) for b, j in zip(bundles[1:], ORDER[1:])]
+    bundles = [bundles[0]] + [shift(bundles[k], "x", k) for k in range(1, SIDE)]
     cache = call(lay_body, jax.ShapeDtypeStruct(kv_blocks.shape, bf16), [SMEM] + [VMEM] * SIDE, VMEM)(place, *bundles)
 
     half = after(half, *bundles[1:])

time: 86 us -> 88.1 us (1.024)
  starting transfers between devices: 57.2 us -> 63.7 us
  waiting for transfers between devices: 12.7 us -> 8.92 us
    all_to_all x1, waiting for transfers between devices: 7.43 us -> 0.01 us  [shards(): parts = lax.all_to_all(parts, RING, split_axis=0, concat_axis=0, tiled=True)]
    all_to_all x1, waiting for transfers between devices: 0.01 us -> 4.28 us  [shards(): lax.all_to_all(spread, RING, split_axis=0, concat_axis=0, tiled=True)]
    ppermute x1, starting transfers between devices: 3.91 us -> 7.47 us  [shards(): other = lax.ppermute(half, 'core', SWAP)]
    all_to_all x1, starting transfers between devices: 7.14 us -> 9.6 us  [shards(): lax.all_to_all(spread, RING, split_axis=0, concat_axis=0, tiled=True)]
  transfers between devices with their start and end apart: 10 -> 10, of which waited for: 3 -> 4; matrix products, arithmetic and copies ran while one was open for 2% -> 2% of each run, Pallas kernels for 5% -> 4%
where the time goes in v12:
time: 88.1 us; the launch traced here: 87.5 us
  starting transfers between devices  63.7 us (72%)
  Pallas kernels  12 us (14%)
  waiting for transfers between devices  8.92 us (10%)
  matrix products  1.99 us (2%)
    ppermute x6, starting transfers between devices, shift(): return lax.ppermute(value, axis, [(i, (i + k) % SIDE) for i in range(SIDE)])  30.3 us
    ppermute x1, starting transfers between devices, shards(): arrived = lax.ppermute(away, 'core', SWAP)  12.4 us
    all_to_all x1, starting transfers between devices, shards(): lax.all_to_all(spread, RING, split_axis=0, concat_axis=0, tiled=True)  9.6 us
    ppermute x1, starting transfers between devices, shards(): other = lax.ppermute(half, 'core', SWAP)  7.47 us
    pallas_call x1, Pallas kernels, shards(): call(hidden_body, [pltpu.VMEM(active.shape, bf16), pltpu.VMEM((rows, widt...  5.07 us
    ppermute x6, waiting for transfers between devices, shift(): return lax.ppermute(value, axis, [(i, (i + k) % SIDE) for i in range(SIDE)])  4.64 us
    all_to_all x1, waiting for transfers between devices, shards(): lax.all_to_all(spread, RING, split_axis=0, concat_axis=0, tiled=True)  4.28 us
    all_to_all x1, starting transfers between devices, shards(): parts = lax.all_to_all(parts, RING, split_axis=0, concat_axis=0, tiled=True)  3.91 us
  transfers between devices with their start and end apart: 10, of which 4 were waited for; matrix products, arithmetic and copies ran while one was open for 2% of the time, Pallas kernels for 4%

profile of v12, /device:TPU:1, one launch (start us, length us, event | category | flops | bytes accessed | tf_op | source)
XLA Modules:
  0.0 87.5 jit_solution(14916684448740747898)
XLA Ops:
  0.6 5.1 %shard_map.95 = (bf16[192,384]{1,0:T(8,128)(2,1)S(1)}, bf16[192,2048]{1,0:T(8,128)(2,1)S(1)}) custom-call(s32[1]{0:T(128)} %bitcast.core_ref.refs_0_, bf16[192,4096]{1,0:T(8,128)(2,1)} %tokens_ref.1, bf16[4096,384]{1,0:T(8,128)(2,1)} %gate_ref.1, bf16[4096,384]{1,0:T(8,128)(2,1)} %up_ref.1, bf16[384,4096]{1,0:T(8,128)(2,1)} %down_ref.1, s32[192,384]{1,0:T(8,128)} %active_ref.1), custom_call_target="tpu_custom_call" | custom-call | flops 1000000 | bytes 1000000 | tf_op jit(solution)/shard_map/pallas_call | solution.py:176
  5.7 12.4 %collective-permute-start = (bf16[192,2048]{1,0:T(8,128)(2,1)S(1)}, bf16[192,2048]{1,0:T(8,128)(2,1)S(1)}, u32[]{:S(2)}, u32[]{:S(2)}) collective-permute-start(bf16[192,2048]{1,0:T(8,128)(2,1)S(1)} %get-tuple-element.15), channel_id=1, source_target_pairs={{0,1},{1,0},{2,3},{3,2},{4,5},{5,4},{6,7},{7,6},{8,9},{9,8},{10,11... | collective-permute-start | bytes 2359304 | tf_op jit(solution)/shard_map/ppermute | solution.py:193
  18.1 2.0 %fusion.own_ref = f32[192,2048]{1,0:T(8,128)S(1)} fusion(bf16[192,384]{1,0:T(8,128)(2,1)S(1)} %get-tuple-element.14, bf16[384,4096]{1,0:T(8,128)(2,1)} %down_ref.1, s32[]{:T(128)S(6)} %select_n.3), kind=kOutput, calls=%fused_computation | convolution fusion | flops 301989888 | bytes 3293188 | tf_op jit(solution)/shard_map/dot_general | solution.py:194
  20.1 0.0 copy-start
  20.1 0.0 copy-start.1
  20.2 0.0 copy-start.2
  20.2 0.0 collective-permute-done.arrived_ref
  20.2 1.0 %shard_map.96 = (bf16[192,2048]{1,0:T(8,128)(2,1)}, f32[8,128]{1,0:T(8,128)S(1)}) custom-call(f32[192,2048]{1,0:T(8,128)S(1)} %fusion.own_ref, bf16[192,2048]{1,0:T(8,128)(2,1)S(1)} %collective-permute-done.arrived_ref), custom_call_target="tpu_custom_call" | custom-call | flops 1000000 | bytes 1000000 | tf_op jit(solution)/shard_map/pallas_call | solution.py:195
  21.1 3.9 %all-to-all-start = ((bf16[24,8,2048]{2,1,0:T(8,128)(2,1)}), bf16[24,8,2048]{2,1,0:T(8,128)(2,1)S(1)}, u32[]{:S(2)}, u32[]{:S(2)}) async-start(bf16[24,8,2048]{2,1,0:T(8,128)(2,1)} %bitcast.9), calls=%async_computation | async-start | bytes 1572864 | tf_op jit(solution)/shard_map/all_to_all | solution.py:204
  25.1 0.1 pad_add_fusion.place_ref
  25.2 1.2 %shard_map.97 = (bf16[4,2,2048]{2,1,0:T(2,128)(2,1)S(1)}, bf16[4,2,2048]{2,1,0:T(2,128)(2,1)S(1)}, bf16[4,2,2048]{2,1,0:T(2,128)(2,1)S(1)}, bf16[4,2,2048]{2,1,0:T(2,128)(2,1)S(1)}) custom-call(s32[4]{0:T(128)S(1)} %pad_add_fusion.place_ref, s32[16,16]{1,0:T(8,128)S(1)} %copy-done.1, s32[16]{0:T(128)S(1)} %copy-done.2, bf16[16,2,2048]{2,1,0:T(2,128)(2,1)S(1)} %copy-done, ...), custom_call_target="tpu_custom_call" | custom-call | flops 1000000 | bytes 1000000 | tf_op jit(solution)/shard_map/pallas_call | solution.py:207
  26.4 11.4 %collective-permute-start.1 = (bf16[4,2,2048]{2,1,0:T(2,128)(2,1)S(1)}, bf16[4,2,2048]{2,1,0:T(2,128)(2,1)S(1)}, u32[]{:S(2)}, u32[]{:S(2)}) collective-permute-start(bf16[4,2,2048]{2,1,0:T(2,128)(2,1)S(1)} %get-tuple-element.19), channel_id=1, source_target_pairs={{0,384},{192,576},{384,0},{576,192},{1,385},{193,577},{385,1},{577... | collective-permute-start | bytes 98312 | tf_op jit(solution)/shard_map/ppermute | solution.py:167
  37.8 4.3 %collective-permute-start.2 = (bf16[4,2,2048]{2,1,0:T(2,128)(2,1)S(1)}, bf16[4,2,2048]{2,1,0:T(2,128)(2,1)S(1)}, u32[]{:S(2)}, u32[]{:S(2)}) collective-permute-start(bf16[4,2,2048]{2,1,0:T(2,128)(2,1)S(1)} %get-tuple-element.20), channel_id=1, source_target_pairs={{0,192},{192,384},{384,576},{576,0},{1,193},{193,385},{385,577},{5... | collective-permute-start | bytes 98312 | tf_op jit(solution)/shard_map/ppermute | solution.py:167
  42.1 4.0 %collective-permute-start.3 = (bf16[4,2,2048]{2,1,0:T(2,128)(2,1)S(1)}, bf16[4,2,2048]{2,1,0:T(2,128)(2,1)S(1)}, u32[]{:S(2)}, u32[]{:S(2)}) collective-permute-start(bf16[4,2,2048]{2,1,0:T(2,128)(2,1)S(1)} %get-tuple-element.21), channel_id=1, source_target_pairs={{0,576},{192,0},{384,192},{576,384},{1,577},{193,1},{385,193},{577... | collective-permute-start | bytes 98312 | tf_op jit(solution)/shard_map/ppermute | solution.py:167
  46.1 1.6 %collective-permute-done.1.refs_1_ = bf16[4,2,2048]{2,1,0:T(2,128)(2,1)S(1)} collective-permute-done((bf16[4,2,2048]{2,1,0:T(2,128)(2,1)S(1)}, bf16[4,2,2048]{2,1,0:T(2,128)(2,1)S(1)}, u32[]{:S(2)}, u32[]{:S(2)}) %collective-permute-start.1) | collective-permute-done | bytes 32800 | tf_op jit(solution)/shard_map/ppermute | solution.py:167
  47.7 0.0 collective-permute-done.2.refs_2_
  47.8 1.1 %collective-permute-done.3.refs_3_ = bf16[4,2,2048]{2,1,0:T(2,128)(2,1)S(1)} collective-permute-done((bf16[4,2,2048]{2,1,0:T(2,128)(2,1)S(1)}, bf16[4,2,2048]{2,1,0:T(2,128)(2,1)S(1)}, u32[]{:S(2)}, u32[]{:S(2)}) %collective-permute-start.3) | collective-permute-done | bytes 32800 | tf_op jit(solution)/shard_map/ppermute | solution.py:167
  48.9 0.6 shard_map.98
  49.5 0.0 all-to-all-done.parts_ref
  49.5 1.2 %shard_map.99 = bf16[24,8,2048]{2,1,0:T(8,128)(2,1)} custom-call(bf16[24,8,2048]{2,1,0:T(8,128)(2,1)S(1)} %all-to-all-done.parts_ref, bf16[4,2,2048]{2,1,0:T(2,128)(2,1)S(1)} %get-tuple-element.22.refs_0_, bf16[4,2,2048]{2,1,0:T(2,128)(2,1)S(1)} %get-tuple-element.23.refs_1_, bf16[4,2,2048]{2,1,0:T(2,128)(2,1)S(1)} %get-tuple-element.24.refs_2_, ...), custom_call_target="tpu_custom_call" | custom-call | flops 1000000 | bytes 1000000 | tf_op jit(solution)/shard_map/pallas_call | solution.py:213
  50.7 9.6 %all-to-all-start.1 = ((bf16[24,8,2048]{2,1,0:T(8,128)(2,1)}), bf16[24,8,2048]{2,1,0:T(8,128)(2,1)S(1)}, u32[]{:S(2)}, u32[]{:S(2)}) async-start(bf16[24,8,2048]{2,1,0:T(8,128)(2,1)} %shard_map.99), calls=%async_computation.1 | async-start | bytes 1572864 | tf_op jit(solution)/shard_map/all_to_all | solution.py:221
  60.3 3.1 %collective-permute-start.4 = (bf16[4,2,2048]{2,1,0:T(2,128)(2,1)S(1)}, bf16[4,2,2048]{2,1,0:T(2,128)(2,1)S(1)}, u32[]{:S(2)}, u32[]{:S(2)}) collective-permute-start(bf16[4,2,2048]{2,1,0:T(2,128)(2,1)S(1)} %get-tuple-element.23.refs_1_), channel_id=1, source_target_pairs={{0,48},{48,96},{96,144},{144,0},{1,49},{49,97},{97,145},{145,1},{2... | collective-permute-start | bytes 98312 | tf_op jit(solution)/shard_map/ppermute | solution.py:167
  63.4 4.4 %collective-permute-start.5 = (bf16[4,2,2048]{2,1,0:T(2,128)(2,1)S(1)}, bf16[4,2,2048]{2,1,0:T(2,128)(2,1)S(1)}, u32[]{:S(2)}, u32[]{:S(2)}) collective-permute-start(bf16[4,2,2048]{2,1,0:T(2,128)(2,1)S(1)} %get-tuple-element.24.refs_2_), channel_id=1, source_target_pairs={{0,96},{48,144},{96,0},{144,48},{1,97},{49,145},{97,1},{145,49},{2... | collective-permute-start | bytes 98312 | tf_op jit(solution)/shard_map/ppermute | solution.py:167
  67.8 3.1 %collective-permute-start.6 = (bf16[4,2,2048]{2,1,0:T(2,128)(2,1)S(1)}, bf16[4,2,2048]{2,1,0:T(2,128)(2,1)S(1)}, u32[]{:S(2)}, u32[]{:S(2)}) collective-permute-start(bf16[4,2,2048]{2,1,0:T(2,128)(2,1)S(1)} %get-tuple-element.25.refs_3_), channel_id=1, source_target_pairs={{0,144},{48,0},{96,48},{144,96},{1,145},{49,1},{97,49},{145,97},{2... | collective-permute-start | bytes 98312 | tf_op jit(solution)/shard_map/ppermute | solution.py:167
  70.8 0.0 collective-permute-done.4.refs_1_
  70.9 0.0 collective-permute-done.5.refs_2_
  70.9 1.9 %collective-permute-done.6.refs_3_ = bf16[4,2,2048]{2,1,0:T(2,128)(2,1)S(1)} collective-permute-done((bf16[4,2,2048]{2,1,0:T(2,128)(2,1)S(1)}, bf16[4,2,2048]{2,1,0:T(2,128)(2,1)S(1)}, u32[]{:S(2)}, u32[]{:S(2)}) %collective-permute-start.6) | collective-permute-done | bytes 32800 | tf_op jit(solution)/shard_map/ppermute | solution.py:167
  72.7 4.3 %all-to-all-done.1 = bf16[24,8,2048]{2,1,0:T(8,128)(2,1)S(1)} async-done(((bf16[24,8,2048]{2,1,0:T(8,128)(2,1)}), bf16[24,8,2048]{2,1,0:T(8,128)(2,1)S(1)}, u32[]{:S(2)}, u32[]{:S(2)}) %all-to-all-start.1) | async-done | bytes 786464 | tf_op jit(solution)/shard_map/all_to_all | solution.py:221
  77.0 7.5 %collective-permute-start.7 = (bf16[192,2048]{1,0:T(8,128)(2,1)S(1)}, bf16[192,2048]{1,0:T(8,128)(2,1)S(1)}, u32[]{:S(2)}, u32[]{:S(2)}) collective-permute-start(bf16[192,2048]{1,0:T(8,128)(2,1)S(1)} %shard_map.100.refs_1_), channel_id=1, source_target_pairs={{0,1},{1,0},{2,3},{3,2},{4,5},{5,4},{6,7},{7,6},{8,9},{9,8},{10,11... | collective-permute-start | bytes 2359304 | tf_op jit(solution)/shard_map/ppermute | solution.py:227
  84.5 1.2 %shard_map.103 = bf16[16,2,2048]{2,1,0:T(2,128)(2,1)} custom-call(s32[4]{0:T(128)S(1)} %pad_add_fusion.place_ref, bf16[4,2,2048]{2,1,0:T(2,128)(2,1)S(1)} %get-tuple-element.22.refs_0_, bf16[4,2,2048]{2,1,0:T(2,128)(2,1)S(1)} %collective-permute-done.4.refs_1_, bf16[4,2,2048]{2,1,0:T(2,128)(2,1)S(1)} %collective-permute-done.5.refs_2_, ...), custom_call_target="tpu_custom_call" | custom-call | flops 1000000 | bytes 1000000 | tf_op jit(solution)/shard_map/pallas_call | solution.py:224
  85.7 0.9 %shard_map.101.refs_2_ = bf16[192,4096]{1,0:T(8,128)(2,1)} custom-call(s32[1]{0:T(128)} %bitcast.core_ref.refs_0_, bf16[192,2048]{1,0:T(8,128)(2,1)S(1)} %shard_map.100.refs_1_), custom_call_target="tpu_custom_call" | custom-call | flops 1000000 | bytes 1000000 | tf_op jit(solution)/shard_map/pallas_call | solution.py:146
  86.6 0.9 %shard_map.102 = bf16[192,4096]{1,0:T(8,128)(2,1)} custom-call(s32[1]{0:T(128)} %bitcast.core_ref.refs_0_, bf16[192,2048]{1,0:T(8,128)(2,1)S(1)} %collective-permute-done.7.refs_1_, bf16[192,4096]{1,0:T(8,128)(2,1)} %shard_map.101.refs_2_), custom_call_target="tpu_custom_call", output_to_operand_aliasing={{}: (2, {})} | custom-call | flops 1000000 | bytes 1000000 | tf_op jit(solution)/shard_map/pallas_call | solution.py:146
  (5 shorter events, 0.0 us)
Async XLA Ops:
  5.7 14.5 %collective-permute-start = (bf16[192,2048]{1,0:T(8,128)(2,1)S(1)}, bf16[192,2048]{1,0:T(8,128)(2,1)S(1)}, u32[]{:S(2)}, u32[]{:S(2)}) collective-permute-start(bf16[192,2048]{1,0:T(8,128)(2,1)S(1)} %get-tuple-element.15), channel_id=1, source_target_pairs={{0,1},{1,0},{2,3},{3,2},{4,5},{5,4},{6,7},{7,6},{8,9},{9,8},{10,11... | collective-permute-start | bytes 2359304 | tf_op jit(solution)/shard_map/ppermute | solution.py:193
  20.1 5.0 %copy-start = (bf16[16,2,2048]{2,1,0:T(2,128)(2,1)S(1)}, bf16[16,2,2048]{2,1,0:T(2,128)(2,1)}, u32[]{:S(2)}) copy-start(bf16[16,2,2048]{2,1,0:T(2,128)(2,1)} %kv_ref.1) | copy-start | bytes 393220
  20.1 5.0 %copy-start.1 = (s32[16,16]{1,0:T(8,128)S(1)}, s32[16,16]{1,0:T(8,128)}, u32[]{:S(2)}) copy-start(s32[16,16]{1,0:T(8,128)} %dest_ref.1) | copy-start | bytes 3076
  20.2 5.0 %copy-start.2 = (s32[16]{0:T(128)S(1)}, s32[16]{0:T(128)}, u32[]{:S(2)}) copy-start(s32[16]{0:T(128)} %lengths_ref.1) | copy-start | bytes 196
  21.1 28.3 %all-to-all-start = ((bf16[24,8,2048]{2,1,0:T(8,128)(2,1)}), bf16[24,8,2048]{2,1,0:T(8,128)(2,1)S(1)}, u32[]{:S(2)}, u32[]{:S(2)}) async-start(bf16[24,8,2048]{2,1,0:T(8,128)(2,1)} %bitcast.9), calls=%async_computation | async-start | bytes 1572864 | tf_op jit(solution)/shard_map/all_to_all | solution.py:204
  26.4 21.4 %collective-permute-start.1 = (bf16[4,2,2048]{2,1,0:T(2,128)(2,1)S(1)}, bf16[4,2,2048]{2,1,0:T(2,128)(2,1)S(1)}, u32[]{:S(2)}, u32[]{:S(2)}) collective-permute-start(bf16[4,2,2048]{2,1,0:T(2,128)(2,1)S(1)} %get-tuple-element.19), channel_id=1, source_target_pairs={{0,384},{192,576},{384,0},{576,192},{1,385},{193,577},{385,1},{577... | collective-permute-start | bytes 98312 | tf_op jit(solution)/shard_map/ppermute | solution.py:167
  37.8 9.9 %collective-permute-start.2 = (bf16[4,2,2048]{2,1,0:T(2,128)(2,1)S(1)}, bf16[4,2,2048]{2,1,0:T(2,128)(2,1)S(1)}, u32[]{:S(2)}, u32[]{:S(2)}) collective-permute-start(bf16[4,2,2048]{2,1,0:T(2,128)(2,1)S(1)} %get-tuple-element.20), channel_id=1, source_target_pairs={{0,192},{192,384},{384,576},{576,0},{1,193},{193,385},{385,577},{5... | collective-permute-start | bytes 98312 | tf_op jit(solution)/shard_map/ppermute | solution.py:167
  42.1 6.8 %collective-permute-start.3 = (bf16[4,2,2048]{2,1,0:T(2,128)(2,1)S(1)}, bf16[4,2,2048]{2,1,0:T(2,128)(2,1)S(1)}, u32[]{:S(2)}, u32[]{:S(2)}) collective-permute-start(bf16[4,2,2048]{2,1,0:T(2,128)(2,1)S(1)} %get-tuple-element.21), channel_id=1, source_target_pairs={{0,576},{192,0},{384,192},{576,384},{1,577},{193,1},{385,193},{577... | collective-permute-start | bytes 98312 | tf_op jit(solution)/shard_map/ppermute | solution.py:167
  50.7 26.3 %all-to-all-start.1 = ((bf16[24,8,2048]{2,1,0:T(8,128)(2,1)}), bf16[24,8,2048]{2,1,0:T(8,128)(2,1)S(1)}, u32[]{:S(2)}, u32[]{:S(2)}) async-start(bf16[24,8,2048]{2,1,0:T(8,128)(2,1)} %shard_map.99), calls=%async_computation.1 | async-start | bytes 1572864 | tf_op jit(solution)/shard_map/all_to_all | solution.py:221
  60.3 10.6 %collective-permute-start.4 = (bf16[4,2,2048]{2,1,0:T(2,128)(2,1)S(1)}, bf16[4,2,2048]{2,1,0:T(2,128)(2,1)S(1)}, u32[]{:S(2)}, u32[]{:S(2)}) collective-permute-start(bf16[4,2,2048]{2,1,0:T(2,128)(2,1)S(1)} %get-tuple-element.23.refs_1_), channel_id=1, source_target_pairs={{0,48},{48,96},{96,144},{144,0},{1,49},{49,97},{97,145},{145,1},{2... | collective-permute-start | bytes 98312 | tf_op jit(solution)/shard_map/ppermute | solution.py:167
  63.4 7.5 %collective-permute-start.5 = (bf16[4,2,2048]{2,1,0:T(2,128)(2,1)S(1)}, bf16[4,2,2048]{2,1,0:T(2,128)(2,1)S(1)}, u32[]{:S(2)}, u32[]{:S(2)}) collective-permute-start(bf16[4,2,2048]{2,1,0:T(2,128)(2,1)S(1)} %get-tuple-element.24.refs_2_), channel_id=1, source_target_pairs={{0,96},{48,144},{96,0},{144,48},{1,97},{49,145},{97,1},{145,49},{2... | collective-permute-start | bytes 98312 | tf_op jit(solution)/shard_map/ppermute | solution.py:167
  67.8 5.0 %collective-permute-start.6 = (bf16[4,2,2048]{2,1,0:T(2,128)(2,1)S(1)}, bf16[4,2,2048]{2,1,0:T(2,128)(2,1)S(1)}, u32[]{:S(2)}, u32[]{:S(2)}) collective-permute-start(bf16[4,2,2048]{2,1,0:T(2,128)(2,1)S(1)} %get-tuple-element.25.refs_3_), channel_id=1, source_target_pairs={{0,144},{48,0},{96,48},{144,96},{1,145},{49,1},{97,49},{145,97},{2... | collective-permute-start | bytes 98312 | tf_op jit(solution)/shard_map/ppermute | solution.py:167
  77.0 9.6 %collective-permute-start.7 = (bf16[192,2048]{1,0:T(8,128)(2,1)S(1)}, bf16[192,2048]{1,0:T(8,128)(2,1)S(1)}, u32[]{:S(2)}, u32[]{:S(2)}) collective-permute-start(bf16[192,2048]{1,0:T(8,128)(2,1)S(1)} %shard_map.100.refs_1_), channel_id=1, source_target_pairs={{0,1},{1,0},{2,3},{3,2},{4,5},{5,4},{6,7},{7,6},{8,9},{9,8},{10,11... | collective-permute-start | bytes 2359304 | tf_op jit(solution)/shard_map/ppermute | solution.py:227

commit v13 on v11

--- a/solution.py
+++ b/solution.py
@@ -70,6 +70,23 @@
     away_ref[...] = jnp.dot(hidden, theirs_ref[...], preferred_element_type=f32).astype(bf16)
 
 
+def own_body(core_ref, hidden_ref, down_ref, out_ref, ours_ref, sems):
+    width = out_ref.shape[1]
+    columns = width // STEPS
+    first = core_ref[0] * width
+    copies = []
+    for i in range(STEPS):
+        source = pl.ds(pl.multiple_of(first + i * columns, columns), columns)
+        copies.append(
+            pltpu.make_async_copy(down_ref.at[:, source], ours_ref.at[:, pl.ds(i * columns, columns)], sems.at[i])
+        )
+        copies[-1].start()
+    for i, copy in enumerate(copies):
+        copy.wait()
+        block = slice(i * columns, (i + 1) * columns)
+        out_ref[:, block] = jnp.dot(hidden_ref[...], ours_ref[:, block], preferred_element_type=f32)
+
+
 def sort_body(place_ref, dest_ref, lengths_ref, kv_ref, mark_ref, *out_refs):
     x, mine, first = place_ref[0], place_ref[1], place_ref[2]
     row = lax.broadcasted_iota(jnp.int32, kv_ref.shape[1:], 0) + first
@@ -189,9 +206,15 @@
         ],
     )(core[None], tokens, gate_weight, up_weight, down_weight, active)
 
-    ours = lax.dynamic_slice_in_dim(down_weight, core * width, width, 1)
     arrived = lax.ppermute(away, "core", SWAP)
-    own = jnp.dot(hidden, ours, preferred_element_type=f32)
+    own = call(
+        own_body,
+        pltpu.VMEM((rows, width), f32),
+        [SMEM, VMEM, ANY],
+        VMEM,
+        vmem=50,
+        scratch_shapes=[pltpu.VMEM((down_weight.shape[0], width), bf16), pltpu.SemaphoreType.DMA((STEPS,))],
+    )(core[None], hidden, down_weight)
     total, mark = call(
         add_body,
         [pltpu.HBM((rows, width), bf16), MARK],

time: 86 us -> 85.3 us (level)
  Pallas kernels: 12 us -> 14.1 us
  matrix products: 1.99 us -> 0 us
    pallas_call x0 -> x1, Pallas kernels: none -> 2.1 us  [shards(): call(own_body, pltpu.VMEM((rows, width), f32), [SMEM, VMEM, ANY], VMEM, v...]
    dot_general x1 -> x0, matrix products: 1.99 us -> none  [shards(): own = jnp.dot(hidden, ours, preferred_element_type=f32)]
  transfers between devices with their start and end apart: 10 -> 10, of which waited for: 3 -> 3; matrix products, arithmetic and copies ran while one was open for 2% -> 0% of each run, Pallas kernels for 5% -> 7%
where the time goes in v13:
time: 85.3 us; the launch traced here: 84.7 us
  starting transfers between devices  56.9 us (67%)
  Pallas kernels  14.1 us (17%)
  waiting for transfers between devices  12.8 us (15%)
  between operations  0.87 us (1%)
    ppermute x6, starting transfers between devices, shift(): return lax.ppermute(value, axis, [(i, (i + k) % SIDE) for i in range(SIDE)])  29.6 us
    ppermute x1, starting transfers between devices, shards(): arrived = lax.ppermute(away, 'core', SWAP)  12.4 us
    all_to_all x1, waiting for transfers between devices, shards(): parts = lax.all_to_all(parts, RING, split_axis=0, concat_axis=0, tiled=True)  7.76 us
    all_to_all x1, starting transfers between devices, shards(): lax.all_to_all(spread, RING, split_axis=0, concat_axis=0, tiled=True)  6.8 us
    pallas_call x1, Pallas kernels, shards(): call(hidden_body, [pltpu.VMEM(active.shape, bf16), pltpu.VMEM((rows, widt...  5.07 us
    ppermute x6, waiting for transfers between devices, shift(): return lax.ppermute(value, axis, [(i, (i + k) % SIDE) for i in range(SIDE)])  5.02 us
    ppermute x1, starting transfers between devices, shards(): other = lax.ppermute(half, 'core', SWAP)  4.17 us
    all_to_all x1, starting transfers between devices, shards(): parts = lax.all_to_all(parts, RING, split_axis=0, concat_axis=0, tiled=True)  3.91 us
  transfers between devices with their start and end apart: 10, of which 3 were waited for; matrix products, arithmetic and copies ran while one was open for 0% of the time, Pallas kernels for 7%

profile of v13, /device:TPU:1, one launch (start us, length us, event | category | flops | bytes accessed | tf_op | source)
XLA Modules:
  0.0 84.7 jit_solution(6063878096456694976)
XLA Ops:
  0.6 5.1 %shard_map.95 = (bf16[192,384]{1,0:T(8,128)(2,1)S(1)}, bf16[192,2048]{1,0:T(8,128)(2,1)S(1)}) custom-call(s32[1]{0:T(128)} %bitcast.core_ref.refs_0_, bf16[192,4096]{1,0:T(8,128)(2,1)} %tokens_ref.1, bf16[4096,384]{1,0:T(8,128)(2,1)} %gate_ref.1, bf16[4096,384]{1,0:T(8,128)(2,1)} %up_ref.1, bf16[384,4096]{1,0:T(8,128)(2,1)} %down_ref.3, s32[192,384]{1,0:T(8,128)} %active_ref.1), custom_call_target="tpu_custom_call" | custom-call | flops 1000000 | bytes 1000000 | tf_op jit(solution)/shard_map/pallas_call | solution.py:193
  5.7 12.4 %collective-permute-start = (bf16[192,2048]{1,0:T(8,128)(2,1)S(1)}, bf16[192,2048]{1,0:T(8,128)(2,1)S(1)}, u32[]{:S(2)}, u32[]{:S(2)}) collective-permute-start(bf16[192,2048]{1,0:T(8,128)(2,1)S(1)} %get-tuple-element.15), channel_id=1, source_target_pairs={{0,1},{1,0},{2,3},{3,2},{4,5},{5,4},{6,7},{7,6},{8,9},{9,8},{10,11... | collective-permute-start | bytes 2359304 | tf_op jit(solution)/shard_map/ppermute | solution.py:209
  18.1 2.1 %shard_map.96.own_ref = f32[192,2048]{1,0:T(8,128)S(1)} custom-call(s32[1]{0:T(128)} %bitcast.core_ref.refs_0_, bf16[192,384]{1,0:T(8,128)(2,1)S(1)} %get-tuple-element.14.hidden_ref, bf16[384,4096]{1,0:T(8,128)(2,1)} %down_ref.3), custom_call_target="tpu_custom_call" | custom-call | flops 1000000 | bytes 1000000 | tf_op jit(solution)/shard_map/pallas_call | solution.py:210
  20.2 0.0 copy-start
  20.3 0.0 copy-start.1
  20.3 0.0 copy-start.2
  20.3 0.0 collective-permute-done.arrived_ref
  20.3 0.9 %shard_map.97 = (bf16[192,2048]{1,0:T(8,128)(2,1)}, f32[8,128]{1,0:T(8,128)S(1)}) custom-call(f32[192,2048]{1,0:T(8,128)S(1)} %shard_map.96.own_ref, bf16[192,2048]{1,0:T(8,128)(2,1)S(1)} %collective-permute-done.arrived_ref), custom_call_target="tpu_custom_call" | custom-call | flops 1000000 | bytes 1000000 | tf_op jit(solution)/shard_map/pallas_call | solution.py:218
  21.2 3.9 %all-to-all-start = ((bf16[24,8,2048]{2,1,0:T(8,128)(2,1)}), bf16[24,8,2048]{2,1,0:T(8,128)(2,1)S(1)}, u32[]{:S(2)}, u32[]{:S(2)}) async-start(bf16[24,8,2048]{2,1,0:T(8,128)(2,1)} %bitcast.8), calls=%async_computation | async-start | bytes 1572864 | tf_op jit(solution)/shard_map/all_to_all | solution.py:227
  25.2 0.1 pad_add_fusion.place_ref
  25.3 1.2 %shard_map.98 = (bf16[4,2,2048]{2,1,0:T(2,128)(2,1)S(1)}, bf16[4,2,2048]{2,1,0:T(2,128)(2,1)S(1)}, bf16[4,2,2048]{2,1,0:T(2,128)(2,1)S(1)}, bf16[4,2,2048]{2,1,0:T(2,128)(2,1)S(1)}) custom-call(s32[4]{0:T(128)S(1)} %pad_add_fusion.place_ref, s32[16,16]{1,0:T(8,128)S(1)} %copy-done.1, s32[16]{0:T(128)S(1)} %copy-done.2, bf16[16,2,2048]{2,1,0:T(2,128)(2,1)S(1)} %copy-done, ...), custom_call_target="tpu_custom_call" | custom-call | flops 1000000 | bytes 1000000 | tf_op jit(solution)/shard_map/pallas_call | solution.py:230
  26.5 1.9 %collective-permute-start.1 = (bf16[4,2,2048]{2,1,0:T(2,128)(2,1)S(1)}, bf16[4,2,2048]{2,1,0:T(2,128)(2,1)S(1)}, u32[]{:S(2)}, u32[]{:S(2)}) collective-permute-start(bf16[4,2,2048]{2,1,0:T(2,128)(2,1)S(1)} %get-tuple-element.19), channel_id=1, source_target_pairs={{0,48},{48,96},{96,144},{144,0},{1,49},{49,97},{97,145},{145,1},{2... | collective-permute-start | bytes 98312 | tf_op jit(solution)/shard_map/ppermute | solution.py:184
  28.4 3.4 %collective-permute-start.2 = (bf16[4,2,2048]{2,1,0:T(2,128)(2,1)S(1)}, bf16[4,2,2048]{2,1,0:T(2,128)(2,1)S(1)}, u32[]{:S(2)}, u32[]{:S(2)}) collective-permute-start(bf16[4,2,2048]{2,1,0:T(2,128)(2,1)S(1)} %get-tuple-element.20), channel_id=1, source_target_pairs={{0,96},{48,144},{96,0},{144,48},{1,97},{49,145},{97,1},{145,49},{2... | collective-permute-start | bytes 98312 | tf_op jit(solution)/shard_map/ppermute | solution.py:184
  31.7 3.2 %collective-permute-start.3 = (bf16[4,2,2048]{2,1,0:T(2,128)(2,1)S(1)}, bf16[4,2,2048]{2,1,0:T(2,128)(2,1)S(1)}, u32[]{:S(2)}, u32[]{:S(2)}) collective-permute-start(bf16[4,2,2048]{2,1,0:T(2,128)(2,1)S(1)} %get-tuple-element.21), channel_id=1, source_target_pairs={{0,144},{48,0},{96,48},{144,96},{1,145},{49,1},{97,49},{145,97},{2... | collective-permute-start | bytes 98312 | tf_op jit(solution)/shard_map/ppermute | solution.py:184
  34.9 0.0 collective-permute-done.1.refs_1_
  34.9 0.0 collective-permute-done.2.refs_2_
  34.9 2.1 %collective-permute-done.3.refs_3_ = bf16[4,2,2048]{2,1,0:T(2,128)(2,1)S(1)} collective-permute-done((bf16[4,2,2048]{2,1,0:T(2,128)(2,1)S(1)}, bf16[4,2,2048]{2,1,0:T(2,128)(2,1)S(1)}, u32[]{:S(2)}, u32[]{:S(2)}) %collective-permute-start.3) | collective-permute-done | bytes 32800 | tf_op jit(solution)/shard_map/ppermute | solution.py:184
  37.1 0.6 shard_map.99
  37.6 7.8 %all-to-all-done.parts_ref = bf16[24,8,2048]{2,1,0:T(8,128)(2,1)S(1)} async-done(((bf16[24,8,2048]{2,1,0:T(8,128)(2,1)}), bf16[24,8,2048]{2,1,0:T(8,128)(2,1)S(1)}, u32[]{:S(2)}, u32[]{:S(2)}) %all-to-all-start) | async-done | bytes 786464 | tf_op jit(solution)/shard_map/all_to_all | solution.py:227
  45.4 1.2 %shard_map.100 = bf16[24,8,2048]{2,1,0:T(8,128)(2,1)} custom-call(bf16[24,8,2048]{2,1,0:T(8,128)(2,1)S(1)} %all-to-all-done.parts_ref, bf16[4,2,2048]{2,1,0:T(2,128)(2,1)S(1)} %get-tuple-element.22.refs_0_, bf16[4,2,2048]{2,1,0:T(2,128)(2,1)S(1)} %get-tuple-element.23.refs_1_, bf16[4,2,2048]{2,1,0:T(2,128)(2,1)S(1)} %get-tuple-element.24.refs_2_, ...), custom_call_target="tpu_custom_call" | custom-call | flops 1000000 | bytes 1000000 | tf_op jit(solution)/shard_map/pallas_call | solution.py:236
  46.6 6.8 %all-to-all-start.1 = ((bf16[24,8,2048]{2,1,0:T(8,128)(2,1)}), bf16[24,8,2048]{2,1,0:T(8,128)(2,1)S(1)}, u32[]{:S(2)}, u32[]{:S(2)}) async-start(bf16[24,8,2048]{2,1,0:T(8,128)(2,1)} %shard_map.100), calls=%async_computation.1 | async-start | bytes 1572864 | tf_op jit(solution)/shard_map/all_to_all | solution.py:244
  53.4 12.9 %collective-permute-start.4 = (bf16[4,2,2048]{2,1,0:T(2,128)(2,1)S(1)}, bf16[4,2,2048]{2,1,0:T(2,128)(2,1)S(1)}, u32[]{:S(2)}, u32[]{:S(2)}) collective-permute-start(bf16[4,2,2048]{2,1,0:T(2,128)(2,1)S(1)} %get-tuple-element.23.refs_1_), channel_id=1, source_target_pairs={{0,384},{192,576},{384,0},{576,192},{1,385},{193,577},{385,1},{577... | collective-permute-start | bytes 98312 | tf_op jit(solution)/shard_map/ppermute | solution.py:184
  66.3 2.9 %collective-permute-start.5 = (bf16[4,2,2048]{2,1,0:T(2,128)(2,1)S(1)}, bf16[4,2,2048]{2,1,0:T(2,128)(2,1)S(1)}, u32[]{:S(2)}, u32[]{:S(2)}) collective-permute-start(bf16[4,2,2048]{2,1,0:T(2,128)(2,1)S(1)} %get-tuple-element.24.refs_2_), channel_id=1, source_target_pairs={{0,192},{192,384},{384,576},{576,0},{1,193},{193,385},{385,577},{5... | collective-permute-start | bytes 98312 | tf_op jit(solution)/shard_map/ppermute | solution.py:184
  69.2 5.3 %collective-permute-start.6 = (bf16[4,2,2048]{2,1,0:T(2,128)(2,1)S(1)}, bf16[4,2,2048]{2,1,0:T(2,128)(2,1)S(1)}, u32[]{:S(2)}, u32[]{:S(2)}) collective-permute-start(bf16[4,2,2048]{2,1,0:T(2,128)(2,1)S(1)} %get-tuple-element.25.refs_3_), channel_id=1, source_target_pairs={{0,576},{192,0},{384,192},{576,384},{1,577},{193,1},{385,193},{577... | collective-permute-start | bytes 98312 | tf_op jit(solution)/shard_map/ppermute | solution.py:184
  74.6 2.9 %collective-permute-done.4.refs_1_ = bf16[4,2,2048]{2,1,0:T(2,128)(2,1)S(1)} collective-permute-done((bf16[4,2,2048]{2,1,0:T(2,128)(2,1)S(1)}, bf16[4,2,2048]{2,1,0:T(2,128)(2,1)S(1)}, u32[]{:S(2)}, u32[]{:S(2)}) %collective-permute-start.4) | collective-permute-done | bytes 32800 | tf_op jit(solution)/shard_map/ppermute | solution.py:184
  77.5 0.0 collective-permute-done.5.refs_2_
  77.5 0.0 collective-permute-done.6.refs_3_
  77.5 0.0 all-to-all-done.1
  77.5 4.2 %collective-permute-start.7 = (bf16[192,2048]{1,0:T(8,128)(2,1)S(1)}, bf16[192,2048]{1,0:T(8,128)(2,1)S(1)}, u32[]{:S(2)}, u32[]{:S(2)}) collective-permute-start(bf16[192,2048]{1,0:T(8,128)(2,1)S(1)} %shard_map.101.refs_1_), channel_id=1, source_target_pairs={{0,1},{1,0},{2,3},{3,2},{4,5},{5,4},{6,7},{7,6},{8,9},{9,8},{10,11... | collective-permute-start | bytes 2359304 | tf_op jit(solution)/shard_map/ppermute | solution.py:250
  81.7 1.2 %shard_map.104 = bf16[16,2,2048]{2,1,0:T(2,128)(2,1)} custom-call(s32[4]{0:T(128)S(1)} %pad_add_fusion.place_ref, bf16[4,2,2048]{2,1,0:T(2,128)(2,1)S(1)} %get-tuple-element.22.refs_0_, bf16[4,2,2048]{2,1,0:T(2,128)(2,1)S(1)} %collective-permute-done.4.refs_1_, bf16[4,2,2048]{2,1,0:T(2,128)(2,1)S(1)} %collective-permute-done.5.refs_2_, ...), custom_call_target="tpu_custom_call" | custom-call | flops 1000000 | bytes 1000000 | tf_op jit(solution)/shard_map/pallas_call | solution.py:247
  82.9 0.9 %shard_map.102.refs_2_ = bf16[192,4096]{1,0:T(8,128)(2,1)} custom-call(s32[1]{0:T(128)} %bitcast.core_ref.refs_0_, bf16[192,2048]{1,0:T(8,128)(2,1)S(1)} %shard_map.101.refs_1_), custom_call_target="tpu_custom_call" | custom-call | flops 1000000 | bytes 1000000 | tf_op jit(solution)/shard_map/pallas_call | solution.py:163
  83.8 0.9 %shard_map.103 = bf16[192,4096]{1,0:T(8,128)(2,1)} custom-call(s32[1]{0:T(128)} %bitcast.core_ref.refs_0_, bf16[192,2048]{1,0:T(8,128)(2,1)S(1)} %collective-permute-done.7.refs_1_, bf16[192,4096]{1,0:T(8,128)(2,1)} %shard_map.102.refs_2_), custom_call_target="tpu_custom_call", output_to_operand_aliasing={{}: (2, {})} | custom-call | flops 1000000 | bytes 1000000 | tf_op jit(solution)/shard_map/pallas_call | solution.py:163
  (5 shorter events, 0.0 us)
Async XLA Ops:
  5.7 14.6 %collective-permute-start = (bf16[192,2048]{1,0:T(8,128)(2,1)S(1)}, bf16[192,2048]{1,0:T(8,128)(2,1)S(1)}, u32[]{:S(2)}, u32[]{:S(2)}) collective-permute-start(bf16[192,2048]{1,0:T(8,128)(2,1)S(1)} %get-tuple-element.15), channel_id=1, source_target_pairs={{0,1},{1,0},{2,3},{3,2},{4,5},{5,4},{6,7},{7,6},{8,9},{9,8},{10,11... | collective-permute-start | bytes 2359304 | tf_op jit(solution)/shard_map/ppermute | solution.py:209
  20.2 5.0 %copy-start = (bf16[16,2,2048]{2,1,0:T(2,128)(2,1)S(1)}, bf16[16,2,2048]{2,1,0:T(2,128)(2,1)}, u32[]{:S(2)}) copy-start(bf16[16,2,2048]{2,1,0:T(2,128)(2,1)} %kv_ref.1) | copy-start | bytes 393220
  20.3 5.0 %copy-start.1 = (s32[16,16]{1,0:T(8,128)S(1)}, s32[16,16]{1,0:T(8,128)}, u32[]{:S(2)}) copy-start(s32[16,16]{1,0:T(8,128)} %dest_ref.1) | copy-start | bytes 3076
  20.3 5.0 %copy-start.2 = (s32[16]{0:T(128)S(1)}, s32[16]{0:T(128)}, u32[]{:S(2)}) copy-start(s32[16]{0:T(128)} %lengths_ref.1) | copy-start | bytes 196
  21.2 24.2 %all-to-all-start = ((bf16[24,8,2048]{2,1,0:T(8,128)(2,1)}), bf16[24,8,2048]{2,1,0:T(8,128)(2,1)S(1)}, u32[]{:S(2)}, u32[]{:S(2)}) async-start(bf16[24,8,2048]{2,1,0:T(8,128)(2,1)} %bitcast.8), calls=%async_computation | async-start | bytes 1572864 | tf_op jit(solution)/shard_map/all_to_all | solution.py:227
  26.5 8.5 %collective-permute-start.1 = (bf16[4,2,2048]{2,1,0:T(2,128)(2,1)S(1)}, bf16[4,2,2048]{2,1,0:T(2,128)(2,1)S(1)}, u32[]{:S(2)}, u32[]{:S(2)}) collective-permute-start(bf16[4,2,2048]{2,1,0:T(2,128)(2,1)S(1)} %get-tuple-element.19), channel_id=1, source_target_pairs={{0,48},{48,96},{96,144},{144,0},{1,49},{49,97},{97,145},{145,1},{2... | collective-permute-start | bytes 98312 | tf_op jit(solution)/shard_map/ppermute | solution.py:184
  28.4 6.5 %collective-permute-start.2 = (bf16[4,2,2048]{2,1,0:T(2,128)(2,1)S(1)}, bf16[4,2,2048]{2,1,0:T(2,128)(2,1)S(1)}, u32[]{:S(2)}, u32[]{:S(2)}) collective-permute-start(bf16[4,2,2048]{2,1,0:T(2,128)(2,1)S(1)} %get-tuple-element.20), channel_id=1, source_target_pairs={{0,96},{48,144},{96,0},{144,48},{1,97},{49,145},{97,1},{145,49},{2... | collective-permute-start | bytes 98312 | tf_op jit(solution)/shard_map/ppermute | solution.py:184
  31.7 5.3 %collective-permute-start.3 = (bf16[4,2,2048]{2,1,0:T(2,128)(2,1)S(1)}, bf16[4,2,2048]{2,1,0:T(2,128)(2,1)S(1)}, u32[]{:S(2)}, u32[]{:S(2)}) collective-permute-start(bf16[4,2,2048]{2,1,0:T(2,128)(2,1)S(1)} %get-tuple-element.21), channel_id=1, source_target_pairs={{0,144},{48,0},{96,48},{144,96},{1,145},{49,1},{97,49},{145,97},{2... | collective-permute-start | bytes 98312 | tf_op jit(solution)/shard_map/ppermute | solution.py:184
  46.6 30.9 %all-to-all-start.1 = ((bf16[24,8,2048]{2,1,0:T(8,128)(2,1)}), bf16[24,8,2048]{2,1,0:T(8,128)(2,1)S(1)}, u32[]{:S(2)}, u32[]{:S(2)}) async-start(bf16[24,8,2048]{2,1,0:T(8,128)(2,1)} %shard_map.100), calls=%async_computation.1 | async-start | bytes 1572864 | tf_op jit(solution)/shard_map/all_to_all | solution.py:244
  53.4 24.1 %collective-permute-start.4 = (bf16[4,2,2048]{2,1,0:T(2,128)(2,1)S(1)}, bf16[4,2,2048]{2,1,0:T(2,128)(2,1)S(1)}, u32[]{:S(2)}, u32[]{:S(2)}) collective-permute-start(bf16[4,2,2048]{2,1,0:T(2,128)(2,1)S(1)} %get-tuple-element.23.refs_1_), channel_id=1, source_target_pairs={{0,384},{192,576},{384,0},{576,192},{1,385},{193,577},{385,1},{577... | collective-permute-start | bytes 98312 | tf_op jit(solution)/shard_map/ppermute | solution.py:184
  66.3 11.2 %collective-permute-start.5 = (bf16[4,2,2048]{2,1,0:T(2,128)(2,1)S(1)}, bf16[4,2,2048]{2,1,0:T(2,128)(2,1)S(1)}, u32[]{:S(2)}, u32[]{:S(2)}) collective-permute-start(bf16[4,2,2048]{2,1,0:T(2,128)(2,1)S(1)} %get-tuple-element.24.refs_2_), channel_id=1, source_target_pairs={{0,192},{192,384},{384,576},{576,0},{1,193},{193,385},{385,577},{5... | collective-permute-start | bytes 98312 | tf_op jit(solution)/shard_map/ppermute | solution.py:184
  69.2 8.2 %collective-permute-start.6 = (bf16[4,2,2048]{2,1,0:T(2,128)(2,1)S(1)}, bf16[4,2,2048]{2,1,0:T(2,128)(2,1)S(1)}, u32[]{:S(2)}, u32[]{:S(2)}) collective-permute-start(bf16[4,2,2048]{2,1,0:T(2,128)(2,1)S(1)} %get-tuple-element.25.refs_3_), channel_id=1, source_target_pairs={{0,576},{192,0},{384,192},{576,384},{1,577},{193,1},{385,193},{577... | collective-permute-start | bytes 98312 | tf_op jit(solution)/shard_map/ppermute | solution.py:184
  77.5 6.3 %collective-permute-start.7 = (bf16[192,2048]{1,0:T(8,128)(2,1)S(1)}, bf16[192,2048]{1,0:T(8,128)(2,1)S(1)}, u32[]{:S(2)}, u32[]{:S(2)}) collective-permute-start(bf16[192,2048]{1,0:T(8,128)(2,1)S(1)} %shard_map.101.refs_1_), channel_id=1, source_target_pairs={{0,1},{1,0},{2,3},{3,2},{4,5},{5,4},{6,7},{7,6},{8,9},{9,8},{10,11... | collective-permute-start | bytes 2359304 | tf_op jit(solution)/shard_map/ppermute | solution.py:250

commit v14 on v13

--- a/solution.py
+++ b/solution.py
@@ -11,7 +11,7 @@
 SWAP = [(0, 1), (1, 0)]
 SIDE = 4
 CHIPS = 24
-ORDER = (0, 2, 1, 3)
+ORDER = (0, 2, 3, 1)
 CHUNKS = 4
 STEPS = 4
 

time: 85.3 us -> 85.8 us (level)
  the two profiles are of different devices: /device:TPU:1 before, /device:TPU:13 now
where the time goes in v14:
time: 85.8 us; the launch traced here: 85.2 us
  starting transfers between devices  58.2 us (68%)
  Pallas kernels  14.1 us (16%)
  waiting for transfers between devices  12 us (14%)
  between operations  0.87 us (1%)
    ppermute x6, starting transfers between devices, shift(): return lax.ppermute(value, axis, [(i, (i + k) % SIDE) for i in range(SIDE)])  32.3 us
    all_to_all x1, starting transfers between devices, shards(): parts = lax.all_to_all(parts, RING, split_axis=0, concat_axis=0, tiled=True)  10.7 us
    all_to_all x1, waiting for transfers between devices, shards(): parts = lax.all_to_all(parts, RING, split_axis=0, concat_axis=0, tiled=True)  7.46 us
    all_to_all x1, starting transfers between devices, shards(): lax.all_to_all(spread, RING, split_axis=0, concat_axis=0, tiled=True)  6.55 us
    ppermute x1, starting transfers between devices, shards(): other = lax.ppermute(half, 'core', SWAP)  6.11 us
    pallas_call x1, Pallas kernels, shards(): call(hidden_body, [pltpu.VMEM(active.shape, bf16), pltpu.VMEM((rows, widt...  5.06 us
    ppermute x6, waiting for transfers between devices, shift(): return lax.ppermute(value, axis, [(i, (i + k) % SIDE) for i in range(SIDE)])  4.5 us
    ppermute x1, starting transfers between devices, shards(): arrived = lax.ppermute(away, 'core', SWAP)  2.58 us
  transfers between devices with their start and end apart: 10, of which 3 were waited for; matrix products, arithmetic and copies ran while one was open for 0% of the time, Pallas kernels for 7%

profile of v14, /device:TPU:13, one launch (start us, length us, event | category | flops | bytes accessed | tf_op | source)
XLA Modules:
  0.0 85.2 jit_solution(5947545343662668969)
XLA Ops:
  0.6 5.1 %shard_map.95 = (bf16[192,384]{1,0:T(8,128)(2,1)S(1)}, bf16[192,2048]{1,0:T(8,128)(2,1)S(1)}) custom-call(s32[1]{0:T(128)} %bitcast.core_ref.refs_0_, bf16[192,4096]{1,0:T(8,128)(2,1)} %tokens_ref.1, bf16[4096,384]{1,0:T(8,128)(2,1)} %gate_ref.1, bf16[4096,384]{1,0:T(8,128)(2,1)} %up_ref.1, bf16[384,4096]{1,0:T(8,128)(2,1)} %down_ref.3, s32[192,384]{1,0:T(8,128)} %active_ref.1), custom_call_target="tpu_custom_call" | custom-call | flops 1000000 | bytes 1000000 | tf_op jit(solution)/shard_map/pallas_call | solution.py:193
  5.7 2.6 %collective-permute-start = (bf16[192,2048]{1,0:T(8,128)(2,1)S(1)}, bf16[192,2048]{1,0:T(8,128)(2,1)S(1)}, u32[]{:S(2)}, u32[]{:S(2)}) collective-permute-start(bf16[192,2048]{1,0:T(8,128)(2,1)S(1)} %get-tuple-element.15), channel_id=1, source_target_pairs={{0,1},{1,0},{2,3},{3,2},{4,5},{5,4},{6,7},{7,6},{8,9},{9,8},{10,11... | collective-permute-start | bytes 2359304 | tf_op jit(solution)/shard_map/ppermute | solution.py:209
  8.3 2.1 %shard_map.96.own_ref = f32[192,2048]{1,0:T(8,128)S(1)} custom-call(s32[1]{0:T(128)} %bitcast.core_ref.refs_0_, bf16[192,384]{1,0:T(8,128)(2,1)S(1)} %get-tuple-element.14.hidden_ref, bf16[384,4096]{1,0:T(8,128)(2,1)} %down_ref.3), custom_call_target="tpu_custom_call" | custom-call | flops 1000000 | bytes 1000000 | tf_op jit(solution)/shard_map/pallas_call | solution.py:210
  10.4 0.0 copy-start
  10.4 0.0 copy-start.1
  10.4 0.0 copy-start.2
  10.4 0.0 collective-permute-done.arrived_ref
  10.5 0.9 %shard_map.97 = (bf16[192,2048]{1,0:T(8,128)(2,1)}, f32[8,128]{1,0:T(8,128)S(1)}) custom-call(f32[192,2048]{1,0:T(8,128)S(1)} %shard_map.96.own_ref, bf16[192,2048]{1,0:T(8,128)(2,1)S(1)} %collective-permute-done.arrived_ref), custom_call_target="tpu_custom_call" | custom-call | flops 1000000 | bytes 1000000 | tf_op jit(solution)/shard_map/pallas_call | solution.py:218
  11.4 10.7 %all-to-all-start = ((bf16[24,8,2048]{2,1,0:T(8,128)(2,1)}), bf16[24,8,2048]{2,1,0:T(8,128)(2,1)S(1)}, u32[]{:S(2)}, u32[]{:S(2)}) async-start(bf16[24,8,2048]{2,1,0:T(8,128)(2,1)} %bitcast.8), calls=%async_computation | async-start | bytes 1572864 | tf_op jit(solution)/shard_map/all_to_all | solution.py:227
  22.1 0.1 pad_add_fusion.place_ref
  22.2 1.2 %shard_map.98 = (bf16[4,2,2048]{2,1,0:T(2,128)(2,1)S(1)}, bf16[4,2,2048]{2,1,0:T(2,128)(2,1)S(1)}, bf16[4,2,2048]{2,1,0:T(2,128)(2,1)S(1)}, bf16[4,2,2048]{2,1,0:T(2,128)(2,1)S(1)}) custom-call(s32[4]{0:T(128)S(1)} %pad_add_fusion.place_ref, s32[16,16]{1,0:T(8,128)S(1)} %copy-done.1, s32[16]{0:T(128)S(1)} %copy-done.2, bf16[16,2,2048]{2,1,0:T(2,128)(2,1)S(1)} %copy-done, ...), custom_call_target="tpu_custom_call" | custom-call | flops 1000000 | bytes 1000000 | tf_op jit(solution)/shard_map/pallas_call | solution.py:230
  23.4 2.8 %collective-permute-start.1 = (bf16[4,2,2048]{2,1,0:T(2,128)(2,1)S(1)}, bf16[4,2,2048]{2,1,0:T(2,128)(2,1)S(1)}, u32[]{:S(2)}, u32[]{:S(2)}) collective-permute-start(bf16[4,2,2048]{2,1,0:T(2,128)(2,1)S(1)} %get-tuple-element.19), channel_id=1, source_target_pairs={{0,48},{48,96},{96,144},{144,0},{1,49},{49,97},{97,145},{145,1},{2... | collective-permute-start | bytes 98312 | tf_op jit(solution)/shard_map/ppermute | solution.py:184
  26.2 3.4 %collective-permute-start.2 = (bf16[4,2,2048]{2,1,0:T(2,128)(2,1)S(1)}, bf16[4,2,2048]{2,1,0:T(2,128)(2,1)S(1)}, u32[]{:S(2)}, u32[]{:S(2)}) collective-permute-start(bf16[4,2,2048]{2,1,0:T(2,128)(2,1)S(1)} %get-tuple-element.20), channel_id=1, source_target_pairs={{0,96},{48,144},{96,0},{144,48},{1,97},{49,145},{97,1},{145,49},{2... | collective-permute-start | bytes 98312 | tf_op jit(solution)/shard_map/ppermute | solution.py:184
  29.6 4.0 %collective-permute-start.3 = (bf16[4,2,2048]{2,1,0:T(2,128)(2,1)S(1)}, bf16[4,2,2048]{2,1,0:T(2,128)(2,1)S(1)}, u32[]{:S(2)}, u32[]{:S(2)}) collective-permute-start(bf16[4,2,2048]{2,1,0:T(2,128)(2,1)S(1)} %get-tuple-element.21), channel_id=1, source_target_pairs={{0,144},{48,0},{96,48},{144,96},{1,145},{49,1},{97,49},{145,97},{2... | collective-permute-start | bytes 98312 | tf_op jit(solution)/shard_map/ppermute | solution.py:184
  33.6 0.0 collective-permute-done.1.refs_1_
  33.6 0.0 collective-permute-done.2.refs_2_
  33.6 1.0 %collective-permute-done.3.refs_3_ = bf16[4,2,2048]{2,1,0:T(2,128)(2,1)S(1)} collective-permute-done((bf16[4,2,2048]{2,1,0:T(2,128)(2,1)S(1)}, bf16[4,2,2048]{2,1,0:T(2,128)(2,1)S(1)}, u32[]{:S(2)}, u32[]{:S(2)}) %collective-permute-start.3) | collective-permute-done | bytes 32800 | tf_op jit(solution)/shard_map/ppermute | solution.py:184
  34.6 0.6 shard_map.99
  35.2 7.5 %all-to-all-done.parts_ref = bf16[24,8,2048]{2,1,0:T(8,128)(2,1)S(1)} async-done(((bf16[24,8,2048]{2,1,0:T(8,128)(2,1)}), bf16[24,8,2048]{2,1,0:T(8,128)(2,1)S(1)}, u32[]{:S(2)}, u32[]{:S(2)}) %all-to-all-start) | async-done | bytes 786464 | tf_op jit(solution)/shard_map/all_to_all | solution.py:227
  42.6 1.2 %shard_map.100 = bf16[24,8,2048]{2,1,0:T(8,128)(2,1)} custom-call(bf16[24,8,2048]{2,1,0:T(8,128)(2,1)S(1)} %all-to-all-done.parts_ref, bf16[4,2,2048]{2,1,0:T(2,128)(2,1)S(1)} %get-tuple-element.22.refs_0_, bf16[4,2,2048]{2,1,0:T(2,128)(2,1)S(1)} %get-tuple-element.23.refs_1_, bf16[4,2,2048]{2,1,0:T(2,128)(2,1)S(1)} %get-tuple-element.24.refs_2_, ...), custom_call_target="tpu_custom_call" | custom-call | flops 1000000 | bytes 1000000 | tf_op jit(solution)/shard_map/pallas_call | solution.py:236
  43.8 6.6 %all-to-all-start.1 = ((bf16[24,8,2048]{2,1,0:T(8,128)(2,1)}), bf16[24,8,2048]{2,1,0:T(8,128)(2,1)S(1)}, u32[]{:S(2)}, u32[]{:S(2)}) async-start(bf16[24,8,2048]{2,1,0:T(8,128)(2,1)} %shard_map.100), calls=%async_computation.1 | async-start | bytes 1572864 | tf_op jit(solution)/shard_map/all_to_all | solution.py:244
  50.4 15.0 %collective-permute-start.4 = (bf16[4,2,2048]{2,1,0:T(2,128)(2,1)S(1)}, bf16[4,2,2048]{2,1,0:T(2,128)(2,1)S(1)}, u32[]{:S(2)}, u32[]{:S(2)}) collective-permute-start(bf16[4,2,2048]{2,1,0:T(2,128)(2,1)S(1)} %get-tuple-element.23.refs_1_), channel_id=1, source_target_pairs={{0,384},{192,576},{384,0},{576,192},{1,385},{193,577},{385,1},{577... | collective-permute-start | bytes 98312 | tf_op jit(solution)/shard_map/ppermute | solution.py:184
  65.4 1.9 %collective-permute-start.5 = (bf16[4,2,2048]{2,1,0:T(2,128)(2,1)S(1)}, bf16[4,2,2048]{2,1,0:T(2,128)(2,1)S(1)}, u32[]{:S(2)}, u32[]{:S(2)}) collective-permute-start(bf16[4,2,2048]{2,1,0:T(2,128)(2,1)S(1)} %get-tuple-element.24.refs_2_), channel_id=1, source_target_pairs={{0,576},{192,0},{384,192},{576,384},{1,577},{193,1},{385,193},{577... | collective-permute-start | bytes 98312 | tf_op jit(solution)/shard_map/ppermute | solution.py:184
  67.4 5.2 %collective-permute-start.6 = (bf16[4,2,2048]{2,1,0:T(2,128)(2,1)S(1)}, bf16[4,2,2048]{2,1,0:T(2,128)(2,1)S(1)}, u32[]{:S(2)}, u32[]{:S(2)}) collective-permute-start(bf16[4,2,2048]{2,1,0:T(2,128)(2,1)S(1)} %get-tuple-element.25.refs_3_), channel_id=1, source_target_pairs={{0,192},{192,384},{384,576},{576,0},{1,193},{193,385},{385,577},{5... | collective-permute-start | bytes 98312 | tf_op jit(solution)/shard_map/ppermute | solution.py:184
  72.5 3.5 %collective-permute-done.4.refs_1_ = bf16[4,2,2048]{2,1,0:T(2,128)(2,1)S(1)} collective-permute-done((bf16[4,2,2048]{2,1,0:T(2,128)(2,1)S(1)}, bf16[4,2,2048]{2,1,0:T(2,128)(2,1)S(1)}, u32[]{:S(2)}, u32[]{:S(2)}) %collective-permute-start.4) | collective-permute-done | bytes 32800 | tf_op jit(solution)/shard_map/ppermute | solution.py:184
  76.0 0.0 collective-permute-done.5.refs_2_
  76.0 0.0 collective-permute-done.6.refs_3_
  76.0 0.0 all-to-all-done.1
  76.1 6.1 %collective-permute-start.7 = (bf16[192,2048]{1,0:T(8,128)(2,1)S(1)}, bf16[192,2048]{1,0:T(8,128)(2,1)S(1)}, u32[]{:S(2)}, u32[]{:S(2)}) collective-permute-start(bf16[192,2048]{1,0:T(8,128)(2,1)S(1)} %shard_map.101.refs_1_), channel_id=1, source_target_pairs={{0,1},{1,0},{2,3},{3,2},{4,5},{5,4},{6,7},{7,6},{8,9},{9,8},{10,11... | collective-permute-start | bytes 2359304 | tf_op jit(solution)/shard_map/ppermute | solution.py:250
  82.2 1.2 %shard_map.104 = bf16[16,2,2048]{2,1,0:T(2,128)(2,1)} custom-call(s32[4]{0:T(128)S(1)} %pad_add_fusion.place_ref, bf16[4,2,2048]{2,1,0:T(2,128)(2,1)S(1)} %get-tuple-element.22.refs_0_, bf16[4,2,2048]{2,1,0:T(2,128)(2,1)S(1)} %collective-permute-done.4.refs_1_, bf16[4,2,2048]{2,1,0:T(2,128)(2,1)S(1)} %collective-permute-done.5.refs_2_, ...), custom_call_target="tpu_custom_call" | custom-call | flops 1000000 | bytes 1000000 | tf_op jit(solution)/shard_map/pallas_call | solution.py:247
  83.4 0.9 %shard_map.102.refs_2_ = bf16[192,4096]{1,0:T(8,128)(2,1)} custom-call(s32[1]{0:T(128)} %bitcast.core_ref.refs_0_, bf16[192,2048]{1,0:T(8,128)(2,1)S(1)} %shard_map.101.refs_1_), custom_call_target="tpu_custom_call" | custom-call | flops 1000000 | bytes 1000000 | tf_op jit(solution)/shard_map/pallas_call | solution.py:163
  84.3 0.9 %shard_map.103 = bf16[192,4096]{1,0:T(8,128)(2,1)} custom-call(s32[1]{0:T(128)} %bitcast.core_ref.refs_0_, bf16[192,2048]{1,0:T(8,128)(2,1)S(1)} %collective-permute-done.7.refs_1_, bf16[192,4096]{1,0:T(8,128)(2,1)} %shard_map.102.refs_2_), custom_call_target="tpu_custom_call", output_to_operand_aliasing={{}: (2, {})} | custom-call | flops 1000000 | bytes 1000000 | tf_op jit(solution)/shard_map/pallas_call | solution.py:163
  (5 shorter events, 0.0 us)
Async XLA Ops:
  5.7 4.7 %collective-permute-start = (bf16[192,2048]{1,0:T(8,128)(2,1)S(1)}, bf16[192,2048]{1,0:T(8,128)(2,1)S(1)}, u32[]{:S(2)}, u32[]{:S(2)}) collective-permute-start(bf16[192,2048]{1,0:T(8,128)(2,1)S(1)} %get-tuple-element.15), channel_id=1, source_target_pairs={{0,1},{1,0},{2,3},{3,2},{4,5},{5,4},{6,7},{7,6},{8,9},{9,8},{10,11... | collective-permute-start | bytes 2359304 | tf_op jit(solution)/shard_map/ppermute | solution.py:209
  10.4 11.8 %copy-start = (bf16[16,2,2048]{2,1,0:T(2,128)(2,1)S(1)}, bf16[16,2,2048]{2,1,0:T(2,128)(2,1)}, u32[]{:S(2)}) copy-start(bf16[16,2,2048]{2,1,0:T(2,128)(2,1)} %kv_ref.1) | copy-start | bytes 393220
  10.4 11.8 %copy-start.1 = (s32[16,16]{1,0:T(8,128)S(1)}, s32[16,16]{1,0:T(8,128)}, u32[]{:S(2)}) copy-start(s32[16,16]{1,0:T(8,128)} %dest_ref.1) | copy-start | bytes 3076
  10.4 11.8 %copy-start.2 = (s32[16]{0:T(128)S(1)}, s32[16]{0:T(128)}, u32[]{:S(2)}) copy-start(s32[16]{0:T(128)} %lengths_ref.1) | copy-start | bytes 196
  11.4 31.2 %all-to-all-start = ((bf16[24,8,2048]{2,1,0:T(8,128)(2,1)}), bf16[24,8,2048]{2,1,0:T(8,128)(2,1)S(1)}, u32[]{:S(2)}, u32[]{:S(2)}) async-start(bf16[24,8,2048]{2,1,0:T(8,128)(2,1)} %bitcast.8), calls=%async_computation | async-start | bytes 1572864 | tf_op jit(solution)/shard_map/all_to_all | solution.py:227
  23.4 10.2 %collective-permute-start.1 = (bf16[4,2,2048]{2,1,0:T(2,128)(2,1)S(1)}, bf16[4,2,2048]{2,1,0:T(2,128)(2,1)S(1)}, u32[]{:S(2)}, u32[]{:S(2)}) collective-permute-start(bf16[4,2,2048]{2,1,0:T(2,128)(2,1)S(1)} %get-tuple-element.19), channel_id=1, source_target_pairs={{0,48},{48,96},{96,144},{144,0},{1,49},{49,97},{97,145},{145,1},{2... | collective-permute-start | bytes 98312 | tf_op jit(solution)/shard_map/ppermute | solution.py:184
  26.2 7.3 %collective-permute-start.2 = (bf16[4,2,2048]{2,1,0:T(2,128)(2,1)S(1)}, bf16[4,2,2048]{2,1,0:T(2,128)(2,1)S(1)}, u32[]{:S(2)}, u32[]{:S(2)}) collective-permute-start(bf16[4,2,2048]{2,1,0:T(2,128)(2,1)S(1)} %get-tuple-element.20), channel_id=1, source_target_pairs={{0,96},{48,144},{96,0},{144,48},{1,97},{49,145},{97,1},{145,49},{2... | collective-permute-start | bytes 98312 | tf_op jit(solution)/shard_map/ppermute | solution.py:184
  29.6 5.0 %collective-permute-start.3 = (bf16[4,2,2048]{2,1,0:T(2,128)(2,1)S(1)}, bf16[4,2,2048]{2,1,0:T(2,128)(2,1)S(1)}, u32[]{:S(2)}, u32[]{:S(2)}) collective-permute-start(bf16[4,2,2048]{2,1,0:T(2,128)(2,1)S(1)} %get-tuple-element.21), channel_id=1, source_target_pairs={{0,144},{48,0},{96,48},{144,96},{1,145},{49,1},{97,49},{145,97},{2... | collective-permute-start | bytes 98312 | tf_op jit(solution)/shard_map/ppermute | solution.py:184
  43.8 32.2 %all-to-all-start.1 = ((bf16[24,8,2048]{2,1,0:T(8,128)(2,1)}), bf16[24,8,2048]{2,1,0:T(8,128)(2,1)S(1)}, u32[]{:S(2)}, u32[]{:S(2)}) async-start(bf16[24,8,2048]{2,1,0:T(8,128)(2,1)} %shard_map.100), calls=%async_computation.1 | async-start | bytes 1572864 | tf_op jit(solution)/shard_map/all_to_all | solution.py:244
  50.4 25.7 %collective-permute-start.4 = (bf16[4,2,2048]{2,1,0:T(2,128)(2,1)S(1)}, bf16[4,2,2048]{2,1,0:T(2,128)(2,1)S(1)}, u32[]{:S(2)}, u32[]{:S(2)}) collective-permute-start(bf16[4,2,2048]{2,1,0:T(2,128)(2,1)S(1)} %get-tuple-element.23.refs_1_), channel_id=1, source_target_pairs={{0,384},{192,576},{384,0},{576,192},{1,385},{193,577},{385,1},{577... | collective-permute-start | bytes 98312 | tf_op jit(solution)/shard_map/ppermute | solution.py:184
  65.4 10.6 %collective-permute-start.5 = (bf16[4,2,2048]{2,1,0:T(2,128)(2,1)S(1)}, bf16[4,2,2048]{2,1,0:T(2,128)(2,1)S(1)}, u32[]{:S(2)}, u32[]{:S(2)}) collective-permute-start(bf16[4,2,2048]{2,1,0:T(2,128)(2,1)S(1)} %get-tuple-element.24.refs_2_), channel_id=1, source_target_pairs={{0,576},{192,0},{384,192},{576,384},{1,577},{193,1},{385,193},{577... | collective-permute-start | bytes 98312 | tf_op jit(solution)/shard_map/ppermute | solution.py:184
  67.4 8.7 %collective-permute-start.6 = (bf16[4,2,2048]{2,1,0:T(2,128)(2,1)S(1)}, bf16[4,2,2048]{2,1,0:T(2,128)(2,1)S(1)}, u32[]{:S(2)}, u32[]{:S(2)}) collective-permute-start(bf16[4,2,2048]{2,1,0:T(2,128)(2,1)S(1)} %get-tuple-element.25.refs_3_), channel_id=1, source_target_pairs={{0,192},{192,384},{384,576},{576,0},{1,193},{193,385},{385,577},{5... | collective-permute-start | bytes 98312 | tf_op jit(solution)/shard_map/ppermute | solution.py:184
  76.1 8.2 %collective-permute-start.7 = (bf16[192,2048]{1,0:T(8,128)(2,1)S(1)}, bf16[192,2048]{1,0:T(8,128)(2,1)S(1)}, u32[]{:S(2)}, u32[]{:S(2)}) collective-permute-start(bf16[192,2048]{1,0:T(8,128)(2,1)S(1)} %shard_map.101.refs_1_), channel_id=1, source_target_pairs={{0,1},{1,0},{2,3},{3,2},{4,5},{5,4},{6,7},{7,6},{8,9},{9,8},{10,11... | collective-permute-start | bytes 2359304 | tf_op jit(solution)/shard_map/ppermute | solution.py:250
